TPU v7x, 32 devices: a whole 2x2x4 slice. The times are simulated.
32 devices in a mesh: edge: 16 (over z, y, core), col: 2 (over x).
Axes of the slice: x: 2, y: 2, z: 4, core: 2. Of those that a mesh axis runs over, the one named last changes fastest.
Arguments:
- head_ids: int32 [131072], P('edge'), may hold values from 0 to 126975, as said below
- relation_ids: int32 [131072], P('edge'), may hold values from 0 to 3199
- tail_ids: int32 [131072], P('edge'), may hold values from 0 to 126975, as said below
- negative_ids: int32 [128, 1024], P('edge'), may hold values from 0 to 126975, as said below
- live_counts: int32 [128], P('edge'), may hold values from 1 to 1024, as said below
- rel_weight: float32 [3200], replicated, may hold values from 0.5 to 2
- rel_count: int32 [3200], replicated, may hold values from 1 to 4
- entity_table: float32 [400, 126976], P('col', 'edge'), may hold values from -0.6 to 0.6
- entity_first: float32 [400, 126976], P('col', 'edge'), may hold values from -0.3 to 0.3
- entity_second: float32 [400, 126976], P('col', 'edge'), may hold values from 0.0025 to 0.01
- relation_table: float32 [3200, 400], P('edge', 'col'), may hold values from -0.6 to 0.6
- relation_first: float32 [3200, 400], P('edge', 'col'), may hold values from -1.2 to 1.2
- relation_second: float32 [3200, 400], P('edge', 'col'), may hold values from 0.04 to 0.16
Outputs:
- loss_pair: float32 [2], replicated
- new_entity: float32 [400, 126976], P('col', 'edge')
- new_entity_first: float32 [400, 126976], P('col', 'edge')
- new_entity_second: float32 [400, 126976], P('col', 'edge')
- new_relation: float32 [3200, 400], P('edge', 'col')
- new_relation_first: float32 [3200, 400], P('edge', 'col')
- new_relation_second: float32 [3200, 400], P('edge', 'col')
Inputs may be any that keep to these rules, and one draw needn't show every extreme that they name: `head_ids`: entity ids. Of the ids that one index of edge names (its heads, tails and negative tails together), at most 2048 lie among the entities of any one index of edge, and exactly 2048 among those of one of them. `tail_ids`: as for head_ids. `negative_ids`: as for head_ids. `live_counts`: some block has all 1024 slots live.
All inputs are finite; a program needn't handle non-finite values.
Results may differ from a plain program's by a relative error of at most 0.005.
Values may be sent and summed in bfloat16 or wider, within the bound.
No kernel may reach another device: no remote copies, remote signals or barrier semaphores. Data moves between devices by JAX's collectives and lax.ppermute only.
A program may use at most 256 MiB of HBM per device.

v0:
```python
import jax
import jax.numpy as jnp
from jax import lax
from jax.sharding import PartitionSpec as P

STEP = 5


MARGIN = 0.1
LEARN_RATE = 0.1
BETA_ONE = 0.5
BETA_TWO = 0.5
EPSILON = 1e-08
DECAY = 0.01
FIRST_DIMS = (((0,), (0,)), ((), ()))
SECOND_DIMS = (((1,), (1,)), ((), ()))
MIDDLE_DIMS = (((1,), (0,)), ((), ()))


def adamw_update(weights, gradient, first, second):
    new_first = BETA_ONE * first + (1.0 - BETA_ONE) * gradient
    new_second = BETA_TWO * second + (1.0 - BETA_TWO) * gradient * gradient
    first_hat = new_first / (1.0 - BETA_ONE**STEP)
    second_hat = new_second / (1.0 - BETA_TWO**STEP)
    updated = weights - LEARN_RATE * (
        first_hat / (jnp.sqrt(second_hat) + EPSILON) + DECAY * weights
    )
    return (updated, new_first, new_second)


def split_blocks(columns, blocks):
    width_own = columns.shape[0]
    return columns.reshape(width_own, blocks, -1).transpose(1, 0, 2)


def join_blocks(stacked):
    return stacked.transpose(1, 0, 2).reshape(stacked.shape[1], -1)


def shards(
    head_ids,
    relation_ids,
    tail_ids,
    negative_ids,
    live_counts,
    rel_weight,
    rel_count,
    entity_table,
    entity_first,
    entity_second,
    relation_table,
    relation_first,
    relation_second,
):
    groups = lax.axis_size("edge")
    width_own, ent_rows = entity_table.shape
    blocks, neg_count = negative_ids.shape
    block_len = head_ids.shape[0] // blocks
    edge_count = blocks * block_len
    all_ids = jnp.concatenate([head_ids, tail_ids, negative_ids.reshape(-1)])
    id_count = all_ids.shape[0]
    capacity = (4 * id_count + 3 * groups - 1) // (3 * groups)
    owners = all_ids // ent_rows
    local_rows = all_ids - owners * ent_rows
    one_hot = (owners[:, None] == jnp.arange(groups, dtype=jnp.int32)[None, :]).astype(jnp.int32)
    ranks = jnp.sum(one_hot * (jnp.cumsum(one_hot, axis=0) - 1), axis=1)
    slots = owners * capacity + ranks
    requests = (
        jnp.zeros((groups * capacity,), jnp.int32)
        .at[slots]
        .set(local_rows)
        .reshape(groups, capacity)
    )
    slot_source = (
        jnp.zeros((groups * capacity,), jnp.int32)
        .at[slots]
        .set(jnp.arange(id_count, dtype=jnp.int32))
    )
    slot_filled = jnp.zeros((groups * capacity,), jnp.bool_).at[slots].set(True)
    asked = lax.all_to_all(requests, "edge", split_axis=0, concat_axis=0, tiled=True)
    asked_flat = asked.reshape(-1)
    found = jnp.take(entity_table.astype(jnp.bfloat16), asked_flat, axis=1).reshape(
        width_own, groups, capacity
    )
    returned = lax.all_to_all(found, "edge", split_axis=1, concat_axis=1, tiled=True).reshape(
        width_own, groups * capacity
    )
    fetched = jnp.take(returned, slots, axis=1)
    head_cols = split_blocks(fetched[:, :edge_count], blocks)
    tail_cols = split_blocks(fetched[:, edge_count : 2 * edge_count], blocks)
    neg_cols = split_blocks(fetched[:, 2 * edge_count :], blocks)
    rel_table = lax.all_gather(relation_table.astype(jnp.bfloat16), "edge", axis=0, tiled=True)
    rel_cols = split_blocks(jnp.take(rel_table.T, relation_ids, axis=1), blocks)
    rel_total = rel_weight.shape[0]
    rel_scale = rel_weight * (rel_total / jnp.sum(rel_weight)) / rel_count.astype(jnp.float32)
    live_mask = (jnp.arange(block_len, dtype=jnp.int32)[None, :] < live_counts[:, None]).astype(
        jnp.float32
    )
    edge_weight = rel_scale[relation_ids].reshape(blocks, block_len) * live_mask / neg_count

    def block_step(loss_sum, pieces):
        head_part, rel_part, tail_part, neg_part, weight_part = pieces
        shifted = head_part.astype(jnp.float32) + rel_part.astype(jnp.float32)
        shifted_low = shifted.astype(jnp.bfloat16)
        neg_float = neg_part.astype(jnp.float32)
        offset = shifted - tail_part.astype(jnp.float32)
        head_full, rel_full, tail_full, neg_full = (
            lax.all_gather(head_part, "col", axis=0, tiled=True),
            lax.all_gather(rel_part, "col", axis=0, tiled=True),
            lax.all_gather(tail_part, "col", axis=0, tiled=True),
            lax.all_gather(neg_part, "col", axis=0, tiled=True),
        )
        shift_full = head_full.astype(jnp.float32) + rel_full.astype(jnp.float32)
        neg_full_float = neg_full.astype(jnp.float32)
        positive = jnp.sum((shift_full - tail_full.astype(jnp.float32)) ** 2, axis=0)
        crossed = lax.dot_general(
            shift_full.astype(jnp.bfloat16),
            neg_full,
            FIRST_DIMS,
            preferred_element_type=jnp.float32,
        )
        negative = (
            jnp.sum(shift_full * shift_full, axis=0)[:, None]
            - 2.0 * crossed
            + jnp.sum(neg_full_float * neg_full_float, axis=0)[None, :]
        )
        margins = MARGIN + positive[:, None] - negative
        loss_sum = loss_sum + jnp.sum(weight_part[:, None] * jax.nn.softplus(margins))
        slopes = weight_part[:, None] * jax.nn.sigmoid(margins)
        row_sums = jnp.sum(slopes, axis=1)[None, :]
        col_sums = jnp.sum(slopes, axis=0)[None, :]
        slopes_low = (2.0 * slopes).astype(jnp.bfloat16)
        grad_shift = (
            2.0 * row_sums * offset
            - 2.0 * row_sums * shifted
            + lax.dot_general(neg_part, slopes_low, SECOND_DIMS, preferred_element_type=jnp.float32)
        )
        grad_tail = -2.0 * row_sums * offset
        grad_neg = -2.0 * col_sums * neg_float + lax.dot_general(
            shifted_low, slopes_low, MIDDLE_DIMS, preferred_element_type=jnp.float32
        )
        return (loss_sum, (grad_shift, grad_tail, grad_neg))

    loss_sum, (grad_shift, grad_tail, grad_neg) = lax.scan(
        block_step,
        jnp.zeros((), jnp.float32),
        (head_cols, rel_cols, tail_cols, neg_cols, edge_weight),
    )
    loss_whole, live_whole = lax.psum((loss_sum, jnp.sum(live_mask)), "edge")
    loss_pair = jnp.stack([loss_whole, live_whole])
    shift_flat = join_blocks(grad_shift)
    id_grads = jnp.concatenate([shift_flat, join_blocks(grad_tail), join_blocks(grad_neg)], axis=1)
    outgoing = jnp.where(
        slot_filled[None, :], jnp.take(id_grads, slot_source, axis=1), 0.0
    ).reshape(width_own, groups, capacity)
    incoming = lax.all_to_all(outgoing, "edge", split_axis=1, concat_axis=1, tiled=True).reshape(
        width_own, groups * capacity
    )
    entity_grad = jax.ops.segment_sum(incoming.T, asked_flat, num_segments=ent_rows).T
    rel_terms = jax.ops.segment_sum(shift_flat.T, relation_ids, num_segments=rel_total)
    relation_grad = lax.psum_scatter(rel_terms, "edge", scatter_dimension=0, tiled=True)
    new_entity, new_entity_first, new_entity_second = adamw_update(
        entity_table, entity_grad, entity_first, entity_second
    )
    new_relation, new_relation_first, new_relation_second = adamw_update(
        relation_table, relation_grad, relation_first, relation_second
    )
    return (
        loss_pair,
        new_entity,
        new_entity_first,
        new_entity_second,
        new_relation,
        new_relation_first,
        new_relation_second,
    )


def solution(mesh):
    placed = (
        P("edge"),
        P("edge"),
        P("edge"),
        P("edge", None),
        P("edge"),
        P(),
        P(),
        P("col", "edge"),
        P("col", "edge"),
        P("col", "edge"),
        P("edge", "col"),
        P("edge", "col"),
        P("edge", "col"),
    )
    return jax.shard_map(
        shards,
        mesh=mesh,
        in_specs=placed,
        out_specs=(
            P(),
            P("col", "edge"),
            P("col", "edge"),
            P("col", "edge"),
            P("edge", "col"),
            P("edge", "col"),
            P("edge", "col"),
        ),
        check_vma=False,
    )
```

profile of v0, /device:TPU:16, one launch (start us, length us, event | category | flops | bytes accessed | tf_op | source)
XLA Modules:
  0.0 2339.9 jit_solution(17955182988779287076)
XLA Ops:
  17.9 90.8 %scatter_custom_fusion = s32[32768]{0:T(1024)} fusion(s32[24576]{0:T(1024)S(1)} %bitcast.175, s32[24576]{0:T(1024)S(1)} %get-tuple-element.143, s32[]{:T(128)} %copy.170), kind=kCustom, calls=%fused_computation.102 | custom fusion | bytes 131076 | tf_op jit(solution)/shard_map/scatter | solution.py:71
  122.0 123.4 %gather_fusion.1 = bf16[32768,200]{1,0:T(8,128)(2,1)} fusion(bf16[200,7936]{0,1:T(8,128)(2,1)} %copy.116, s32[32768]{0:T(1024)S(1)} %broadcast_clamp_fusion), kind=kCustom, calls=%fused_computation.1 | custom fusion | bytes 26345472 | tf_op jit(solution)/shard_map/jit(_take)/gather | solution.py:82
  245.4 20.9 copy.117
  284.9 45.5 %gather_fusion = f32[8192]{0:T(1024)S(1)} fusion(f32[3200]{0:T(1024)S(1)} %convert_divide_fusion, s32[8192]{0:T(1024)S(1)} %fusion.40), kind=kCustom, calls=%fused_computation | custom fusion | bytes 98304 | tf_op jit(solution)/shard_map/gather | solution.py:99
  330.5 90.4 %scatter_custom_fusion.2 = s32[32768]{0:T(1024)S(1)} fusion(s32[24576]{0:T(1024)S(1)} %bitcast.176, s32[24576]{0:T(1024)S(1)} %iota.15, s32[]{:T(128)} %copy.170), kind=kCustom, calls=%fused_computation.100 | custom fusion | bytes 131076 | tf_op jit(solution)/shard_map/scatter | solution.py:77
  421.6 102.6 %scatter_custom_fusion.1 = pred[32768]{0:T(1024)(128)(4,1)S(1)} fusion(s32[24576]{0:T(1024)S(1)} %bitcast.177, pred[24576]{0:T(1024)(128)(4,1)S(1)} %broadcast.275, pred[]{:T(512)} %constant.137.clone.1), kind=kCustom, calls=%fused_computation.104 | custom fusion | bytes 32769 | tf_op jit(solution)/shard_map/scatter | solution.py:79
  527.6 32.8 %gather_fusion.3 = bf16[8192,200]{1,0:T(8,128)(2,1)} fusion(bf16[200,3200]{0,1:T(8,128)(2,1)} %bitcast.151, s32[8192]{0:T(1024)S(1)} %fusion.40), kind=kCustom, calls=%fused_computation.3 | custom fusion | bytes 6586368 | tf_op jit(solution)/shard_map/jit(_take)/gather | solution.py:93
  576.3 20.7 copy.118
  597.0 98.7 %gather_fusion.2 = bf16[24576,200]{1,0:T(8,128)(2,1)} fusion(bf16[200,32768]{0,1:T(8,128)(2,1)} %bitcast.150, s32[24576]{0:T(1024)S(1)} %copy-done.4), kind=kCustom, calls=%fused_computation.2 | custom fusion | bytes 19759104 | tf_op jit(solution)/shard_map/jit(_take)/gather | solution.py:88
  695.7 13.8 select_bitcast_fusion
  732.9 469.1 %while.16 = (s32[]{:T(128)}, f32[]{:T(128)}, f32[8,200,1024]{2,1,0:T(8,128)}, f32[8,200,1024]{2,1,0:T(8,128)}, f32[8,200,1024]{2,1,0:T(8,128)}, /*index=5*/f32[8...) while((s32[]{:T(128)}, f32[]{:T(128)}, ...), condition=%wide.region_13.14_spmd, body=%wide.region_6.0_spmd.sunk | while | flops 1711848448 | bytes 33151632 | solution.py:144
  733.1 11.7 all-gather.10
  745.9 10.8 all-gather.11
  815.5 11.1 all-gather.9
  852.1 12.1 all-gather.10
  865.3 11.3 all-gather.11
  877.6 10.9 all-gather.9
  969.2 12.4 all-gather.10
  982.6 12.1 all-gather.11
  1061.4 11.0 all-gather.8
  1087.8 12.9 all-gather.10
  1122.1 10.7 all-gather.8
  1227.5 21.1 pad_maximum_fusion
  1248.6 130.7 %gather_fusion.4 = f32[32768,200]{1,0:T(8,128)} fusion(f32[200,24576]{0,1:T(8,128)} %pad_maximum_fusion, s32[32768]{0:T(1024)S(1)} %copy-done.3), kind=kCustom, calls=%fused_computation.4 | custom fusion | bytes 52559872 | tf_op jit(solution)/shard_map/jit(_take)/gather | solution.py:154
  1379.4 31.2 %copy.127 = f32[200,16,2048]{2,0,1:T(8,128)} copy(f32[200,16,2048]{0,2,1:T(8,128)} %bitcast.152) | data formatting | bytes 52428800 | tf_op jit(solution)/shard_map/jit(_take)/gather | solution.py:154
  1410.6 20.2 select_select_fusion
  1438.0 46.5 %scatter_custom_fusion.4 = f32[3200,200]{1,0:T(8,128)} fusion(s32[8192]{0:T(1024)} %param.16, f32[8192,200]{1,0:T(8,128)} %bitcast.157, f32[]{:T(128)} %constant.77.clone.1), kind=kCustom, calls=%fused_computation.67 | custom fusion | flops 1638400 | bytes 2560512 | tf_op jit(solution)/shard_map/scatter-add | solution.py:160
  1509.8 531.3 %all-reduce.2 = (f32[1]{0:T(128)}, f32[1]{0:T(128)}) all-reduce(f32[1]{0:T(128)} %bitcast.33, f32[1]{0:T(128)} %bitcast.32), channel_id=1, replica_groups=mesh['edge'=16,'col'=2] {'edge'}, use_global_device_ids=true, to_apply=%region_16.17 | all-reduce | flops 2 | bytes 16 | tf_op jit(solution)/shard_map/psum | solution.py:149
  2044.8 19.1 copy.139
  2063.9 29.1 %copy.129 = f32[32768,200]{1,0:T(8,128)} copy(f32[32768,200]{0,1:T(8,128)} %bitcast.153) | data formatting | bytes 52428800 | tf_op jit(solution)/shard_map/transpose | solution.py:159
  2093.1 192.3 %scatter_custom_fusion.3 = f32[7936,200]{1,0:T(8,128)} fusion(s32[32768]{0:T(1024)} %bitcast.171, f32[32768,200]{1,0:T(8,128)} %copy.129, f32[]{:T(128)} %constant.77.clone.1), kind=kCustom, calls=%fused_computation.60 | custom fusion | flops 6553600 | bytes 6349312 | tf_op jit(solution)/shard_map/scatter-add | solution.py:159
  2285.4 21.7 multiply_subtract_fusion
  (236 shorter events, 508.9 us)
Async XLA Ops:
  7.2 8.7 copy-start.13
  7.2 8.6 copy-start.11
  17.9 90.8 %copy-start.5 = (s32[24576,1]{0,1:T(1,128)}, s32[24576,1]{0,1:T(1,128)S(1)}, u32[]{:S(2)}) copy-start(s32[24576,1]{0,1:T(1,128)S(1)} %compare_select_fusion.2) | copy-start | bytes 294916
  108.7 13.1 all-to-all-start
  121.8 144.5 %copy-start = (s32[16,1,2048]{2,1,0:T(1,128)}, s32[16,1,2048]{2,1,0:T(1,128)S(1)}, u32[]{:S(2)}) copy-start(s32[16,1,2048]{2,1,0:T(1,128)S(1)} %all-to-all-done) | copy-start | bytes 393220
  276.6 6.2 copy-start.1
  276.6 6.9 copy-start.14
  276.6 8.2 copy-start.15
  276.6 8.3 copy-start.12
  276.6 299.7 %all-to-all-start.1 = ((bf16[200,16,2048]{2,0,1:T(8,128)(2,1)}), bf16[200,16,2048]{2,0,1:T(8,128)(2,1)}, u32[]{:S(2)}, u32[]{:S(2)}) async-start(bf16[200,16,2048]{2,0,1:T(8,128)(2,1)} %broadcast_select_fusion), calls=%async_computation.1 | async-start | bytes 26214400 | tf_op jit(solution)/shard_map/all_to_all | solution.py:85
  282.8 244.9 %all-gather.14.cloned.1.call-start = ((), (), s32[]{:S(2)}) async-start(), calls=%async_computation.4 | async-start | bytes 1740800 | tf_op jit(solution)/shard_map/all_gather | solution.py:92
  284.9 45.6 %copy-start.6 = (s32[24576,1]{0,1:T(1,128)S(1)}, s32[24576,1]{0,1:T(1,128)}, u32[]{:S(2)}) copy-start(s32[24576,1]{0,1:T(1,128)} %copy-done.5) | copy-start | bytes 294916
  284.9 240.0 %copy-start.16 = (s32[8]{0:T(128)S(1)}, s32[8]{0:T(128)}, u32[]{:S(2)}) copy-start(s32[8]{0:T(128)} %param.19) | copy-start | bytes 100
  568.9 28.2 %copy-start.4 = (s32[24576]{0:T(1024)S(1)}, s32[24576]{0:T(1024)}, u32[]{:S(2)}) copy-start(s32[24576]{0:T(1024)} %broadcast_clamp_fusion.1) | copy-start | bytes 294916
  1227.5 21.1 copy-start.3
  1379.4 31.2 %copy-start.9 = (pred[16,2048]{1,0:T(8,128)(4,1)S(1)}, pred[16,2048]{1,0:T(8,128)(4,1)}, u32[]{:S(2)}) copy-start(pred[16,2048]{1,0:T(8,128)(4,1)} %broadcast_in_dim.114) | copy-start | bytes 98308
  1379.4 31.2 %copy-start.10 = (pred[16,2048]{1,0:T(8,128)(4,1)S(1)}, pred[16,2048]{1,0:T(8,128)(4,1)}, u32[]{:S(2)}) copy-start(pred[16,2048]{1,0:T(8,128)(4,1)} %broadcast_in_dim.112) | copy-start | bytes 98308
  1430.8 614.0 %all-to-all-start.2 = ((f32[200,16,2048]{2,0,1:T(8,128)}), f32[200,16,2048]{2,0,1:T(8,128)}, u32[]{:S(2)}, u32[]{:S(2)}) async-start(f32[200,16,2048]{2,0,1:T(8,128)} %select_select_fusion), calls=%async_computation.2 | async-start | bytes 52428800 | tf_op jit(solution)/shard_map/all_to_all | solution.py:156
  1438.0 605.0 %reduce-scatter.2.cloned.1.call-start = ((), (), s32[]{:S(2)}) async-start(), calls=%async_computation.5 | async-start | bytes 3481600 | tf_op jit(solution)/shard_map/reduce_scatter | solution.py:161
  1501.4 541.6 %copy-start.2 = (f32[200,200]{1,0:T(8,128)S(1)}, f32[200,200]{1,0:T(8,128)}, u32[]{:S(2)}) copy-start(f32[200,200]{1,0:T(8,128)} %param.25) | copy-start | bytes 480004
  1501.4 541.6 %copy-start.7 = (f32[200,200]{1,0:T(8,128)S(1)}, f32[200,200]{1,0:T(8,128)}, u32[]{:S(2)}) copy-start(f32[200,200]{1,0:T(8,128)} %param.26) | copy-start | bytes 480004
  1501.4 541.6 %copy-start.8 = (f32[200,200]{1,0:T(8,128)S(1)}, f32[200,200]{1,0:T(8,128)}, u32[]{:S(2)}) copy-start(f32[200,200]{1,0:T(8,128)} %param.27) | copy-start | bytes 480004
Sparse Core Ops, SparseCore 0:
  286.3 183.9 all-gather.13
  1484.7 402.1 reduce-scatter.1
where the time goes:
time: 2350 us; the launch traced here: 2340 us
  local copies, waits for them, and re-layouts  983 us (42%)
  blocking collectives  848 us (36%)
  other arithmetic  369 us (16%)
  matrix products  91.9 us (4%)
    psum x1, blocking collectives, shards(): loss_whole, live_whole = lax.psum((loss_sum, jnp.sum(live_mask)), 'edge')  531 us
    scatter-add x1, other arithmetic, shards(): jax.ops.segment_sum(incoming.T, asked_flat, num_segments=ent_rows)  192 us
    gather x2, local copies, waits for them, and re-layouts, shards(): jnp.take(id_grads, slot_source, axis=1)  162 us
    gather x2, local copies, waits for them, and re-layouts, shards(): jnp.take(entity_table.astype(jnp.bfloat16), asked_flat, axis=1)  144 us
    scatter x1, local copies, waits for them, and re-layouts, shards(): slot_filled = jnp.zeros((groups * capacity,), jnp.bool_).at[slots].set(True)  103 us
    gather x1, local copies, waits for them, and re-layouts, shards(): fetched = jnp.take(returned, slots, axis=1)  98.7 us
    scatter x1, local copies, waits for them, and re-layouts, shards(): requests = jnp.zeros((groups * capacity,), jnp.int32).at[slots].set(local...  90.8 us
    scatter x1, local copies, waits for them, and re-layouts, shards(): slot_source = jnp.zeros((groups * capacity,), jnp.int32).at[slots].set(jn...  90.4 us
  transfers between devices with their start and end apart: 5, of which 1 were waited for; matrix products, arithmetic and copies ran while one was open for 16% of the time, Pallas kernels for 0%

commit v1 on v0

v1 whole, which is shorter than its diff:
```python
import functools

import jax
import jax.numpy as jnp
from jax import lax
from jax.experimental import pallas as pl
from jax.experimental.pallas import tpu as pltpu
from jax.sharding import PartitionSpec as P

STEP = 5


MARGIN = 0.1
LEARN_RATE = 0.1
BETA_ONE = 0.5
BETA_TWO = 0.5
EPSILON = 1e-08
DECAY = 0.01
LANES = 128
UNROLL = 8
PARTS = 4
NN = (((1,), (0,)), ((), ()))
NT = (((1,), (1,)), ((), ()))
TN = (((0,), (0,)), ((), ()))
F32 = jnp.float32
BF16 = jnp.bfloat16
SMEM = pltpu.SMEM
VMEM = pltpu.VMEM


def params():
    return pltpu.CompilerParams(vmem_limit_bytes=60 << 20)


def cost(flops, moved):
    return pl.CostEstimate(flops=int(flops), bytes_accessed=int(moved), transcendentals=0)


def whole(space):
    return pl.BlockSpec(memory_space=space)


def adamw_update(weights, gradient, first, second):
    new_first = BETA_ONE * first + (1.0 - BETA_ONE) * gradient
    new_second = BETA_TWO * second + (1.0 - BETA_TWO) * gradient * gradient
    first_hat = new_first / (1.0 - BETA_ONE**STEP)
    second_hat = new_second / (1.0 - BETA_TWO**STEP)
    updated = weights - LEARN_RATE * (
        first_hat / (jnp.sqrt(second_hat) + EPSILON) + DECAY * weights
    )
    return (updated, new_first, new_second)


def width_slices(width):
    return [(at, min(LANES, width - at)) for at in range(0, width, LANES)]


def owner_lists(all_ids, groups, capacity, ent_rows):
    count = all_ids.shape[0]
    owners = all_ids // ent_rows
    local_rows = all_ids - owners * ent_rows
    chunk = 256
    mine = owners[None, :] == jnp.arange(groups, dtype=jnp.int32)[:, None]
    mine = mine.astype(BF16).reshape(groups, count // chunk, chunk)
    before = jnp.triu(jnp.ones((chunk, chunk), BF16), 1)
    inner = jnp.dot(mine, before, preferred_element_type=F32)
    sums = jnp.sum(mine.astype(F32), axis=2)
    carry = jnp.cumsum(sums, axis=1) - sums
    ranks = jnp.sum(mine.astype(F32) * (inner + carry[:, :, None]), axis=0)
    ranks = ranks.astype(jnp.int32).reshape(count)
    counts = jnp.sum(sums, axis=1).astype(jnp.int32)
    high = owners * (capacity // LANES) + ranks // LANES
    low = ranks % LANES
    tall = groups * capacity // LANES
    left = (jnp.arange(tall, dtype=jnp.int32)[:, None] == high[None, :]).astype(BF16)
    right = (jnp.arange(LANES, dtype=jnp.int32)[:, None] == low[None, :]).astype(BF16)
    places = jnp.arange(1, count + 1, dtype=jnp.int32)
    parts = jnp.stack([places // 256, places % 256, local_rows // 256, local_rows % 256])
    right = (parts.astype(BF16)[:, None, :] * right[None]).reshape(PARTS * LANES, count)
    found = lax.dot_general(left, right, NT, preferred_element_type=F32).astype(jnp.int32)
    found = found.reshape(tall, PARTS, LANES)
    place = found[:, 0] * 256 + found[:, 1]
    place_list = jnp.where(place > 0, place - 1, count).reshape(groups, capacity)
    row_list = jnp.where(place > 0, found[:, 2] * 256 + found[:, 3], ent_rows)
    return place_list, row_list.reshape(groups, capacity), counts


def relation_rows_kernel(n_slices, ids_ref, *refs):
    tables, outs = refs[:n_slices], refs[n_slices:]
    count = outs[0].shape[0]

    def body(step, carry):
        for lane in range(UNROLL):
            at = step * UNROLL + lane
            row = ids_ref[at]
            for table, out in zip(tables, outs):
                out[pl.ds(at, 1), :] = table[pl.ds(row, 1), :]
        return carry

    lax.fori_loop(0, count // UNROLL, body, 0)


def relation_rows(relation_ids, tables):
    count = relation_ids.shape[0]
    n = len(tables)
    return pl.pallas_call(
        functools.partial(relation_rows_kernel, n),
        out_shape=[jax.ShapeDtypeStruct((count, LANES), F32)] * n,
        in_specs=[whole(SMEM)] + [whole(VMEM)] * n,
        out_specs=[whole(VMEM)] * n,
        compiler_params=params(),
        cost_estimate=cost(0, 30e6 * n),
        name="relation_rows",
    )(relation_ids, *tables)


def fetch_kernel(capacity, counts_ref, place_ref, row_ref, dense_ref, out_ref, rows):
    shard = pl.program_id(0)
    depth, ent_rows = dense_ref.shape[1:]
    step_cols = 256 if ent_rows % 256 == 0 else 128

    if depth < LANES:

        @pl.when(shard == 0)
        def _():
            rows[...] = jnp.zeros_like(rows)

    def turn(step, carry):
        cols = pl.ds(pl.multiple_of(step * step_cols, step_cols), step_cols)
        rows[cols, :depth] = dense_ref[0, :, cols].astype(F32).T
        return carry

    lax.fori_loop(0, ent_rows // step_cols, turn, 0)
    trips = (counts_ref[shard] + UNROLL - 1) // UNROLL

    def body(step, carry):
        for lane in range(UNROLL):
            at = shard * capacity + step * UNROLL + lane
            out_ref[pl.ds(place_ref[at], 1), :] = rows[pl.ds(row_ref[at], 1), :]
        return carry

    lax.fori_loop(0, trips, body, 0)


def fetch(counts, place_list, row_list, dense):
    groups, depth, ent_rows = dense.shape
    capacity = place_list.shape[1]
    id_count = 3 * groups * capacity // 4
    return pl.pallas_call(
        functools.partial(fetch_kernel, capacity),
        out_shape=jax.ShapeDtypeStruct((id_count + 8, LANES), F32),
        grid=(groups,),
        in_specs=[whole(SMEM)] * 3
        + [pl.BlockSpec((1, depth, ent_rows), lambda shard: (shard, 0, 0))],
        out_specs=whole(VMEM),
        scratch_shapes=[pltpu.VMEM((ent_rows + 8, LANES), F32)],
        compiler_params=params(),
        cost_estimate=cost(0, 250e6),
        name="fetch_rows",
    )(counts, place_list.reshape(-1), row_list.reshape(-1), dense)


def prepare_kernel(depth, head_ref, tail_ref, neg_ref, rel_ref, off_ref, tail_out, pair_ref, sums_ref):
    lane = lax.broadcasted_iota(jnp.int32, head_ref.shape, 1)
    inside = lane < depth
    rel = rel_ref[...]
    tail = tail_ref[...]
    shifted = head_ref[...] + jnp.where(inside, rel, 0.0)
    off_ref[...] = jnp.where(inside, shifted - tail, rel)
    tail_out[...] = tail.astype(BF16)
    shifted_t = shifted.T
    offset_t = (shifted - tail).T
    neg_t = neg_ref[...].T
    pair_ref[0] = shifted_t[:depth].astype(BF16)
    pair_ref[1] = neg_t[:depth].astype(BF16)
    sums_ref[0:1, :] = jnp.sum(offset_t * offset_t, axis=0, keepdims=True) - jnp.sum(
        shifted_t * shifted_t, axis=0, keepdims=True
    )
    sums_ref[1:2, :] = jnp.sum(neg_t * neg_t, axis=0, keepdims=True)


def prepare(fetched, rel_rows, depth, blocks, block_len):
    edge_count = blocks * block_len

    def rows(at):
        return pl.BlockSpec((block_len, LANES), lambda b: (at * blocks + b, 0))

    return pl.pallas_call(
        functools.partial(prepare_kernel, depth),
        out_shape=[
            jax.ShapeDtypeStruct((edge_count, LANES), F32),
            jax.ShapeDtypeStruct((edge_count, LANES), BF16),
            jax.ShapeDtypeStruct((2, depth, edge_count), BF16),
            jax.ShapeDtypeStruct((2, edge_count), F32),
        ],
        grid=(blocks,),
        in_specs=[rows(0), rows(1), rows(2), rows(0)],
        out_specs=[
            rows(0),
            rows(0),
            pl.BlockSpec((2, depth, block_len), lambda b: (0, 0, b)),
            pl.BlockSpec((2, block_len), lambda b: (0, b)),
        ],
        compiler_params=params(),
        cost_estimate=cost(0, 40e6),
        name="prepare",
    )(fetched, fetched, fetched, rel_rows)


def block_kernel(slices, n_col, live_ref, *refs):
    n = len(slices)
    pairs = [refs[k * n : (k + 1) * n] for k in range(n_col)]
    at = n * n_col
    sums_ref = refs[at]
    offs = refs[at + 1 : at + 1 + n]
    tails = refs[at + 1 + n : at + 1 + 2 * n]
    grads = refs[at + 1 + 2 * n : at + 1 + 3 * n]
    loss_ref = refs[at + 1 + 3 * n]
    shift_scr, neg_scr, cross, slopes, row_bias, row_sum = refs[at + 2 + 3 * n :]
    block = pl.program_id(0)
    length = cross.shape[0]
    width = sum(depth for _, depth in slices)
    for k in range(n_col):
        for (start, depth), pair in zip(slices, pairs[k]):
            shift_scr[k, start : start + depth, :] = pair[0]
            neg_scr[k, start : start + depth, :] = pair[1]
    bias = jnp.sum(sums_ref[:, 0, :], axis=0, keepdims=True) + MARGIN
    neg_norm = jnp.sum(sums_ref[:, 1, :], axis=0, keepdims=True)
    row_bias[...] = jnp.broadcast_to(bias, (LANES, length)).T

    tile = min(256, length)

    def matmul(step, carry):
        part = pl.ds(pl.multiple_of(step * tile, tile), tile)
        total = None
        for k in range(n_col):
            term = lax.dot_general(
                shift_scr[k, :, part], neg_scr[k], TN, preferred_element_type=F32
            )
            total = term if total is None else total + term
        cross[part, :] = total
        return carry

    lax.fori_loop(0, length // tile, matmul, 0)

    live = live_ref[block]
    small = 64

    def pairwise(step, carry):
        loss, cols = carry
        begin = pl.multiple_of(step * small, small)
        part = pl.ds(begin, small)
        place = begin + lax.broadcasted_iota(jnp.int32, (small, 1), 0)
        scale = offs[-1][part, LANES - 1 : LANES]
        weight = jnp.where(place < live, scale, 0.0) / length
        margins = 2.0 * cross[part, :] + (row_bias[part, 0:1] - neg_norm)
        fall = jnp.exp(-jnp.abs(margins))
        under = 1.0 + fall
        inverse = 1.0 / under
        logs = jnp.where(fall < 2.0**-11, fall * (1.0 - 0.5 * fall), jnp.log(under))
        soft = jnp.maximum(margins, 0.0) + logs
        slope = weight * jnp.where(margins >= 0.0, inverse, fall * inverse)
        row_sum[part, :] = jnp.broadcast_to(
            jnp.sum(slope, axis=1, keepdims=True), (small, LANES)
        )
        slopes[part, :] = (2.0 * slope).astype(BF16)
        loss = loss + jnp.sum((weight * soft).reshape(small // 8, 8, length), axis=0)
        cols = cols + jnp.sum(slope.reshape(small // 8, 8, length), axis=0)
        return loss, cols

    zero = jnp.zeros((8, length), F32)
    loss, cols = lax.fori_loop(0, length // small, pairwise, (zero, zero))
    col_sum = jnp.sum(cols, axis=0, keepdims=True)
    loss_part = jnp.sum(loss.reshape(8, length // LANES, LANES), axis=1)

    @pl.when(block == 0)
    def _():
        loss_ref[...] = loss_part

    @pl.when(block > 0)
    def _():
        loss_ref[...] += loss_part

    def edges(step, carry):
        part = pl.ds(pl.multiple_of(step * tile, tile), tile)
        moved = lax.dot_general(slopes[part, :], neg_scr[0], NT, preferred_element_type=F32)
        twice = -2.0 * row_sum[part, :]
        for (start, depth), off, tail, grad in zip(slices, offs, tails, grads):
            grad[0, part, :depth] = (
                twice[:, :depth] * tail[part, :depth].astype(F32) + moved[:, start : start + depth]
            )
            grad[1, part, :] = twice * off[part, :]
        return carry

    lax.fori_loop(0, length // tile, edges, 0)

    moved = lax.dot_general(shift_scr[0], slopes[...], NN, preferred_element_type=F32)
    moved = moved - 2.0 * col_sum * neg_scr[0].astype(F32)
    for (start, depth), grad in zip(slices, grads):
        grad[2, :, :depth] = moved[start : start + depth, :].T


def block_math(live_counts, pairs, sums, offs, tails, slices, block_len):
    n, n_col = len(slices), len(pairs)
    blocks = live_counts.shape[0]
    edge_count = blocks * block_len
    width = sum(depth for _, depth in slices)
    flat = [piece for per_col in pairs for piece in per_col]

    def rows():
        return pl.BlockSpec((block_len, LANES), lambda b: (b, 0))

    return pl.pallas_call(
        functools.partial(block_kernel, slices, n_col),
        out_shape=[jax.ShapeDtypeStruct((3, edge_count, LANES), F32)] * n
        + [jax.ShapeDtypeStruct((8, LANES), F32)],
        grid=(blocks,),
        in_specs=[whole(SMEM)]
        + [
            pl.BlockSpec((2, piece.shape[1], block_len), lambda b: (0, 0, b)) for piece in flat
        ]
        + [pl.BlockSpec((sums.shape[0], 2, block_len), lambda b: (0, 0, b))]
        + [rows() for _ in range(2 * n)],
        out_specs=[pl.BlockSpec((3, block_len, LANES), lambda b: (0, b, 0))] * n
        + [pl.BlockSpec((8, LANES), lambda b: (0, 0))],
        scratch_shapes=[
            pltpu.VMEM((n_col, width, block_len), BF16),
            pltpu.VMEM((n_col, width, block_len), BF16),
            pltpu.VMEM((block_len, block_len), F32),
            pltpu.VMEM((block_len, block_len), BF16),
            pltpu.VMEM((block_len, LANES), F32),
            pltpu.VMEM((block_len, LANES), F32),
        ],
        compiler_params=params(),
        cost_estimate=cost(blocks * 8 * block_len * block_len * width, 200e6),
        name="block_math",
    )(live_counts, *flat, sums, *offs, *tails)


def outgoing_kernel(slices, capacity, begin, counts_ref, place_ref, *refs):
    n = len(slices)
    grads, out_ref, tiles = refs[:n], refs[n], refs[n + 1 :]
    groups, width, chunk = out_ref.shape

    def owner(group, carry):
        wanted = jnp.clip(counts_ref[group] - begin, 0, chunk)

        def body(step, inner):
            for lane in range(UNROLL):
                at = step * UNROLL + lane
                place = place_ref[group * capacity + begin + at]
                for grad, tile in zip(grads, tiles):
                    tile[pl.ds(at, 1), :] = grad[pl.ds(place, 1), :]
            return inner

        lax.fori_loop(0, (wanted + UNROLL - 1) // UNROLL, body, 0)
        for (start, depth), tile in zip(slices, tiles):
            out_ref[group, start : start + depth, :] = tile[...].T[:depth].astype(BF16)
        return carry

    lax.fori_loop(0, groups, owner, 0)


def outgoing(counts, place_list, grads, slices, begin, chunk):
    groups, capacity = place_list.shape
    n = len(slices)
    width = sum(depth for _, depth in slices)
    return pl.pallas_call(
        functools.partial(outgoing_kernel, slices, capacity, begin),
        out_shape=jax.ShapeDtypeStruct((groups, width, chunk), BF16),
        in_specs=[whole(SMEM)] * 2 + [whole(VMEM)] * n,
        out_specs=whole(VMEM),
        scratch_shapes=[pltpu.VMEM((chunk, LANES), F32)] * n,
        compiler_params=params(),
        cost_estimate=cost(0, 80e6),
        name="outgoing",
    )(counts, place_list.reshape(-1), *grads)


def collect_kernel(slices, capacity, begin, first, counts_ref, row_ref, came_ref, *refs):
    n = len(slices)
    olds = () if first else refs[:n]
    refs = refs if first else refs[n:]
    totals, tiles = refs[:n], refs[n:]
    groups, width, chunk = came_ref.shape
    for k in range(n):
        totals[k][...] = jnp.zeros_like(totals[k]) if first else olds[k][...]

    def source(group, carry):
        wanted = jnp.clip(counts_ref[group] - begin, 0, chunk)

        @pl.when(wanted > 0)
        def _():
            for (start, depth), tile in zip(slices, tiles):
                tile[:, :depth] = came_ref[group, start : start + depth, :].astype(F32).T

            def body(step, inner):
                for lane in range(UNROLL):
                    at = step * UNROLL + lane
                    row = row_ref[group * capacity + begin + at]
                    for total, tile in zip(totals, tiles):
                        total[pl.ds(row, 1), :] = total[pl.ds(row, 1), :] + tile[pl.ds(at, 1), :]
                return inner

            lax.fori_loop(0, (wanted + UNROLL - 1) // UNROLL, body, 0)

        return carry

    lax.fori_loop(0, groups, source, 0)


def collect(counts, row_list, came, totals, slices, begin, ent_rows):
    capacity = row_list.shape[1]
    chunk = came.shape[2]
    n = len(slices)
    first = totals is None
    given = () if first else tuple(totals)
    return pl.pallas_call(
        functools.partial(collect_kernel, slices, capacity, begin, first),
        out_shape=[jax.ShapeDtypeStruct((ent_rows + 8, LANES), F32)] * n,
        in_specs=[whole(SMEM)] * 2 + [whole(VMEM)] * (1 + len(given)),
        out_specs=[whole(VMEM)] * n,
        scratch_shapes=[pltpu.VMEM((chunk, LANES), F32)] * n,
        compiler_params=params(),
        cost_estimate=cost(0, 120e6),
        name="collect",
    )(counts, row_list.reshape(-1), came, *given)


def relation_sums_kernel(n, ids_ref, *refs):
    grads, totals = refs[:n], refs[n:]
    count = grads[0].shape[1]
    for total in totals:
        total[...] = jnp.zeros_like(total)

    def body(step, carry):
        for lane in range(UNROLL):
            at = step * UNROLL + lane
            row = ids_ref[at]
            for grad, total in zip(grads, totals):
                total[pl.ds(row, 1), :] = total[pl.ds(row, 1), :] + grad[0, pl.ds(at, 1), :]
        return carry

    lax.fori_loop(0, count // UNROLL, body, 0)


def relation_sums(relation_ids, grads, rel_total):
    n = len(grads)
    count = relation_ids.shape[0]
    return pl.pallas_call(
        functools.partial(relation_sums_kernel, n),
        out_shape=[jax.ShapeDtypeStruct((rel_total, LANES), F32)] * n,
        grid=(1,),
        in_specs=[whole(SMEM)]
        + [pl.BlockSpec((1, count, LANES), lambda i: (0, 0, 0))] * n,
        out_specs=[whole(VMEM)] * n,
        compiler_params=params(),
        cost_estimate=cost(0, 120e6),
        name="relation_sums",
    )(relation_ids, *grads)


def update_kernel(slices, weights_ref, first_ref, second_ref, *refs):
    n = len(slices)
    totals, outs, scr = refs[:n], refs[n : n + 3], refs[n + 3]
    for (start, depth), total in zip(slices, totals):
        scr[start : start + depth, :] = total[...].T[:depth]
    results = adamw_update(weights_ref[...], scr[...], first_ref[...], second_ref[...])
    for out, result in zip(outs, results):
        out[...] = result


def update_entities(weights, totals, first, second, slices):
    width, ent_rows = weights.shape
    cols = 256 if ent_rows % 256 == 0 else 128
    n = len(slices)
    table = pl.BlockSpec((width, cols), lambda i: (0, i))
    return pl.pallas_call(
        functools.partial(update_kernel, slices),
        out_shape=[jax.ShapeDtypeStruct((width, ent_rows), F32)] * 3,
        grid=(ent_rows // cols,),
        in_specs=[table] * 3 + [pl.BlockSpec((cols, LANES), lambda i: (i, 0))] * n,
        out_specs=[table] * 3,
        scratch_shapes=[pltpu.VMEM((width, cols), F32)],
        compiler_params=params(),
        cost_estimate=cost(0, 60e6),
        name="update_entities",
    )(weights, first, second, *totals)


def shards(
    head_ids,
    relation_ids,
    tail_ids,
    negative_ids,
    live_counts,
    rel_weight,
    rel_count,
    entity_table,
    entity_first,
    entity_second,
    relation_table,
    relation_first,
    relation_second,
):
    groups = lax.axis_size("edge")
    n_col = lax.axis_size("col")
    width, ent_rows = entity_table.shape
    blocks, neg_count = negative_ids.shape
    block_len = head_ids.shape[0] // blocks
    edge_count = blocks * block_len
    slices = width_slices(width)
    n = len(slices)
    all_ids = jnp.concatenate([head_ids, tail_ids, negative_ids.reshape(-1)])
    id_count = all_ids.shape[0]
    capacity = (4 * id_count + 3 * groups - 1) // (3 * groups)
    rel_total = rel_weight.shape[0]

    table_low = entity_table.astype(BF16)
    rel_table = lax.all_gather(relation_table.astype(BF16), "edge", axis=0, tiled=True)
    dense = [
        lax.all_gather(table_low[start : start + depth], "edge", axis=0, tiled=False)
        for start, depth in slices
    ]

    place_list, row_list, counts = owner_lists(all_ids, groups, capacity, ent_rows)
    asked = lax.all_to_all(row_list, "edge", split_axis=0, concat_axis=0, tiled=True)
    asked_counts = jnp.sum((asked < ent_rows).astype(jnp.int32), axis=1)
    safe_places = jnp.minimum(place_list, id_count - 1)

    rel_scale = rel_weight * (rel_total / jnp.sum(rel_weight)) / rel_count.astype(F32)
    rel_slices = []
    for k, (start, depth) in enumerate(slices):
        piece = rel_table[:, start : start + depth].astype(F32)
        if k < n - 1:
            rel_slices.append(piece)
        else:
            gap = jnp.zeros((rel_total, LANES - 1 - depth), F32)
            rel_slices.append(jnp.concatenate([piece, gap, rel_scale[:, None]], axis=1))
    rel_rows = relation_rows(relation_ids, rel_slices)

    offs, tails, own, others, sums = [], [], [], [[] for _ in range(n_col - 1)], []
    for k, (start, depth) in enumerate(slices):
        fetched = fetch(counts, place_list, row_list, dense[k])
        off, tail, pair, part = prepare(fetched, rel_rows[k], depth, blocks, block_len)
        offs.append(off)
        tails.append(tail)
        own.append(pair)
        sums.append(part)
        for away in range(1, n_col):
            turn = [(c, (c + away) % n_col) for c in range(n_col)]
            others[away - 1].append(lax.ppermute(pair, "col", turn))
            sums.append(lax.ppermute(part, "col", turn))
    sums = jnp.stack(sums)

    *grads, loss_tile = block_math(
        live_counts, [own] + others, sums, offs, tails, slices, block_len
    )
    live = jnp.sum(jnp.minimum(live_counts, block_len)).astype(F32)
    whole_pair = lax.psum(jnp.stack([jnp.sum(loss_tile), live]), ("edge", "col"))
    loss_pair = whole_pair / n_col

    flat = [grad.reshape(id_count, LANES) for grad in grads]
    chunks = 4
    chunk = capacity // chunks
    arrived = []
    for k in range(chunks):
        sent = outgoing(counts, safe_places, flat, slices, k * chunk, chunk)
        arrived.append(lax.all_to_all(sent, "edge", split_axis=0, concat_axis=0, tiled=True))
    totals = None
    for k in range(chunks):
        totals = collect(asked_counts, asked, arrived[k], totals, slices, k * chunk, ent_rows)

    rel_terms = relation_sums(relation_ids, grads, rel_total)
    rel_terms = jnp.concatenate(
        [term[:, :depth] for (start, depth), term in zip(slices, rel_terms)], axis=1
    )
    relation_grad = lax.psum_scatter(rel_terms, "edge", scatter_dimension=0, tiled=True)
    new_entity, new_entity_first, new_entity_second = update_entities(
        entity_table, totals, entity_first, entity_second, slices
    )
    new_relation, new_relation_first, new_relation_second = adamw_update(
        relation_table, relation_grad, relation_first, relation_second
    )
    return (
        loss_pair,
        new_entity,
        new_entity_first,
        new_entity_second,
        new_relation,
        new_relation_first,
        new_relation_second,
    )


def solution(mesh):
    placed = (
        P("edge"),
        P("edge"),
        P("edge"),
        P("edge", None),
        P("edge"),
        P(),
        P(),
        P("col", "edge"),
        P("col", "edge"),
        P("col", "edge"),
        P("edge", "col"),
        P("edge", "col"),
        P("edge", "col"),
    )
    return jax.shard_map(
        shards,
        mesh=mesh,
        in_specs=placed,
        out_specs=(
            P(),
            P("col", "edge"),
            P("col", "edge"),
            P("col", "edge"),
            P("edge", "col"),
            P("edge", "col"),
            P("edge", "col"),
        ),
        check_vma=False,
    )
```

time: 2350 us -> 1160 us (0.49)
  local copies, waits for them, and re-layouts: 983 us -> 9.42 us
  blocking collectives: 848 us -> 54.5 us
  Pallas kernels: 0 us -> 642 us
  waiting for transfers between devices: 7.5 us -> 354 us
  other arithmetic: 369 us -> 37.7 us
  matrix products: 91.9 us -> 12.1 us
    pallas_call x0 -> x16, Pallas kernels: none -> 642 us  [the longest x2 214 us: fetch(): pl.pallas_call(functools.partial(fetch_kernel, capacity), out_shape=jax.S...]
    gather x8 -> x0, local copies, waits for them, and re-layouts: 489 us -> none  [the longest x2 162 us: shards(): jnp.take(id_grads, slot_source, axis=1)]
    psum x1, blocking collectives: 531 us -> 54.5 us  [shards(): lax.psum(jnp.stack([jnp.sum(loss_tile), live]), ('edge', 'col'))]
    all_gather x32 -> x0, blocking collectives: 317 us -> none  [the longest x8 85.1 us: block_step(): lax.all_gather(rel_part, 'col', axis=0, tiled=True)]
    scatter x3 -> x0, local copies, waits for them, and re-layouts: 284 us -> none  [the longest x1 103 us: shards(): slot_filled = jnp.zeros((groups * capacity,), jnp.bool_).at[slots].set(True)]
    scatter-add x2 -> x0, other arithmetic: 239 us -> none  [the longest x1 192 us: shards(): jax.ops.segment_sum(incoming.T, asked_flat, num_segments=ent_rows)]
    all_gather x1 -> x3, waiting for transfers between devices: 0.01 us -> 146 us  [the longest x2 142 us: shards(): lax.all_gather(table_low[start:start + depth], 'edge', axis=0, tiled=False)]
    all_to_all x3 -> x5, waiting for transfers between devices: 7.46 us -> 150 us  [the longest x4 150 us: shards(): lax.all_to_all(sent, 'edge', split_axis=0, concat_axis=0, tiled=True)]
  transfers between devices with their start and end apart: 5 -> 13, of which waited for: 1 -> 8; matrix products, arithmetic and copies ran while one was open for 16% -> 5% of each run, Pallas kernels for 0% -> 52%
where the time goes in v1:
time: 1160 us; the launch traced here: 1150 us
  Pallas kernels  642 us (55%)
  waiting for transfers between devices  354 us (31%)
  blocking collectives  54.5 us (5%)
  other arithmetic  37.7 us (3%)
  starting transfers between devices  28.6 us (2%)
  between operations  15.4 us (1%)
  matrix products  12.1 us (1%)
    pallas_call x2, Pallas kernels, fetch(): pl.pallas_call(functools.partial(fetch_kernel, capacity), out_shape=jax.S...  214 us
    all_to_all x4, waiting for transfers between devices, shards(): lax.all_to_all(sent, 'edge', split_axis=0, concat_axis=0, tiled=True)  150 us
    all_gather x2, waiting for transfers between devices, shards(): lax.all_gather(table_low[start:start + depth], 'edge', axis=0, tiled=False)  142 us
    pallas_call x4, Pallas kernels, collect(): pl.pallas_call(functools.partial(collect_kernel, slices, capacity, begin,...  138 us
    pallas_call x4, Pallas kernels, outgoing(): pl.pallas_call(functools.partial(outgoing_kernel, slices, capacity, begin...  95.3 us
    pallas_call x1, Pallas kernels, block_math(): pl.pallas_call(functools.partial(block_kernel, slices, n_col), out_shape=...  86 us
    psum x1, blocking collectives, shards(): lax.psum(jnp.stack([jnp.sum(loss_tile), live]), ('edge', 'col'))  54.5 us
    ppermute x2, waiting for transfers between devices, shards(): sums.append(lax.ppermute(part, 'col', turn))  47.7 us
  transfers between devices with their start and end apart: 13, of which 8 were waited for; matrix products, arithmetic and copies ran while one was open for 5% of the time, Pallas kernels for 52%

profile of v1, /device:TPU:16, one launch (start us, length us, event | category | flops | bytes accessed | tf_op | source)
XLA Modules:
  0.0 1153.2 jit_solution(16715964047495567566)
XLA Ops:
  22.5 8.8 broadcast_multiply_fusion
  31.3 11.6 %fusion.6 = s32[256,512]{1,0:T(8,128)S(1)} fusion(bf16[512,24576]{1,0:T(8,128)(2,1)} %bitcast.40, s32[24576]{0:T(1024)S(1)} %get-tuple-element.71), kind=kOutput, calls=%fused_computation.15 | convolution fusion | flops 6448873472 | bytes 25788416 | tf_op jit(solution)/shard_map/dot_general | solution.py:80
  46.1 3.8 all-gather.6.cloned.1.call-done
  54.3 19.3 %relation_rows.1 = (f32[8192,128]{1,0:T(8,128)}, f32[8192,128]{1,0:T(8,128)}) custom-call(s32[8192]{0:T(1024)} %ids_ref.3, f32[3200,128]{1,0:T(8,128)} %slice_convert_fusion.1.refs_0_, f32[3200,128]{1,0:T(8,128)} %pad_maximum_fusion.1.refs_1_), custom_call_target="tpu_custom_call" | custom-call | bytes 60000000 | tf_op jit(solution)/shard_map/relation_rows/pallas_call | solution.py:106
  73.6 142.4 %all-gather.8.cloned.1.call-done = bf16[2048,7936]{1,0:T(8,128)(2,1)} async-done(((bf16[128,7936]{1,0:T(8,128)(2,1)}), bf16[2048,7936]{1,0:T(8,128)(2,1)}) %all-gather.8.cloned.1.call-update) | async-done | bytes 32505872 | tf_op jit(solution)/shard_map/all_gather | solution.py:522
  216.0 106.7 %fetch_rows.2.head_ref.tail_ref.neg_ref = f32[24584,128]{1,0:T(8,128)} custom-call(s32[16]{0:T(128)} %convert_element_type.65.counts_ref, s32[32768]{0:T(1024)} %bitcast.46, s32[32768]{0:T(1024)} %bitcast.5.row_ref, bf16[16,128,7936]{2,1,0:T(8,128)(2,1)} %bitcast.39), custom_call_target="tpu_custom_call" | custom-call | bytes 250000000 | tf_op jit(solution)/shard_map/fetch_rows/pallas_call | solution.py:149
  322.6 11.7 %prepare.2 = (f32[8192,128]{1,0:T(8,128)}, bf16[8192,128]{1,0:T(8,128)(2,1)}, bf16[2,128,8192]{2,1,0:T(8,128)(2,1)}, f32[2,8192]{1,0:T(2,128)}) custom-call(f32[24584,128]{1,0:T(8,128)} %fetch_rows.2.head_ref.tail_ref.neg_ref, f32[24584,128]{1,0:T(8,128)} %fetch_rows.2.head_ref.tail_ref.neg_ref, f32[24584,128]{1,0:T(8,128)} %fetch_rows.2.head_ref.tail_ref.neg_ref, ...), custom_call_target="tpu_custom_call" | custom-call | bytes 40000000 | tf_op jit(solution)/shard_map/prepare/pallas_call | solution.py:188
  335.8 107.3 %fetch_rows.3.head_ref.tail_ref.neg_ref = f32[24584,128]{1,0:T(8,128)} custom-call(s32[16]{0:T(128)} %convert_element_type.65.counts_ref, s32[32768]{0:T(1024)} %bitcast.47, s32[32768]{0:T(1024)} %bitcast.5.row_ref, bf16[16,72,7936]{2,1,0:T(8,128)(2,1)} %bitcast.41), custom_call_target="tpu_custom_call" | custom-call | bytes 250000000 | tf_op jit(solution)/shard_map/fetch_rows/pallas_call | solution.py:149
  443.0 11.1 prepare.3
  454.7 5.2 all-to-all-start
  462.7 47.0 %collective-permute-done.3 = f32[2,8192]{1,0:T(2,128)S(1)} collective-permute-done((f32[2,8192]{1,0:T(2,128)}, f32[2,8192]{1,0:T(2,128)S(1)}, u32[]{:S(2)}, u32[]{:S(2)}) %collective-permute-start.3) | collective-permute-done | bytes 65568 | tf_op jit(solution)/shard_map/ppermute | solution.py:553
  513.4 86.0 %block_math.1 = (f32[3,8192,128]{2,1,0:T(8,128)}, f32[3,8192,128]{2,1,0:T(8,128)}, f32[8,128]{1,0:T(8,128)}) custom-call(s32[8]{0:T(128)} %live_ref.1, bf16[2,128,8192]{2,1,0:T(8,128)(2,1)} %get-tuple-element.34.refs_0_, bf16[2,72,8192]{2,1,0:T(8,128)(2,1)} %get-tuple-element.36.refs_1_, bf16[2,128,8192]{2,1,0:T(8,128)(2,1)} %collective-permute-done.refs_2_, ...), custom_call_target="tpu_custom_call" | custom-call | flops 13421772800 | bytes 200000000 | tf_op jit(solution)/shard_map/block_math/pallas_call | solution.py:313
  599.4 26.8 %outgoing.5 = bf16[16,200,512]{2,1,0:T(8,128)(2,1)} custom-call(s32[16]{0:T(128)} %convert_element_type.65.counts_ref, s32[32768]{0:T(1024)} %broadcast_minimum_fusion.place_ref, f32[24576,128]{1,0:T(8,128)} %bitcast.31, f32[24576,128]{1,0:T(8,128)} %bitcast.35), custom_call_target="tpu_custom_call" | custom-call | bytes 80000000 | tf_op jit(solution)/shard_map/outgoing/pallas_call | solution.py:368
  626.2 5.1 all-to-all-start.2
  631.3 27.7 %outgoing.6 = bf16[16,200,512]{2,1,0:T(8,128)(2,1)} custom-call(s32[16]{0:T(128)} %convert_element_type.65.counts_ref, s32[32768]{0:T(1024)} %broadcast_minimum_fusion.place_ref, f32[24576,128]{1,0:T(8,128)} %bitcast.32, f32[24576,128]{1,0:T(8,128)} %bitcast.36), custom_call_target="tpu_custom_call" | custom-call | bytes 80000000 | tf_op jit(solution)/shard_map/outgoing/pallas_call | solution.py:368
  659.0 45.2 %all-to-all-done.2.came_ref = bf16[16,200,512]{2,1,0:T(8,128)(2,1)S(1)} async-done(((bf16[16,200,512]{2,1,0:T(8,128)(2,1)}), bf16[16,200,512]{2,1,0:T(8,128)(2,1)S(1)}, u32[]{:S(2)}, u32[]{:S(2)}) %all-to-all-start.2) | async-done | bytes 3276832 | tf_op jit(solution)/shard_map/all_to_all | solution.py:569
  704.3 4.7 all-to-all-start.3
  708.9 27.7 %outgoing.7 = bf16[16,200,512]{2,1,0:T(8,128)(2,1)} custom-call(s32[16]{0:T(128)} %convert_element_type.65.counts_ref, s32[32768]{0:T(1024)} %broadcast_minimum_fusion.place_ref, f32[24576,128]{1,0:T(8,128)} %bitcast.33, f32[24576,128]{1,0:T(8,128)} %bitcast.37), custom_call_target="tpu_custom_call" | custom-call | bytes 80000000 | tf_op jit(solution)/shard_map/outgoing/pallas_call | solution.py:368
  736.6 45.3 %all-to-all-done.3.came_ref = bf16[16,200,512]{2,1,0:T(8,128)(2,1)} async-done(((bf16[16,200,512]{2,1,0:T(8,128)(2,1)}), bf16[16,200,512]{2,1,0:T(8,128)(2,1)}, u32[]{:S(2)}, u32[]{:S(2)}) %all-to-all-start.3) | async-done | bytes 3276832 | tf_op jit(solution)/shard_map/all_to_all | solution.py:569
  782.0 4.7 all-to-all-start.4
  786.7 13.1 %outgoing.4 = bf16[16,200,512]{2,1,0:T(8,128)(2,1)} custom-call(s32[16]{0:T(128)} %convert_element_type.65.counts_ref, s32[32768]{0:T(1024)} %broadcast_minimum_fusion.place_ref, f32[24576,128]{1,0:T(8,128)} %bitcast.34, f32[24576,128]{1,0:T(8,128)} %bitcast.38), custom_call_target="tpu_custom_call" | custom-call | bytes 80000000 | tf_op jit(solution)/shard_map/outgoing/pallas_call | solution.py:368
  799.8 59.8 %all-to-all-done.4.came_ref = bf16[16,200,512]{2,1,0:T(8,128)(2,1)S(1)} async-done(((bf16[16,200,512]{2,1,0:T(8,128)(2,1)}), bf16[16,200,512]{2,1,0:T(8,128)(2,1)S(1)}, u32[]{:S(2)}, u32[]{:S(2)}) %all-to-all-start.4) | async-done | bytes 3276832 | tf_op jit(solution)/shard_map/all_to_all | solution.py:569
  861.3 4.7 all-to-all-start.1
  866.0 35.6 %relation_sums.1 = (f32[3200,128]{1,0:T(8,128)}, f32[3200,128]{1,0:T(8,128)}) custom-call(s32[8192]{0:T(1024)} %ids_ref.3, f32[3,8192,128]{2,1,0:T(8,128)} %get-tuple-element.44.refs_0_, f32[3,8192,128]{2,1,0:T(8,128)} %get-tuple-element.45.refs_1_), custom_call_target="tpu_custom_call" | custom-call | bytes 120000000 | tf_op jit(solution)/shard_map/relation_sums/pallas_call | solution.py:450
  901.6 3.9 pad_maximum_fusion
  909.6 54.5 %psum.7 = f32[2]{0:T(128)S(1)} all-reduce(f32[2]{0:T(128)S(1)} %pad_maximum_fusion.4), channel_id=1, replica_groups=mesh['edge'=16,'col'=2] {'edge','col'}, use_global_device_ids=true, to_apply=%region_7.8 | all-reduce | flops 2 | bytes 16 | tf_op jit(solution)/shard_map/psum | solution.py:560
  964.7 9.3 reduce-scatter.2.cloned.1.call-done
  976.1 41.8 %collect.4 = (f32[7944,128]{1,0:T(8,128)}, f32[7944,128]{1,0:T(8,128)}) custom-call(s32[16]{0:T(128)} %fusion.12.counts_ref, s32[32768]{0:T(1024)} %bitcast.42, bf16[16,200,512]{2,1,0:T(8,128)(2,1)} %copy-done.2), custom_call_target="tpu_custom_call" | custom-call | bytes 120000000 | tf_op jit(solution)/shard_map/collect/pallas_call | solution.py:418
  1018.0 43.8 %collect.5 = (f32[7944,128]{1,0:T(8,128)}, f32[7944,128]{1,0:T(8,128)}) custom-call(s32[16]{0:T(128)} %fusion.12.counts_ref, s32[32768]{0:T(1024)} %bitcast.43, bf16[16,200,512]{2,1,0:T(8,128)(2,1)} %all-to-all-done.3.came_ref, f32[7944,128]{1,0:T(8,128)} %get-tuple-element.46.refs_0_, f32[7944,128]{1,0:T(8,128)} %get-tuple-element.47.refs_1_), custom_call_target="tpu_custom_call" | custom-call | bytes 120000000 | tf_op jit(solution)/shard_map/collect/pallas_call | solution.py:418
  1061.8 42.0 %collect.6 = (f32[7944,128]{1,0:T(8,128)}, f32[7944,128]{1,0:T(8,128)}) custom-call(s32[16]{0:T(128)} %fusion.12.counts_ref, s32[32768]{0:T(1024)} %bitcast.44, bf16[16,200,512]{2,1,0:T(8,128)(2,1)} %copy-done, f32[7944,128]{1,0:T(8,128)} %get-tuple-element.48.refs_0_, f32[7944,128]{1,0:T(8,128)} %get-tuple-element.49.refs_1_), custom_call_target="tpu_custom_call" | custom-call | bytes 120000000 | tf_op jit(solution)/shard_map/collect/pallas_call | solution.py:418
  1105.5 10.8 collect.7
  1116.3 30.3 %update_entities.1 = (f32[200,7936]{1,0:T(8,128)}, f32[200,7936]{1,0:T(8,128)}, f32[200,7936]{1,0:T(8,128)}) custom-call(f32[200,7936]{1,0:T(8,128)} %weights_ref.1, f32[200,7936]{1,0:T(8,128)} %first_ref.1, f32[200,7936]{1,0:T(8,128)} %second_ref.1, f32[7944,128]{1,0:T(8,128)} %get-tuple-element.52.refs_0_, f32[7944,128]{1,0:T(8,128)} %get-tuple-element.53.refs_1_), custom_call_target="tpu_custom_call" | custom-call | bytes 60000000 | tf_op jit(solution)/shard_map/update_entities/pallas_call | solution.py:478
  (94 shorter events, 40.1 us)
Async XLA Ops:
  7.2 42.8 %all-gather.6.cloned.1.call-start = ((), (), s32[]{:S(2)}) async-start(), calls=%async_computation.6 | async-start | bytes 1740800 | tf_op jit(solution)/shard_map/all_gather | solution.py:520
  8.8 207.2 %all-gather.8.cloned.1.call-start = ((), (), s32[]{:S(2)}) async-start(), calls=%async_computation.8 | async-start | bytes 34537472 | tf_op jit(solution)/shard_map/all_gather | solution.py:522
  13.4 1.2 copy-start.8
  13.4 1.3 copy-start.6
  13.4 1.3 copy-start.7
  13.5 322.3 %all-gather.10.cloned.1.call-start = ((), (), s32[]{:S(2)}) async-start(), calls=%async_computation.9 | async-start | bytes 19427328 | tf_op jit(solution)/shard_map/all_gather | solution.py:522
  31.3 11.8 %copy-start.9 = (f32[3200]{0:T(1024)S(1)}, f32[3200]{0:T(1024)}, u32[]{:S(2)}) copy-start(f32[3200]{0:T(1024)} %param.18) | copy-start | bytes 38404
  31.3 13.1 %copy-start.11 = (s32[3200]{0:T(1024)S(1)}, s32[3200]{0:T(1024)}, u32[]{:S(2)}) copy-start(s32[3200]{0:T(1024)} %param.19) | copy-start | bytes 38404
  50.0 3.0 copy-start.5
  334.3 177.7 %collective-permute-start = (bf16[2,128,8192]{2,1,0:T(8,128)(2,1)}, bf16[2,128,8192]{2,1,0:T(8,128)(2,1)}, u32[]{:S(2)}, u32[]{:S(2)}) collective-permute-start(bf16[2,128,8192]{2,1,0:T(8,128)(2,1)} %get-tuple-element.34.refs_0_), channel_id=1, source_target_pairs={{0,1},{1,0},{2,3},{3,2},{4,5},{5,4},{6,7},{7,6},{8,9},{9,8},{10,11... | collective-permute-start | bytes 12582920 | tf_op jit(solution)/shard_map/ppermute | solution.py:552
  443.0 18.4 %copy-start.10 = (f32[2,8192]{1,0:T(2,128)S(1)}, f32[2,8192]{1,0:T(2,128)}, u32[]{:S(2)}) copy-start(f32[2,8192]{1,0:T(2,128)} %get-tuple-element.37) | copy-start | bytes 196612
  443.0 19.0 %copy-start.4 = (s32[256,1,128]{2,1,0:T(1,128)S(1)}, s32[256,1,128]{2,1,0:T(1,128)}, u32[]{:S(2)}) copy-start(s32[256,1,128]{2,1,0:T(1,128)} %get-tuple-element.70) | copy-start | bytes 393220
  454.2 57.9 %collective-permute-start.1 = (bf16[2,72,8192]{2,1,0:T(8,128)(2,1)}, bf16[2,72,8192]{2,1,0:T(8,128)(2,1)S(1)}, u32[]{:S(2)}, u32[]{:S(2)}) collective-permute-start(bf16[2,72,8192]{2,1,0:T(8,128)(2,1)} %get-tuple-element.36.refs_1_), channel_id=1, source_target_pairs={{0,1},{1,0},{2,3},{3,2},{4,5},{5,4},{6,7},{7,6},{8,9},{9,8},{10,11... | collective-permute-start | bytes 7077896 | tf_op jit(solution)/shard_map/ppermute | solution.py:552
  454.7 171.5 %all-to-all-start = ((s32[16,1,2048]{2,1,0:T(1,128)}), s32[16,1,2048]{2,1,0:T(1,128)S(1)}, u32[]{:S(2)}, u32[]{:S(2)}) async-start(s32[16,1,2048]{2,1,0:T(1,128)} %bitcast.14), calls=%async_computation | async-start | bytes 262144 | tf_op jit(solution)/shard_map/all_to_all | solution.py:527
  460.0 49.7 %collective-permute-start.3 = (f32[2,8192]{1,0:T(2,128)}, f32[2,8192]{1,0:T(2,128)S(1)}, u32[]{:S(2)}, u32[]{:S(2)}) collective-permute-start(f32[2,8192]{1,0:T(2,128)} %get-tuple-element.38), channel_id=1, source_target_pairs={{0,1},{1,0},{2,3},{3,2},{4,5},{5,4},{6,7},{7,6},{8,9},{9,8},{10,11... | collective-permute-start | bytes 196616 | tf_op jit(solution)/shard_map/ppermute | solution.py:553
  461.4 48.9 %collective-permute-start.2 = (f32[2,8192]{1,0:T(2,128)S(1)}, f32[2,8192]{1,0:T(2,128)S(1)}, u32[]{:S(2)}, u32[]{:S(2)}) collective-permute-start(f32[2,8192]{1,0:T(2,128)S(1)} %copy-done.10), channel_id=1, source_target_pairs={{0,1},{1,0},{2,3},{3,2},{4,5},{5,4},{6,7},{7,6},{8,9},{9,8},{10,11... | collective-permute-start | bytes 196616 | tf_op jit(solution)/shard_map/ppermute | solution.py:553
  512.0 1.4 copy-start.13
  626.2 282.5 %copy-start.3 = (s32[16,1,2048]{2,1,0:T(1,128)}, s32[16,1,2048]{2,1,0:T(1,128)S(1)}, u32[]{:S(2)}) copy-start(s32[16,1,2048]{2,1,0:T(1,128)S(1)} %all-to-all-done) | copy-start | bytes 393220
  626.2 78.0 %all-to-all-start.2 = ((bf16[16,200,512]{2,1,0:T(8,128)(2,1)}), bf16[16,200,512]{2,1,0:T(8,128)(2,1)S(1)}, u32[]{:S(2)}, u32[]{:S(2)}) async-start(bf16[16,200,512]{2,1,0:T(8,128)(2,1)} %outgoing.5), calls=%async_computation.2 | async-start | bytes 6553600 | tf_op jit(solution)/shard_map/all_to_all | solution.py:569
  704.3 32.4 %copy-start = (bf16[16,200,512]{2,1,0:T(8,128)(2,1)}, bf16[16,200,512]{2,1,0:T(8,128)(2,1)S(1)}, u32[]{:S(2)}) copy-start(bf16[16,200,512]{2,1,0:T(8,128)(2,1)S(1)} %all-to-all-done.2.came_ref) | copy-start | bytes 9830404
  704.3 77.7 %all-to-all-start.3 = ((bf16[16,200,512]{2,1,0:T(8,128)(2,1)}), bf16[16,200,512]{2,1,0:T(8,128)(2,1)}, u32[]{:S(2)}, u32[]{:S(2)}) async-start(bf16[16,200,512]{2,1,0:T(8,128)(2,1)} %outgoing.6), calls=%async_computation.3 | async-start | bytes 6553600 | tf_op jit(solution)/shard_map/all_to_all | solution.py:569
  782.0 77.6 %all-to-all-start.4 = ((bf16[16,200,512]{2,1,0:T(8,128)(2,1)}), bf16[16,200,512]{2,1,0:T(8,128)(2,1)S(1)}, u32[]{:S(2)}, u32[]{:S(2)}) async-start(bf16[16,200,512]{2,1,0:T(8,128)(2,1)} %outgoing.7), calls=%async_computation.4 | async-start | bytes 6553600 | tf_op jit(solution)/shard_map/all_to_all | solution.py:569
  859.6 1.7 copy-start.2
  861.3 242.5 %all-to-all-start.1 = ((bf16[16,200,512]{2,1,0:T(8,128)(2,1)}), bf16[16,200,512]{2,1,0:T(8,128)(2,1)S(1)}, u32[]{:S(2)}, u32[]{:S(2)}) async-start(bf16[16,200,512]{2,1,0:T(8,128)(2,1)} %outgoing.4), calls=%async_computation.1 | async-start | bytes 6553600 | tf_op jit(solution)/shard_map/all_to_all | solution.py:569
  866.0 108.0 %reduce-scatter.2.cloned.1.call-start = ((), (), s32[]{:S(2)}) async-start(), calls=%async_computation.7 | async-start | bytes 3481600 | tf_op jit(solution)/shard_map/reduce_scatter | solution.py:578
  905.5 0.7 copy-start.14
  905.5 1.9 copy-start.12
  1103.8 1.7 copy-start.1
Sparse Core Ops, SparseCore 0:
  10.7 39.1 all-gather.5
  52.1 163.8 all-gather.7
  217.6 96.2 all-gather.9
  905.6 68.3 reduce-scatter.1

commit v2 on v1

--- a/solution.py
+++ b/solution.py
@@ -19,6 +19,10 @@
 LANES = 128
 UNROLL = 8
 PARTS = 4
+PIECES = 4
+HALVES = 2
+CHUNKS = 4
+REL_PAD = 256
 NN = (((1,), (0,)), ((), ()))
 NT = (((1,), (1,)), ((), ()))
 TN = (((0,), (0,)), ((), ()))
@@ -55,20 +59,30 @@
     return [(at, min(LANES, width - at)) for at in range(0, width, LANES)]
 
 
+def piece_bounds(ent_rows):
+    tiles = ent_rows // LANES
+    cuts = [LANES * ((tiles * k + PIECES - 1) // PIECES) for k in range(PIECES)]
+    return cuts + [ent_rows]
+
+
 def owner_lists(all_ids, groups, capacity, ent_rows):
     count = all_ids.shape[0]
     owners = all_ids // ent_rows
     local_rows = all_ids - owners * ent_rows
     chunk = 256
-    mine = owners[None, :] == jnp.arange(groups, dtype=jnp.int32)[:, None]
-    mine = mine.astype(BF16).reshape(groups, count // chunk, chunk)
+    pieces = sum((local_rows >= cut).astype(jnp.int32) for cut in piece_bounds(ent_rows)[1:-1])
+    buckets = owners * PIECES + pieces
+    mine = buckets[None, :] == jnp.arange(groups * PIECES, dtype=jnp.int32)[:, None]
+    mine = mine.astype(BF16).reshape(groups * PIECES, count // chunk, chunk)
     before = jnp.triu(jnp.ones((chunk, chunk), BF16), 1)
     inner = jnp.dot(mine, before, preferred_element_type=F32)
     sums = jnp.sum(mine.astype(F32), axis=2)
-    carry = jnp.cumsum(sums, axis=1) - sums
+    in_bucket = jnp.sum(sums, axis=1).reshape(groups, PIECES)
+    ends = jnp.cumsum(in_bucket, axis=1)
+    carry = jnp.cumsum(sums, axis=1) - sums + (ends - in_bucket).reshape(-1, 1)
     ranks = jnp.sum(mine.astype(F32) * (inner + carry[:, :, None]), axis=0)
     ranks = ranks.astype(jnp.int32).reshape(count)
-    counts = jnp.sum(sums, axis=1).astype(jnp.int32)
+    starts = jnp.concatenate([jnp.zeros((groups, 1), F32), ends], axis=1).astype(jnp.int32)
     high = owners * (capacity // LANES) + ranks // LANES
     low = ranks % LANES
     tall = groups * capacity // LANES
@@ -82,42 +96,66 @@
     place = found[:, 0] * 256 + found[:, 1]
     place_list = jnp.where(place > 0, place - 1, count).reshape(groups, capacity)
     row_list = jnp.where(place > 0, found[:, 2] * 256 + found[:, 3], ent_rows)
-    return place_list, row_list.reshape(groups, capacity), counts
-
-
-def relation_rows_kernel(n_slices, ids_ref, *refs):
-    tables, outs = refs[:n_slices], refs[n_slices:]
-    count = outs[0].shape[0]
+    return place_list, row_list.reshape(groups, capacity), starts
+
+
+def relation_rows_kernel(ids_ref, table_ref, scale_ref, out_ref, columns, rows):
+    groups, depth, span = table_ref.shape
+    columns[...] = jnp.zeros_like(columns)
+
+    def turn(group, carry):
+        columns[:depth, :] = table_ref[group].astype(F32)
+        if depth < LANES:
+            columns[LANES - 1 :, :] = scale_ref[pl.ds(group, 1), :]
+        rows[pl.ds(pl.multiple_of(group * span, span), span), :] = columns[...].T
+        return carry
+
+    lax.fori_loop(0, groups, turn, 0)
 
     def body(step, carry):
         for lane in range(UNROLL):
             at = step * UNROLL + lane
-            row = ids_ref[at]
-            for table, out in zip(tables, outs):
-                out[pl.ds(at, 1), :] = table[pl.ds(row, 1), :]
-        return carry
-
-    lax.fori_loop(0, count // UNROLL, body, 0)
-
-
-def relation_rows(relation_ids, tables):
-    count = relation_ids.shape[0]
-    n = len(tables)
+            out_ref[pl.ds(at, 1), :] = rows[pl.ds(ids_ref[at], 1), :]
+        return carry
+
+    lax.fori_loop(0, out_ref.shape[0] // UNROLL, body, 0)
+
+
+def relation_rows(places, dense, scale):
+    count = places.shape[0]
+    groups, depth, span = dense.shape
     return pl.pallas_call(
-        functools.partial(relation_rows_kernel, n),
-        out_shape=[jax.ShapeDtypeStruct((count, LANES), F32)] * n,
-        in_specs=[whole(SMEM)] + [whole(VMEM)] * n,
-        out_specs=[whole(VMEM)] * n,
+        relation_rows_kernel,
+        out_shape=jax.ShapeDtypeStruct((count, LANES), F32),
+        grid=(1,),
+        in_specs=[
+            whole(SMEM),
+            pl.BlockSpec((groups, depth, REL_PAD), lambda i: (0, 0, span // REL_PAD - 1)),
+            whole(VMEM),
+        ],
+        out_specs=whole(VMEM),
+        scratch_shapes=[
+            pltpu.VMEM((LANES, REL_PAD), F32),
+            pltpu.VMEM((groups * REL_PAD, LANES), F32),
+        ],
         compiler_params=params(),
-        cost_estimate=cost(0, 30e6 * n),
+        cost_estimate=cost(0, 30e6),
         name="relation_rows",
-    )(relation_ids, *tables)
-
-
-def fetch_kernel(capacity, counts_ref, place_ref, row_ref, dense_ref, out_ref, rows):
+    )(places, dense, scale)
+
+
+def fetch_kernel(capacity, piece, begin, end, starts_ref, place_ref, row_ref, dense_ref, *refs):
+    (old_ref,) = refs[:1] if piece > 0 else (None,)
+    out_ref, rows, kept, sem = refs[-4:]
     shard = pl.program_id(0)
-    depth, ent_rows = dense_ref.shape[1:]
-    step_cols = 256 if ent_rows % 256 == 0 else 128
+    depth = dense_ref.shape[1]
+    step_cols = 256 if begin % 256 == 0 and end % 256 == 0 else 128
+
+    if piece > 0:
+
+        @pl.when(shard == 0)
+        def _():
+            pltpu.make_async_copy(old_ref, kept, sem).start()
 
     if depth < LANES:
 
@@ -127,37 +165,66 @@
 
     def turn(step, carry):
         cols = pl.ds(pl.multiple_of(step * step_cols, step_cols), step_cols)
-        rows[cols, :depth] = dense_ref[0, :, cols].astype(F32).T
-        return carry
-
-    lax.fori_loop(0, ent_rows // step_cols, turn, 0)
-    trips = (counts_ref[shard] + UNROLL - 1) // UNROLL
+        into = pl.ds(pl.multiple_of(begin + step * step_cols, step_cols), step_cols)
+        rows[into, :depth] = dense_ref[0, :, cols].astype(F32).T
+        return carry
+
+    lax.fori_loop(0, (end - begin) // step_cols, turn, 0, unroll=True)
+
+    if piece > 0:
+
+        @pl.when(shard == 0)
+        def _():
+            pltpu.make_async_copy(old_ref, kept, sem).wait()
+
+    first = starts_ref[shard * (PIECES + 1) + piece] + shard * capacity
+    wanted = starts_ref[shard * (PIECES + 1) + piece + 1] + shard * capacity - first
+
+    def move(at):
+        kept[pl.ds(place_ref[at], 1), :] = rows[pl.ds(row_ref[at], 1), :]
 
     def body(step, carry):
         for lane in range(UNROLL):
-            at = shard * capacity + step * UNROLL + lane
-            out_ref[pl.ds(place_ref[at], 1), :] = rows[pl.ds(row_ref[at], 1), :]
-        return carry
-
+            move(first + step * UNROLL + lane)
+        return carry
+
+    def last(step, carry):
+        move(first + step)
+        return carry
+
+    trips = wanted // UNROLL
     lax.fori_loop(0, trips, body, 0)
-
-
-def fetch(counts, place_list, row_list, dense):
-    groups, depth, ent_rows = dense.shape
-    capacity = place_list.shape[1]
-    id_count = 3 * groups * capacity // 4
+    lax.fori_loop(trips * UNROLL, wanted, last, 0)
+
+    @pl.when(shard == pl.num_programs(0) - 1)
+    def _():
+        copy = pltpu.make_async_copy(kept, out_ref, sem)
+        copy.start()
+        copy.wait()
+
+
+def fetch(starts, place_list, row_list, dense, old, piece, begin, end, ent_rows, id_count):
+    groups, depth, _ = dense.shape
+    capacity = place_list.shape[0] // groups
+    given = [] if old is None else [old]
     return pl.pallas_call(
-        functools.partial(fetch_kernel, capacity),
-        out_shape=jax.ShapeDtypeStruct((id_count + 8, LANES), F32),
+        functools.partial(fetch_kernel, capacity, piece, begin, end),
+        out_shape=jax.ShapeDtypeStruct((id_count, LANES), F32),
         grid=(groups,),
         in_specs=[whole(SMEM)] * 3
-        + [pl.BlockSpec((1, depth, ent_rows), lambda shard: (shard, 0, 0))],
-        out_specs=whole(VMEM),
-        scratch_shapes=[pltpu.VMEM((ent_rows + 8, LANES), F32)],
+        + [pl.BlockSpec((1, depth, end - begin), lambda shard: (shard, 0, 0))]
+        + [whole(pl.ANY)] * len(given),
+        out_specs=whole(pl.ANY),
+        input_output_aliases={4: 0} if given else {},
+        scratch_shapes=[
+            pltpu.VMEM((ent_rows, LANES), F32),
+            pltpu.VMEM((id_count, LANES), F32),
+            pltpu.SemaphoreType.DMA,
+        ],
         compiler_params=params(),
-        cost_estimate=cost(0, 250e6),
+        cost_estimate=cost(0, 100e6),
         name="fetch_rows",
-    )(counts, place_list.reshape(-1), row_list.reshape(-1), dense)
+    )(starts, place_list, row_list, dense, *given)
 
 
 def prepare_kernel(depth, head_ref, tail_ref, neg_ref, rel_ref, off_ref, tail_out, pair_ref, sums_ref):
@@ -179,11 +246,15 @@
     sums_ref[1:2, :] = jnp.sum(neg_t * neg_t, axis=0, keepdims=True)
 
 
-def prepare(fetched, rel_rows, depth, blocks, block_len):
-    edge_count = blocks * block_len
+def prepare(fetched, rel_rows, depth, blocks, block_len, half):
+    part = blocks // HALVES
+    edge_count = part * block_len
 
     def rows(at):
-        return pl.BlockSpec((block_len, LANES), lambda b: (at * blocks + b, 0))
+        return pl.BlockSpec((block_len, LANES), lambda b: (at * blocks + half * part + b, 0))
+
+    def outs(*shape):
+        return pl.BlockSpec(shape + (block_len,), lambda b: (0,) * len(shape) + (b,))
 
     return pl.pallas_call(
         functools.partial(prepare_kernel, depth),
@@ -193,39 +264,41 @@
             jax.ShapeDtypeStruct((2, depth, edge_count), BF16),
             jax.ShapeDtypeStruct((2, edge_count), F32),
         ],
-        grid=(blocks,),
+        grid=(part,),
         in_specs=[rows(0), rows(1), rows(2), rows(0)],
         out_specs=[
-            rows(0),
-            rows(0),
-            pl.BlockSpec((2, depth, block_len), lambda b: (0, 0, b)),
-            pl.BlockSpec((2, block_len), lambda b: (0, b)),
+            pl.BlockSpec((block_len, LANES), lambda b: (b, 0)),
+            pl.BlockSpec((block_len, LANES), lambda b: (b, 0)),
+            outs(2, depth),
+            outs(2),
         ],
         compiler_params=params(),
-        cost_estimate=cost(0, 40e6),
+        cost_estimate=cost(0, 20e6),
         name="prepare",
     )(fetched, fetched, fetched, rel_rows)
 
 
-def block_kernel(slices, n_col, live_ref, *refs):
+def block_kernel(slices, n_col, half, me_ref, live_ref, *refs):
     n = len(slices)
     pairs = [refs[k * n : (k + 1) * n] for k in range(n_col)]
-    at = n * n_col
-    sums_ref = refs[at]
-    offs = refs[at + 1 : at + 1 + n]
-    tails = refs[at + 1 + n : at + 1 + 2 * n]
-    grads = refs[at + 1 + 2 * n : at + 1 + 3 * n]
-    loss_ref = refs[at + 1 + 3 * n]
-    shift_scr, neg_scr, cross, slopes, row_bias, row_sum = refs[at + 2 + 3 * n :]
+    refs = refs[n_col * n :]
+    sums_refs, refs = refs[:n_col], refs[n_col:]
+    offs, tails, refs = refs[:n], refs[n : 2 * n], refs[2 * n :]
+    if half > 0:
+        refs = refs[n:]
+    grads, refs = refs[:n], refs[n:]
+    loss_ref, shift_scr, neg_scr, sums_scr, cross, slopes, row_bias, row_sum = refs
     block = pl.program_id(0)
     length = cross.shape[0]
-    width = sum(depth for _, depth in slices)
+    me = me_ref[0]
     for k in range(n_col):
+        slot = lax.rem(me + (n_col - k), n_col)
         for (start, depth), pair in zip(slices, pairs[k]):
-            shift_scr[k, start : start + depth, :] = pair[0]
-            neg_scr[k, start : start + depth, :] = pair[1]
-    bias = jnp.sum(sums_ref[:, 0, :], axis=0, keepdims=True) + MARGIN
-    neg_norm = jnp.sum(sums_ref[:, 1, :], axis=0, keepdims=True)
+            shift_scr[slot, start : start + depth, :] = pair[0]
+            neg_scr[slot, start : start + depth, :] = pair[1]
+        sums_scr[slot] = sums_refs[k][...]
+    bias = jnp.sum(sums_scr[:, 0, :], axis=0, keepdims=True) + MARGIN
+    neg_norm = jnp.sum(sums_scr[:, 1, :], axis=0, keepdims=True)
     row_bias[...] = jnp.broadcast_to(bias, (LANES, length)).T
 
     tile = min(256, length)
@@ -243,7 +316,7 @@
 
     lax.fori_loop(0, length // tile, matmul, 0)
 
-    live = live_ref[block]
+    live = live_ref[half * pl.num_programs(0) + block]
     small = 64
 
     def pairwise(step, carry):
@@ -283,7 +356,7 @@
 
     def edges(step, carry):
         part = pl.ds(pl.multiple_of(step * tile, tile), tile)
-        moved = lax.dot_general(slopes[part, :], neg_scr[0], NT, preferred_element_type=F32)
+        moved = lax.dot_general(slopes[part, :], neg_scr[me], NT, preferred_element_type=F32)
         twice = -2.0 * row_sum[part, :]
         for (start, depth), off, tail, grad in zip(slices, offs, tails, grads):
             grad[0, part, :depth] = (
@@ -294,52 +367,60 @@
 
     lax.fori_loop(0, length // tile, edges, 0)
 
-    moved = lax.dot_general(shift_scr[0], slopes[...], NN, preferred_element_type=F32)
-    moved = moved - 2.0 * col_sum * neg_scr[0].astype(F32)
+    moved = lax.dot_general(shift_scr[me], slopes[...], NN, preferred_element_type=F32)
+    moved = moved - 2.0 * col_sum * neg_scr[me].astype(F32)
     for (start, depth), grad in zip(slices, grads):
         grad[2, :, :depth] = moved[start : start + depth, :].T
 
 
-def block_math(live_counts, pairs, sums, offs, tails, slices, block_len):
+def block_math(me, live_counts, pairs, sums, offs, tails, old, slices, block_len, half):
     n, n_col = len(slices), len(pairs)
     blocks = live_counts.shape[0]
-    edge_count = blocks * block_len
+    part = blocks // HALVES
     width = sum(depth for _, depth in slices)
     flat = [piece for per_col in pairs for piece in per_col]
+    given = [] if old is None else old
 
     def rows():
         return pl.BlockSpec((block_len, LANES), lambda b: (b, 0))
 
+    first_old = 2 + len(flat) + n_col + 2 * n
     return pl.pallas_call(
-        functools.partial(block_kernel, slices, n_col),
-        out_shape=[jax.ShapeDtypeStruct((3, edge_count, LANES), F32)] * n
+        functools.partial(block_kernel, slices, n_col, half),
+        out_shape=[jax.ShapeDtypeStruct((3, blocks * block_len, LANES), F32)] * n
         + [jax.ShapeDtypeStruct((8, LANES), F32)],
-        grid=(blocks,),
-        in_specs=[whole(SMEM)]
+        grid=(part,),
+        in_specs=[whole(SMEM)] * 2
         + [
             pl.BlockSpec((2, piece.shape[1], block_len), lambda b: (0, 0, b)) for piece in flat
         ]
-        + [pl.BlockSpec((sums.shape[0], 2, block_len), lambda b: (0, 0, b))]
-        + [rows() for _ in range(2 * n)],
-        out_specs=[pl.BlockSpec((3, block_len, LANES), lambda b: (0, b, 0))] * n
+        + [pl.BlockSpec((2, block_len), lambda b: (0, b))] * n_col
+        + [rows() for _ in range(2 * n)]
+        + [whole(pl.ANY)] * len(given),
+        out_specs=[
+            pl.BlockSpec((3, block_len, LANES), lambda b: (0, half * part + b, 0))
+        ]
+        * n
         + [pl.BlockSpec((8, LANES), lambda b: (0, 0))],
+        input_output_aliases={first_old + k: k for k in range(len(given))},
         scratch_shapes=[
             pltpu.VMEM((n_col, width, block_len), BF16),
             pltpu.VMEM((n_col, width, block_len), BF16),
+            pltpu.VMEM((n_col, 2, block_len), F32),
             pltpu.VMEM((block_len, block_len), F32),
             pltpu.VMEM((block_len, block_len), BF16),
             pltpu.VMEM((block_len, LANES), F32),
             pltpu.VMEM((block_len, LANES), F32),
         ],
         compiler_params=params(),
-        cost_estimate=cost(blocks * 8 * block_len * block_len * width, 200e6),
+        cost_estimate=cost(part * 8 * block_len * block_len * width, 120e6),
         name="block_math",
-    )(live_counts, *flat, sums, *offs, *tails)
+    )(me, live_counts, *flat, *sums, *offs, *tails, *given)
 
 
 def outgoing_kernel(slices, capacity, begin, counts_ref, place_ref, *refs):
     n = len(slices)
-    grads, out_ref, tiles = refs[:n], refs[n], refs[n + 1 :]
+    grads, out_ref, tiles = refs[:n], refs[-n - 1], refs[-n:]
     groups, width, chunk = out_ref.shape
 
     def owner(group, carry):
@@ -361,20 +442,20 @@
     lax.fori_loop(0, groups, owner, 0)
 
 
-def outgoing(counts, place_list, grads, slices, begin, chunk):
+def outgoing(counts, place_list, grads, slices, begin, chunk, after):
     groups, capacity = place_list.shape
     n = len(slices)
     width = sum(depth for _, depth in slices)
     return pl.pallas_call(
         functools.partial(outgoing_kernel, slices, capacity, begin),
         out_shape=jax.ShapeDtypeStruct((groups, width, chunk), BF16),
-        in_specs=[whole(SMEM)] * 2 + [whole(VMEM)] * n,
+        in_specs=[whole(SMEM)] * 2 + [whole(VMEM)] * n + [whole(pl.ANY)] * len(after),
         out_specs=whole(VMEM),
         scratch_shapes=[pltpu.VMEM((chunk, LANES), F32)] * n,
         compiler_params=params(),
         cost_estimate=cost(0, 80e6),
         name="outgoing",
-    )(counts, place_list.reshape(-1), *grads)
+    )(counts, place_list.reshape(-1), *grads, *after)
 
 
 def collect_kernel(slices, capacity, begin, first, counts_ref, row_ref, came_ref, *refs):
@@ -472,13 +553,13 @@
 
 def update_entities(weights, totals, first, second, slices):
     width, ent_rows = weights.shape
-    cols = 256 if ent_rows % 256 == 0 else 128
+    cols = 1024
     n = len(slices)
     table = pl.BlockSpec((width, cols), lambda i: (0, i))
     return pl.pallas_call(
         functools.partial(update_kernel, slices),
         out_shape=[jax.ShapeDtypeStruct((width, ent_rows), F32)] * 3,
-        grid=(ent_rows // cols,),
+        grid=(pl.cdiv(ent_rows, cols),),
         in_specs=[table] * 3 + [pl.BlockSpec((cols, LANES), lambda i: (i, 0))] * n,
         out_specs=[table] * 3,
         scratch_shapes=[pltpu.VMEM((width, cols), F32)],
@@ -517,61 +598,93 @@
     rel_total = rel_weight.shape[0]
 
     table_low = entity_table.astype(BF16)
-    rel_table = lax.all_gather(relation_table.astype(BF16), "edge", axis=0, tiled=True)
-    dense = [
-        lax.all_gather(table_low[start : start + depth], "edge", axis=0, tiled=False)
-        for start, depth in slices
-    ]
-
-    place_list, row_list, counts = owner_lists(all_ids, groups, capacity, ent_rows)
+    rel_own = rel_total // groups
+    rel_low = jnp.pad(relation_table.astype(BF16).T, ((0, 0), (0, REL_PAD - rel_own)))
+    bounds = piece_bounds(ent_rows)
+    dense = []
+    for start, depth in slices:
+        for piece in range(PIECES):
+            sent = table_low[start : start + depth, bounds[piece] : bounds[piece + 1]]
+            if piece == 0:
+                sent = jnp.concatenate([sent, rel_low[start : start + depth]], axis=1)
+            dense.append(lax.all_gather(sent, "edge", axis=0, tiled=False))
+
+    place_list, row_list, starts = owner_lists(all_ids, groups, capacity, ent_rows)
+    counts = starts[:, PIECES]
     asked = lax.all_to_all(row_list, "edge", split_axis=0, concat_axis=0, tiled=True)
     asked_counts = jnp.sum((asked < ent_rows).astype(jnp.int32), axis=1)
     safe_places = jnp.minimum(place_list, id_count - 1)
+    starts, place_flat, row_flat = starts.reshape(-1), place_list.reshape(-1), row_list.reshape(-1)
 
     rel_scale = rel_weight * (rel_total / jnp.sum(rel_weight)) / rel_count.astype(F32)
-    rel_slices = []
+    rel_scale = jnp.pad(rel_scale.reshape(groups, rel_own), ((0, 0), (0, REL_PAD - rel_own)))
+    rel_places = relation_ids + (relation_ids // rel_own) * (REL_PAD - rel_own)
+
+    me = lax.axis_index("col").astype(jnp.int32).reshape(1)
+    offs = [[] for _ in range(HALVES)]
+    tails = [[] for _ in range(HALVES)]
+    pairs = [[[] for _ in range(n_col)] for _ in range(HALVES)]
+    parts = [[] for _ in range(HALVES)]
     for k, (start, depth) in enumerate(slices):
-        piece = rel_table[:, start : start + depth].astype(F32)
-        if k < n - 1:
-            rel_slices.append(piece)
-        else:
-            gap = jnp.zeros((rel_total, LANES - 1 - depth), F32)
-            rel_slices.append(jnp.concatenate([piece, gap, rel_scale[:, None]], axis=1))
-    rel_rows = relation_rows(relation_ids, rel_slices)
-
-    offs, tails, own, others, sums = [], [], [], [[] for _ in range(n_col - 1)], []
-    for k, (start, depth) in enumerate(slices):
-        fetched = fetch(counts, place_list, row_list, dense[k])
-        off, tail, pair, part = prepare(fetched, rel_rows[k], depth, blocks, block_len)
-        offs.append(off)
-        tails.append(tail)
-        own.append(pair)
-        sums.append(part)
+        rel_rows = relation_rows(rel_places, dense[k * PIECES], rel_scale)
+        fetched = None
+        for piece in range(PIECES):
+            fetched = fetch(
+                starts,
+                place_flat,
+                row_flat,
+                dense[k * PIECES + piece],
+                fetched,
+                piece,
+                bounds[piece],
+                bounds[piece + 1],
+                ent_rows,
+                id_count,
+            )
+        for half in range(HALVES):
+            off, tail, pair, part = prepare(fetched, rel_rows, depth, blocks, block_len, half)
+            offs[half].append(off)
+            tails[half].append(tail)
+            parts[half].append(part)
+            pairs[half][0].append(pair)
+            for away in range(1, n_col):
+                turn = [(c, (c + away) % n_col) for c in range(n_col)]
+                pairs[half][away].append(lax.ppermute(pair, "col", turn))
+
+    grads, loss_tiles = None, []
+    for half in range(HALVES):
+        part = functools.reduce(jnp.add, parts[half])
+        sums = [part]
         for away in range(1, n_col):
             turn = [(c, (c + away) % n_col) for c in range(n_col)]
-            others[away - 1].append(lax.ppermute(pair, "col", turn))
             sums.append(lax.ppermute(part, "col", turn))
-    sums = jnp.stack(sums)
-
-    *grads, loss_tile = block_math(
-        live_counts, [own] + others, sums, offs, tails, slices, block_len
-    )
+        *grads, loss_tile = block_math(
+            me, live_counts, pairs[half], sums, offs[half], tails[half], grads, slices, block_len, half
+        )
+        loss_tiles.append(loss_tile)
     live = jnp.sum(jnp.minimum(live_counts, block_len)).astype(F32)
-    whole_pair = lax.psum(jnp.stack([jnp.sum(loss_tile), live]), ("edge", "col"))
-    loss_pair = whole_pair / n_col
-
+    loss_own = jnp.sum(functools.reduce(jnp.add, loss_tiles))
+    loss_row = jnp.zeros((8, LANES), F32).at[0, 0].set(loss_own).at[0, 1].set(live)
+    loss_all = lax.all_gather(loss_row, "edge", axis=0, tiled=False)
+    loss_pair = jnp.sum(loss_all[:, 0, :2], axis=0)
+
+    rel_terms = relation_sums(relation_ids, grads, rel_total)
     flat = [grad.reshape(id_count, LANES) for grad in grads]
-    chunks = 4
-    chunk = capacity // chunks
-    arrived = []
-    for k in range(chunks):
-        sent = outgoing(counts, safe_places, flat, slices, k * chunk, chunk)
+    chunk = capacity // CHUNKS
+    arrived, totals, after = [], None, rel_terms[:1]
+    for k in range(CHUNKS):
+        sent = outgoing(
+            counts, safe_places, flat, slices, k * chunk, chunk, after if k > 0 else []
+        )
         arrived.append(lax.all_to_all(sent, "edge", split_axis=0, concat_axis=0, tiled=True))
-    totals = None
-    for k in range(chunks):
-        totals = collect(asked_counts, asked, arrived[k], totals, slices, k * chunk, ent_rows)
-
-    rel_terms = relation_sums(relation_ids, grads, rel_total)
+        if k > 0:
+            totals = collect(
+                asked_counts, asked, arrived[k - 1], totals, slices, (k - 1) * chunk, ent_rows
+            )
+            after = totals[:1]
+    k = CHUNKS - 1
+    totals = collect(asked_counts, asked, arrived[k], totals, slices, k * chunk, ent_rows)
+
     rel_terms = jnp.concatenate(
         [term[:, :depth] for (start, depth), term in zip(slices, rel_terms)], axis=1
     )

time: 1160 us -> 1180 us (1.017)
  waiting for transfers between devices: 354 us -> 299 us
  blocking collectives: 54.5 us -> 94 us
  Pallas kernels: 642 us -> 661 us
    all_to_all x4, waiting for transfers between devices: 150 us -> 29 us  [shards(): lax.all_to_all(sent, 'edge', split_axis=0, concat_axis=0, tiled=True)]
    all_gather x0 -> x1, blocking collectives: none -> 94 us  [shards(): loss_all = lax.all_gather(loss_row, 'edge', axis=0, tiled=False)]
    all_gather x3 -> x8, waiting for transfers between devices: 146 us -> 231 us  [shards(): dense.append(lax.all_gather(sent, 'edge', axis=0, tiled=False))]
    psum x1 -> x0, blocking collectives: 54.5 us -> none  [shards(): lax.psum(jnp.stack([jnp.sum(loss_tile), live]), ('edge', 'col'))]
    pallas_call x4 -> x12, Pallas kernels: 319 us -> 351 us  [the longest x8 228 us: fetch(): pl.pallas_call(functools.partial(fetch_kernel, capacity, piece, begin, en...]
    ppermute x2, waiting for transfers between devices: 47.7 us -> 24 us  [shards(): sums.append(lax.ppermute(part, 'col', turn))]
    ppermute x2 -> x4, waiting for transfers between devices: 0.01 us -> 12.7 us  [shards(): pairs[half][away].append(lax.ppermute(pair, 'col', turn))]
    pallas_call x1, Pallas kernels: 30.3 us -> 18.1 us  [update_entities(): pl.pallas_call(functools.partial(update_kernel, slices), out_shape=[jax.S...]
  transfers between devices with their start and end apart: 13 -> 20, of which waited for: 8 -> 12; matrix products, arithmetic and copies ran while one was open for 5% -> 4% of each run, Pallas kernels for 52% -> 55%
where the time goes in v2:
time: 1180 us; the launch traced here: 1160 us
  Pallas kernels  661 us (56%)
  waiting for transfers between devices  299 us (25%)
  blocking collectives  94 us (8%)
  other arithmetic  34 us (3%)
  starting transfers between devices  30.4 us (3%)
  between operations  15.7 us (1%)
  local copies, waits for them, and re-layouts  15.4 us (1%)
  matrix products  13.7 us (1%)
    all_gather x8, waiting for transfers between devices, shards(): dense.append(lax.all_gather(sent, 'edge', axis=0, tiled=False))  231 us
    pallas_call x8, Pallas kernels, fetch(): pl.pallas_call(functools.partial(fetch_kernel, capacity, piece, begin, en...  228 us
    pallas_call x4, Pallas kernels, collect(): pl.pallas_call(functools.partial(collect_kernel, slices, capacity, begin,...  136 us
    pallas_call x4, Pallas kernels, outgoing(): pl.pallas_call(functools.partial(outgoing_kernel, slices, capacity, begin...  95.2 us
    all_gather x1, blocking collectives, shards(): loss_all = lax.all_gather(loss_row, 'edge', axis=0, tiled=False)  94 us
    pallas_call x2, Pallas kernels, block_math(): pl.pallas_call(functools.partial(block_kernel, slices, n_col, half), out_...  90.5 us
    pallas_call x1, Pallas kernels, relation_sums(): pl.pallas_call(functools.partial(relation_sums_kernel, n), out_shape=[jax...  35.6 us
    pallas_call x2, Pallas kernels, relation_rows(): pl.pallas_call(relation_rows_kernel, out_shape=jax.ShapeDtypeStruct((coun...  32.5 us
  transfers between devices with their start and end apart: 20, of which 12 were waited for; matrix products, arithmetic and copies ran while one was open for 4% of the time, Pallas kernels for 55%

profile of v2, /device:TPU:16, one launch (start us, length us, event | category | flops | bytes accessed | tf_op | source)
XLA Modules:
  0.0 1163.0 jit_solution(794429717399878053)
XLA Ops:
  38.9 11.6 fusion.7
  55.2 40.1 %all-gather.23.cloned.1.call-done = bf16[2048,2304]{1,0:T(8,128)(2,1)} async-done(((bf16[128,2304]{1,0:T(8,128)(2,1)}), bf16[2048,2304]{1,0:T(8,128)(2,1)}) %all-gather.23.cloned.1.call-update) | async-done | bytes 9437200 | tf_op jit(solution)/shard_map/all_gather | solution.py:610
  95.3 25.5 %fetch_rows.8.refs_0_ = f32[24576,128]{1,0:T(8,128)} custom-call(s32[80]{0:T(128)} %reshape.869.starts_ref, s32[32768]{0:T(1024)} %bitcast.53, s32[32768]{0:T(1024)} %bitcast.6.row_ref, bf16[16,128,2304]{2,1,0:T(8,128)(2,1)} %bitcast.48), custom_call_target="tpu_custom_call" | custom-call | bytes 100000000 | tf_op jit(solution)/shard_map/fetch_rows/pallas_call | solution.py:210
  120.7 47.4 %all-gather.21.cloned.1.call-done = bf16[2048,1920]{1,0:T(8,128)(2,1)} async-done(((bf16[128,1920]{1,0:T(8,128)(2,1)}), bf16[2048,1920]{1,0:T(8,128)(2,1)}) %all-gather.21.cloned.1.call-update) | async-done | bytes 7864336 | tf_op jit(solution)/shard_map/all_gather | solution.py:610
  168.1 29.6 %fetch_rows.9.refs_0_ = f32[24576,128]{1,0:T(8,128)} custom-call(s32[80]{0:T(128)} %reshape.869.starts_ref, s32[32768]{0:T(1024)} %bitcast.54, s32[32768]{0:T(1024)} %bitcast.6.row_ref, bf16[16,128,1920]{2,1,0:T(8,128)(2,1)} %bitcast.63, f32[24576,128]{1,0:T(8,128)} %fetch_rows.8.refs_0_), custom_call_target="tpu_custom_call", output_to_operand_aliasing={{}: (4, {})} | custom-call | bytes 100000000 | tf_op jit(solution)/shard_map/fetch_rows/pallas_call | solution.py:210
  197.8 46.3 %all-gather.19.cloned.1.call-done = bf16[2048,2048]{1,0:T(8,128)(2,1)} async-done(((bf16[128,2048]{1,0:T(8,128)(2,1)}), bf16[2048,2048]{1,0:T(8,128)(2,1)}) %all-gather.19.cloned.1.call-update) | async-done | bytes 8388624 | tf_op jit(solution)/shard_map/all_gather | solution.py:610
  244.0 30.1 %fetch_rows.10.refs_0_ = f32[24576,128]{1,0:T(8,128)} custom-call(s32[80]{0:T(128)} %reshape.869.starts_ref, s32[32768]{0:T(1024)} %bitcast.55, s32[32768]{0:T(1024)} %bitcast.6.row_ref, bf16[16,128,2048]{2,1,0:T(8,128)(2,1)} %bitcast.62, f32[24576,128]{1,0:T(8,128)} %fetch_rows.9.refs_0_), custom_call_target="tpu_custom_call", output_to_operand_aliasing={{}: (4, {})} | custom-call | bytes 100000000 | tf_op jit(solution)/shard_map/fetch_rows/pallas_call | solution.py:210
  274.2 42.0 %all-gather.17.cloned.1.call-done = bf16[2048,1920]{1,0:T(8,128)(2,1)} async-done(((bf16[128,1920]{1,0:T(8,128)(2,1)}), bf16[2048,1920]{1,0:T(8,128)(2,1)}) %all-gather.17.cloned.1.call-update) | async-done | bytes 7864336 | tf_op jit(solution)/shard_map/all_gather | solution.py:610
  316.1 29.8 %fetch_rows.11.head_ref.tail_ref.neg_ref = f32[24576,128]{1,0:T(8,128)} custom-call(s32[80]{0:T(128)} %reshape.869.starts_ref, s32[32768]{0:T(1024)} %bitcast.56, s32[32768]{0:T(1024)} %bitcast.6.row_ref, bf16[16,128,1920]{2,1,0:T(8,128)(2,1)} %bitcast.64, f32[24576,128]{1,0:T(8,128)} %fetch_rows.10.refs_0_), custom_call_target="tpu_custom_call", output_to_operand_aliasing={{}: (4, {})} | custom-call | bytes 100000000 | tf_op jit(solution)/shard_map/fetch_rows/pallas_call | solution.py:210
  345.9 16.3 %relation_rows.2.rel_ref = f32[8192,128]{1,0:T(8,128)} custom-call(s32[8192]{0:T(1024)} %fusion.26.ids_ref, bf16[16,128,2304]{2,1,0:T(8,128)(2,1)} %bitcast.49, f32[16,256]{1,0:T(8,128)} %pad.20.scale_ref), custom_call_target="tpu_custom_call" | custom-call | bytes 30000000 | tf_op jit(solution)/shard_map/relation_rows/pallas_call | solution.py:127
  376.9 25.3 %fetch_rows.12.refs_0_ = f32[24576,128]{1,0:T(8,128)} custom-call(s32[80]{0:T(128)} %reshape.869.starts_ref, s32[32768]{0:T(1024)} %bitcast.57, s32[32768]{0:T(1024)} %bitcast.6.row_ref, bf16[16,72,2304]{2,1,0:T(8,128)(2,1)} %bitcast.51), custom_call_target="tpu_custom_call" | custom-call | bytes 100000000 | tf_op jit(solution)/shard_map/fetch_rows/pallas_call | solution.py:210
  402.2 16.2 %relation_rows.3.rel_ref = f32[8192,128]{1,0:T(8,128)} custom-call(s32[8192]{0:T(1024)} %fusion.26.ids_ref, bf16[16,72,2304]{2,1,0:T(8,128)(2,1)} %bitcast.52, f32[16,256]{1,0:T(8,128)} %pad.20.scale_ref), custom_call_target="tpu_custom_call" | custom-call | bytes 30000000 | tf_op jit(solution)/shard_map/relation_rows/pallas_call | solution.py:127
  425.5 29.1 %fetch_rows.13.refs_0_ = f32[24576,128]{1,0:T(8,128)} custom-call(s32[80]{0:T(128)} %reshape.869.starts_ref, s32[32768]{0:T(1024)} %bitcast.58, s32[32768]{0:T(1024)} %bitcast.6.row_ref, bf16[16,72,1920]{2,1,0:T(8,128)(2,1)} %bitcast.70, f32[24576,128]{1,0:T(8,128)} %fetch_rows.12.refs_0_), custom_call_target="tpu_custom_call", output_to_operand_aliasing={{}: (4, {})} | custom-call | bytes 100000000 | tf_op jit(solution)/shard_map/fetch_rows/pallas_call | solution.py:210
  454.7 25.1 %all-gather.27.cloned.1.call-done = bf16[1152,2048]{1,0:T(8,128)(2,1)} async-done(((bf16[72,2048]{1,0:T(8,128)(2,1)}), bf16[1152,2048]{1,0:T(8,128)(2,1)}) %all-gather.27.cloned.1.call-update) | async-done | bytes 4718608 | tf_op jit(solution)/shard_map/all_gather | solution.py:610
  479.8 29.6 %fetch_rows.14.refs_0_ = f32[24576,128]{1,0:T(8,128)} custom-call(s32[80]{0:T(128)} %reshape.869.starts_ref, s32[32768]{0:T(1024)} %bitcast.59, s32[32768]{0:T(1024)} %bitcast.6.row_ref, bf16[16,72,2048]{2,1,0:T(8,128)(2,1)} %bitcast.69, f32[24576,128]{1,0:T(8,128)} %fetch_rows.13.refs_0_), custom_call_target="tpu_custom_call", output_to_operand_aliasing={{}: (4, {})} | custom-call | bytes 100000000 | tf_op jit(solution)/shard_map/fetch_rows/pallas_call | solution.py:210
  509.4 22.8 %all-gather.25.cloned.1.call-done = bf16[1152,1920]{1,0:T(8,128)(2,1)} async-done(((bf16[72,1920]{1,0:T(8,128)(2,1)}), bf16[1152,1920]{1,0:T(8,128)(2,1)}) %all-gather.25.cloned.1.call-update) | async-done | bytes 4423696 | tf_op jit(solution)/shard_map/all_gather | solution.py:610
  532.2 28.9 %fetch_rows.15.head_ref.tail_ref.neg_ref = f32[24576,128]{1,0:T(8,128)} custom-call(s32[80]{0:T(128)} %reshape.869.starts_ref, s32[32768]{0:T(1024)} %bitcast.60, s32[32768]{0:T(1024)} %bitcast.6.row_ref, bf16[16,72,1920]{2,1,0:T(8,128)(2,1)} %bitcast.71, f32[24576,128]{1,0:T(8,128)} %fetch_rows.14.refs_0_), custom_call_target="tpu_custom_call", output_to_operand_aliasing={{}: (4, {})} | custom-call | bytes 100000000 | tf_op jit(solution)/shard_map/fetch_rows/pallas_call | solution.py:210
  583.8 12.7 %collective-permute-done.1.refs_3_ = bf16[2,72,4096]{2,1,0:T(8,128)(2,1)} collective-permute-done((bf16[2,72,4096]{2,1,0:T(8,128)(2,1)}, bf16[2,72,4096]{2,1,0:T(8,128)(2,1)}, u32[]{:S(2)}, u32[]{:S(2)}) %collective-permute-start.1) | collective-permute-done | bytes 1179680 | tf_op jit(solution)/shard_map/ppermute | solution.py:652
  597.9 24.0 %collective-permute-done.2.refs_5_ = f32[2,4096]{1,0:T(2,128)S(1)} collective-permute-done((f32[2,4096]{1,0:T(2,128)S(1)}, f32[2,4096]{1,0:T(2,128)S(1)}, u32[]{:S(2)}, u32[]{:S(2)}) %collective-permute-start.2) | collective-permute-done | bytes 32800 | tf_op jit(solution)/shard_map/ppermute | solution.py:660
  622.6 45.2 %block_math.2 = (f32[3,8192,128]{2,1,0:T(8,128)}, f32[3,8192,128]{2,1,0:T(8,128)}, f32[8,128]{1,0:T(8,128)}) custom-call(s32[1]{0:T(128)} %bitcast.me_ref, s32[8]{0:T(128)} %live_ref.3, bf16[2,128,4096]{2,1,0:T(8,128)(2,1)} %get-tuple-element.66.refs_0_, bf16[2,72,4096]{2,1,0:T(8,128)(2,1)} %get-tuple-element.67.refs_1_, ...), custom_call_target="tpu_custom_call" | custom-call | flops 6710886400 | bytes 120000000 | tf_op jit(solution)/shard_map/block_math/pallas_call | solution.py:388
  669.5 45.3 %block_math.3 = (f32[3,8192,128]{2,1,0:T(8,128)}, f32[3,8192,128]{2,1,0:T(8,128)}, f32[8,128]{1,0:T(8,128)}) custom-call(s32[1]{0:T(128)} %bitcast.me_ref, s32[8]{0:T(128)} %live_ref.3, bf16[2,128,4096]{2,1,0:T(8,128)(2,1)} %get-tuple-element.75.refs_0_, ...), custom_call_target="tpu_custom_call", output_to_operand_aliasing={{0}: (12, {}), {1}: (13, {})} | custom-call | flops 6710886400 | bytes 120000000 | tf_op jit(solution)/shard_map/block_math/pallas_call | solution.py:388
  714.8 27.7 %outgoing.5 = bf16[16,200,512]{2,1,0:T(8,128)(2,1)} custom-call(s32[16]{0:T(128)} %slice_reduce_fusion.counts_ref, s32[32768]{0:T(1024)} %broadcast_minimum_fusion.place_ref, f32[24576,128]{1,0:T(8,128)} %bitcast.40, f32[24576,128]{1,0:T(8,128)} %bitcast.44), custom_call_target="tpu_custom_call" | custom-call | bytes 80000000 | tf_op jit(solution)/shard_map/outgoing/pallas_call | solution.py:449
  747.1 35.6 %relation_sums.1 = (f32[3200,128]{1,0:T(8,128)}, f32[3200,128]{1,0:T(8,128)}) custom-call(s32[8192]{0:T(1024)} %ids_ref.1, f32[3,8192,128]{2,1,0:T(8,128)} %get-tuple-element.86.refs_0_, f32[3,8192,128]{2,1,0:T(8,128)} %get-tuple-element.87.refs_1_), custom_call_target="tpu_custom_call" | custom-call | bytes 120000000 | tf_op jit(solution)/shard_map/relation_sums/pallas_call | solution.py:531
  782.7 27.7 %outgoing.4 = bf16[16,200,512]{2,1,0:T(8,128)(2,1)} custom-call(s32[16]{0:T(128)} %slice_reduce_fusion.counts_ref, s32[32768]{0:T(1024)} %broadcast_minimum_fusion.place_ref, f32[24576,128]{1,0:T(8,128)} %bitcast.41, f32[24576,128]{1,0:T(8,128)} %bitcast.45, f32[3200,128]{1,0:T(8,128)} %get-tuple-element.88.refs_2_), custom_call_target="tpu_custom_call" | custom-call | bytes 80000000 | tf_op jit(solution)/shard_map/outgoing/pallas_call | solution.py:449
  827.3 41.8 %collect.4 = (f32[7944,128]{1,0:T(8,128)}, f32[7944,128]{1,0:T(8,128)}) custom-call(s32[16]{0:T(128)} %fusion.12.counts_ref, s32[32768]{0:T(1024)} %bitcast.65, bf16[16,200,512]{2,1,0:T(8,128)(2,1)} %copy-done.3), custom_call_target="tpu_custom_call" | custom-call | bytes 120000000 | tf_op jit(solution)/shard_map/collect/pallas_call | solution.py:499
  869.1 26.8 %outgoing.7 = bf16[16,200,512]{2,1,0:T(8,128)(2,1)} custom-call(s32[16]{0:T(128)} %slice_reduce_fusion.counts_ref, s32[32768]{0:T(1024)} %broadcast_minimum_fusion.place_ref, f32[24576,128]{1,0:T(8,128)} %bitcast.42, f32[24576,128]{1,0:T(8,128)} %bitcast.46, f32[7944,128]{1,0:T(8,128)} %get-tuple-element.89.refs_0_.refs_2_), custom_call_target="tpu_custom_call" | custom-call | bytes 80000000 | tf_op jit(solution)/shard_map/outgoing/pallas_call | solution.py:449
  905.6 43.9 %collect.5 = (f32[7944,128]{1,0:T(8,128)}, f32[7944,128]{1,0:T(8,128)}) custom-call(s32[16]{0:T(128)} %fusion.12.counts_ref, s32[32768]{0:T(1024)} %bitcast.66, bf16[16,200,512]{2,1,0:T(8,128)(2,1)} %copy-done.2, f32[7944,128]{1,0:T(8,128)} %get-tuple-element.89.refs_0_.refs_2_, f32[7944,128]{1,0:T(8,128)} %get-tuple-element.90.refs_1_), custom_call_target="tpu_custom_call" | custom-call | bytes 120000000 | tf_op jit(solution)/shard_map/collect/pallas_call | solution.py:499
  949.6 13.0 %outgoing.6 = bf16[16,200,512]{2,1,0:T(8,128)(2,1)} custom-call(s32[16]{0:T(128)} %slice_reduce_fusion.counts_ref, s32[32768]{0:T(1024)} %broadcast_minimum_fusion.place_ref, f32[24576,128]{1,0:T(8,128)} %bitcast.43, f32[24576,128]{1,0:T(8,128)} %bitcast.47, f32[7944,128]{1,0:T(8,128)} %get-tuple-element.91.refs_2_.refs_0_), custom_call_target="tpu_custom_call" | custom-call | bytes 80000000 | tf_op jit(solution)/shard_map/outgoing/pallas_call | solution.py:449
  962.6 16.0 %all-to-all-done.4.came_ref = bf16[16,200,512]{2,1,0:T(8,128)(2,1)S(1)} async-done(((bf16[16,200,512]{2,1,0:T(8,128)(2,1)}), bf16[16,200,512]{2,1,0:T(8,128)(2,1)S(1)}, u32[]{:S(2)}, u32[]{:S(2)}) %all-to-all-start.4) | async-done | bytes 3276832 | tf_op jit(solution)/shard_map/all_to_all | solution.py:679
  991.9 94.0 %all_gather.74 = f32[16,8,128]{2,1,0:T(8,128)S(1)} all-gather(f32[1,8,128]{2,1,0:T(8,128)S(1)} %scatter.9), channel_id=1, replica_groups=mesh['edge'=16,'col'=2] {'edge'}, dimensions={0}, use_global_device_ids=true | all-gather | bytes 69632 | tf_op jit(solution)/shard_map/all_gather | solution.py:668
  1088.4 41.4 %collect.6 = (f32[7944,128]{1,0:T(8,128)}, f32[7944,128]{1,0:T(8,128)}) custom-call(s32[16]{0:T(128)} %fusion.12.counts_ref, s32[32768]{0:T(1024)} %bitcast.67, bf16[16,200,512]{2,1,0:T(8,128)(2,1)} %copy-done.1, f32[7944,128]{1,0:T(8,128)} %get-tuple-element.91.refs_2_.refs_0_, f32[7944,128]{1,0:T(8,128)} %get-tuple-element.92.refs_1_), custom_call_target="tpu_custom_call" | custom-call | bytes 120000000 | tf_op jit(solution)/shard_map/collect/pallas_call | solution.py:499
  1138.3 18.1 %update_entities.1 = (f32[200,7936]{1,0:T(8,128)}, f32[200,7936]{1,0:T(8,128)}, f32[200,7936]{1,0:T(8,128)}) custom-call(f32[200,7936]{1,0:T(8,128)} %weights_ref.1, f32[200,7936]{1,0:T(8,128)} %first_ref.1, f32[200,7936]{1,0:T(8,128)} %second_ref.1, f32[7944,128]{1,0:T(8,128)} %get-tuple-element.95.refs_0_, f32[7944,128]{1,0:T(8,128)} %get-tuple-element.96.refs_1_), custom_call_target="tpu_custom_call" | custom-call | bytes 60000000 | tf_op jit(solution)/shard_map/update_entities/pallas_call | solution.py:559
  (156 shorter events, 138.4 us)
Async XLA Ops:
  7.2 88.1 %all-gather.23.cloned.1.call-start = ((), (), s32[]{:S(2)}) async-start(), calls=%async_computation.10 | async-start | bytes 10027008 | tf_op jit(solution)/shard_map/all_gather | solution.py:610
  13.5 6.8 copy-start.11
  13.6 154.5 %all-gather.21.cloned.1.call-start = ((), (), s32[]{:S(2)}) async-start(), calls=%async_computation.9 | async-start | bytes 8355840 | tf_op jit(solution)/shard_map/all_gather | solution.py:610
  14.7 229.3 %all-gather.19.cloned.1.call-start = ((), (), s32[]{:S(2)}) async-start(), calls=%async_computation.8 | async-start | bytes 8912896 | tf_op jit(solution)/shard_map/all_gather | solution.py:610
  15.4 300.7 %all-gather.17.cloned.1.call-start = ((), (), s32[]{:S(2)}) async-start(), calls=%async_computation.7 | async-start | bytes 8355840 | tf_op jit(solution)/shard_map/all_gather | solution.py:610
  16.0 360.9 %all-gather.31.cloned.1.call-start = ((), (), s32[]{:S(2)}) async-start(), calls=%async_computation.14 | async-start | bytes 5640192 | tf_op jit(solution)/shard_map/all_gather | solution.py:610
  17.7 407.8 %all-gather.29.cloned.1.call-start = ((), (), s32[]{:S(2)}) async-start(), calls=%async_computation.13 | async-start | bytes 4700160 | tf_op jit(solution)/shard_map/all_gather | solution.py:610
  18.6 461.2 %all-gather.27.cloned.1.call-start = ((), (), s32[]{:S(2)}) async-start(), calls=%async_computation.12 | async-start | bytes 5013504 | tf_op jit(solution)/shard_map/all_gather | solution.py:610
  19.4 512.8 %all-gather.25.cloned.1.call-start = ((), (), s32[]{:S(2)}) async-start(), calls=%async_computation.11 | async-start | bytes 4700160 | tf_op jit(solution)/shard_map/all_gather | solution.py:610
  38.9 12.5 %copy-start.14 = (f32[3200]{0:T(1024)S(1)}, f32[3200]{0:T(1024)}, u32[]{:S(2)}) copy-start(f32[3200]{0:T(1024)} %param.22) | copy-start | bytes 38404
  38.9 13.8 %copy-start.20 = (s32[3200]{0:T(1024)S(1)}, s32[3200]{0:T(1024)}, u32[]{:S(2)}) copy-start(s32[3200]{0:T(1024)} %param.23) | copy-start | bytes 38404
  38.9 14.5 %copy-start.9 = (s32[8192]{0:T(1024)S(1)}, s32[8192]{0:T(1024)}, u32[]{:S(2)}) copy-start(s32[8192]{0:T(1024)} %ids_ref.1) | copy-start | bytes 98308
  368.5 253.4 %collective-permute-start = (bf16[2,128,4096]{2,1,0:T(8,128)(2,1)}, bf16[2,128,4096]{2,1,0:T(8,128)(2,1)}, u32[]{:S(2)}, u32[]{:S(2)}) collective-permute-start(bf16[2,128,4096]{2,1,0:T(8,128)(2,1)} %get-tuple-element.66.refs_0_), channel_id=1, source_target_pairs={{0,1},{1,0},{2,3},{3,2},{4,5},{5,4},{6,7},{7,6},{8,9},{9,8},{10,11... | collective-permute-start | bytes 6291464 | tf_op jit(solution)/shard_map/ppermute | solution.py:652
  376.4 291.5 %collective-permute-start.3 = (bf16[2,128,4096]{2,1,0:T(8,128)(2,1)}, bf16[2,128,4096]{2,1,0:T(8,128)(2,1)S(1)}, u32[]{:S(2)}, u32[]{:S(2)}) collective-permute-start(bf16[2,128,4096]{2,1,0:T(8,128)(2,1)} %get-tuple-element.75.refs_0_), channel_id=1, source_target_pairs={{0,1},{1,0},{2,3},{3,2},{4,5},{5,4},{6,7},{7,6},{8,9},{9,8},{10,11... | collective-permute-start | bytes 6291464 | tf_op jit(solution)/shard_map/ppermute | solution.py:652
  567.3 29.1 %collective-permute-start.1 = (bf16[2,72,4096]{2,1,0:T(8,128)(2,1)}, bf16[2,72,4096]{2,1,0:T(8,128)(2,1)}, u32[]{:S(2)}, u32[]{:S(2)}) collective-permute-start(bf16[2,72,4096]{2,1,0:T(8,128)(2,1)} %get-tuple-element.67.refs_1_), channel_id=1, source_target_pairs={{0,1},{1,0},{2,3},{3,2},{4,5},{5,4},{6,7},{7,6},{8,9},{9,8},{10,11... | collective-permute-start | bytes 3538952 | tf_op jit(solution)/shard_map/ppermute | solution.py:652
  568.8 173.7 %all-to-all-start = ((s32[16,1,2048]{2,1,0:T(1,128)}), s32[16,1,2048]{2,1,0:T(1,128)S(1)}, u32[]{:S(2)}, u32[]{:S(2)}) async-start(s32[16,1,2048]{2,1,0:T(1,128)} %bitcast.21), calls=%async_computation | async-start | bytes 262144 | tf_op jit(solution)/shard_map/all_to_all | solution.py:614
  573.2 7.5 copy-start.16
  573.2 7.5 copy-start.18
  573.2 9.8 copy-start.15
  579.5 88.4 %collective-permute-start.4 = (bf16[2,72,4096]{2,1,0:T(8,128)(2,1)}, bf16[2,72,4096]{2,1,0:T(8,128)(2,1)S(1)}, u32[]{:S(2)}, u32[]{:S(2)}) collective-permute-start(bf16[2,72,4096]{2,1,0:T(8,128)(2,1)} %get-tuple-element.76.refs_1_), channel_id=1, source_target_pairs={{0,1},{1,0},{2,3},{3,2},{4,5},{5,4},{6,7},{7,6},{8,9},{9,8},{10,11... | collective-permute-start | bytes 3538952 | tf_op jit(solution)/shard_map/ppermute | solution.py:652
  580.7 41.3 %copy-start.17 = (f32[2,4096]{1,0:T(2,128)}, f32[2,4096]{1,0:T(2,128)S(1)}, u32[]{:S(2)}) copy-start(f32[2,4096]{1,0:T(2,128)S(1)} %add.245.refs_4_) | copy-start | bytes 98308
  580.7 41.2 %collective-permute-start.2 = (f32[2,4096]{1,0:T(2,128)S(1)}, f32[2,4096]{1,0:T(2,128)S(1)}, u32[]{:S(2)}, u32[]{:S(2)}) collective-permute-start(f32[2,4096]{1,0:T(2,128)S(1)} %add.245.refs_4_), channel_id=1, source_target_pairs={{0,1},{1,0},{2,3},{3,2},{4,5},{5,4},{6,7},{7,6},{8,9},{9,8},{10,11... | collective-permute-start | bytes 98312 | tf_op jit(solution)/shard_map/ppermute | solution.py:660
  583.8 84.0 %copy-start.13 = (f32[2,4096]{1,0:T(2,128)}, f32[2,4096]{1,0:T(2,128)S(1)}, u32[]{:S(2)}) copy-start(f32[2,4096]{1,0:T(2,128)S(1)} %add.246.refs_4_) | copy-start | bytes 98308
  596.4 71.4 %collective-permute-start.5 = (f32[2,4096]{1,0:T(2,128)S(1)}, f32[2,4096]{1,0:T(2,128)S(1)}, u32[]{:S(2)}, u32[]{:S(2)}) collective-permute-start(f32[2,4096]{1,0:T(2,128)S(1)} %add.246.refs_4_), channel_id=1, source_target_pairs={{0,1},{1,0},{2,3},{3,2},{4,5},{5,4},{6,7},{7,6},{8,9},{9,8},{10,11... | collective-permute-start | bytes 98312 | tf_op jit(solution)/shard_map/ppermute | solution.py:660
  742.5 83.9 %copy-start.4 = (s32[16,1,2048]{2,1,0:T(1,128)}, s32[16,1,2048]{2,1,0:T(1,128)S(1)}, u32[]{:S(2)}) copy-start(s32[16,1,2048]{2,1,0:T(1,128)S(1)} %all-to-all-done) | copy-start | bytes 393220
  742.5 77.5 %all-to-all-start.2 = ((bf16[16,200,512]{2,1,0:T(8,128)(2,1)}), bf16[16,200,512]{2,1,0:T(8,128)(2,1)S(1)}, u32[]{:S(2)}, u32[]{:S(2)}) async-start(bf16[16,200,512]{2,1,0:T(8,128)(2,1)} %outgoing.5), calls=%async_computation.2 | async-start | bytes 6553600 | tf_op jit(solution)/shard_map/all_to_all | solution.py:679
  821.7 77.6 %all-to-all-start.1 = ((bf16[16,200,512]{2,1,0:T(8,128)(2,1)}), bf16[16,200,512]{2,1,0:T(8,128)(2,1)S(1)}, u32[]{:S(2)}, u32[]{:S(2)}) async-start(bf16[16,200,512]{2,1,0:T(8,128)(2,1)} %outgoing.4), calls=%async_computation.1 | async-start | bytes 6553600 | tf_op jit(solution)/shard_map/all_to_all | solution.py:679
  901.0 77.6 %all-to-all-start.4 = ((bf16[16,200,512]{2,1,0:T(8,128)(2,1)}), bf16[16,200,512]{2,1,0:T(8,128)(2,1)S(1)}, u32[]{:S(2)}, u32[]{:S(2)}) async-start(bf16[16,200,512]{2,1,0:T(8,128)(2,1)} %outgoing.7), calls=%async_computation.4 | async-start | bytes 6553600 | tf_op jit(solution)/shard_map/all_to_all | solution.py:679
  978.6 8.7 copy-start.1
  978.6 151.3 %all-to-all-start.3 = ((bf16[16,200,512]{2,1,0:T(8,128)(2,1)}), bf16[16,200,512]{2,1,0:T(8,128)(2,1)}, u32[]{:S(2)}, u32[]{:S(2)}) async-start(bf16[16,200,512]{2,1,0:T(8,128)(2,1)} %outgoing.6), calls=%async_computation.3 | async-start | bytes 6553600 | tf_op jit(solution)/shard_map/all_to_all | solution.py:679
  983.3 103.1 %reduce-scatter.2.cloned.1.call-start = ((), (), s32[]{:S(2)}) async-start(), calls=%async_computation.6 | async-start | bytes 3481600 | tf_op jit(solution)/shard_map/reduce_scatter | solution.py:691
  983.3 103.1 %copy-start.8 = (f32[200,200]{1,0:T(8,128)S(1)}, f32[200,200]{1,0:T(8,128)}, u32[]{:S(2)}) copy-start(f32[200,200]{1,0:T(8,128)} %param.27) | copy-start | bytes 480004
  (13 other events, 46.9 us)
Sparse Core Ops, SparseCore 0:
  13.7 81.5 all-gather.22
  98.1 69.9 all-gather.20
  170.8 73.1 all-gather.18
  246.2 69.9 all-gather.16
  318.1 54.9 all-gather.30
  375.1 50.3 all-gather.28
  427.8 51.9 all-gather.26
  481.9 50.2 all-gather.24
  988.5 88.3 reduce-scatter.1

commit v3 on v2

--- a/solution.py
+++ b/solution.py
@@ -19,10 +19,8 @@
 LANES = 128
 UNROLL = 8
 PARTS = 4
-PIECES = 4
 HALVES = 2
-CHUNKS = 4
-REL_PAD = 256
+TURN = 512
 NN = (((1,), (0,)), ((), ()))
 NT = (((1,), (1,)), ((), ()))
 TN = (((0,), (0,)), ((), ()))
@@ -59,30 +57,20 @@
     return [(at, min(LANES, width - at)) for at in range(0, width, LANES)]
 
 
-def piece_bounds(ent_rows):
-    tiles = ent_rows // LANES
-    cuts = [LANES * ((tiles * k + PIECES - 1) // PIECES) for k in range(PIECES)]
-    return cuts + [ent_rows]
-
-
 def owner_lists(all_ids, groups, capacity, ent_rows):
     count = all_ids.shape[0]
     owners = all_ids // ent_rows
     local_rows = all_ids - owners * ent_rows
     chunk = 256
-    pieces = sum((local_rows >= cut).astype(jnp.int32) for cut in piece_bounds(ent_rows)[1:-1])
-    buckets = owners * PIECES + pieces
-    mine = buckets[None, :] == jnp.arange(groups * PIECES, dtype=jnp.int32)[:, None]
-    mine = mine.astype(BF16).reshape(groups * PIECES, count // chunk, chunk)
+    mine = owners[None, :] == jnp.arange(groups, dtype=jnp.int32)[:, None]
+    mine = mine.astype(BF16).reshape(groups, count // chunk, chunk)
     before = jnp.triu(jnp.ones((chunk, chunk), BF16), 1)
     inner = jnp.dot(mine, before, preferred_element_type=F32)
     sums = jnp.sum(mine.astype(F32), axis=2)
-    in_bucket = jnp.sum(sums, axis=1).reshape(groups, PIECES)
-    ends = jnp.cumsum(in_bucket, axis=1)
-    carry = jnp.cumsum(sums, axis=1) - sums + (ends - in_bucket).reshape(-1, 1)
+    carry = jnp.cumsum(sums, axis=1) - sums
     ranks = jnp.sum(mine.astype(F32) * (inner + carry[:, :, None]), axis=0)
     ranks = ranks.astype(jnp.int32).reshape(count)
-    starts = jnp.concatenate([jnp.zeros((groups, 1), F32), ends], axis=1).astype(jnp.int32)
+    counts = jnp.sum(sums, axis=1).astype(jnp.int32)
     high = owners * (capacity // LANES) + ranks // LANES
     low = ranks % LANES
     tall = groups * capacity // LANES
@@ -96,135 +84,127 @@
     place = found[:, 0] * 256 + found[:, 1]
     place_list = jnp.where(place > 0, place - 1, count).reshape(groups, capacity)
     row_list = jnp.where(place > 0, found[:, 2] * 256 + found[:, 3], ent_rows)
-    return place_list, row_list.reshape(groups, capacity), starts
-
-
-def relation_rows_kernel(ids_ref, table_ref, scale_ref, out_ref, columns, rows):
-    groups, depth, span = table_ref.shape
-    columns[...] = jnp.zeros_like(columns)
-
-    def turn(group, carry):
-        columns[:depth, :] = table_ref[group].astype(F32)
-        if depth < LANES:
-            columns[LANES - 1 :, :] = scale_ref[pl.ds(group, 1), :]
-        rows[pl.ds(pl.multiple_of(group * span, span), span), :] = columns[...].T
-        return carry
-
-    lax.fori_loop(0, groups, turn, 0)
+    return place_list, row_list.reshape(groups, capacity), counts
+
+
+def relation_rows_kernel(n_slices, ids_ref, *refs):
+    tables, outs = refs[:n_slices], refs[n_slices:]
+    count = outs[0].shape[0]
 
     def body(step, carry):
         for lane in range(UNROLL):
             at = step * UNROLL + lane
-            out_ref[pl.ds(at, 1), :] = rows[pl.ds(ids_ref[at], 1), :]
+            row = ids_ref[at]
+            for table, out in zip(tables, outs):
+                out[pl.ds(at, 1), :] = table[pl.ds(row, 1), :]
         return carry
 
-    lax.fori_loop(0, out_ref.shape[0] // UNROLL, body, 0)
-
-
-def relation_rows(places, dense, scale):
-    count = places.shape[0]
-    groups, depth, span = dense.shape
+    lax.fori_loop(0, count // UNROLL, body, 0)
+
+
+def relation_rows(relation_ids, tables):
+    count = relation_ids.shape[0]
+    n = len(tables)
     return pl.pallas_call(
-        relation_rows_kernel,
-        out_shape=jax.ShapeDtypeStruct((count, LANES), F32),
-        grid=(1,),
-        in_specs=[
-            whole(SMEM),
-            pl.BlockSpec((groups, depth, REL_PAD), lambda i: (0, 0, span // REL_PAD - 1)),
-            whole(VMEM),
+        functools.partial(relation_rows_kernel, n),
+        out_shape=[jax.ShapeDtypeStruct((count, LANES), F32)] * n,
+        in_specs=[whole(SMEM)] + [whole(VMEM)] * n,
+        out_specs=[whole(VMEM)] * n,
+        compiler_params=params(),
+        cost_estimate=cost(0, 30e6 * n),
+        name="relation_rows",
+    )(relation_ids, *tables)
+
+
+def fetch_kernel(capacity, moves, counts_ref, place_ref, row_ref, dense_ref, out_ref, *rows):
+    shard = pl.program_id(0)
+    last = pl.num_programs(0) - 1
+    depth, ent_rows = dense_ref.shape[1:]
+    turns = ent_rows // TURN
+    rest = ent_rows - turns * TURN
+
+    if depth < LANES:
+
+        @pl.when(shard == 0)
+        def _():
+            for ref in rows:
+                ref[...] = jnp.zeros_like(ref)
+
+    def turn(into, begin, size):
+        cols = pl.ds(begin, size)
+        into[cols, :depth] = dense_ref[0, :, cols].astype(F32).T
+
+    def move(source, at):
+        out_ref[pl.ds(place_ref[at], 1), :] = source[pl.ds(row_ref[at], 1), :]
+
+    def step(into, source):
+        base = (shard - 1) * capacity
+
+        def remaining(first):
+            def body(trip, carry):
+                for lane in range(UNROLL):
+                    move(source, base + first + trip * UNROLL + lane)
+                return carry
+
+            wanted = counts_ref[jnp.maximum(shard - 1, 0)] - first
+            lax.fori_loop(0, (wanted + UNROLL - 1) // UNROLL, body, 0)
+
+        def only_turn(trip, carry):
+            turn(into, pl.multiple_of(trip * TURN, TURN), TURN)
+            return carry
+
+        def both(trip, carry):
+            turn(into, pl.multiple_of(trip * TURN, TURN), TURN)
+            for lane in range(moves):
+                move(source, base + trip * moves + lane)
+            return carry
+
+        @pl.when(shard == 0)
+        def _():
+            lax.fori_loop(0, turns, only_turn, 0)
+
+        @pl.when((shard > 0) & (shard < last))
+        def _():
+            lax.fori_loop(0, turns, both, 0)
+            remaining(turns * moves)
+
+        @pl.when(shard == last)
+        def _():
+            remaining(0)
+
+        if rest:
+
+            @pl.when(shard < last)
+            def _():
+                turn(into, turns * TURN, rest)
+
+    for parity in range(2):
+
+        @pl.when(lax.rem(shard, 2) == parity)
+        def _():
+            step(rows[parity], rows[1 - parity])
+
+
+def fetch(counts, place_list, row_list, dense, id_count):
+    groups, depth, ent_rows = dense.shape
+    capacity = place_list.shape[0] // groups
+    moves = (id_count // groups) // (ent_rows // TURN) // UNROLL * UNROLL
+    return pl.pallas_call(
+        functools.partial(fetch_kernel, capacity, moves),
+        out_shape=jax.ShapeDtypeStruct((id_count + 8, LANES), F32),
+        grid=(groups + 1,),
+        in_specs=[whole(SMEM)] * 3
+        + [
+            pl.BlockSpec(
+                (1, depth, ent_rows), lambda shard: (jnp.minimum(shard, groups - 1), 0, 0)
+            )
         ],
         out_specs=whole(VMEM),
-        scratch_shapes=[
-            pltpu.VMEM((LANES, REL_PAD), F32),
-            pltpu.VMEM((groups * REL_PAD, LANES), F32),
-        ],
+        scratch_shapes=[pltpu.VMEM((ent_rows + 8, LANES), F32)] * 2,
         compiler_params=params(),
-        cost_estimate=cost(0, 30e6),
-        name="relation_rows",
-    )(places, dense, scale)
-
-
-def fetch_kernel(capacity, piece, begin, end, starts_ref, place_ref, row_ref, dense_ref, *refs):
-    (old_ref,) = refs[:1] if piece > 0 else (None,)
-    out_ref, rows, kept, sem = refs[-4:]
-    shard = pl.program_id(0)
-    depth = dense_ref.shape[1]
-    step_cols = 256 if begin % 256 == 0 and end % 256 == 0 else 128
-
-    if piece > 0:
-
-        @pl.when(shard == 0)
-        def _():
-            pltpu.make_async_copy(old_ref, kept, sem).start()
-
-    if depth < LANES:
-
-        @pl.when(shard == 0)
-        def _():
-            rows[...] = jnp.zeros_like(rows)
-
-    def turn(step, carry):
-        cols = pl.ds(pl.multiple_of(step * step_cols, step_cols), step_cols)
-        into = pl.ds(pl.multiple_of(begin + step * step_cols, step_cols), step_cols)
-        rows[into, :depth] = dense_ref[0, :, cols].astype(F32).T
-        return carry
-
-    lax.fori_loop(0, (end - begin) // step_cols, turn, 0, unroll=True)
-
-    if piece > 0:
-
-        @pl.when(shard == 0)
-        def _():
-            pltpu.make_async_copy(old_ref, kept, sem).wait()
-
-    first = starts_ref[shard * (PIECES + 1) + piece] + shard * capacity
-    wanted = starts_ref[shard * (PIECES + 1) + piece + 1] + shard * capacity - first
-
-    def move(at):
-        kept[pl.ds(place_ref[at], 1), :] = rows[pl.ds(row_ref[at], 1), :]
-
-    def body(step, carry):
-        for lane in range(UNROLL):
-            move(first + step * UNROLL + lane)
-        return carry
-
-    def last(step, carry):
-        move(first + step)
-        return carry
-
-    trips = wanted // UNROLL
-    lax.fori_loop(0, trips, body, 0)
-    lax.fori_loop(trips * UNROLL, wanted, last, 0)
-
-    @pl.when(shard == pl.num_programs(0) - 1)
-    def _():
-        copy = pltpu.make_async_copy(kept, out_ref, sem)
-        copy.start()
-        copy.wait()
-
-
-def fetch(starts, place_list, row_list, dense, old, piece, begin, end, ent_rows, id_count):
-    groups, depth, _ = dense.shape
-    capacity = place_list.shape[0] // groups
-    given = [] if old is None else [old]
-    return pl.pallas_call(
-        functools.partial(fetch_kernel, capacity, piece, begin, end),
-        out_shape=jax.ShapeDtypeStruct((id_count, LANES), F32),
-        grid=(groups,),
-        in_specs=[whole(SMEM)] * 3
-        + [pl.BlockSpec((1, depth, end - begin), lambda shard: (shard, 0, 0))]
-        + [whole(pl.ANY)] * len(given),
-        out_specs=whole(pl.ANY),
-        input_output_aliases={4: 0} if given else {},
-        scratch_shapes=[
-            pltpu.VMEM((ent_rows, LANES), F32),
-            pltpu.VMEM((id_count, LANES), F32),
-            pltpu.SemaphoreType.DMA,
-        ],
-        compiler_params=params(),
-        cost_estimate=cost(0, 100e6),
+        cost_estimate=cost(0, 170e6),
         name="fetch_rows",
-    )(starts, place_list, row_list, dense, *given)
+    )(counts, place_list, row_list, dense)
 
 
 def prepare_kernel(depth, head_ref, tail_ref, neg_ref, rel_ref, off_ref, tail_out, pair_ref, sums_ref):
@@ -294,81 +274,81 @@
     for k in range(n_col):
         slot = lax.rem(me + (n_col - k), n_col)
         for (start, depth), pair in zip(slices, pairs[k]):
-            shift_scr[slot, start : start + depth, :] = pair[0]
+            shift_scr[slot, start : start + depth, :] = 2.0 * pair[0]
             neg_scr[slot, start : start + depth, :] = pair[1]
         sums_scr[slot] = sums_refs[k][...]
     bias = jnp.sum(sums_scr[:, 0, :], axis=0, keepdims=True) + MARGIN
     neg_norm = jnp.sum(sums_scr[:, 1, :], axis=0, keepdims=True)
     row_bias[...] = jnp.broadcast_to(bias, (LANES, length)).T
 
-    tile = min(256, length)
-
-    def matmul(step, carry):
-        part = pl.ds(pl.multiple_of(step * tile, tile), tile)
-        total = None
+    live = live_ref[half * pl.num_programs(0) + block]
+    tile = 256
+    small = 128
+    lane_tiles = [slice(at, at + LANES) for at in range(0, length, LANES)]
+    cols = jnp.zeros((8, length), F32)
+    loss = jnp.zeros((8, LANES), F32)
+    def products(at):
+        part = slice(at, at + tile)
+        doubled = None
         for k in range(n_col):
             term = lax.dot_general(
                 shift_scr[k, :, part], neg_scr[k], TN, preferred_element_type=F32
             )
-            total = term if total is None else total + term
-        cross[part, :] = total
-        return carry
-
-    lax.fori_loop(0, length // tile, matmul, 0)
-
-    live = live_ref[half * pl.num_programs(0) + block]
-    small = 64
-
-    def pairwise(step, carry):
-        loss, cols = carry
-        begin = pl.multiple_of(step * small, small)
-        part = pl.ds(begin, small)
-        place = begin + lax.broadcasted_iota(jnp.int32, (small, 1), 0)
-        scale = offs[-1][part, LANES - 1 : LANES]
-        weight = jnp.where(place < live, scale, 0.0) / length
-        margins = 2.0 * cross[part, :] + (row_bias[part, 0:1] - neg_norm)
-        fall = jnp.exp(-jnp.abs(margins))
-        under = 1.0 + fall
-        inverse = 1.0 / under
-        logs = jnp.where(fall < 2.0**-11, fall * (1.0 - 0.5 * fall), jnp.log(under))
-        soft = jnp.maximum(margins, 0.0) + logs
-        slope = weight * jnp.where(margins >= 0.0, inverse, fall * inverse)
-        row_sum[part, :] = jnp.broadcast_to(
-            jnp.sum(slope, axis=1, keepdims=True), (small, LANES)
-        )
-        slopes[part, :] = (2.0 * slope).astype(BF16)
-        loss = loss + jnp.sum((weight * soft).reshape(small // 8, 8, length), axis=0)
-        cols = cols + jnp.sum(slope.reshape(small // 8, 8, length), axis=0)
-        return loss, cols
-
-    zero = jnp.zeros((8, length), F32)
-    loss, cols = lax.fori_loop(0, length // small, pairwise, (zero, zero))
+            doubled = term if doubled is None else doubled + term
+        cross[part, :] = doubled
+
+    def moves(at):
+        part = slice(at, at + tile)
+        moved = lax.dot_general(slopes[part, :], neg_scr[me], NT, preferred_element_type=F32)
+        fade = -row_sum[part, :]
+        for (start, depth), off, tail, grad in zip(slices, offs, tails, grads):
+            grad[0, part, :depth] = (
+                fade[:, :depth] * tail[part, :depth].astype(F32) + moved[:, start : start + depth]
+            )
+            grad[1, part, :] = fade * off[part, :]
+
+    products(0)
+    for begin in range(0, length, tile):
+        if begin + tile < length:
+            products(begin + tile)
+        for at in range(begin, begin + tile, small):
+            part = slice(at, at + small)
+            place = at + lax.broadcasted_iota(jnp.int32, (small, 1), 0)
+            scale = offs[-1][part, LANES - 1 : LANES]
+            weight = jnp.where(place < live, scale, 0.0) / length
+            margins = cross[part, :] + (row_bias[part, 0:1] - neg_norm)
+            fall = jnp.exp(-jnp.abs(margins))
+            under = 1.0 + fall
+            guess = pl.reciprocal(under, approx=True)
+            inverse = guess * (2.0 - under * guess)
+            twice = (2.0 * weight) * (jnp.where(margins >= 0.0, 1.0, fall) * inverse)
+            row_sum[part, :] = jnp.broadcast_to(
+                jnp.sum(twice, axis=1, keepdims=True), (small, LANES)
+            )
+            slopes[part, :] = twice.astype(BF16)
+            cols = cols + jnp.sum(twice.reshape(small // 8, 8, length), axis=0)
+            over = jnp.maximum(margins, 0.0)
+            lifts = [fall[:, lanes] for lanes in lane_tiles]
+            while len(lifts) > 1:
+                lifts = [a + b + a * b for a, b in zip(lifts[::2], lifts[1::2])]
+            lift = lifts[0]
+            soft = functools.reduce(jnp.add, [over[:, lanes] for lanes in lane_tiles]) + jnp.where(
+                lift < 2.0**-11, lift * (1.0 - 0.5 * lift), jnp.log(1.0 + lift)
+            )
+            loss = loss + jnp.sum((weight * soft).reshape(small // 8, 8, LANES), axis=0)
+        moves(begin)
     col_sum = jnp.sum(cols, axis=0, keepdims=True)
-    loss_part = jnp.sum(loss.reshape(8, length // LANES, LANES), axis=1)
 
     @pl.when(block == 0)
     def _():
-        loss_ref[...] = loss_part
+        loss_ref[...] = loss
 
     @pl.when(block > 0)
     def _():
-        loss_ref[...] += loss_part
-
-    def edges(step, carry):
-        part = pl.ds(pl.multiple_of(step * tile, tile), tile)
-        moved = lax.dot_general(slopes[part, :], neg_scr[me], NT, preferred_element_type=F32)
-        twice = -2.0 * row_sum[part, :]
-        for (start, depth), off, tail, grad in zip(slices, offs, tails, grads):
-            grad[0, part, :depth] = (
-                twice[:, :depth] * tail[part, :depth].astype(F32) + moved[:, start : start + depth]
-            )
-            grad[1, part, :] = twice * off[part, :]
-        return carry
-
-    lax.fori_loop(0, length // tile, edges, 0)
+        loss_ref[...] += loss
 
     moved = lax.dot_general(shift_scr[me], slopes[...], NN, preferred_element_type=F32)
-    moved = moved - 2.0 * col_sum * neg_scr[me].astype(F32)
+    moved = 0.5 * moved - col_sum * neg_scr[me].astype(F32)
     for (start, depth), grad in zip(slices, grads):
         grad[2, :, :depth] = moved[start : start + depth, :].T
 
@@ -509,7 +489,7 @@
 
 
 def relation_sums_kernel(n, ids_ref, *refs):
-    grads, totals = refs[:n], refs[n:]
+    grads, totals = refs[:n], refs[-n:]
     count = grads[0].shape[1]
     for total in totals:
         total[...] = jnp.zeros_like(total)
@@ -525,7 +505,7 @@
     lax.fori_loop(0, count // UNROLL, body, 0)
 
 
-def relation_sums(relation_ids, grads, rel_total):
+def relation_sums(relation_ids, grads, rel_total, after):
     n = len(grads)
     count = relation_ids.shape[0]
     return pl.pallas_call(
@@ -533,12 +513,13 @@
         out_shape=[jax.ShapeDtypeStruct((rel_total, LANES), F32)] * n,
         grid=(1,),
         in_specs=[whole(SMEM)]
-        + [pl.BlockSpec((1, count, LANES), lambda i: (0, 0, 0))] * n,
+        + [pl.BlockSpec((1, count, LANES), lambda i: (0, 0, 0))] * n
+        + [whole(pl.ANY)] * len(after),
         out_specs=[whole(VMEM)] * n,
         compiler_params=params(),
         cost_estimate=cost(0, 120e6),
         name="relation_sums",
-    )(relation_ids, *grads)
+    )(relation_ids, *grads, *after)
 
 
 def update_kernel(slices, weights_ref, first_ref, second_ref, *refs):
@@ -567,6 +548,17 @@
         cost_estimate=cost(0, 60e6),
         name="update_entities",
     )(weights, first, second, *totals)
+
+
+def chunk_bounds(capacity):
+    units = capacity // LANES
+    small = max(1, 3 * units // 16)
+    large = (units - 2 * small) // 2
+    sizes = [small, large, units - 2 * small - large, small]
+    bounds = [0]
+    for size in sizes:
+        bounds.append(bounds[-1] + size * LANES)
+    return bounds
 
 
 def shards(
@@ -598,27 +590,30 @@
     rel_total = rel_weight.shape[0]
 
     table_low = entity_table.astype(BF16)
+    dense = [
+        lax.all_gather(table_low[start : start + depth], "edge", axis=0, tiled=False)
+        for start, depth in slices
+    ]
     rel_own = rel_total // groups
-    rel_low = jnp.pad(relation_table.astype(BF16).T, ((0, 0), (0, REL_PAD - rel_own)))
-    bounds = piece_bounds(ent_rows)
-    dense = []
-    for start, depth in slices:
-        for piece in range(PIECES):
-            sent = table_low[start : start + depth, bounds[piece] : bounds[piece + 1]]
-            if piece == 0:
-                sent = jnp.concatenate([sent, rel_low[start : start + depth]], axis=1)
-            dense.append(lax.all_gather(sent, "edge", axis=0, tiled=False))
-
-    place_list, row_list, starts = owner_lists(all_ids, groups, capacity, ent_rows)
-    counts = starts[:, PIECES]
+    rel_low = jnp.broadcast_to(relation_table.astype(BF16)[None], (groups, rel_own, width))
+    rel_table = lax.all_to_all(rel_low, "edge", split_axis=0, concat_axis=0, tiled=True)
+    rel_table = rel_table.reshape(rel_total, width)
+
+    place_list, row_list, counts = owner_lists(all_ids, groups, capacity, ent_rows)
     asked = lax.all_to_all(row_list, "edge", split_axis=0, concat_axis=0, tiled=True)
     asked_counts = jnp.sum((asked < ent_rows).astype(jnp.int32), axis=1)
     safe_places = jnp.minimum(place_list, id_count - 1)
-    starts, place_flat, row_flat = starts.reshape(-1), place_list.reshape(-1), row_list.reshape(-1)
+    place_flat, row_flat = place_list.reshape(-1), row_list.reshape(-1)
 
     rel_scale = rel_weight * (rel_total / jnp.sum(rel_weight)) / rel_count.astype(F32)
-    rel_scale = jnp.pad(rel_scale.reshape(groups, rel_own), ((0, 0), (0, REL_PAD - rel_own)))
-    rel_places = relation_ids + (relation_ids // rel_own) * (REL_PAD - rel_own)
+    rel_slices = []
+    for k, (start, depth) in enumerate(slices):
+        piece = rel_table[:, start : start + depth].astype(F32)
+        if k == n - 1:
+            gap = jnp.zeros((rel_total, LANES - 1 - depth), F32)
+            piece = jnp.concatenate([piece, gap, rel_scale[:, None]], axis=1)
+        rel_slices.append(piece)
+    rel_rows = relation_rows(relation_ids, rel_slices)
 
     me = lax.axis_index("col").astype(jnp.int32).reshape(1)
     offs = [[] for _ in range(HALVES)]
@@ -626,23 +621,9 @@
     pairs = [[[] for _ in range(n_col)] for _ in range(HALVES)]
     parts = [[] for _ in range(HALVES)]
     for k, (start, depth) in enumerate(slices):
-        rel_rows = relation_rows(rel_places, dense[k * PIECES], rel_scale)
-        fetched = None
-        for piece in range(PIECES):
-            fetched = fetch(
-                starts,
-                place_flat,
-                row_flat,
-                dense[k * PIECES + piece],
-                fetched,
-                piece,
-                bounds[piece],
-                bounds[piece + 1],
-                ent_rows,
-                id_count,
-            )
+        fetched = fetch(counts, place_flat, row_flat, dense[k], id_count)
         for half in range(HALVES):
-            off, tail, pair, part = prepare(fetched, rel_rows, depth, blocks, block_len, half)
+            off, tail, pair, part = prepare(fetched, rel_rows[k], depth, blocks, block_len, half)
             offs[half].append(off)
             tails[half].append(tail)
             parts[half].append(part)
@@ -664,31 +645,39 @@
         loss_tiles.append(loss_tile)
     live = jnp.sum(jnp.minimum(live_counts, block_len)).astype(F32)
     loss_own = jnp.sum(functools.reduce(jnp.add, loss_tiles))
-    loss_row = jnp.zeros((8, LANES), F32).at[0, 0].set(loss_own).at[0, 1].set(live)
-    loss_all = lax.all_gather(loss_row, "edge", axis=0, tiled=False)
+    loss_row = jnp.zeros((LANES,), F32).at[0].set(loss_own).at[1].set(live)
+    loss_all = lax.all_to_all(
+        jnp.broadcast_to(loss_row, (groups, 1, LANES)), "edge", split_axis=0, concat_axis=0, tiled=True
+    )
     loss_pair = jnp.sum(loss_all[:, 0, :2], axis=0)
 
-    rel_terms = relation_sums(relation_ids, grads, rel_total)
     flat = [grad.reshape(id_count, LANES) for grad in grads]
-    chunk = capacity // CHUNKS
-    arrived, totals, after = [], None, rel_terms[:1]
-    for k in range(CHUNKS):
+    bounds = chunk_bounds(capacity)
+    chunks = len(bounds) - 1
+    arrived, totals, after = [], None, []
+    for k in range(chunks):
         sent = outgoing(
-            counts, safe_places, flat, slices, k * chunk, chunk, after if k > 0 else []
+            counts, safe_places, flat, slices, bounds[k], bounds[k + 1] - bounds[k], after
         )
         arrived.append(lax.all_to_all(sent, "edge", split_axis=0, concat_axis=0, tiled=True))
+        after = []
         if k > 0:
             totals = collect(
-                asked_counts, asked, arrived[k - 1], totals, slices, (k - 1) * chunk, ent_rows
+                asked_counts, asked, arrived[k - 1], totals, slices, bounds[k - 1], ent_rows
             )
             after = totals[:1]
-    k = CHUNKS - 1
-    totals = collect(asked_counts, asked, arrived[k], totals, slices, k * chunk, ent_rows)
-
-    rel_terms = jnp.concatenate(
-        [term[:, :depth] for (start, depth), term in zip(slices, rel_terms)], axis=1
-    )
-    relation_grad = lax.psum_scatter(rel_terms, "edge", scatter_dimension=0, tiled=True)
+        if k == 1:
+            rel_terms = relation_sums(relation_ids, grads, rel_total, [totals[0], loss_all])
+            after = rel_terms[:1]
+            rel_terms = jnp.concatenate(
+                [term[:, :depth] for (start, depth), term in zip(slices, rel_terms)], axis=1
+            )
+            relation_grad = lax.psum_scatter(rel_terms, "edge", scatter_dimension=0, tiled=True)
+        if k == chunks - 2:
+            after = [totals[0], relation_grad]
+    k = chunks - 1
+    totals = collect(asked_counts, asked, arrived[k], totals, slices, bounds[k], ent_rows)
+
     new_entity, new_entity_first, new_entity_second = update_entities(
         entity_table, totals, entity_first, entity_second, slices
     )

time: 1180 us -> 893 us (0.76)
  Pallas kernels: 661 us -> 483 us
  blocking collectives: 94 us -> 0 us
  starting transfers between devices: 30.4 us -> 47.1 us
  waiting for transfers between devices: 299 us -> 283 us
    pallas_call x10 -> x3, Pallas kernels: 260 us -> 118 us  [the longest x2 98.7 us: fetch(): pl.pallas_call(functools.partial(fetch_kernel, capacity, moves), out_shap...]
    all_gather x1 -> x0, blocking collectives: 94 us -> none  [shards(): loss_all = lax.all_gather(loss_row, 'edge', axis=0, tiled=False)]
    all_gather x8 -> x2, waiting for transfers between devices: 231 us -> 145 us  [shards(): lax.all_gather(table_low[start:start + depth], 'edge', axis=0, tiled=False)]
    reduce_scatter x1, waiting for transfers between devices: 0.01 us -> 46.3 us  [shards(): lax.psum_scatter(rel_terms, 'edge', scatter_dimension=0, tiled=True)]
    pallas_call x2, Pallas kernels: 90.5 us -> 52 us  [block_math(): pl.pallas_call(functools.partial(block_kernel, slices, n_col, half), out_...]
    all_to_all x0 -> x2, waiting for transfers between devices: none -> 22.6 us  [the longest x1 22.6 us: shards(): lax.all_to_all(rel_low, 'edge', split_axis=0, concat_axis=0, tiled=True)]
  transfers between devices with their start and end apart: 20 -> 16, of which waited for: 12 -> 8; matrix products, arithmetic and copies ran while one was open for 4% -> 5% of each run, Pallas kernels for 55% -> 52%
where the time goes in v3:
time: 893 us; the launch traced here: 887 us
  Pallas kernels  483 us (54%)
  waiting for transfers between devices  283 us (32%)
  starting transfers between devices  47.1 us (5%)
  other arithmetic  33.3 us (4%)
  between operations  15.6 us (2%)
  matrix products  12.2 us (1%)
  local copies, waits for them, and re-layouts  12 us (1%)
    all_gather x2, waiting for transfers between devices, shards(): lax.all_gather(table_low[start:start + depth], 'edge', axis=0, tiled=False)  145 us
    pallas_call x4, Pallas kernels, collect(): pl.pallas_call(functools.partial(collect_kernel, slices, capacity, begin,...  138 us
    pallas_call x2, Pallas kernels, fetch(): pl.pallas_call(functools.partial(fetch_kernel, capacity, moves), out_shap...  98.7 us
    pallas_call x4, Pallas kernels, outgoing(): pl.pallas_call(functools.partial(outgoing_kernel, slices, capacity, begin...  96.3 us
    pallas_call x2, Pallas kernels, block_math(): pl.pallas_call(functools.partial(block_kernel, slices, n_col, half), out_...  52 us
    reduce_scatter x1, waiting for transfers between devices, shards(): lax.psum_scatter(rel_terms, 'edge', scatter_dimension=0, tiled=True)  46.3 us
    pallas_call x1, Pallas kernels, relation_sums(): pl.pallas_call(functools.partial(relation_sums_kernel, n), out_shape=[jax...  35.5 us
    all_to_all x4, waiting for transfers between devices, shards(): lax.all_to_all(sent, 'edge', split_axis=0, concat_axis=0, tiled=True)  33.8 us
  transfers between devices with their start and end apart: 16, of which 8 were waited for; matrix products, arithmetic and copies ran while one was open for 5% of the time, Pallas kernels for 52%

profile of v3, /device:TPU:16, one launch (start us, length us, event | category | flops | bytes accessed | tf_op | source)
XLA Modules:
  0.0 887.1 jit_solution(4418680502304810204)
XLA Ops:
  13.1 6.2 all-to-all-start
  27.9 8.7 broadcast_multiply_fusion
  36.6 11.7 %fusion.6 = s32[256,512]{1,0:T(8,128)S(1)} fusion(bf16[512,24576]{1,0:T(8,128)(2,1)} %bitcast.38, s32[24576]{0:T(1024)S(1)} %get-tuple-element.117), kind=kOutput, calls=%fused_computation.15 | convolution fusion | flops 6448873472 | bytes 25788416 | tf_op jit(solution)/shard_map/dot_general | solution.py:82
  52.1 22.6 %all-to-all-done = bf16[16,200,200]{2,1,0:T(8,128)(2,1)} async-done(((bf16[16,200,200]{2,1,0:T(8,128)(2,1)}), bf16[16,200,200]{2,1,0:T(8,128)(2,1)}, u32[]{:S(2)}, u32[]{:S(2)}) %all-to-all-start) | async-done | bytes 1280032 | tf_op jit(solution)/shard_map/all_to_all | solution.py:599
  80.0 19.4 %relation_rows.1 = (f32[8192,128]{1,0:T(8,128)}, f32[8192,128]{1,0:T(8,128)}) custom-call(s32[8192]{0:T(1024)} %ids_ref.3, f32[3200,128]{1,0:T(8,128)} %slice_convert_fusion.1.refs_0_, f32[3200,128]{1,0:T(8,128)} %pad_maximum_fusion.1.refs_1_), custom_call_target="tpu_custom_call" | custom-call | bytes 60000000 | tf_op jit(solution)/shard_map/relation_rows/pallas_call | solution.py:108
  99.4 110.6 %all-gather.5.cloned.1.call-done = bf16[2048,7936]{1,0:T(8,128)(2,1)} async-done(((bf16[128,7936]{1,0:T(8,128)(2,1)}), bf16[2048,7936]{1,0:T(8,128)(2,1)}) %all-gather.5.cloned.1.call-update) | async-done | bytes 32505872 | tf_op jit(solution)/shard_map/all_gather | solution.py:594
  210.0 49.0 %fetch_rows.2.head_ref.tail_ref.neg_ref = f32[24584,128]{1,0:T(8,128)} custom-call(s32[16]{0:T(128)} %convert_element_type.65.counts_ref, s32[32768]{0:T(1024)} %bitcast.44, s32[32768]{0:T(1024)} %bitcast.6.row_ref, bf16[16,128,7936]{2,1,0:T(8,128)(2,1)} %bitcast.37), custom_call_target="tpu_custom_call" | custom-call | bytes 170000000 | tf_op jit(solution)/shard_map/fetch_rows/pallas_call | solution.py:192
  259.0 6.3 prepare.4
  266.8 6.8 prepare.6
  274.0 34.2 %all-gather.7.cloned.1.call-done = bf16[1152,7936]{1,0:T(8,128)(2,1)} async-done(((bf16[72,7936]{1,0:T(8,128)(2,1)}), bf16[1152,7936]{1,0:T(8,128)(2,1)}) %all-gather.7.cloned.1.call-update) | async-done | bytes 18284560 | tf_op jit(solution)/shard_map/all_gather | solution.py:594
  308.1 49.6 %fetch_rows.3.head_ref.tail_ref.neg_ref = f32[24584,128]{1,0:T(8,128)} custom-call(s32[16]{0:T(128)} %convert_element_type.65.counts_ref, s32[32768]{0:T(1024)} %bitcast.45, s32[32768]{0:T(1024)} %bitcast.6.row_ref, bf16[16,72,7936]{2,1,0:T(8,128)(2,1)} %bitcast.39), custom_call_target="tpu_custom_call" | custom-call | bytes 170000000 | tf_op jit(solution)/shard_map/fetch_rows/pallas_call | solution.py:192
  365.3 6.3 prepare.7
  381.1 11.9 %collective-permute-done.1.refs_3_ = bf16[2,72,4096]{2,1,0:T(8,128)(2,1)} collective-permute-done((bf16[2,72,4096]{2,1,0:T(8,128)(2,1)}, bf16[2,72,4096]{2,1,0:T(8,128)(2,1)}, u32[]{:S(2)}, u32[]{:S(2)}) %collective-permute-start.1) | collective-permute-done | bytes 1179680 | tf_op jit(solution)/shard_map/ppermute | solution.py:633
  394.4 24.1 %collective-permute-done.2.refs_5_ = f32[2,4096]{1,0:T(2,128)S(1)} collective-permute-done((f32[2,4096]{1,0:T(2,128)S(1)}, f32[2,4096]{1,0:T(2,128)S(1)}, u32[]{:S(2)}, u32[]{:S(2)}) %collective-permute-start.2) | collective-permute-done | bytes 32800 | tf_op jit(solution)/shard_map/ppermute | solution.py:641
  419.2 25.9 %block_math.2 = (f32[3,8192,128]{2,1,0:T(8,128)}, f32[3,8192,128]{2,1,0:T(8,128)}, f32[8,128]{1,0:T(8,128)}) custom-call(s32[1]{0:T(128)} %bitcast.me_ref, s32[8]{0:T(128)} %live_ref.3, bf16[2,128,4096]{2,1,0:T(8,128)(2,1)} %get-tuple-element.69.refs_0_, bf16[2,72,4096]{2,1,0:T(8,128)(2,1)} %get-tuple-element.71.refs_1_, ...), custom_call_target="tpu_custom_call" | custom-call | flops 6710886400 | bytes 120000000 | tf_op jit(solution)/shard_map/block_math/pallas_call | solution.py:368
  446.5 26.0 %block_math.3 = (f32[3,8192,128]{2,1,0:T(8,128)}, f32[3,8192,128]{2,1,0:T(8,128)}, f32[8,128]{1,0:T(8,128)}) custom-call(s32[1]{0:T(128)} %bitcast.me_ref, s32[8]{0:T(128)} %live_ref.3, bf16[2,128,4096]{2,1,0:T(8,128)(2,1)} %get-tuple-element.79.refs_0_, ...), custom_call_target="tpu_custom_call", output_to_operand_aliasing={{0}: (12, {}), {1}: (13, {})} | custom-call | flops 6710886400 | bytes 120000000 | tf_op jit(solution)/shard_map/block_math/pallas_call | solution.py:368
  480.9 23.5 %outgoing.5 = bf16[16,200,384]{2,1,0:T(8,128)(2,1)} custom-call(s32[16]{0:T(128)} %convert_element_type.65.counts_ref, s32[32768]{0:T(1024)} %broadcast_minimum_fusion.place_ref, f32[24576,128]{1,0:T(8,128)} %bitcast.29, f32[24576,128]{1,0:T(8,128)} %bitcast.33), custom_call_target="tpu_custom_call" | custom-call | bytes 80000000 | tf_op jit(solution)/shard_map/outgoing/pallas_call | solution.py:429
  505.0 6.0 all-to-all-start.4
  511.1 32.4 %outgoing.4 = bf16[16,200,640]{2,1,0:T(8,128)(2,1)} custom-call(s32[16]{0:T(128)} %convert_element_type.65.counts_ref, s32[32768]{0:T(1024)} %broadcast_minimum_fusion.place_ref, f32[24576,128]{1,0:T(8,128)} %bitcast.30, f32[24576,128]{1,0:T(8,128)} %bitcast.34), custom_call_target="tpu_custom_call" | custom-call | bytes 80000000 | tf_op jit(solution)/shard_map/outgoing/pallas_call | solution.py:429
  543.5 23.0 %all-to-all-done.4.came_ref = bf16[16,200,384]{2,1,0:T(8,128)(2,1)S(1)} async-done(((bf16[16,200,384]{2,1,0:T(8,128)(2,1)}), bf16[16,200,384]{2,1,0:T(8,128)(2,1)S(1)}, u32[]{:S(2)}, u32[]{:S(2)}) %all-to-all-start.4) | async-done | bytes 2457632 | tf_op jit(solution)/shard_map/all_to_all | solution.py:662
  573.5 33.7 %collect.4 = (f32[7944,128]{1,0:T(8,128)}, f32[7944,128]{1,0:T(8,128)}) custom-call(s32[16]{0:T(128)} %fusion.12.counts_ref, s32[32768]{0:T(1024)} %bitcast.40, bf16[16,200,384]{2,1,0:T(8,128)(2,1)} %copy-done.1), custom_call_target="tpu_custom_call" | custom-call | bytes 120000000 | tf_op jit(solution)/shard_map/collect/pallas_call | solution.py:479
  607.2 35.5 %relation_sums.1 = (f32[3200,128]{1,0:T(8,128)}, f32[3200,128]{1,0:T(8,128)}) custom-call(s32[8192]{0:T(1024)} %ids_ref.3, f32[3,8192,128]{2,1,0:T(8,128)} %get-tuple-element.90.refs_0_, f32[3,8192,128]{2,1,0:T(8,128)} %get-tuple-element.91.refs_1_, f32[7944,128]{1,0:T(8,128)} %get-tuple-element.92.refs_0_.refs_2_, f32[16,1,128]{2,1,0:T(1,128)} %copy-done.16), custom_call_target="tpu_custom_call" | custom-call | bytes 120000000 | tf_op jit(solution)/shard_map/relation_sums/pallas_call | solution.py:511
  642.8 27.9 %outgoing.7 = bf16[16,200,640]{2,1,0:T(8,128)(2,1)} custom-call(s32[16]{0:T(128)} %convert_element_type.65.counts_ref, s32[32768]{0:T(1024)} %broadcast_minimum_fusion.place_ref, f32[24576,128]{1,0:T(8,128)} %bitcast.31, f32[24576,128]{1,0:T(8,128)} %bitcast.35, f32[3200,128]{1,0:T(8,128)} %get-tuple-element.95.refs_2_), custom_call_target="tpu_custom_call" | custom-call | bytes 80000000 | tf_op jit(solution)/shard_map/outgoing/pallas_call | solution.py:429
  670.6 6.3 all-to-all-start.6
  679.0 53.0 %collect.5 = (f32[7944,128]{1,0:T(8,128)}, f32[7944,128]{1,0:T(8,128)}) custom-call(s32[16]{0:T(128)} %fusion.12.counts_ref, s32[32768]{0:T(1024)} %bitcast.41, bf16[16,200,640]{2,1,0:T(8,128)(2,1)} %all-to-all-done.3.came_ref, f32[7944,128]{1,0:T(8,128)} %get-tuple-element.92.refs_0_.refs_2_, f32[7944,128]{1,0:T(8,128)} %get-tuple-element.93.refs_1_), custom_call_target="tpu_custom_call" | custom-call | bytes 120000000 | tf_op jit(solution)/shard_map/collect/pallas_call | solution.py:479
  732.0 46.3 %reduce-scatter.2.cloned.1.call-done.refs_3_ = f32[200,200]{1,0:T(8,128)} async-done(((f32[3200,200]{1,0:T(8,128)}), f32[200,200]{1,0:T(8,128)}) %reduce-scatter.2.cloned.1.call-update) | async-done | bytes 160016 | tf_op jit(solution)/shard_map/reduce_scatter | solution.py:675
  778.3 12.5 %outgoing.6 = bf16[16,200,384]{2,1,0:T(8,128)(2,1)} custom-call(s32[16]{0:T(128)} %convert_element_type.65.counts_ref, s32[32768]{0:T(1024)} %broadcast_minimum_fusion.place_ref, f32[24576,128]{1,0:T(8,128)} %bitcast.32, f32[24576,128]{1,0:T(8,128)} %bitcast.36, f32[7944,128]{1,0:T(8,128)} %get-tuple-element.94.refs_2_.refs_0_, ...), custom_call_target="tpu_custom_call" | custom-call | bytes 80000000 | tf_op jit(solution)/shard_map/outgoing/pallas_call | solution.py:429
  790.9 6.7 all-to-all-start.5
  799.0 43.1 %collect.6 = (f32[7944,128]{1,0:T(8,128)}, f32[7944,128]{1,0:T(8,128)}) custom-call(s32[16]{0:T(128)} %fusion.12.counts_ref, s32[32768]{0:T(1024)} %bitcast.42, bf16[16,200,640]{2,1,0:T(8,128)(2,1)} %all-to-all-done.6.came_ref, f32[7944,128]{1,0:T(8,128)} %get-tuple-element.94.refs_2_.refs_0_, f32[7944,128]{1,0:T(8,128)} %get-tuple-element.97.refs_1_), custom_call_target="tpu_custom_call" | custom-call | bytes 120000000 | tf_op jit(solution)/shard_map/collect/pallas_call | solution.py:479
  842.1 10.8 %all-to-all-done.5.came_ref = bf16[16,200,384]{2,1,0:T(8,128)(2,1)S(1)} async-done(((bf16[16,200,384]{2,1,0:T(8,128)(2,1)}), bf16[16,200,384]{2,1,0:T(8,128)(2,1)S(1)}, u32[]{:S(2)}, u32[]{:S(2)}) %all-to-all-start.5) | async-done | bytes 2457632 | tf_op jit(solution)/shard_map/all_to_all | solution.py:662
  854.4 8.1 collect.7
  862.5 18.1 %update_entities.1 = (f32[200,7936]{1,0:T(8,128)}, f32[200,7936]{1,0:T(8,128)}, f32[200,7936]{1,0:T(8,128)}) custom-call(f32[200,7936]{1,0:T(8,128)} %weights_ref.1, f32[200,7936]{1,0:T(8,128)} %first_ref.1, f32[200,7936]{1,0:T(8,128)} %second_ref.1, f32[7944,128]{1,0:T(8,128)} %get-tuple-element.100.refs_0_, f32[7944,128]{1,0:T(8,128)} %get-tuple-element.101.refs_1_), custom_call_target="tpu_custom_call" | custom-call | bytes 60000000 | tf_op jit(solution)/shard_map/update_entities/pallas_call | solution.py:540
  (131 shorter events, 65.0 us)
Async XLA Ops:
  7.2 202.8 %all-gather.5.cloned.1.call-start = ((), (), s32[]{:S(2)}) async-start(), calls=%async_computation.9 | async-start | bytes 34537472 | tf_op jit(solution)/shard_map/all_gather | solution.py:594
  13.1 61.6 %all-to-all-start = ((bf16[16,200,200]{2,1,0:T(8,128)(2,1)}), bf16[16,200,200]{2,1,0:T(8,128)(2,1)}, u32[]{:S(2)}, u32[]{:S(2)}) async-start(bf16[16,200,200]{2,1,0:T(8,128)(2,1)} %broadcast_in_dim.43), calls=%async_computation | async-start | bytes 3276800 | tf_op jit(solution)/shard_map/all_to_all | solution.py:599
  19.3 288.8 %all-gather.7.cloned.1.call-start = ((), (), s32[]{:S(2)}) async-start(), calls=%async_computation.10 | async-start | bytes 19427328 | tf_op jit(solution)/shard_map/all_gather | solution.py:594
  36.6 12.4 %copy-start.18 = (f32[3200]{0:T(1024)S(1)}, f32[3200]{0:T(1024)}, u32[]{:S(2)}) copy-start(f32[3200]{0:T(1024)} %param.22) | copy-start | bytes 38404
  36.6 13.7 %copy-start.24 = (s32[3200]{0:T(1024)S(1)}, s32[3200]{0:T(1024)}, u32[]{:S(2)}) copy-start(s32[3200]{0:T(1024)} %param.23) | copy-start | bytes 38404
  265.3 153.2 %collective-permute-start = (bf16[2,128,4096]{2,1,0:T(8,128)(2,1)}, bf16[2,128,4096]{2,1,0:T(8,128)(2,1)}, u32[]{:S(2)}, u32[]{:S(2)}) collective-permute-start(bf16[2,128,4096]{2,1,0:T(8,128)(2,1)} %get-tuple-element.69.refs_0_), channel_id=1, source_target_pairs={{0,1},{1,0},{2,3},{3,2},{4,5},{5,4},{6,7},{7,6},{8,9},{9,8},{10,11... | collective-permute-start | bytes 6291464 | tf_op jit(solution)/shard_map/ppermute | solution.py:633
  273.7 171.5 %collective-permute-start.3 = (bf16[2,128,4096]{2,1,0:T(8,128)(2,1)}, bf16[2,128,4096]{2,1,0:T(8,128)(2,1)S(1)}, u32[]{:S(2)}, u32[]{:S(2)}) collective-permute-start(bf16[2,128,4096]{2,1,0:T(8,128)(2,1)} %get-tuple-element.79.refs_0_), channel_id=1, source_target_pairs={{0,1},{1,0},{2,3},{3,2},{4,5},{5,4},{6,7},{7,6},{8,9},{9,8},{10,11... | collective-permute-start | bytes 6291464 | tf_op jit(solution)/shard_map/ppermute | solution.py:633
  363.8 13.6 %copy-start.20 = (f32[2,4096]{1,0:T(2,128)S(1)}, f32[2,4096]{1,0:T(2,128)}, u32[]{:S(2)}) copy-start(f32[2,4096]{1,0:T(2,128)} %get-tuple-element.72) | copy-start | bytes 98308
  363.8 13.6 %copy-start.22 = (f32[2,4096]{1,0:T(2,128)S(1)}, f32[2,4096]{1,0:T(2,128)}, u32[]{:S(2)}) copy-start(f32[2,4096]{1,0:T(2,128)} %get-tuple-element.73) | copy-start | bytes 98308
  363.8 15.2 %copy-start.26 = (s32[8]{0:T(128)S(1)}, s32[8]{0:T(128)}, u32[]{:S(2)}) copy-start(s32[8]{0:T(128)} %live_ref.3) | copy-start | bytes 100
  363.8 16.5 %copy-start.19 = (f32[2,4096]{1,0:T(2,128)S(1)}, f32[2,4096]{1,0:T(2,128)}, u32[]{:S(2)}) copy-start(f32[2,4096]{1,0:T(2,128)} %get-tuple-element.81) | copy-start | bytes 98308
  363.8 29.2 %collective-permute-start.1 = (bf16[2,72,4096]{2,1,0:T(8,128)(2,1)}, bf16[2,72,4096]{2,1,0:T(8,128)(2,1)}, u32[]{:S(2)}, u32[]{:S(2)}) collective-permute-start(bf16[2,72,4096]{2,1,0:T(8,128)(2,1)} %get-tuple-element.71.refs_1_), channel_id=1, source_target_pairs={{0,1},{1,0},{2,3},{3,2},{4,5},{5,4},{6,7},{7,6},{8,9},{9,8},{10,11... | collective-permute-start | bytes 3538952 | tf_op jit(solution)/shard_map/ppermute | solution.py:633
  371.7 73.4 %collective-permute-start.4 = (bf16[2,72,4096]{2,1,0:T(8,128)(2,1)}, bf16[2,72,4096]{2,1,0:T(8,128)(2,1)}, u32[]{:S(2)}, u32[]{:S(2)}) collective-permute-start(bf16[2,72,4096]{2,1,0:T(8,128)(2,1)} %get-tuple-element.80.refs_1_), channel_id=1, source_target_pairs={{0,1},{1,0},{2,3},{3,2},{4,5},{5,4},{6,7},{7,6},{8,9},{9,8},{10,11... | collective-permute-start | bytes 3538952 | tf_op jit(solution)/shard_map/ppermute | solution.py:633
  372.2 102.3 %all-to-all-start.2 = ((s32[16,1,2048]{2,1,0:T(1,128)}), s32[16,1,2048]{2,1,0:T(1,128)S(1)}, u32[]{:S(2)}, u32[]{:S(2)}) async-start(s32[16,1,2048]{2,1,0:T(1,128)} %bitcast.12), calls=%async_computation.2 | async-start | bytes 262144 | tf_op jit(solution)/shard_map/all_to_all | solution.py:603
  377.4 41.1 %copy-start.21 = (f32[2,4096]{1,0:T(2,128)}, f32[2,4096]{1,0:T(2,128)S(1)}, u32[]{:S(2)}) copy-start(f32[2,4096]{1,0:T(2,128)S(1)} %add.196.refs_4_) | copy-start | bytes 98308
  377.4 41.1 %collective-permute-start.2 = (f32[2,4096]{1,0:T(2,128)S(1)}, f32[2,4096]{1,0:T(2,128)S(1)}, u32[]{:S(2)}, u32[]{:S(2)}) collective-permute-start(f32[2,4096]{1,0:T(2,128)S(1)} %add.196.refs_4_), channel_id=1, source_target_pairs={{0,1},{1,0},{2,3},{3,2},{4,5},{5,4},{6,7},{7,6},{8,9},{9,8},{10,11... | collective-permute-start | bytes 98312 | tf_op jit(solution)/shard_map/ppermute | solution.py:641
  381.0 64.1 %copy-start.15 = (f32[2,4096]{1,0:T(2,128)}, f32[2,4096]{1,0:T(2,128)S(1)}, u32[]{:S(2)}) copy-start(f32[2,4096]{1,0:T(2,128)S(1)} %add.197.refs_4_) | copy-start | bytes 98308
  393.0 52.1 %collective-permute-start.5 = (f32[2,4096]{1,0:T(2,128)S(1)}, f32[2,4096]{1,0:T(2,128)S(1)}, u32[]{:S(2)}, u32[]{:S(2)}) collective-permute-start(f32[2,4096]{1,0:T(2,128)S(1)} %add.197.refs_4_), channel_id=1, source_target_pairs={{0,1},{1,0},{2,3},{3,2},{4,5},{5,4},{6,7},{7,6},{8,9},{9,8},{10,11... | collective-permute-start | bytes 98312 | tf_op jit(solution)/shard_map/ppermute | solution.py:641
  446.5 26.1 %copy-start.25 = (f32[8,128]{1,0:T(8,128)S(1)}, f32[8,128]{1,0:T(8,128)}, u32[]{:S(2)}) copy-start(f32[8,128]{1,0:T(8,128)} %get-tuple-element.78) | copy-start | bytes 12292
  446.5 33.8 %copy-start.4 = (s32[256,1,128]{2,1,0:T(1,128)S(1)}, s32[256,1,128]{2,1,0:T(1,128)}, u32[]{:S(2)}) copy-start(s32[256,1,128]{2,1,0:T(1,128)} %get-tuple-element.116) | copy-start | bytes 393220
  474.5 98.0 %copy-start.3 = (s32[16,1,2048]{2,1,0:T(1,128)}, s32[16,1,2048]{2,1,0:T(1,128)S(1)}, u32[]{:S(2)}) copy-start(s32[16,1,2048]{2,1,0:T(1,128)S(1)} %all-to-all-done.2) | copy-start | bytes 393220
  475.2 29.3 %all-to-all-start.1 = ((f32[16,1,128]{2,1,0:T(1,128)}), f32[16,1,128]{2,1,0:T(1,128)S(1)}, u32[]{:S(2)}, u32[]{:S(2)}) async-start(f32[16,1,128]{2,1,0:T(1,128)} %broadcast_in_dim.46), calls=%async_computation.1 | async-start | bytes 16384 | tf_op jit(solution)/shard_map/all_to_all | solution.py:649
  505.0 61.4 %all-to-all-start.4 = ((bf16[16,200,384]{2,1,0:T(8,128)(2,1)}), bf16[16,200,384]{2,1,0:T(8,128)(2,1)S(1)}, u32[]{:S(2)}, u32[]{:S(2)}) async-start(bf16[16,200,384]{2,1,0:T(8,128)(2,1)} %outgoing.5), calls=%async_computation.4 | async-start | bytes 4915200 | tf_op jit(solution)/shard_map/all_to_all | solution.py:662
  567.9 102.8 %all-to-all-start.3 = ((bf16[16,200,640]{2,1,0:T(8,128)(2,1)}), bf16[16,200,640]{2,1,0:T(8,128)(2,1)}, u32[]{:S(2)}, u32[]{:S(2)}) async-start(bf16[16,200,640]{2,1,0:T(8,128)(2,1)} %outgoing.4), calls=%async_computation.3 | async-start | bytes 8192000 | tf_op jit(solution)/shard_map/all_to_all | solution.py:662
  670.6 120.2 %all-to-all-start.6 = ((bf16[16,200,640]{2,1,0:T(8,128)(2,1)}), bf16[16,200,640]{2,1,0:T(8,128)(2,1)}, u32[]{:S(2)}, u32[]{:S(2)}) async-start(bf16[16,200,640]{2,1,0:T(8,128)(2,1)} %outgoing.7), calls=%async_computation.7 | async-start | bytes 8192000 | tf_op jit(solution)/shard_map/all_to_all | solution.py:662
  677.0 101.3 %reduce-scatter.2.cloned.1.call-start = ((), (), s32[]{:S(2)}) async-start(), calls=%async_computation.8 | async-start | bytes 3481600 | tf_op jit(solution)/shard_map/reduce_scatter | solution.py:675
  790.8 6.7 copy-start.17
  790.8 7.3 copy-start.7
  790.8 7.3 copy-start.9
  790.8 7.3 copy-start.10
  790.8 7.3 copy-start.11
  790.9 62.1 %all-to-all-start.5 = ((bf16[16,200,384]{2,1,0:T(8,128)(2,1)}), bf16[16,200,384]{2,1,0:T(8,128)(2,1)S(1)}, u32[]{:S(2)}, u32[]{:S(2)}) async-start(bf16[16,200,384]{2,1,0:T(8,128)(2,1)} %outgoing.6), calls=%async_computation.6 | async-start | bytes 4915200 | tf_op jit(solution)/shard_map/all_to_all | solution.py:662
  (12 other events, 24.0 us)
Sparse Core Ops, SparseCore 0:
  11.9 198.0 all-gather.4
  211.6 96.5 all-gather.6
  681.6 96.5 reduce-scatter.1

commit v4 on v3

--- a/solution.py
+++ b/solution.py
@@ -21,6 +21,8 @@
 PARTS = 4
 HALVES = 2
 TURN = 512
+REL_PAD = 256
+TERMS = 3
 NN = (((1,), (0,)), ((), ()))
 NT = (((1,), (1,)), ((), ()))
 TN = (((0,), (0,)), ((), ()))
@@ -87,39 +89,66 @@
     return place_list, row_list.reshape(groups, capacity), counts
 
 
-def relation_rows_kernel(n_slices, ids_ref, *refs):
-    tables, outs = refs[:n_slices], refs[n_slices:]
-    count = outs[0].shape[0]
+def relation_rows_kernel(slices, ids_ref, scale_ref, *refs):
+    n = len(slices)
+    tables, outs = refs[:n], refs[-2 * n - 1 : -n - 1]
+    columns, rows = refs[-n - 1], refs[-n:]
+    groups = tables[0].shape[0]
+    for (_, depth), table, into in zip(slices, tables, rows):
+        columns[...] = jnp.zeros_like(columns)
+
+        def turn(group, carry):
+            columns[:depth, :] = table[group, :depth].astype(F32)
+            if depth < LANES:
+                columns[LANES - 1 :, :] = scale_ref[pl.ds(group, 1), :]
+            into[pl.ds(pl.multiple_of(group * REL_PAD, REL_PAD), REL_PAD), :] = columns[...].T
+            return carry
+
+        lax.fori_loop(0, groups, turn, 0, unroll=4)
 
     def body(step, carry):
         for lane in range(UNROLL):
             at = step * UNROLL + lane
             row = ids_ref[at]
-            for table, out in zip(tables, outs):
-                out[pl.ds(at, 1), :] = table[pl.ds(row, 1), :]
+            for source, out in zip(rows, outs):
+                out[pl.ds(at, 1), :] = source[pl.ds(row, 1), :]
         return carry
 
-    lax.fori_loop(0, count // UNROLL, body, 0)
-
-
-def relation_rows(relation_ids, tables):
-    count = relation_ids.shape[0]
-    n = len(tables)
-    return pl.pallas_call(
-        functools.partial(relation_rows_kernel, n),
+    lax.fori_loop(0, outs[0].shape[0] // UNROLL, body, 0)
+
+
+def relation_rows(places, dense, scale, slices, after):
+    count = places.shape[0]
+    groups, depth, span = dense.shape
+    n = len(slices)
+    first = span // REL_PAD - n
+
+    def columns(k):
+        return pl.BlockSpec((groups, depth, REL_PAD), lambda i: (0, 0, first + k))
+
+    return pl.pallas_call(
+        functools.partial(relation_rows_kernel, slices),
         out_shape=[jax.ShapeDtypeStruct((count, LANES), F32)] * n,
-        in_specs=[whole(SMEM)] + [whole(VMEM)] * n,
+        grid=(1,),
+        in_specs=[whole(SMEM), whole(VMEM)]
+        + [columns(k) for k in range(n)]
+        + [whole(pl.ANY)] * len(after),
         out_specs=[whole(VMEM)] * n,
-        compiler_params=params(),
-        cost_estimate=cost(0, 30e6 * n),
+        scratch_shapes=[pltpu.VMEM((LANES, REL_PAD), F32)]
+        + [pltpu.VMEM((groups * REL_PAD, LANES), F32)] * n,
+        compiler_params=params(),
+        cost_estimate=cost(0, 80e6),
         name="relation_rows",
-    )(relation_ids, *tables)
-
-
-def fetch_kernel(capacity, moves, counts_ref, place_ref, row_ref, dense_ref, out_ref, *rows):
+    )(places, scale, *[dense] * n, *after)
+
+
+def fetch_kernel(
+    capacity, moves, ent_rows, counts_ref, place_ref, row_ref, dense_ref, *refs
+):
     shard = pl.program_id(0)
     last = pl.num_programs(0) - 1
-    depth, ent_rows = dense_ref.shape[1:]
+    out_ref, rows = refs[-3], refs[-2:]
+    depth = dense_ref.shape[1]
     turns = ent_rows // TURN
     rest = ent_rows - turns * TURN
 
@@ -185,12 +214,12 @@
             step(rows[parity], rows[1 - parity])
 
 
-def fetch(counts, place_list, row_list, dense, id_count):
-    groups, depth, ent_rows = dense.shape
+def fetch(counts, place_list, row_list, dense, id_count, ent_rows, after):
+    groups, depth, _ = dense.shape
     capacity = place_list.shape[0] // groups
     moves = (id_count // groups) // (ent_rows // TURN) // UNROLL * UNROLL
     return pl.pallas_call(
-        functools.partial(fetch_kernel, capacity, moves),
+        functools.partial(fetch_kernel, capacity, moves, ent_rows),
         out_shape=jax.ShapeDtypeStruct((id_count + 8, LANES), F32),
         grid=(groups + 1,),
         in_specs=[whole(SMEM)] * 3
@@ -198,16 +227,47 @@
             pl.BlockSpec(
                 (1, depth, ent_rows), lambda shard: (jnp.minimum(shard, groups - 1), 0, 0)
             )
-        ],
+        ]
+        + [whole(pl.ANY)] * len(after),
         out_specs=whole(VMEM),
         scratch_shapes=[pltpu.VMEM((ent_rows + 8, LANES), F32)] * 2,
         compiler_params=params(),
         cost_estimate=cost(0, 170e6),
         name="fetch_rows",
-    )(counts, place_list, row_list, dense)
-
-
-def prepare_kernel(depth, head_ref, tail_ref, neg_ref, rel_ref, off_ref, tail_out, pair_ref, sums_ref):
+    )(counts, place_list, row_list, dense, *after)
+
+
+def column_sum(values):
+    return jnp.sum(values * values, axis=0, keepdims=True)
+
+
+def negatives_kernel(neg_ref, low_ref, norm_ref):
+    neg_t = neg_ref[...].T
+    low_ref[...] = neg_t[: low_ref.shape[0]].astype(BF16)
+    norm_ref[...] = column_sum(neg_t)
+
+
+def negatives(fetched, depth, blocks, block_len):
+    count = blocks * block_len
+    return pl.pallas_call(
+        negatives_kernel,
+        out_shape=[
+            jax.ShapeDtypeStruct((depth, count), BF16),
+            jax.ShapeDtypeStruct((1, count), F32),
+        ],
+        grid=(blocks,),
+        in_specs=[pl.BlockSpec((block_len, LANES), lambda b: (2 * blocks + b, 0))],
+        out_specs=[
+            pl.BlockSpec((depth, block_len), lambda b: (0, b)),
+            pl.BlockSpec((1, block_len), lambda b: (0, b)),
+        ],
+        compiler_params=params(),
+        cost_estimate=cost(0, 10e6),
+        name="negatives",
+    )(fetched)
+
+
+def edge_parts(depth, head_ref, tail_ref, rel_ref, off_ref, tail_out):
     lane = lax.broadcasted_iota(jnp.int32, head_ref.shape, 1)
     inside = lane < depth
     rel = rel_ref[...]
@@ -216,53 +276,107 @@
     off_ref[...] = jnp.where(inside, shifted - tail, rel)
     tail_out[...] = tail.astype(BF16)
     shifted_t = shifted.T
-    offset_t = (shifted - tail).T
+    return shifted_t, column_sum((shifted - tail).T) - column_sum(shifted_t)
+
+
+def edges_kernel(depth, head_ref, tail_ref, rel_ref, off_ref, tail_out, low_ref, bias_ref):
+    shifted_t, bias = edge_parts(depth, head_ref, tail_ref, rel_ref, off_ref, tail_out)
+    low_ref[...] = shifted_t[:depth].astype(BF16)
+    bias_ref[...] = bias
+
+
+def edges(fetched, rel_rows, depth, blocks, block_len):
+    count = blocks * block_len
+
+    def rows(at):
+        return pl.BlockSpec((block_len, LANES), lambda b: (at * blocks + b, 0))
+
+    return pl.pallas_call(
+        functools.partial(edges_kernel, depth),
+        out_shape=[
+            jax.ShapeDtypeStruct((count, LANES), F32),
+            jax.ShapeDtypeStruct((count, LANES), BF16),
+            jax.ShapeDtypeStruct((depth, count), BF16),
+            jax.ShapeDtypeStruct((1, count), F32),
+        ],
+        grid=(blocks,),
+        in_specs=[rows(0), rows(1), rows(0)],
+        out_specs=[
+            rows(0),
+            rows(0),
+            pl.BlockSpec((depth, block_len), lambda b: (0, b)),
+            pl.BlockSpec((1, block_len), lambda b: (0, b)),
+        ],
+        compiler_params=params(),
+        cost_estimate=cost(0, 30e6),
+        name="edges",
+    )(fetched, fetched, rel_rows)
+
+
+def last_rows(depth):
+    return (depth + 7) // 8 * 8
+
+
+def with_terms(columns, total, depth):
+    place = lax.broadcasted_iota(jnp.int32, (8, total.shape[1]), 0)
+    left = total
+    terms = jnp.zeros(place.shape, F32)
+    for k in range(TERMS):
+        term = left.astype(BF16).astype(F32)
+        left = left - term
+        terms = jnp.where(place == k, term, terms)
+    return jnp.concatenate([columns[: last_rows(depth)], terms], axis=0).astype(BF16)
+
+
+def last_kernel(depth, n_given, head_ref, tail_ref, neg_ref, rel_ref, *refs):
+    biases, norms = refs[:n_given], refs[n_given : 2 * n_given]
+    off_ref, tail_out, pair_ref = refs[2 * n_given :]
+    shifted_t, bias = edge_parts(depth, head_ref, tail_ref, rel_ref, off_ref, tail_out)
     neg_t = neg_ref[...].T
-    pair_ref[0] = shifted_t[:depth].astype(BF16)
-    pair_ref[1] = neg_t[:depth].astype(BF16)
-    sums_ref[0:1, :] = jnp.sum(offset_t * offset_t, axis=0, keepdims=True) - jnp.sum(
-        shifted_t * shifted_t, axis=0, keepdims=True
-    )
-    sums_ref[1:2, :] = jnp.sum(neg_t * neg_t, axis=0, keepdims=True)
-
-
-def prepare(fetched, rel_rows, depth, blocks, block_len, half):
+    norm = column_sum(neg_t)
+    for ref in biases:
+        bias = bias + ref[...]
+    for ref in norms:
+        norm = norm + ref[...]
+    pair_ref[0] = with_terms(shifted_t, bias, depth)
+    pair_ref[1] = with_terms(neg_t, norm, depth)
+
+
+def last_slice(fetched, rel_rows, biases, norms, depth, blocks, block_len, half):
     part = blocks // HALVES
-    edge_count = part * block_len
+    count = part * block_len
+    tall = last_rows(depth) + 8
 
     def rows(at):
         return pl.BlockSpec((block_len, LANES), lambda b: (at * blocks + half * part + b, 0))
 
-    def outs(*shape):
-        return pl.BlockSpec(shape + (block_len,), lambda b: (0,) * len(shape) + (b,))
-
-    return pl.pallas_call(
-        functools.partial(prepare_kernel, depth),
+    return pl.pallas_call(
+        functools.partial(last_kernel, depth, len(biases)),
         out_shape=[
-            jax.ShapeDtypeStruct((edge_count, LANES), F32),
-            jax.ShapeDtypeStruct((edge_count, LANES), BF16),
-            jax.ShapeDtypeStruct((2, depth, edge_count), BF16),
-            jax.ShapeDtypeStruct((2, edge_count), F32),
+            jax.ShapeDtypeStruct((count, LANES), F32),
+            jax.ShapeDtypeStruct((count, LANES), BF16),
+            jax.ShapeDtypeStruct((2, tall, count), BF16),
         ],
         grid=(part,),
-        in_specs=[rows(0), rows(1), rows(2), rows(0)],
+        in_specs=[rows(0), rows(1), rows(2), rows(0)]
+        + [pl.BlockSpec((1, block_len), lambda b: (0, half * part + b))]
+        * (len(biases) + len(norms)),
         out_specs=[
             pl.BlockSpec((block_len, LANES), lambda b: (b, 0)),
             pl.BlockSpec((block_len, LANES), lambda b: (b, 0)),
-            outs(2, depth),
-            outs(2),
+            pl.BlockSpec((2, tall, block_len), lambda b: (0, 0, b)),
         ],
         compiler_params=params(),
         cost_estimate=cost(0, 20e6),
-        name="prepare",
-    )(fetched, fetched, fetched, rel_rows)
+        name="last_slice",
+    )(fetched, fetched, fetched, rel_rows, *biases, *norms)
 
 
 def block_kernel(slices, n_col, half, me_ref, live_ref, *refs):
     n = len(slices)
-    pairs = [refs[k * n : (k + 1) * n] for k in range(n_col)]
-    refs = refs[n_col * n :]
-    sums_refs, refs = refs[:n_col], refs[n_col:]
+    per_col = 2 * n - 1
+    given = [refs[k * per_col : (k + 1) * per_col] for k in range(n_col)]
+    refs = refs[n_col * per_col :]
     offs, tails, refs = refs[:n], refs[n : 2 * n], refs[2 * n :]
     if half > 0:
         refs = refs[n:]
@@ -273,10 +387,17 @@
     me = me_ref[0]
     for k in range(n_col):
         slot = lax.rem(me + (n_col - k), n_col)
-        for (start, depth), pair in zip(slices, pairs[k]):
-            shift_scr[slot, start : start + depth, :] = 2.0 * pair[0]
-            neg_scr[slot, start : start + depth, :] = pair[1]
-        sums_scr[slot] = sums_refs[k][...]
+        for m, (start, depth) in enumerate(slices):
+            if m < n - 1:
+                shift, neg = given[k][2 * m][...], given[k][2 * m + 1][...]
+            else:
+                pair = given[k][-1]
+                shift, neg = pair[0, :depth, :], pair[1, :depth, :]
+                for row in range(2):
+                    terms = pair[row, last_rows(depth) : last_rows(depth) + 8, :].astype(F32)
+                    sums_scr[slot, row : row + 1] = jnp.sum(terms, axis=0, keepdims=True)
+            shift_scr[slot, start : start + depth, :] = 2.0 * shift
+            neg_scr[slot, start : start + depth, :] = neg
     bias = jnp.sum(sums_scr[:, 0, :], axis=0, keepdims=True) + MARGIN
     neg_norm = jnp.sum(sums_scr[:, 1, :], axis=0, keepdims=True)
     row_bias[...] = jnp.broadcast_to(bias, (LANES, length)).T
@@ -353,36 +474,39 @@
         grad[2, :, :depth] = moved[start : start + depth, :].T
 
 
-def block_math(me, live_counts, pairs, sums, offs, tails, old, slices, block_len, half):
-    n, n_col = len(slices), len(pairs)
+def block_math(me, live_counts, given, offs, tails, old, slices, block_len, half):
+    n, n_col = len(slices), len(given)
     blocks = live_counts.shape[0]
     part = blocks // HALVES
     width = sum(depth for _, depth in slices)
-    flat = [piece for per_col in pairs for piece in per_col]
-    given = [] if old is None else old
-
-    def rows():
-        return pl.BlockSpec((block_len, LANES), lambda b: (b, 0))
-
-    first_old = 2 + len(flat) + n_col + 2 * n
+    flat = [piece for per_col in given for piece in per_col]
+    kept = [] if old is None else old
+
+    def columns(piece):
+        if piece.ndim == 3:
+            return pl.BlockSpec((2, piece.shape[1], block_len), lambda b: (0, 0, b))
+        return pl.BlockSpec((piece.shape[0], block_len), lambda b: (0, half * part + b))
+
+    def rows(array):
+        first = half * part if array.shape[0] > part * block_len else 0
+        return pl.BlockSpec((block_len, LANES), lambda b: (first + b, 0))
+
+    first_old = 2 + len(flat) + 2 * n
     return pl.pallas_call(
         functools.partial(block_kernel, slices, n_col, half),
         out_shape=[jax.ShapeDtypeStruct((3, blocks * block_len, LANES), F32)] * n
         + [jax.ShapeDtypeStruct((8, LANES), F32)],
         grid=(part,),
         in_specs=[whole(SMEM)] * 2
-        + [
-            pl.BlockSpec((2, piece.shape[1], block_len), lambda b: (0, 0, b)) for piece in flat
-        ]
-        + [pl.BlockSpec((2, block_len), lambda b: (0, b))] * n_col
-        + [rows() for _ in range(2 * n)]
-        + [whole(pl.ANY)] * len(given),
+        + [columns(piece) for piece in flat]
+        + [rows(array) for array in offs + tails]
+        + [whole(pl.ANY)] * len(kept),
         out_specs=[
             pl.BlockSpec((3, block_len, LANES), lambda b: (0, half * part + b, 0))
         ]
         * n
         + [pl.BlockSpec((8, LANES), lambda b: (0, 0))],
-        input_output_aliases={first_old + k: k for k in range(len(given))},
+        input_output_aliases={first_old + k: k for k in range(len(kept))},
         scratch_shapes=[
             pltpu.VMEM((n_col, width, block_len), BF16),
             pltpu.VMEM((n_col, width, block_len), BF16),
@@ -395,7 +519,7 @@
         compiler_params=params(),
         cost_estimate=cost(part * 8 * block_len * block_len * width, 120e6),
         name="block_math",
-    )(me, live_counts, *flat, *sums, *offs, *tails, *given)
+    )(me, live_counts, *flat, *offs, *tails, *kept)
 
 
 def outgoing_kernel(slices, capacity, begin, counts_ref, place_ref, *refs):
@@ -441,8 +565,7 @@
 def collect_kernel(slices, capacity, begin, first, counts_ref, row_ref, came_ref, *refs):
     n = len(slices)
     olds = () if first else refs[:n]
-    refs = refs if first else refs[n:]
-    totals, tiles = refs[:n], refs[n:]
+    totals, tiles = refs[-2 * n : -n], refs[-n:]
     groups, width, chunk = came_ref.shape
     for k in range(n):
         totals[k][...] = jnp.zeros_like(totals[k]) if first else olds[k][...]
@@ -470,7 +593,7 @@
     lax.fori_loop(0, groups, source, 0)
 
 
-def collect(counts, row_list, came, totals, slices, begin, ent_rows):
+def collect(counts, row_list, came, totals, slices, begin, ent_rows, after):
     capacity = row_list.shape[1]
     chunk = came.shape[2]
     n = len(slices)
@@ -479,13 +602,15 @@
     return pl.pallas_call(
         functools.partial(collect_kernel, slices, capacity, begin, first),
         out_shape=[jax.ShapeDtypeStruct((ent_rows + 8, LANES), F32)] * n,
-        in_specs=[whole(SMEM)] * 2 + [whole(VMEM)] * (1 + len(given)),
+        in_specs=[whole(SMEM)] * 2
+        + [whole(VMEM)] * (1 + len(given))
+        + [whole(pl.ANY)] * len(after),
         out_specs=[whole(VMEM)] * n,
         scratch_shapes=[pltpu.VMEM((chunk, LANES), F32)] * n,
         compiler_params=params(),
         cost_estimate=cost(0, 120e6),
         name="collect",
-    )(counts, row_list.reshape(-1), came, *given)
+    )(counts, row_list.reshape(-1), came, *given, *after)
 
 
 def relation_sums_kernel(n, ids_ref, *refs):
@@ -552,9 +677,7 @@
 
 def chunk_bounds(capacity):
     units = capacity // LANES
-    small = max(1, 3 * units // 16)
-    large = (units - 2 * small) // 2
-    sizes = [small, large, units - 2 * small - large, small]
+    sizes = [3, 6, 5, 2] if units == 16 else [units // 4] * 3 + [units - 3 * (units // 4)]
     bounds = [0]
     for size in sizes:
         bounds.append(bounds[-1] + size * LANES)
@@ -589,15 +712,17 @@
     capacity = (4 * id_count + 3 * groups - 1) // (3 * groups)
     rel_total = rel_weight.shape[0]
 
-    table_low = entity_table.astype(BF16)
-    dense = [
-        lax.all_gather(table_low[start : start + depth], "edge", axis=0, tiled=False)
-        for start, depth in slices
-    ]
     rel_own = rel_total // groups
-    rel_low = jnp.broadcast_to(relation_table.astype(BF16)[None], (groups, rel_own, width))
-    rel_table = lax.all_to_all(rel_low, "edge", split_axis=0, concat_axis=0, tiled=True)
-    rel_table = rel_table.reshape(rel_total, width)
+    rel_low = jnp.pad(relation_table.astype(BF16).T, ((0, 0), (0, REL_PAD - rel_own)))
+    dense = []
+    for k, (start, depth) in enumerate(slices):
+        sent = entity_table[start : start + depth].astype(BF16)
+        if k == 0:
+            behind = [
+                jnp.pad(rel_low[at : at + size], ((0, depth - size), (0, 0))) for at, size in slices
+            ]
+            sent = jnp.concatenate([sent] + behind, axis=1)
+        dense.append(lax.all_gather(sent, "edge", axis=0, tiled=False))
 
     place_list, row_list, counts = owner_lists(all_ids, groups, capacity, ent_rows)
     asked = lax.all_to_all(row_list, "edge", split_axis=0, concat_axis=0, tiled=True)
@@ -606,41 +731,52 @@
     place_flat, row_flat = place_list.reshape(-1), row_list.reshape(-1)
 
     rel_scale = rel_weight * (rel_total / jnp.sum(rel_weight)) / rel_count.astype(F32)
-    rel_slices = []
-    for k, (start, depth) in enumerate(slices):
-        piece = rel_table[:, start : start + depth].astype(F32)
-        if k == n - 1:
-            gap = jnp.zeros((rel_total, LANES - 1 - depth), F32)
-            piece = jnp.concatenate([piece, gap, rel_scale[:, None]], axis=1)
-        rel_slices.append(piece)
-    rel_rows = relation_rows(relation_ids, rel_slices)
+    rel_scale = jnp.pad(rel_scale.reshape(groups, rel_own), ((0, 0), (0, REL_PAD - rel_own)))
+    rel_places = relation_ids + (relation_ids // rel_own) * (REL_PAD - rel_own)
+
+    def from_others(array):
+        turns = [[(c, (c + away) % n_col) for c in range(n_col)] for away in range(1, n_col)]
+        return [lax.ppermute(array, "col", turn) for turn in turns]
 
     me = lax.axis_index("col").astype(jnp.int32).reshape(1)
+    given = [[[] for _ in range(n_col)] for _ in range(HALVES)]
     offs = [[] for _ in range(HALVES)]
     tails = [[] for _ in range(HALVES)]
-    pairs = [[[] for _ in range(n_col)] for _ in range(HALVES)]
-    parts = [[] for _ in range(HALVES)]
+    biases, norms, first_sent, rel_rows = [], [], [], None
     for k, (start, depth) in enumerate(slices):
-        fetched = fetch(counts, place_flat, row_flat, dense[k], id_count)
+        early = [asked] + first_sent if k > 0 else []
+        fetched = fetch(counts, place_flat, row_flat, dense[k], id_count, ent_rows, early)
+        if k < n - 1:
+            neg_low, norm = negatives(fetched, depth, blocks, block_len)
+            neg_all = [neg_low] + from_others(neg_low)
+            if rel_rows is None:
+                rel_rows = relation_rows(rel_places, dense[0], rel_scale, slices, [neg_low])
+            off, tail, low, bias = edges(fetched, rel_rows[k], depth, blocks, block_len)
+            low_all = [low] + from_others(low)
+            first_sent = neg_all[1:]
+            biases.append(bias)
+            norms.append(norm)
+            for half in range(HALVES):
+                offs[half].append(off)
+                tails[half].append(tail)
+                for col in range(n_col):
+                    given[half][col] += [low_all[col], neg_all[col]]
+            continue
+        if rel_rows is None:
+            rel_rows = relation_rows(rel_places, dense[0], rel_scale, slices, [])
         for half in range(HALVES):
-            off, tail, pair, part = prepare(fetched, rel_rows[k], depth, blocks, block_len, half)
+            off, tail, pair = last_slice(
+                fetched, rel_rows[k], biases, norms, depth, blocks, block_len, half
+            )
             offs[half].append(off)
             tails[half].append(tail)
-            parts[half].append(part)
-            pairs[half][0].append(pair)
-            for away in range(1, n_col):
-                turn = [(c, (c + away) % n_col) for c in range(n_col)]
-                pairs[half][away].append(lax.ppermute(pair, "col", turn))
+            for col, piece in enumerate([pair] + from_others(pair)):
+                given[half][col].append(piece)
 
     grads, loss_tiles = None, []
     for half in range(HALVES):
-        part = functools.reduce(jnp.add, parts[half])
-        sums = [part]
-        for away in range(1, n_col):
-            turn = [(c, (c + away) % n_col) for c in range(n_col)]
-            sums.append(lax.ppermute(part, "col", turn))
         *grads, loss_tile = block_math(
-            me, live_counts, pairs[half], sums, offs[half], tails[half], grads, slices, block_len, half
+            me, live_counts, given[half], offs[half], tails[half], grads, slices, block_len, half
         )
         loss_tiles.append(loss_tile)
     live = jnp.sum(jnp.minimum(live_counts, block_len)).astype(F32)
@@ -661,22 +797,29 @@
         )
         arrived.append(lax.all_to_all(sent, "edge", split_axis=0, concat_axis=0, tiled=True))
         after = []
-        if k > 0:
-            totals = collect(
-                asked_counts, asked, arrived[k - 1], totals, slices, bounds[k - 1], ent_rows
-            )
-            after = totals[:1]
         if k == 1:
-            rel_terms = relation_sums(relation_ids, grads, rel_total, [totals[0], loss_all])
+            rel_terms = relation_sums(relation_ids, grads, rel_total, [arrived[0], loss_all])
             after = rel_terms[:1]
             rel_terms = jnp.concatenate(
                 [term[:, :depth] for (start, depth), term in zip(slices, rel_terms)], axis=1
             )
             relation_grad = lax.psum_scatter(rel_terms, "edge", scatter_dimension=0, tiled=True)
-        if k == chunks - 2:
-            after = [totals[0], relation_grad]
+        if k == chunks - 1:
+            after = [relation_grad]
+        if k > 0:
+            totals = collect(
+                asked_counts,
+                asked,
+                arrived[k - 1],
+                totals,
+                slices,
+                bounds[k - 1],
+                ent_rows,
+                after,
+            )
+            after = [totals[0], rel_terms]
     k = chunks - 1
-    totals = collect(asked_counts, asked, arrived[k], totals, slices, bounds[k], ent_rows)
+    totals = collect(asked_counts, asked, arrived[k], totals, slices, bounds[k], ent_rows, [])
 
     new_entity, new_entity_first, new_entity_second = update_entities(
         entity_table, totals, entity_first, entity_second, slices

time: 893 us -> 843 us (0.944)
  waiting for transfers between devices: 283 us -> 235 us
  starting transfers between devices: 47.1 us -> 29.7 us
  blocking collectives: 0 us -> 10.5 us
  Pallas kernels: 483 us -> 492 us
    reduce_scatter x1, waiting for transfers between devices: 46.3 us -> 0.01 us  [shards(): lax.psum_scatter(rel_terms, 'edge', scatter_dimension=0, tiled=True)]
    all_to_all x4, waiting for transfers between devices: 33.8 us -> 67.1 us  [shards(): lax.all_to_all(sent, 'edge', split_axis=0, concat_axis=0, tiled=True)]
    all_to_all x2 -> x0, waiting for transfers between devices: 22.6 us -> none  [the longest x1 22.6 us: shards(): lax.all_to_all(rel_low, 'edge', split_axis=0, concat_axis=0, tiled=True)]
    ppermute x6 -> x4, waiting for transfers between devices: 36 us -> 24.3 us  [from_others(): return [lax.ppermute(array, 'col', turn) for turn in turns]]
    all_to_all x2 -> x0, starting transfers between devices: 11.3 us -> none  [the longest x1 6.18 us: shards(): lax.all_to_all(rel_low, 'edge', split_axis=0, concat_axis=0, tiled=True)]
    all_to_all x0 -> x1, blocking collectives: none -> 10.5 us  [shards(): lax.all_to_all(row_list, 'edge', split_axis=0, concat_axis=0, tiled=True)]
  transfers between devices with their start and end apart: 16 -> 12, of which waited for: 8 -> 6; matrix products, arithmetic and copies ran while one was open for 5% -> 5% of each run, Pallas kernels for 52% -> 52%
where the time goes in v4:
time: 843 us; the launch traced here: 836 us
  Pallas kernels  492 us (58%)
  waiting for transfers between devices  235 us (28%)
  other arithmetic  30.6 us (4%)
  starting transfers between devices  29.7 us (4%)
  between operations  15.5 us (2%)
  matrix products  12.3 us (1%)
  blocking collectives  10.5 us (1%)
  local copies, waits for them, and re-layouts  10.1 us (1%)
    all_gather x2, waiting for transfers between devices, shards(): dense.append(lax.all_gather(sent, 'edge', axis=0, tiled=False))  143 us
    pallas_call x4, Pallas kernels, collect(): pl.pallas_call(functools.partial(collect_kernel, slices, capacity, begin,...  140 us
    pallas_call x2, Pallas kernels, fetch(): pl.pallas_call(functools.partial(fetch_kernel, capacity, moves, ent_rows)...  98.7 us
    pallas_call x4, Pallas kernels, outgoing(): pl.pallas_call(functools.partial(outgoing_kernel, slices, capacity, begin...  96.1 us
    all_to_all x4, waiting for transfers between devices, shards(): lax.all_to_all(sent, 'edge', split_axis=0, concat_axis=0, tiled=True)  67.1 us
    pallas_call x2, Pallas kernels, block_math(): pl.pallas_call(functools.partial(block_kernel, slices, n_col, half), out_...  52.3 us
    pallas_call x1, Pallas kernels, relation_sums(): pl.pallas_call(functools.partial(relation_sums_kernel, n), out_shape=[jax...  35.6 us
    ppermute x4, waiting for transfers between devices, from_others(): return [lax.ppermute(array, 'col', turn) for turn in turns]  24.3 us
  transfers between devices with their start and end apart: 12, of which 6 were waited for; matrix products, arithmetic and copies ran while one was open for 5% of the time, Pallas kernels for 52%

profile of v4, /device:TPU:16, one launch (start us, length us, event | category | flops | bytes accessed | tf_op | source)
XLA Modules:
  0.0 835.6 jit_solution(16719929352259135183)
XLA Ops:
  22.3 8.6 %broadcast_multiply_fusion = bf16[4,128,24576]{2,1,0:T(8,128)(2,1)} fusion(bf16[128,24576]{1,0:T(8,128)(2,1)S(1)} %fusion.2, bf16[4,24576]{1,0:T(4,128)(2,1)S(1)} %pad_maximum_fusion.1), kind=kLoop, calls=%fused_computation.2 | loop fusion | flops 12582912 | bytes 31653888 | tf_op jit(solution)/shard_map/mul | solution.py:83
  30.9 11.8 %fusion.8 = s32[256,512]{1,0:T(8,128)S(1)} fusion(bf16[512,24576]{1,0:T(8,128)(2,1)} %bitcast.46, s32[24576]{0:T(1024)S(1)} %get-tuple-element.109), kind=kOutput, calls=%fused_computation.17 | convolution fusion | flops 6448873472 | bytes 25788416 | tf_op jit(solution)/shard_map/dot_general | solution.py:84
  44.0 143.4 %all-gather.5.cloned.1.call-done = bf16[2048,8448]{1,0:T(8,128)(2,1)} async-done(((bf16[128,8448]{1,0:T(8,128)(2,1)}), bf16[2048,8448]{1,0:T(8,128)(2,1)}) %all-gather.5.cloned.1.call-update) | async-done | bytes 34603024 | tf_op jit(solution)/shard_map/all_gather | solution.py:725
  187.4 49.1 %fetch_rows.2.neg_ref.head_ref.tail_ref = f32[24584,128]{1,0:T(8,128)} custom-call(s32[16]{0:T(128)} %convert_element_type.63.counts_ref, s32[32768]{0:T(1024)} %bitcast.52, s32[32768]{0:T(1024)} %bitcast.55, bf16[16,128,8448]{2,1,0:T(8,128)(2,1)} %bitcast.43), custom_call_target="tpu_custom_call" | custom-call | bytes 170000000 | tf_op jit(solution)/shard_map/fetch_rows/pallas_call | solution.py:221
  236.5 6.9 negatives.1
  247.6 20.4 %relation_rows.1 = (f32[8192,128]{1,0:T(8,128)}, f32[8192,128]{1,0:T(8,128)}) custom-call(s32[8192]{0:T(1024)} %fusion.28.ids_ref, f32[16,256]{1,0:T(8,128)} %pad.19.scale_ref, bf16[16,128,8448]{2,1,0:T(8,128)(2,1)} %bitcast.44, bf16[16,128,8448]{2,1,0:T(8,128)(2,1)} %bitcast.45, bf16[128,8192]{1,0:T(8,128)(2,1)} %get-tuple-element.64.refs_2_.refs_1_), custom_call_target="tpu_custom_call" | custom-call | bytes 80000000 | tf_op jit(solution)/shard_map/relation_rows/pallas_call | solution.py:129
  268.0 10.2 %edges.1 = (f32[8192,128]{1,0:T(8,128)}, bf16[8192,128]{1,0:T(8,128)(2,1)}, bf16[128,8192]{1,0:T(8,128)(2,1)}, f32[1,8192]{1,0:T(1,128)}) custom-call(f32[24584,128]{1,0:T(8,128)} %fetch_rows.2.neg_ref.head_ref.tail_ref, f32[24584,128]{1,0:T(8,128)} %fetch_rows.2.neg_ref.head_ref.tail_ref, f32[8192,128]{1,0:T(8,128)} %get-tuple-element.65.rel_ref), custom_call_target="tpu_custom_call" | custom-call | bytes 30000000 | tf_op jit(solution)/shard_map/edges/pallas_call | solution.py:294
  279.0 10.5 %all_to_all.33 = s32[16,1,2048]{2,1,0:T(1,128)S(1)} all-to-all(s32[16,1,2048]{2,1,0:T(1,128)S(1)} %bitcast.57), channel_id=1, replica_groups=mesh['edge'=16,'col'=2] {'edge'}, dimensions={0} | all-to-all | bytes 262144 | tf_op jit(solution)/shard_map/all_to_all | solution.py:728
  293.4 49.6 %fetch_rows.3.head_ref.tail_ref.neg_ref = f32[24584,128]{1,0:T(8,128)} custom-call(s32[16]{0:T(128)} %convert_element_type.63.counts_ref, s32[32768]{0:T(1024)} %bitcast.53, s32[32768]{0:T(1024)} %bitcast.56, bf16[16,72,7936]{2,1,0:T(8,128)(2,1)} %bitcast.47, s32[16,2048]{1,0:T(8,128)} %bitcast.59, bf16[128,8192]{1,0:T(8,128)(2,1)} %copy-done.1), custom_call_target="tpu_custom_call" | custom-call | bytes 170000000 | tf_op jit(solution)/shard_map/fetch_rows/pallas_call | solution.py:221
  343.1 6.4 last_slice.2
  351.0 6.4 last_slice.3
  359.3 22.3 %collective-permute-done.2.refs_5_ = bf16[2,80,4096]{2,1,0:T(8,128)(2,1)} collective-permute-done((bf16[2,80,4096]{2,1,0:T(8,128)(2,1)}, bf16[2,80,4096]{2,1,0:T(8,128)(2,1)}, u32[]{:S(2)}, u32[]{:S(2)}) %collective-permute-start.2) | collective-permute-done | bytes 1310752 | tf_op jit(solution)/shard_map/ppermute | solution.py:739
  381.6 26.0 %block_math.2 = (f32[3,8192,128]{2,1,0:T(8,128)}, f32[3,8192,128]{2,1,0:T(8,128)}, f32[8,128]{1,0:T(8,128)}) custom-call(s32[1]{0:T(128)} %bitcast.me_ref, s32[8]{0:T(128)} %live_ref.3, bf16[128,8192]{1,0:T(8,128)(2,1)} %get-tuple-element.66.refs_0_, bf16[128,8192]{1,0:T(8,128)(2,1)} %get-tuple-element.64.refs_2_.refs_1_, ...), custom_call_target="tpu_custom_call" | custom-call | flops 6710886400 | bytes 120000000 | tf_op jit(solution)/shard_map/block_math/pallas_call | solution.py:495
  408.6 26.3 %block_math.3 = (f32[3,8192,128]{2,1,0:T(8,128)}, f32[3,8192,128]{2,1,0:T(8,128)}, f32[8,128]{1,0:T(8,128)}) custom-call(s32[1]{0:T(128)} %bitcast.me_ref, s32[8]{0:T(128)} %live_ref.3, bf16[128,8192]{1,0:T(8,128)(2,1)} %get-tuple-element.66.refs_0_, ...), custom_call_target="tpu_custom_call", output_to_operand_aliasing={{0}: (12, {}), {1}: (13, {})} | custom-call | flops 6710886400 | bytes 120000000 | tf_op jit(solution)/shard_map/block_math/pallas_call | solution.py:495
  437.6 5.2 all-to-all-start.1
  443.4 23.5 %outgoing.5 = bf16[16,200,384]{2,1,0:T(8,128)(2,1)} custom-call(s32[16]{0:T(128)} %convert_element_type.63.counts_ref, s32[32768]{0:T(1024)} %broadcast_minimum_fusion.place_ref, f32[24576,128]{1,0:T(8,128)} %bitcast.35, f32[24576,128]{1,0:T(8,128)} %bitcast.39), custom_call_target="tpu_custom_call" | custom-call | bytes 80000000 | tf_op jit(solution)/shard_map/outgoing/pallas_call | solution.py:553
  466.9 6.0 all-to-all-start.3
  472.9 36.6 %outgoing.4 = bf16[16,200,768]{2,1,0:T(8,128)(2,1)} custom-call(s32[16]{0:T(128)} %convert_element_type.63.counts_ref, s32[32768]{0:T(1024)} %broadcast_minimum_fusion.place_ref, f32[24576,128]{1,0:T(8,128)} %bitcast.36, f32[24576,128]{1,0:T(8,128)} %bitcast.40), custom_call_target="tpu_custom_call" | custom-call | bytes 80000000 | tf_op jit(solution)/shard_map/outgoing/pallas_call | solution.py:553
  509.5 18.8 %all-to-all-done.3.refs_2_.came_ref = bf16[16,200,384]{2,1,0:T(8,128)(2,1)S(1)} async-done(((bf16[16,200,384]{2,1,0:T(8,128)(2,1)}), bf16[16,200,384]{2,1,0:T(8,128)(2,1)S(1)}, u32[]{:S(2)}, u32[]{:S(2)}) %all-to-all-start.3) | async-done | bytes 2457632 | tf_op jit(solution)/shard_map/all_to_all | solution.py:798
  529.7 4.7 all-to-all-start.2
  535.1 35.6 %relation_sums.1 = (f32[3200,128]{1,0:T(8,128)}, f32[3200,128]{1,0:T(8,128)}) custom-call(s32[8192]{0:T(1024)} %ids_ref.1, f32[3,8192,128]{2,1,0:T(8,128)} %get-tuple-element.82.refs_0_, f32[3,8192,128]{2,1,0:T(8,128)} %get-tuple-element.83.refs_1_, bf16[16,200,384]{2,1,0:T(8,128)(2,1)} %copy-done, f32[16,1,128]{2,1,0:T(1,128)} %copy-done.16), custom_call_target="tpu_custom_call" | custom-call | bytes 120000000 | tf_op jit(solution)/shard_map/relation_sums/pallas_call | solution.py:636
  570.7 33.8 %collect.4 = (f32[7944,128]{1,0:T(8,128)}, f32[7944,128]{1,0:T(8,128)}) custom-call(s32[16]{0:T(128)} %convert_reduce_fusion.2.counts_ref, s32[32768]{0:T(1024)} %bitcast.48, bf16[16,200,384]{2,1,0:T(8,128)(2,1)} %copy-done, f32[3200,128]{1,0:T(8,128)} %get-tuple-element.84.refs_0_), custom_call_target="tpu_custom_call" | custom-call | bytes 120000000 | tf_op jit(solution)/shard_map/collect/pallas_call | solution.py:602
  606.4 24.2 %outgoing.7 = bf16[16,200,640]{2,1,0:T(8,128)(2,1)} custom-call(s32[16]{0:T(128)} %convert_element_type.63.counts_ref, s32[32768]{0:T(1024)} %broadcast_minimum_fusion.place_ref, f32[24576,128]{1,0:T(8,128)} %bitcast.37, f32[24576,128]{1,0:T(8,128)} %bitcast.41, f32[7944,128]{1,0:T(8,128)} %get-tuple-element.85.refs_0_.refs_2_, ...), custom_call_target="tpu_custom_call" | custom-call | bytes 80000000 | tf_op jit(solution)/shard_map/outgoing/pallas_call | solution.py:553
  630.6 12.0 %all-to-all-done.2.came_ref = bf16[16,200,768]{2,1,0:T(8,128)(2,1)} async-done(((bf16[16,200,768]{2,1,0:T(8,128)(2,1)}), bf16[16,200,768]{2,1,0:T(8,128)(2,1)}, u32[]{:S(2)}, u32[]{:S(2)}) %all-to-all-start.2) | async-done | bytes 4915232 | tf_op jit(solution)/shard_map/all_to_all | solution.py:798
  642.6 4.7 all-to-all-start.5
  648.0 61.7 %collect.5 = (f32[7944,128]{1,0:T(8,128)}, f32[7944,128]{1,0:T(8,128)}) custom-call(s32[16]{0:T(128)} %convert_reduce_fusion.2.counts_ref, s32[32768]{0:T(1024)} %bitcast.49, bf16[16,200,768]{2,1,0:T(8,128)(2,1)} %all-to-all-done.2.came_ref, f32[7944,128]{1,0:T(8,128)} %get-tuple-element.85.refs_0_.refs_2_, f32[7944,128]{1,0:T(8,128)} %get-tuple-element.86.refs_1_), custom_call_target="tpu_custom_call" | custom-call | bytes 120000000 | tf_op jit(solution)/shard_map/collect/pallas_call | solution.py:602
  709.7 11.8 %outgoing.6 = bf16[16,200,256]{2,1,0:T(8,128)(2,1)} custom-call(s32[16]{0:T(128)} %convert_element_type.63.counts_ref, s32[32768]{0:T(1024)} %broadcast_minimum_fusion.place_ref, f32[24576,128]{1,0:T(8,128)} %bitcast.38, f32[24576,128]{1,0:T(8,128)} %bitcast.42, f32[7944,128]{1,0:T(8,128)} %get-tuple-element.87.refs_2_.refs_0_, ...), custom_call_target="tpu_custom_call" | custom-call | bytes 80000000 | tf_op jit(solution)/shard_map/outgoing/pallas_call | solution.py:553
  721.5 36.3 %all-to-all-done.5.came_ref = bf16[16,200,640]{2,1,0:T(8,128)(2,1)} async-done(((bf16[16,200,640]{2,1,0:T(8,128)(2,1)}), bf16[16,200,640]{2,1,0:T(8,128)(2,1)}, u32[]{:S(2)}, u32[]{:S(2)}) %all-to-all-start.5) | async-done | bytes 4096032 | tf_op jit(solution)/shard_map/all_to_all | solution.py:798
  757.8 4.7 all-to-all-start.4
  764.9 36.0 %collect.6 = (f32[7944,128]{1,0:T(8,128)}, f32[7944,128]{1,0:T(8,128)}) custom-call(s32[16]{0:T(128)} %convert_reduce_fusion.2.counts_ref, s32[32768]{0:T(1024)} %bitcast.50, bf16[16,200,640]{2,1,0:T(8,128)(2,1)} %all-to-all-done.5.came_ref, f32[7944,128]{1,0:T(8,128)} %get-tuple-element.87.refs_2_.refs_0_, f32[7944,128]{1,0:T(8,128)} %get-tuple-element.89.refs_1_, ...), custom_call_target="tpu_custom_call" | custom-call | bytes 120000000 | tf_op jit(solution)/shard_map/collect/pallas_call | solution.py:602
  802.1 9.0 %collect.7 = (f32[7944,128]{1,0:T(8,128)}, f32[7944,128]{1,0:T(8,128)}) custom-call(s32[16]{0:T(128)} %convert_reduce_fusion.2.counts_ref, s32[32768]{0:T(1024)} %bitcast.51, bf16[16,200,256]{2,1,0:T(8,128)(2,1)} %copy-done.3, f32[7944,128]{1,0:T(8,128)} %get-tuple-element.90.refs_0_, f32[7944,128]{1,0:T(8,128)} %get-tuple-element.91.refs_1_), custom_call_target="tpu_custom_call" | custom-call | bytes 120000000 | tf_op jit(solution)/shard_map/collect/pallas_call | solution.py:602
  811.0 18.1 %update_entities.1 = (f32[200,7936]{1,0:T(8,128)}, f32[200,7936]{1,0:T(8,128)}, f32[200,7936]{1,0:T(8,128)}) custom-call(f32[200,7936]{1,0:T(8,128)} %weights_ref.1, f32[200,7936]{1,0:T(8,128)} %first_ref.1, f32[200,7936]{1,0:T(8,128)} %second_ref.1, f32[7944,128]{1,0:T(8,128)} %get-tuple-element.92.refs_0_, f32[7944,128]{1,0:T(8,128)} %get-tuple-element.93.refs_1_), custom_call_target="tpu_custom_call" | custom-call | bytes 60000000 | tf_op jit(solution)/shard_map/update_entities/pallas_call | solution.py:665
  (112 shorter events, 39.7 us)
Async XLA Ops:
  7.2 180.3 %all-gather.5.cloned.1.call-start = ((), (), s32[]{:S(2)}) async-start(), calls=%async_computation.8 | async-start | bytes 36765696 | tf_op jit(solution)/shard_map/all_gather | solution.py:725
  11.7 2.7 copy-start.15
  11.7 2.8 copy-start.13
  11.7 2.8 copy-start.14
  13.2 277.0 %all-gather.7.cloned.1.call-start = ((), (), s32[]{:S(2)}) async-start(), calls=%async_computation.9 | async-start | bytes 19427328 | tf_op jit(solution)/shard_map/all_gather | solution.py:725
  236.5 8.4 %copy-start.18 = (f32[3200]{0:T(1024)S(1)}, f32[3200]{0:T(1024)}, u32[]{:S(2)}) copy-start(f32[3200]{0:T(1024)} %param.22) | copy-start | bytes 38404
  236.5 9.7 %copy-start.19 = (s32[3200]{0:T(1024)S(1)}, s32[3200]{0:T(1024)}, u32[]{:S(2)}) copy-start(s32[3200]{0:T(1024)} %param.23) | copy-start | bytes 38404
  236.5 10.4 %copy-start.12 = (s32[8192]{0:T(1024)S(1)}, s32[8192]{0:T(1024)}, u32[]{:S(2)}) copy-start(s32[8192]{0:T(1024)} %ids_ref.1) | copy-start | bytes 98308
  243.4 48.7 %collective-permute-start = (bf16[128,8192]{1,0:T(8,128)(2,1)}, bf16[128,8192]{1,0:T(8,128)(2,1)S(1)}, u32[]{:S(2)}, u32[]{:S(2)}) collective-permute-start(bf16[128,8192]{1,0:T(8,128)(2,1)} %get-tuple-element.64.refs_2_.refs_1_), channel_id=1, source_target_pairs={{0,1},{1,0},{2,3},{3,2},{4,5},{5,4},{6,7},{7,6},{8,9},{9,8},{10,11... | collective-permute-start | bytes 6291464 | tf_op jit(solution)/shard_map/ppermute | solution.py:739
  268.0 11.0 %copy-start.6 = (s32[256,1,128]{2,1,0:T(1,128)S(1)}, s32[256,1,128]{2,1,0:T(1,128)}, u32[]{:S(2)}) copy-start(s32[256,1,128]{2,1,0:T(1,128)} %get-tuple-element.107) | copy-start | bytes 393220
  278.3 81.0 %collective-permute-start.1 = (bf16[128,8192]{1,0:T(8,128)(2,1)}, bf16[128,8192]{1,0:T(8,128)(2,1)}, u32[]{:S(2)}, u32[]{:S(2)}) collective-permute-start(bf16[128,8192]{1,0:T(8,128)(2,1)} %get-tuple-element.66.refs_0_), channel_id=1, source_target_pairs={{0,1},{1,0},{2,3},{3,2},{4,5},{5,4},{6,7},{7,6},{8,9},{9,8},{10,11... | collective-permute-start | bytes 6291464 | tf_op jit(solution)/shard_map/ppermute | solution.py:739
  289.4 245.0 %copy-start.4 = (s32[16,1,2048]{2,1,0:T(1,128)}, s32[16,1,2048]{2,1,0:T(1,128)S(1)}, u32[]{:S(2)}) copy-start(s32[16,1,2048]{2,1,0:T(1,128)S(1)} %all_to_all.33) | copy-start | bytes 393220
  292.1 1.3 copy-start.1
  349.5 8.5 %copy-start.21 = (s32[8]{0:T(128)S(1)}, s32[8]{0:T(128)}, u32[]{:S(2)}) copy-start(s32[8]{0:T(128)} %live_ref.3) | copy-start | bytes 100
  349.5 32.1 %collective-permute-start.2 = (bf16[2,80,4096]{2,1,0:T(8,128)(2,1)}, bf16[2,80,4096]{2,1,0:T(8,128)(2,1)}, u32[]{:S(2)}, u32[]{:S(2)}) collective-permute-start(bf16[2,80,4096]{2,1,0:T(8,128)(2,1)} %get-tuple-element.70.refs_2_), channel_id=1, source_target_pairs={{0,1},{1,0},{2,3},{3,2},{4,5},{5,4},{6,7},{7,6},{8,9},{9,8},{10,11... | collective-permute-start | bytes 3932168 | tf_op jit(solution)/shard_map/ppermute | solution.py:739
  357.4 50.1 %collective-permute-start.3 = (bf16[2,80,4096]{2,1,0:T(8,128)(2,1)}, bf16[2,80,4096]{2,1,0:T(8,128)(2,1)S(1)}, u32[]{:S(2)}, u32[]{:S(2)}) collective-permute-start(bf16[2,80,4096]{2,1,0:T(8,128)(2,1)} %get-tuple-element.76.refs_2_), channel_id=1, source_target_pairs={{0,1},{1,0},{2,3},{3,2},{4,5},{5,4},{6,7},{7,6},{8,9},{9,8},{10,11... | collective-permute-start | bytes 3932168 | tf_op jit(solution)/shard_map/ppermute | solution.py:739
  408.6 26.3 %copy-start.20 = (f32[8,128]{1,0:T(8,128)S(1)}, f32[8,128]{1,0:T(8,128)}, u32[]{:S(2)}) copy-start(f32[8,128]{1,0:T(8,128)} %get-tuple-element.75) | copy-start | bytes 12292
  408.6 34.1 %copy-start.5 = (s32[256,1,128]{2,1,0:T(1,128)S(1)}, s32[256,1,128]{2,1,0:T(1,128)}, u32[]{:S(2)}) copy-start(s32[256,1,128]{2,1,0:T(1,128)} %get-tuple-element.108) | copy-start | bytes 393220
  437.6 29.4 %all-to-all-start.1 = ((f32[16,1,128]{2,1,0:T(1,128)}), f32[16,1,128]{2,1,0:T(1,128)S(1)}, u32[]{:S(2)}, u32[]{:S(2)}) async-start(f32[16,1,128]{2,1,0:T(1,128)} %broadcast_in_dim.31), calls=%async_computation.1 | async-start | bytes 16384 | tf_op jit(solution)/shard_map/all_to_all | solution.py:785
  466.9 42.6 %copy-start.16 = (f32[16,1,128]{2,1,0:T(1,128)}, f32[16,1,128]{2,1,0:T(1,128)S(1)}, u32[]{:S(2)}) copy-start(f32[16,1,128]{2,1,0:T(1,128)S(1)} %all-to-all-done.1.refs_3_) | copy-start | bytes 24580
  466.9 61.4 %all-to-all-start.3 = ((bf16[16,200,384]{2,1,0:T(8,128)(2,1)}), bf16[16,200,384]{2,1,0:T(8,128)(2,1)S(1)}, u32[]{:S(2)}, u32[]{:S(2)}) async-start(bf16[16,200,384]{2,1,0:T(8,128)(2,1)} %outgoing.5), calls=%async_computation.3 | async-start | bytes 4915200 | tf_op jit(solution)/shard_map/all_to_all | solution.py:798
  528.3 1.4 copy-start
  529.7 112.8 %all-to-all-start.2 = ((bf16[16,200,768]{2,1,0:T(8,128)(2,1)}), bf16[16,200,768]{2,1,0:T(8,128)(2,1)}, u32[]{:S(2)}, u32[]{:S(2)}) async-start(bf16[16,200,768]{2,1,0:T(8,128)(2,1)} %outgoing.4), calls=%async_computation.2 | async-start | bytes 9830400 | tf_op jit(solution)/shard_map/all_to_all | solution.py:798
  570.7 33.8 %copy-start.2 = (f32[3200,128]{1,0:T(8,128)S(1)}, f32[3200,128]{1,0:T(8,128)}, u32[]{:S(2)}) copy-start(f32[3200,128]{1,0:T(8,128)} %get-tuple-element.84.refs_0_) | copy-start | bytes 4915204
  570.7 33.8 %copy-start.7 = (f32[3200,128]{1,0:T(8,128)S(1)}, f32[3200,128]{1,0:T(8,128)}, u32[]{:S(2)}) copy-start(f32[3200,128]{1,0:T(8,128)} %get-tuple-element.88) | copy-start | bytes 4915204
  642.6 115.2 %all-to-all-start.5 = ((bf16[16,200,640]{2,1,0:T(8,128)(2,1)}), bf16[16,200,640]{2,1,0:T(8,128)(2,1)}, u32[]{:S(2)}, u32[]{:S(2)}) async-start(bf16[16,200,640]{2,1,0:T(8,128)(2,1)} %outgoing.7), calls=%async_computation.5 | async-start | bytes 8192000 | tf_op jit(solution)/shard_map/all_to_all | solution.py:798
  647.2 115.8 %reduce-scatter.2.cloned.1.call-start = ((), (), s32[]{:S(2)}) async-start(), calls=%async_computation.7 | async-start | bytes 3481600 | tf_op jit(solution)/shard_map/reduce_scatter | solution.py:806
  709.7 52.8 %copy-start.17 = (f32[16,1,128]{2,1,0:T(1,128)S(1)}, f32[16,1,128]{2,1,0:T(1,128)}, u32[]{:S(2)}) copy-start(f32[16,1,128]{2,1,0:T(1,128)} %copy-done.16) | copy-start | bytes 24580
  709.7 53.3 %copy-start.9 = (f32[200,200]{1,0:T(8,128)S(1)}, f32[200,200]{1,0:T(8,128)}, u32[]{:S(2)}) copy-start(f32[200,200]{1,0:T(8,128)} %param.27) | copy-start | bytes 480004
  709.7 53.3 %copy-start.10 = (f32[200,200]{1,0:T(8,128)S(1)}, f32[200,200]{1,0:T(8,128)}, u32[]{:S(2)}) copy-start(f32[200,200]{1,0:T(8,128)} %param.28) | copy-start | bytes 480004
  709.7 53.3 %copy-start.11 = (f32[200,200]{1,0:T(8,128)S(1)}, f32[200,200]{1,0:T(8,128)}, u32[]{:S(2)}) copy-start(f32[200,200]{1,0:T(8,128)} %param.29) | copy-start | bytes 480004
  757.8 43.1 %all-to-all-start.4 = ((bf16[16,200,256]{2,1,0:T(8,128)(2,1)}), bf16[16,200,256]{2,1,0:T(8,128)(2,1)S(1)}, u32[]{:S(2)}, u32[]{:S(2)}) async-start(bf16[16,200,256]{2,1,0:T(8,128)(2,1)} %outgoing.6), calls=%async_computation.4 | async-start | bytes 3276800 | tf_op jit(solution)/shard_map/all_to_all | solution.py:798
  (2 other events, 2.2 us)
Sparse Core Ops, SparseCore 0:
  13.3 174.0 all-gather.4
  189.0 96.1 all-gather.6
  651.9 96.3 reduce-scatter.1

commit v5 on v4

--- a/solution.py
+++ b/solution.py
@@ -19,7 +19,7 @@
 LANES = 128
 UNROLL = 8
 PARTS = 4
-HALVES = 2
+HALVES = 4
 TURN = 512
 REL_PAD = 256
 TERMS = 3
@@ -330,7 +330,7 @@
 
 def last_kernel(depth, n_given, head_ref, tail_ref, neg_ref, rel_ref, *refs):
     biases, norms = refs[:n_given], refs[n_given : 2 * n_given]
-    off_ref, tail_out, pair_ref = refs[2 * n_given :]
+    off_ref, tail_out, pair_ref = refs[-3:]
     shifted_t, bias = edge_parts(depth, head_ref, tail_ref, rel_ref, off_ref, tail_out)
     neg_t = neg_ref[...].T
     norm = column_sum(neg_t)
@@ -342,7 +342,7 @@
     pair_ref[1] = with_terms(neg_t, norm, depth)
 
 
-def last_slice(fetched, rel_rows, biases, norms, depth, blocks, block_len, half):
+def last_slice(fetched, rel_rows, biases, norms, depth, blocks, block_len, half, after):
     part = blocks // HALVES
     count = part * block_len
     tall = last_rows(depth) + 8
@@ -360,7 +360,8 @@
         grid=(part,),
         in_specs=[rows(0), rows(1), rows(2), rows(0)]
         + [pl.BlockSpec((1, block_len), lambda b: (0, half * part + b))]
-        * (len(biases) + len(norms)),
+        * (len(biases) + len(norms))
+        + [whole(pl.ANY)] * len(after),
         out_specs=[
             pl.BlockSpec((block_len, LANES), lambda b: (b, 0)),
             pl.BlockSpec((block_len, LANES), lambda b: (b, 0)),
@@ -369,7 +370,7 @@
         compiler_params=params(),
         cost_estimate=cost(0, 20e6),
         name="last_slice",
-    )(fetched, fetched, fetched, rel_rows, *biases, *norms)
+    )(fetched, fetched, fetched, rel_rows, *biases, *norms, *after)
 
 
 def block_kernel(slices, n_col, half, me_ref, live_ref, *refs):
@@ -378,9 +379,7 @@
     given = [refs[k * per_col : (k + 1) * per_col] for k in range(n_col)]
     refs = refs[n_col * per_col :]
     offs, tails, refs = refs[:n], refs[n : 2 * n], refs[2 * n :]
-    if half > 0:
-        refs = refs[n:]
-    grads, refs = refs[:n], refs[n:]
+    grad, refs = refs[-9], refs[-8:]
     loss_ref, shift_scr, neg_scr, sums_scr, cross, slopes, row_bias, row_sum = refs
     block = pl.program_id(0)
     length = cross.shape[0]
@@ -422,11 +421,13 @@
         part = slice(at, at + tile)
         moved = lax.dot_general(slopes[part, :], neg_scr[me], NT, preferred_element_type=F32)
         fade = -row_sum[part, :]
-        for (start, depth), off, tail, grad in zip(slices, offs, tails, grads):
-            grad[0, part, :depth] = (
-                fade[:, :depth] * tail[part, :depth].astype(F32) + moved[:, start : start + depth]
+        for m, (start, depth) in enumerate(slices):
+            into = pl.ds(n * at + m, tile, stride=n)
+            grad[0, into, :depth] = (
+                fade[:, :depth] * tails[m][part, :depth].astype(F32)
+                + moved[:, start : start + depth]
             )
-            grad[1, part, :] = fade * off[part, :]
+            grad[1, into, :] = fade * offs[m][part, :]
 
     products(0)
     for begin in range(0, length, tile):
@@ -470,17 +471,17 @@
 
     moved = lax.dot_general(shift_scr[me], slopes[...], NN, preferred_element_type=F32)
     moved = 0.5 * moved - col_sum * neg_scr[me].astype(F32)
-    for (start, depth), grad in zip(slices, grads):
-        grad[2, :, :depth] = moved[start : start + depth, :].T
-
-
-def block_math(me, live_counts, given, offs, tails, old, slices, block_len, half):
+    for m, (start, depth) in enumerate(slices):
+        grad[2, pl.ds(m, length, stride=n), :depth] = moved[start : start + depth, :].T
+
+
+def block_math(me, live_counts, given, offs, tails, old, slices, block_len, half, after):
     n, n_col = len(slices), len(given)
     blocks = live_counts.shape[0]
     part = blocks // HALVES
     width = sum(depth for _, depth in slices)
     flat = [piece for per_col in given for piece in per_col]
-    kept = [] if old is None else old
+    kept = [] if old is None else [old]
 
     def columns(piece):
         if piece.ndim == 3:
@@ -494,18 +495,19 @@
     first_old = 2 + len(flat) + 2 * n
     return pl.pallas_call(
         functools.partial(block_kernel, slices, n_col, half),
-        out_shape=[jax.ShapeDtypeStruct((3, blocks * block_len, LANES), F32)] * n
-        + [jax.ShapeDtypeStruct((8, LANES), F32)],
+        out_shape=[
+            jax.ShapeDtypeStruct((3, n * blocks * block_len, LANES), F32),
+            jax.ShapeDtypeStruct((8, LANES), F32),
+        ],
         grid=(part,),
         in_specs=[whole(SMEM)] * 2
         + [columns(piece) for piece in flat]
         + [rows(array) for array in offs + tails]
-        + [whole(pl.ANY)] * len(kept),
+        + [whole(pl.ANY)] * len(kept + after),
         out_specs=[
-            pl.BlockSpec((3, block_len, LANES), lambda b: (0, half * part + b, 0))
-        ]
-        * n
-        + [pl.BlockSpec((8, LANES), lambda b: (0, 0))],
+            pl.BlockSpec((3, n * block_len, LANES), lambda b: (0, half * part + b, 0)),
+            pl.BlockSpec((8, LANES), lambda b: (0, 0)),
+        ],
         input_output_aliases={first_old + k: k for k in range(len(kept))},
         scratch_shapes=[
             pltpu.VMEM((n_col, width, block_len), BF16),
@@ -519,12 +521,16 @@
         compiler_params=params(),
         cost_estimate=cost(part * 8 * block_len * block_len * width, 120e6),
         name="block_math",
-    )(me, live_counts, *flat, *offs, *tails, *kept)
-
-
-def outgoing_kernel(slices, capacity, begin, counts_ref, place_ref, *refs):
-    n = len(slices)
-    grads, out_ref, tiles = refs[:n], refs[-n - 1], refs[-n:]
+    )(me, live_counts, *flat, *offs, *tails, *kept, *after)
+
+
+def pair_of(row, n):
+    return pl.ds(pl.multiple_of(row * n, n), n)
+
+
+def outgoing_kernel(slices, capacity, begin, counts_ref, place_ref, grad, *refs):
+    n = len(slices)
+    out_ref, tile = refs[-2:]
     groups, width, chunk = out_ref.shape
 
     def owner(group, carry):
@@ -534,56 +540,54 @@
             for lane in range(UNROLL):
                 at = step * UNROLL + lane
                 place = place_ref[group * capacity + begin + at]
-                for grad, tile in zip(grads, tiles):
-                    tile[pl.ds(at, 1), :] = grad[pl.ds(place, 1), :]
+                tile[pair_of(at, n), :] = grad[pair_of(place, n), :]
             return inner
 
         lax.fori_loop(0, (wanted + UNROLL - 1) // UNROLL, body, 0)
-        for (start, depth), tile in zip(slices, tiles):
-            out_ref[group, start : start + depth, :] = tile[...].T[:depth].astype(BF16)
+        for m, (start, depth) in enumerate(slices):
+            piece = tile[pl.ds(m, chunk, stride=n), :].T
+            out_ref[group, start : start + depth, :] = piece[:depth].astype(BF16)
         return carry
 
     lax.fori_loop(0, groups, owner, 0)
 
 
-def outgoing(counts, place_list, grads, slices, begin, chunk, after):
+def outgoing(counts, place_list, grad, slices, begin, chunk, after):
     groups, capacity = place_list.shape
     n = len(slices)
     width = sum(depth for _, depth in slices)
     return pl.pallas_call(
         functools.partial(outgoing_kernel, slices, capacity, begin),
         out_shape=jax.ShapeDtypeStruct((groups, width, chunk), BF16),
-        in_specs=[whole(SMEM)] * 2 + [whole(VMEM)] * n + [whole(pl.ANY)] * len(after),
+        in_specs=[whole(SMEM)] * 2 + [whole(VMEM)] + [whole(pl.ANY)] * len(after),
         out_specs=whole(VMEM),
-        scratch_shapes=[pltpu.VMEM((chunk, LANES), F32)] * n,
+        scratch_shapes=[pltpu.VMEM((n * chunk, LANES), F32)],
         compiler_params=params(),
         cost_estimate=cost(0, 80e6),
         name="outgoing",
-    )(counts, place_list.reshape(-1), *grads, *after)
+    )(counts, place_list.reshape(-1), grad, *after)
 
 
 def collect_kernel(slices, capacity, begin, first, counts_ref, row_ref, came_ref, *refs):
     n = len(slices)
-    olds = () if first else refs[:n]
-    totals, tiles = refs[-2 * n : -n], refs[-n:]
+    total, tile = refs[-2:]
     groups, width, chunk = came_ref.shape
-    for k in range(n):
-        totals[k][...] = jnp.zeros_like(totals[k]) if first else olds[k][...]
+    total[...] = jnp.zeros_like(total) if first else refs[0][...]
 
     def source(group, carry):
         wanted = jnp.clip(counts_ref[group] - begin, 0, chunk)
 
         @pl.when(wanted > 0)
         def _():
-            for (start, depth), tile in zip(slices, tiles):
-                tile[:, :depth] = came_ref[group, start : start + depth, :].astype(F32).T
+            for m, (start, depth) in enumerate(slices):
+                piece = came_ref[group, start : start + depth, :].astype(F32)
+                tile[pl.ds(m, chunk, stride=n), :depth] = piece.T
 
             def body(step, inner):
                 for lane in range(UNROLL):
                     at = step * UNROLL + lane
-                    row = row_ref[group * capacity + begin + at]
-                    for total, tile in zip(totals, tiles):
-                        total[pl.ds(row, 1), :] = total[pl.ds(row, 1), :] + tile[pl.ds(at, 1), :]
+                    into = pair_of(row_ref[group * capacity + begin + at], n)
+                    total[into, :] = total[into, :] + tile[pair_of(at, n), :]
                 return inner
 
             lax.fori_loop(0, (wanted + UNROLL - 1) // UNROLL, body, 0)
@@ -593,71 +597,66 @@
     lax.fori_loop(0, groups, source, 0)
 
 
-def collect(counts, row_list, came, totals, slices, begin, ent_rows, after):
+def collect(counts, row_list, came, total, slices, begin, ent_rows, after):
     capacity = row_list.shape[1]
     chunk = came.shape[2]
     n = len(slices)
-    first = totals is None
-    given = () if first else tuple(totals)
-    return pl.pallas_call(
-        functools.partial(collect_kernel, slices, capacity, begin, first),
-        out_shape=[jax.ShapeDtypeStruct((ent_rows + 8, LANES), F32)] * n,
+    given = [] if total is None else [total]
+    return pl.pallas_call(
+        functools.partial(collect_kernel, slices, capacity, begin, total is None),
+        out_shape=jax.ShapeDtypeStruct((n * (ent_rows + 8), LANES), F32),
         in_specs=[whole(SMEM)] * 2
         + [whole(VMEM)] * (1 + len(given))
         + [whole(pl.ANY)] * len(after),
-        out_specs=[whole(VMEM)] * n,
-        scratch_shapes=[pltpu.VMEM((chunk, LANES), F32)] * n,
+        out_specs=whole(VMEM),
+        scratch_shapes=[pltpu.VMEM((n * chunk, LANES), F32)],
         compiler_params=params(),
         cost_estimate=cost(0, 120e6),
         name="collect",
     )(counts, row_list.reshape(-1), came, *given, *after)
 
 
-def relation_sums_kernel(n, ids_ref, *refs):
-    grads, totals = refs[:n], refs[-n:]
-    count = grads[0].shape[1]
-    for total in totals:
-        total[...] = jnp.zeros_like(total)
+def relation_sums_kernel(n, ids_ref, grad, *refs):
+    total = refs[-1]
+    total[...] = jnp.zeros_like(total)
 
     def body(step, carry):
         for lane in range(UNROLL):
             at = step * UNROLL + lane
-            row = ids_ref[at]
-            for grad, total in zip(grads, totals):
-                total[pl.ds(row, 1), :] = total[pl.ds(row, 1), :] + grad[0, pl.ds(at, 1), :]
+            into = pair_of(ids_ref[at], n)
+            total[into, :] = total[into, :] + grad[0, pair_of(at, n), :]
         return carry
 
-    lax.fori_loop(0, count // UNROLL, body, 0)
-
-
-def relation_sums(relation_ids, grads, rel_total, after):
-    n = len(grads)
+    lax.fori_loop(0, grad.shape[1] // n // UNROLL, body, 0)
+
+
+def relation_sums(relation_ids, grad, n, rel_total, after):
     count = relation_ids.shape[0]
     return pl.pallas_call(
         functools.partial(relation_sums_kernel, n),
-        out_shape=[jax.ShapeDtypeStruct((rel_total, LANES), F32)] * n,
+        out_shape=jax.ShapeDtypeStruct((n * rel_total, LANES), F32),
         grid=(1,),
-        in_specs=[whole(SMEM)]
-        + [pl.BlockSpec((1, count, LANES), lambda i: (0, 0, 0))] * n
+        in_specs=[whole(SMEM), pl.BlockSpec((1, n * count, LANES), lambda i: (0, 0, 0))]
         + [whole(pl.ANY)] * len(after),
-        out_specs=[whole(VMEM)] * n,
+        out_specs=whole(VMEM),
         compiler_params=params(),
         cost_estimate=cost(0, 120e6),
         name="relation_sums",
-    )(relation_ids, *grads, *after)
-
-
-def update_kernel(slices, weights_ref, first_ref, second_ref, *refs):
-    n = len(slices)
-    totals, outs, scr = refs[:n], refs[n : n + 3], refs[n + 3]
-    for (start, depth), total in zip(slices, totals):
-        scr[start : start + depth, :] = total[...].T[:depth]
+    )(relation_ids, grad, *after)
+
+
+def update_kernel(slices, weights_ref, first_ref, second_ref, total, *refs):
+    n = len(slices)
+    outs, scr = refs[:3], refs[3]
+    cols = weights_ref.shape[1]
+    for m, (start, depth) in enumerate(slices):
+        scr[start : start + depth, :] = total[pl.ds(m, cols, stride=n), :].T[:depth]
     results = adamw_update(weights_ref[...], scr[...], first_ref[...], second_ref[...])
     for out, result in zip(outs, results):
         out[...] = result
 
 
-def update_entities(weights, totals, first, second, slices):
+def update_entities(weights, total, first, second, slices):
     width, ent_rows = weights.shape
     cols = 1024
     n = len(slices)
@@ -666,13 +665,18 @@
         functools.partial(update_kernel, slices),
         out_shape=[jax.ShapeDtypeStruct((width, ent_rows), F32)] * 3,
         grid=(pl.cdiv(ent_rows, cols),),
-        in_specs=[table] * 3 + [pl.BlockSpec((cols, LANES), lambda i: (i, 0))] * n,
+        in_specs=[table] * 3 + [pl.BlockSpec((n * cols, LANES), lambda i: (i, 0))],
         out_specs=[table] * 3,
         scratch_shapes=[pltpu.VMEM((width, cols), F32)],
         compiler_params=params(),
         cost_estimate=cost(0, 60e6),
         name="update_entities",
-    )(weights, first, second, *totals)
+    )(weights, first, second, total)
+
+
+def add_across(value, groups, step):
+    turn = [(g, g ^ step) for g in range(groups)]
+    return value + lax.ppermute(value, "edge", turn)
 
 
 def chunk_bounds(capacity):
@@ -744,7 +748,7 @@
     tails = [[] for _ in range(HALVES)]
     biases, norms, first_sent, rel_rows = [], [], [], None
     for k, (start, depth) in enumerate(slices):
-        early = [asked] + first_sent if k > 0 else []
+        early = first_sent if k > 0 else [asked]
         fetched = fetch(counts, place_flat, row_flat, dense[k], id_count, ent_rows, early)
         if k < n - 1:
             neg_low, norm = negatives(fetched, depth, blocks, block_len)
@@ -764,65 +768,81 @@
             continue
         if rel_rows is None:
             rel_rows = relation_rows(rel_places, dense[0], rel_scale, slices, [])
-        for half in range(HALVES):
-            off, tail, pair = last_slice(
-                fetched, rel_rows[k], biases, norms, depth, blocks, block_len, half
-            )
-            offs[half].append(off)
-            tails[half].append(tail)
-            for col, piece in enumerate([pair] + from_others(pair)):
-                given[half][col].append(piece)
-
-    grads, loss_tiles = None, []
+
+    def finish(half, after):
+        off, tail, pair = last_slice(
+            fetched, rel_rows[-1], biases, norms, slices[-1][1], blocks, block_len, half, after
+        )
+        offs[half].append(off)
+        tails[half].append(tail)
+        for col, piece in enumerate([pair] + from_others(pair)):
+            given[half][col].append(piece)
+
+    grad, loss_tiles = None, []
+    finish(0, [])
     for half in range(HALVES):
-        *grads, loss_tile = block_math(
-            me, live_counts, given[half], offs[half], tails[half], grads, slices, block_len, half
+        after = []
+        if half + 1 < HALVES:
+            finish(half + 1, [given[half][-1][-1]] + loss_tiles[-1:])
+            after = offs[half + 1][-1:]
+        grad, loss_tile = block_math(
+            me,
+            live_counts,
+            given[half],
+            offs[half],
+            tails[half],
+            grad,
+            slices,
+            block_len,
+            half,
+            after,
         )
         loss_tiles.append(loss_tile)
     live = jnp.sum(jnp.minimum(live_counts, block_len)).astype(F32)
     loss_own = jnp.sum(functools.reduce(jnp.add, loss_tiles))
-    loss_row = jnp.zeros((LANES,), F32).at[0].set(loss_own).at[1].set(live)
-    loss_all = lax.all_to_all(
-        jnp.broadcast_to(loss_row, (groups, 1, LANES)), "edge", split_axis=0, concat_axis=0, tiled=True
-    )
-    loss_pair = jnp.sum(loss_all[:, 0, :2], axis=0)
-
-    flat = [grad.reshape(id_count, LANES) for grad in grads]
+    lane = jnp.arange(LANES, dtype=jnp.int32)[None, :]
+    loss_row = jnp.where(lane == 0, loss_own, jnp.where(lane == 1, live, 0.0))
+    step = 1
+    loss_rows = []
+    while step < groups:
+        loss_row = add_across(loss_row, groups, step)
+        loss_rows.append(loss_row)
+        step *= 2
+
+    def loss_step(k):
+        return loss_rows[min(k, len(loss_rows) - 1)]
+
+    flat = grad.reshape(n * id_count, LANES)
     bounds = chunk_bounds(capacity)
     chunks = len(bounds) - 1
-    arrived, totals, after = [], None, []
+    arrived, total, after = [], None, []
     for k in range(chunks):
+        after = after + [loss_step(0)] if k == 1 else after
         sent = outgoing(
             counts, safe_places, flat, slices, bounds[k], bounds[k + 1] - bounds[k], after
         )
         arrived.append(lax.all_to_all(sent, "edge", split_axis=0, concat_axis=0, tiled=True))
         after = []
         if k == 1:
-            rel_terms = relation_sums(relation_ids, grads, rel_total, [arrived[0], loss_all])
-            after = rel_terms[:1]
-            rel_terms = jnp.concatenate(
-                [term[:, :depth] for (start, depth), term in zip(slices, rel_terms)], axis=1
+            rel_terms = relation_sums(
+                relation_ids, grad, n, rel_total, [arrived[0], loss_step(1)]
             )
+            after = [rel_terms, loss_step(2)]
+            rel_terms = rel_terms.reshape(rel_total, n * LANES)[:, :width]
             relation_grad = lax.psum_scatter(rel_terms, "edge", scatter_dimension=0, tiled=True)
         if k == chunks - 1:
             after = [relation_grad]
         if k > 0:
-            totals = collect(
-                asked_counts,
-                asked,
-                arrived[k - 1],
-                totals,
-                slices,
-                bounds[k - 1],
-                ent_rows,
-                after,
+            total = collect(
+                asked_counts, asked, arrived[k - 1], total, slices, bounds[k - 1], ent_rows, after
             )
-            after = [totals[0], rel_terms]
+            after = [total, rel_terms, loss_step(3)]
     k = chunks - 1
-    totals = collect(asked_counts, asked, arrived[k], totals, slices, bounds[k], ent_rows, [])
+    total = collect(asked_counts, asked, arrived[k], total, slices, bounds[k], ent_rows, [])
+    loss_pair = loss_step(groups)[0, :2]
 
     new_entity, new_entity_first, new_entity_second = update_entities(
-        entity_table, totals, entity_first, entity_second, slices
+        entity_table, total, entity_first, entity_second, slices
     )
     new_relation, new_relation_first, new_relation_second = adamw_update(
         relation_table, relation_grad, relation_first, relation_second

time: 843 us -> 935 us (1.11)
  waiting for transfers between devices: 235 us -> 330 us
  Pallas kernels: 492 us -> 471 us
  starting transfers between devices: 29.7 us -> 46.4 us
  blocking collectives: 10.5 us -> 0 us
    ppermute x0 -> x4, waiting for transfers between devices: none -> 96 us  [add_across(): return value + lax.ppermute(value, 'edge', turn)]
    pallas_call x4, Pallas kernels: 140 us -> 116 us  [collect(): pl.pallas_call(functools.partial(collect_kernel, slices, capacity, begin,...]
    all_to_all x1 -> x0, blocking collectives: 10.5 us -> none  [shards(): lax.all_to_all(row_list, 'edge', split_axis=0, concat_axis=0, tiled=True)]
    ppermute x0 -> x4, starting transfers between devices: none -> 10.1 us  [add_across(): return value + lax.ppermute(value, 'edge', turn)]
    pallas_call x2 -> x4, Pallas kernels: 52.3 us -> 59.6 us  [block_math(): pl.pallas_call(functools.partial(block_kernel, slices, n_col, half), out_...]
    ppermute x4 -> x6, waiting for transfers between devices: 24.3 us -> 21 us  [from_others(): return [lax.ppermute(array, 'col', turn) for turn in turns]]
  transfers between devices with their start and end apart: 12 -> 18, of which waited for: 6 -> 12; matrix products, arithmetic and copies ran while one was open for 5% -> 5% of each run, Pallas kernels for 52% -> 43%
where the time goes in v5:
time: 935 us; the launch traced here: 926 us
  Pallas kernels  471 us (50%)
  waiting for transfers between devices  330 us (35%)
  starting transfers between devices  46.4 us (5%)
  other arithmetic  32.1 us (3%)
  local copies, waits for them, and re-layouts  17.9 us (2%)
  between operations  16.1 us (2%)
  matrix products  12.3 us (1%)
    all_gather x2, waiting for transfers between devices, shards(): dense.append(lax.all_gather(sent, 'edge', axis=0, tiled=False))  138 us
    pallas_call x4, Pallas kernels, collect(): pl.pallas_call(functools.partial(collect_kernel, slices, capacity, begin,...  116 us
    pallas_call x2, Pallas kernels, fetch(): pl.pallas_call(functools.partial(fetch_kernel, capacity, moves, ent_rows)...  98.8 us
    pallas_call x4, Pallas kernels, outgoing(): pl.pallas_call(functools.partial(outgoing_kernel, slices, capacity, begin...  96.2 us
    ppermute x4, waiting for transfers between devices, add_across(): return value + lax.ppermute(value, 'edge', turn)  96 us
    all_to_all x4, waiting for transfers between devices, shards(): lax.all_to_all(sent, 'edge', split_axis=0, concat_axis=0, tiled=True)  67.4 us
    pallas_call x4, Pallas kernels, block_math(): pl.pallas_call(functools.partial(block_kernel, slices, n_col, half), out_...  59.6 us
    pallas_call x1, Pallas kernels, relation_sums(): pl.pallas_call(functools.partial(relation_sums_kernel, n), out_shape=jax....  30.1 us
  transfers between devices with their start and end apart: 18, of which 12 were waited for; matrix products, arithmetic and copies ran while one was open for 5% of the time, Pallas kernels for 43%

profile of v5, /device:TPU:16, one launch (start us, length us, event | category | flops | bytes accessed | tf_op | source)
XLA Modules:
  0.0 925.6 jit_solution(6572447663723980512)
XLA Ops:
  24.7 8.6 broadcast_multiply_fusion
  33.2 11.8 %fusion.8 = s32[256,512]{1,0:T(8,128)S(1)} fusion(bf16[512,24576]{1,0:T(8,128)(2,1)} %bitcast.44, s32[24576]{0:T(1024)S(1)} %get-tuple-element.81), kind=kOutput, calls=%fused_computation.16 | convolution fusion | flops 6448873472 | bytes 25788416 | tf_op jit(solution)/shard_map/dot_general | solution.py:84
  53.3 6.5 all-to-all-done
  60.5 131.9 %all-gather.5.cloned.1.call-done = bf16[2048,8448]{1,0:T(8,128)(2,1)} async-done(((bf16[128,8448]{1,0:T(8,128)(2,1)}), bf16[2048,8448]{1,0:T(8,128)(2,1)}) %all-gather.5.cloned.1.call-update) | async-done | bytes 34603024 | tf_op jit(solution)/shard_map/all_gather | solution.py:729
  192.4 49.1 %fetch_rows.2.neg_ref.head_ref.tail_ref = f32[24584,128]{1,0:T(8,128)} custom-call(s32[16]{0:T(128)} %convert_element_type.63.counts_ref, s32[32768]{0:T(1024)} %bitcast.50, s32[32768]{0:T(1024)} %bitcast.6.row_ref, bf16[16,128,8448]{2,1,0:T(8,128)(2,1)} %bitcast.38, s32[16,2048]{1,0:T(8,128)} %bitcast.53), custom_call_target="tpu_custom_call" | custom-call | bytes 170000000 | tf_op jit(solution)/shard_map/fetch_rows/pallas_call | solution.py:221
  241.5 6.9 negatives.1
  252.6 20.4 %relation_rows.1 = (f32[8192,128]{1,0:T(8,128)}, f32[8192,128]{1,0:T(8,128)}) custom-call(s32[8192]{0:T(1024)} %fusion.28.ids_ref, f32[16,256]{1,0:T(8,128)} %pad.14.scale_ref, bf16[16,128,8448]{2,1,0:T(8,128)(2,1)} %bitcast.39, bf16[16,128,8448]{2,1,0:T(8,128)(2,1)} %bitcast.40, bf16[128,8192]{1,0:T(8,128)(2,1)} %get-tuple-element.38.refs_2_.refs_1_), custom_call_target="tpu_custom_call" | custom-call | bytes 80000000 | tf_op jit(solution)/shard_map/relation_rows/pallas_call | solution.py:129
  273.0 10.2 %edges.1 = (f32[8192,128]{1,0:T(8,128)}, bf16[8192,128]{1,0:T(8,128)(2,1)}, bf16[128,8192]{1,0:T(8,128)(2,1)}, f32[1,8192]{1,0:T(1,128)}) custom-call(f32[24584,128]{1,0:T(8,128)} %fetch_rows.2.neg_ref.head_ref.tail_ref, f32[24584,128]{1,0:T(8,128)} %fetch_rows.2.neg_ref.head_ref.tail_ref, f32[8192,128]{1,0:T(8,128)} %get-tuple-element.39.rel_ref), custom_call_target="tpu_custom_call" | custom-call | bytes 30000000 | tf_op jit(solution)/shard_map/edges/pallas_call | solution.py:294
  290.2 7.0 collective-permute-done.refs_0_.refs_4_
  298.5 49.7 %fetch_rows.3.head_ref.tail_ref.neg_ref = f32[24584,128]{1,0:T(8,128)} custom-call(s32[16]{0:T(128)} %convert_element_type.63.counts_ref, s32[32768]{0:T(1024)} %bitcast.51, s32[32768]{0:T(1024)} %bitcast.6.row_ref, bf16[16,72,7936]{2,1,0:T(8,128)(2,1)} %bitcast.45, bf16[128,8192]{1,0:T(8,128)(2,1)} %copy-done), custom_call_target="tpu_custom_call" | custom-call | bytes 170000000 | tf_op jit(solution)/shard_map/fetch_rows/pallas_call | solution.py:221
  353.3 14.0 %collective-permute-done.2.refs_2_.refs_5_ = bf16[2,80,2048]{2,1,0:T(8,128)(2,1)S(1)} collective-permute-done((bf16[2,80,2048]{2,1,0:T(8,128)(2,1)}, bf16[2,80,2048]{2,1,0:T(8,128)(2,1)S(1)}, u32[]{:S(2)}, u32[]{:S(2)}) %collective-permute-start.2) | collective-permute-done | bytes 655392 | tf_op jit(solution)/shard_map/ppermute | solution.py:743
  373.2 14.8 %block_math.4 = (f32[3,16384,128]{2,1,0:T(8,128)}, f32[8,128]{1,0:T(8,128)}) custom-call(s32[1]{0:T(128)} %bitcast.me_ref, s32[8]{0:T(128)} %live_ref.7, bf16[128,8192]{1,0:T(8,128)(2,1)} %get-tuple-element.40.refs_0_, bf16[128,8192]{1,0:T(8,128)(2,1)} %get-tuple-element.38.refs_2_.refs_1_, bf16[2,80,2048]{2,1,0:T(8,128)(2,1)} %get-tuple-element.44.refs_2_, ...), custom_call_target="tpu_custom_call" | custom-call | flops 3355443200 | bytes 120000000 | tf_op jit(solution)/shard_map/block_math/pallas_call | solution.py:496
  393.0 15.0 %block_math.5 = (f32[3,16384,128]{2,1,0:T(8,128)}, f32[8,128]{1,0:T(8,128)}) custom-call(s32[1]{0:T(128)} %bitcast.me_ref, s32[8]{0:T(128)} %live_ref.7, bf16[128,8192]{1,0:T(8,128)(2,1)} %get-tuple-element.40.refs_0_, bf16[128,8192]{1,0:T(8,128)(2,1)} %get-tuple-element.38.refs_2_.refs_1_, ...), custom_call_target="tpu_custom_call", output_to_operand_aliasing={{0}: (12, {})} | custom-call | flops 3355443200 | bytes 120000000 | tf_op jit(solution)/shard_map/block_math/pallas_call | solution.py:496
  414.7 14.8 %block_math.6 = (f32[3,16384,128]{2,1,0:T(8,128)}, f32[8,128]{1,0:T(8,128)}) custom-call(s32[1]{0:T(128)} %bitcast.me_ref, s32[8]{0:T(128)} %live_ref.7, bf16[128,8192]{1,0:T(8,128)(2,1)} %get-tuple-element.40.refs_0_, bf16[128,8192]{1,0:T(8,128)(2,1)} %get-tuple-element.38.refs_2_.refs_1_, ...), custom_call_target="tpu_custom_call", output_to_operand_aliasing={{0}: (12, {})} | custom-call | flops 3355443200 | bytes 120000000 | tf_op jit(solution)/shard_map/block_math/pallas_call | solution.py:496
  430.3 15.1 %block_math.7 = (f32[3,16384,128]{2,1,0:T(8,128)}, f32[8,128]{1,0:T(8,128)}) custom-call(s32[1]{0:T(128)} %bitcast.me_ref, s32[8]{0:T(128)} %live_ref.7, bf16[128,8192]{1,0:T(8,128)(2,1)} %get-tuple-element.40.refs_0_, bf16[128,8192]{1,0:T(8,128)(2,1)} %get-tuple-element.38.refs_2_.refs_1_, ...), custom_call_target="tpu_custom_call", output_to_operand_aliasing={{0}: (12, {})} | custom-call | flops 3355443200 | bytes 120000000 | tf_op jit(solution)/shard_map/block_math/pallas_call | solution.py:496
  445.3 23.5 %outgoing.5 = bf16[16,200,384]{2,1,0:T(8,128)(2,1)} custom-call(s32[16]{0:T(128)} %convert_element_type.63.counts_ref, s32[32768]{0:T(1024)} %broadcast_minimum_fusion.place_ref, f32[49152,128]{1,0:T(8,128)} %bitcast.34), custom_call_target="tpu_custom_call" | custom-call | bytes 80000000 | tf_op jit(solution)/shard_map/outgoing/pallas_call | solution.py:559
  479.2 36.6 %outgoing.4 = bf16[16,200,768]{2,1,0:T(8,128)(2,1)} custom-call(s32[16]{0:T(128)} %convert_element_type.63.counts_ref, s32[32768]{0:T(1024)} %broadcast_minimum_fusion.place_ref, f32[49152,128]{1,0:T(8,128)} %bitcast.35, f32[1,128]{1,0:T(1,128)} %fusion.35.refs_0_), custom_call_target="tpu_custom_call" | custom-call | bytes 80000000 | tf_op jit(solution)/shard_map/outgoing/pallas_call | solution.py:559
  515.8 13.8 %all-to-all-done.2.refs_0_.came_ref = bf16[16,200,384]{2,1,0:T(8,128)(2,1)S(1)} async-done(((bf16[16,200,384]{2,1,0:T(8,128)(2,1)}), bf16[16,200,384]{2,1,0:T(8,128)(2,1)S(1)}, u32[]{:S(2)}, u32[]{:S(2)}) %all-to-all-start.2) | async-done | bytes 2457632 | tf_op jit(solution)/shard_map/all_to_all | solution.py:824
  537.3 20.9 %collective-permute-done.7 = f32[1,128]{1,0:T(1,128)S(1)} collective-permute-done((f32[1,128]{1,0:T(1,128)S(1)}, f32[1,128]{1,0:T(1,128)S(1)}, u32[]{:S(2)}, u32[]{:S(2)}) %collective-permute-start.7) | collective-permute-done | bytes 544 | tf_op jit(solution)/shard_map/ppermute | solution.py:679
  558.8 8.4 collective-permute-start.8
  567.2 50.4 %collective-permute-done.8 = f32[1,128]{1,0:T(1,128)S(1)} collective-permute-done((f32[1,128]{1,0:T(1,128)S(1)}, f32[1,128]{1,0:T(1,128)S(1)}, u32[]{:S(2)}, u32[]{:S(2)}) %collective-permute-start.8) | collective-permute-done | bytes 544 | tf_op jit(solution)/shard_map/ppermute | solution.py:679
  618.3 23.8 %collective-permute-done.9 = f32[1,128]{1,0:T(1,128)S(1)} collective-permute-done((f32[1,128]{1,0:T(1,128)S(1)}, f32[1,128]{1,0:T(1,128)S(1)}, u32[]{:S(2)}, u32[]{:S(2)}) %collective-permute-start.9) | collective-permute-done | bytes 544 | tf_op jit(solution)/shard_map/ppermute | solution.py:679
  642.6 30.1 %relation_sums.1.refs_0_ = f32[6400,128]{1,0:T(8,128)} custom-call(s32[8192]{0:T(1024)} %ids_ref.1, f32[3,16384,128]{2,1,0:T(8,128)} %get-tuple-element.65.grad, bf16[16,200,384]{2,1,0:T(8,128)(2,1)} %copy-done.1, f32[1,128]{1,0:T(1,128)} %copy-done.25), custom_call_target="tpu_custom_call" | custom-call | bytes 120000000 | tf_op jit(solution)/shard_map/relation_sums/pallas_call | solution.py:635
  677.6 27.8 %collect.4.refs_0_ = f32[15888,128]{1,0:T(8,128)} custom-call(s32[16]{0:T(128)} %convert_reduce_fusion.2.counts_ref, s32[32768]{0:T(1024)} %bitcast.46, bf16[16,200,384]{2,1,0:T(8,128)(2,1)} %copy-done.1, f32[6400,128]{1,0:T(8,128)} %relation_sums.1.refs_0_, f32[1,128]{1,0:T(1,128)} %copy-done.27), custom_call_target="tpu_custom_call" | custom-call | bytes 120000000 | tf_op jit(solution)/shard_map/collect/pallas_call | solution.py:605
  705.4 24.2 %outgoing.7 = bf16[16,200,640]{2,1,0:T(8,128)(2,1)} custom-call(s32[16]{0:T(128)} %convert_element_type.63.counts_ref, s32[32768]{0:T(1024)} %broadcast_minimum_fusion.place_ref, f32[49152,128]{1,0:T(8,128)} %bitcast.36, f32[15888,128]{1,0:T(8,128)} %collect.4.refs_0_, f32[3200,200]{1,0:T(8,128)} %bitcast.41, f32[1,128]{1,0:T(1,128)} %add.219.refs_2_), custom_call_target="tpu_custom_call" | custom-call | bytes 80000000 | tf_op jit(solution)/shard_map/outgoing/pallas_call | solution.py:559
  729.6 7.5 all-to-all-start.4
  737.9 50.2 %collect.5.refs_0_ = f32[15888,128]{1,0:T(8,128)} custom-call(s32[16]{0:T(128)} %convert_reduce_fusion.2.counts_ref, s32[32768]{0:T(1024)} %bitcast.47, bf16[16,200,768]{2,1,0:T(8,128)(2,1)} %all-to-all-done.1.came_ref, f32[15888,128]{1,0:T(8,128)} %collect.4.refs_0_), custom_call_target="tpu_custom_call" | custom-call | bytes 120000000 | tf_op jit(solution)/shard_map/collect/pallas_call | solution.py:605
  788.1 11.9 %outgoing.6 = bf16[16,200,256]{2,1,0:T(8,128)(2,1)} custom-call(s32[16]{0:T(128)} %convert_element_type.63.counts_ref, s32[32768]{0:T(1024)} %broadcast_minimum_fusion.place_ref, f32[49152,128]{1,0:T(8,128)} %bitcast.37, f32[15888,128]{1,0:T(8,128)} %collect.5.refs_0_, f32[3200,200]{1,0:T(8,128)} %bitcast.43, f32[1,128]{1,0:T(1,128)} %add.219.refs_2_), custom_call_target="tpu_custom_call" | custom-call | bytes 80000000 | tf_op jit(solution)/shard_map/outgoing/pallas_call | solution.py:559
  800.0 47.7 %all-to-all-done.4.came_ref = bf16[16,200,640]{2,1,0:T(8,128)(2,1)} async-done(((bf16[16,200,640]{2,1,0:T(8,128)(2,1)}), bf16[16,200,640]{2,1,0:T(8,128)(2,1)}, u32[]{:S(2)}, u32[]{:S(2)}) %all-to-all-start.4) | async-done | bytes 4096032 | tf_op jit(solution)/shard_map/all_to_all | solution.py:824
  855.2 29.4 %collect.6.refs_0_ = f32[15888,128]{1,0:T(8,128)} custom-call(s32[16]{0:T(128)} %convert_reduce_fusion.2.counts_ref, s32[32768]{0:T(1024)} %bitcast.48, bf16[16,200,640]{2,1,0:T(8,128)(2,1)} %all-to-all-done.4.came_ref, f32[15888,128]{1,0:T(8,128)} %collect.5.refs_0_, f32[200,200]{1,0:T(8,128)} %reduce-scatter.2.cloned.1.call-done.refs_1_), custom_call_target="tpu_custom_call" | custom-call | bytes 120000000 | tf_op jit(solution)/shard_map/collect/pallas_call | solution.py:605
  891.7 8.7 collect.7.total
  900.3 18.2 %update_entities.1 = (f32[200,7936]{1,0:T(8,128)}, f32[200,7936]{1,0:T(8,128)}, f32[200,7936]{1,0:T(8,128)}) custom-call(f32[200,7936]{1,0:T(8,128)} %weights_ref.1, f32[200,7936]{1,0:T(8,128)} %first_ref.1, f32[200,7936]{1,0:T(8,128)} %second_ref.1, f32[15888,128]{1,0:T(8,128)} %collect.7.total), custom_call_target="tpu_custom_call" | custom-call | bytes 60000000 | tf_op jit(solution)/shard_map/update_entities/pallas_call | solution.py:664
  (141 shorter events, 100.7 us)
Async XLA Ops:
  7.2 185.2 %all-gather.5.cloned.1.call-start = ((), (), s32[]{:S(2)}) async-start(), calls=%async_computation.7 | async-start | bytes 36765696 | tf_op jit(solution)/shard_map/all_gather | solution.py:729
  16.1 274.1 %all-gather.7.cloned.1.call-start = ((), (), s32[]{:S(2)}) async-start(), calls=%async_computation.8 | async-start | bytes 19427328 | tf_op jit(solution)/shard_map/all_gather | solution.py:729
  46.4 13.4 %all-to-all-start = ((s32[16,1,2048]{2,1,0:T(1,128)}), s32[16,1,2048]{2,1,0:T(1,128)S(1)}, u32[]{:S(2)}, u32[]{:S(2)}) async-start(s32[16,1,2048]{2,1,0:T(1,128)} %bitcast.9), calls=%async_computation | async-start | bytes 262144 | tf_op jit(solution)/shard_map/all_to_all | solution.py:732
  59.8 181.7 %copy-start.3 = (s32[16,1,2048]{2,1,0:T(1,128)}, s32[16,1,2048]{2,1,0:T(1,128)S(1)}, u32[]{:S(2)}) copy-start(s32[16,1,2048]{2,1,0:T(1,128)S(1)} %all-to-all-done) | copy-start | bytes 393220
  241.5 8.4 copy-start.17
  241.5 9.7 %copy-start.20 = (s32[3200]{0:T(1024)S(1)}, s32[3200]{0:T(1024)}, u32[]{:S(2)}) copy-start(s32[3200]{0:T(1024)} %param.19) | copy-start | bytes 38404
  241.5 10.5 %copy-start.16 = (s32[8192]{0:T(1024)S(1)}, s32[8192]{0:T(1024)}, u32[]{:S(2)}) copy-start(s32[8192]{0:T(1024)} %ids_ref.1) | copy-start | bytes 98308
  248.5 48.7 %collective-permute-start = (bf16[128,8192]{1,0:T(8,128)(2,1)}, bf16[128,8192]{1,0:T(8,128)(2,1)S(1)}, u32[]{:S(2)}, u32[]{:S(2)}) collective-permute-start(bf16[128,8192]{1,0:T(8,128)(2,1)} %get-tuple-element.38.refs_2_.refs_1_), channel_id=1, source_target_pairs={{0,1},{1,0},{2,3},{3,2},{4,5},{5,4},{6,7},{7,6},{8,9},{9,8},{10,11... | collective-permute-start | bytes 6291464 | tf_op jit(solution)/shard_map/ppermute | solution.py:743
  283.2 90.0 %collective-permute-start.1 = (bf16[128,8192]{1,0:T(8,128)(2,1)}, bf16[128,8192]{1,0:T(8,128)(2,1)}, u32[]{:S(2)}, u32[]{:S(2)}) collective-permute-start(bf16[128,8192]{1,0:T(8,128)(2,1)} %get-tuple-element.40.refs_0_), channel_id=1, source_target_pairs={{0,1},{1,0},{2,3},{3,2},{4,5},{5,4},{6,7},{7,6},{8,9},{9,8},{10,11... | collective-permute-start | bytes 6291464 | tf_op jit(solution)/shard_map/ppermute | solution.py:743
  351.8 15.5 %collective-permute-start.2 = (bf16[2,80,2048]{2,1,0:T(8,128)(2,1)}, bf16[2,80,2048]{2,1,0:T(8,128)(2,1)S(1)}, u32[]{:S(2)}, u32[]{:S(2)}) collective-permute-start(bf16[2,80,2048]{2,1,0:T(8,128)(2,1)} %get-tuple-element.44.refs_2_), channel_id=1, source_target_pairs={{0,1},{1,0},{2,3},{3,2},{4,5},{5,4},{6,7},{7,6},{8,9},{9,8},{10,11... | collective-permute-start | bytes 1966088 | tf_op jit(solution)/shard_map/ppermute | solution.py:743
  371.8 16.2 %collective-permute-start.3 = (bf16[2,80,2048]{2,1,0:T(8,128)(2,1)}, bf16[2,80,2048]{2,1,0:T(8,128)(2,1)S(1)}, u32[]{:S(2)}, u32[]{:S(2)}) collective-permute-start(bf16[2,80,2048]{2,1,0:T(8,128)(2,1)} %get-tuple-element.51.refs_2_), channel_id=1, source_target_pairs={{0,1},{1,0},{2,3},{3,2},{4,5},{5,4},{6,7},{7,6},{8,9},{9,8},{10,11... | collective-permute-start | bytes 1966088 | tf_op jit(solution)/shard_map/ppermute | solution.py:743
  392.5 15.5 %collective-permute-start.4 = (bf16[2,80,2048]{2,1,0:T(8,128)(2,1)}, bf16[2,80,2048]{2,1,0:T(8,128)(2,1)S(1)}, u32[]{:S(2)}, u32[]{:S(2)}) collective-permute-start(bf16[2,80,2048]{2,1,0:T(8,128)(2,1)} %get-tuple-element.56.refs_2_), channel_id=1, source_target_pairs={{0,1},{1,0},{2,3},{3,2},{4,5},{5,4},{6,7},{7,6},{8,9},{9,8},{10,11... | collective-permute-start | bytes 1966088 | tf_op jit(solution)/shard_map/ppermute | solution.py:743
  412.5 16.9 %collective-permute-start.5 = (bf16[2,80,2048]{2,1,0:T(8,128)(2,1)}, bf16[2,80,2048]{2,1,0:T(8,128)(2,1)S(1)}, u32[]{:S(2)}, u32[]{:S(2)}) collective-permute-start(bf16[2,80,2048]{2,1,0:T(8,128)(2,1)} %get-tuple-element.61.refs_2_), channel_id=1, source_target_pairs={{0,1},{1,0},{2,3},{3,2},{4,5},{5,4},{6,7},{7,6},{8,9},{9,8},{10,11... | collective-permute-start | bytes 1966088 | tf_op jit(solution)/shard_map/ppermute | solution.py:743
  468.9 6.7 copy-start.22
  468.9 6.7 copy-start.23
  468.9 60.7 %all-to-all-start.2 = ((bf16[16,200,384]{2,1,0:T(8,128)(2,1)}), bf16[16,200,384]{2,1,0:T(8,128)(2,1)S(1)}, u32[]{:S(2)}, u32[]{:S(2)}) async-start(bf16[16,200,384]{2,1,0:T(8,128)(2,1)} %outgoing.5), calls=%async_computation.2 | async-start | bytes 4915200 | tf_op jit(solution)/shard_map/all_to_all | solution.py:824
  476.8 1.2 collective-permute-start.6
  515.8 20.0 %copy-start.26 = (f32[1,128]{1,0:T(1,128)S(1)}, f32[1,128]{1,0:T(1,128)}, u32[]{:S(2)}) copy-start(f32[1,128]{1,0:T(1,128)} %fusion.35.refs_0_) | copy-start | bytes 1540
  515.8 101.8 %copy-start.4 = (s32[16,1,2048]{2,1,0:T(1,128)S(1)}, s32[16,1,2048]{2,1,0:T(1,128)}, u32[]{:S(2)}) copy-start(s32[16,1,2048]{2,1,0:T(1,128)} %copy-done.3) | copy-start | bytes 393220
  531.1 198.6 %all-to-all-start.1 = ((bf16[16,200,768]{2,1,0:T(8,128)(2,1)}), bf16[16,200,768]{2,1,0:T(8,128)(2,1)}, u32[]{:S(2)}, u32[]{:S(2)}) async-start(bf16[16,200,768]{2,1,0:T(8,128)(2,1)} %outgoing.4), calls=%async_computation.1 | async-start | bytes 9830400 | tf_op jit(solution)/shard_map/all_to_all | solution.py:824
  535.8 22.4 %collective-permute-start.7 = (f32[1,128]{1,0:T(1,128)S(1)}, f32[1,128]{1,0:T(1,128)S(1)}, u32[]{:S(2)}, u32[]{:S(2)}) collective-permute-start(f32[1,128]{1,0:T(1,128)S(1)} %copy-done.26), channel_id=1, source_target_pairs={{0,4},{2,6},{4,0},{6,2},{8,12},{10,14},{12,8},{14,10},{16,20},{18,... | collective-permute-start | bytes 1544 | tf_op jit(solution)/shard_map/ppermute | solution.py:679
  558.8 83.8 %copy-start.25 = (f32[1,128]{1,0:T(1,128)}, f32[1,128]{1,0:T(1,128)S(1)}, u32[]{:S(2)}) copy-start(f32[1,128]{1,0:T(1,128)S(1)} %fusion.36.refs_1_) | copy-start | bytes 1540
  558.8 58.8 %collective-permute-start.8 = (f32[1,128]{1,0:T(1,128)S(1)}, f32[1,128]{1,0:T(1,128)S(1)}, u32[]{:S(2)}, u32[]{:S(2)}) collective-permute-start(f32[1,128]{1,0:T(1,128)S(1)} %fusion.36.refs_1_), channel_id=1, source_target_pairs={{0,8},{2,10},{4,12},{6,14},{8,0},{10,2},{12,4},{14,6},{16,24},{18,... | collective-permute-start | bytes 1544 | tf_op jit(solution)/shard_map/ppermute | solution.py:679
  617.6 55.1 %copy-start.27 = (f32[1,128]{1,0:T(1,128)}, f32[1,128]{1,0:T(1,128)S(1)}, u32[]{:S(2)}) copy-start(f32[1,128]{1,0:T(1,128)S(1)} %add.218.refs_1_) | copy-start | bytes 1540
  617.6 24.5 %collective-permute-start.9 = (f32[1,128]{1,0:T(1,128)S(1)}, f32[1,128]{1,0:T(1,128)S(1)}, u32[]{:S(2)}, u32[]{:S(2)}) collective-permute-start(f32[1,128]{1,0:T(1,128)S(1)} %add.218.refs_1_), channel_id=1, source_target_pairs={{0,16},{2,18},{4,20},{6,22},{8,24},{10,26},{12,28},{14,30},{16,0},... | collective-permute-start | bytes 1544 | tf_op jit(solution)/shard_map/ppermute | solution.py:679
  729.6 118.0 %all-to-all-start.4 = ((bf16[16,200,640]{2,1,0:T(8,128)(2,1)}), bf16[16,200,640]{2,1,0:T(8,128)(2,1)}, u32[]{:S(2)}, u32[]{:S(2)}) async-start(bf16[16,200,640]{2,1,0:T(8,128)(2,1)} %outgoing.7), calls=%async_computation.4 | async-start | bytes 8192000 | tf_op jit(solution)/shard_map/all_to_all | solution.py:824
  737.2 116.1 %reduce-scatter.2.cloned.1.call-start = ((), (), s32[]{:S(2)}) async-start(), calls=%async_computation.6 | async-start | bytes 3481600 | tf_op jit(solution)/shard_map/reduce_scatter | solution.py:832
  788.1 64.7 %copy-start.24 = (f32[1,128]{1,0:T(1,128)S(1)}, f32[1,128]{1,0:T(1,128)}, u32[]{:S(2)}) copy-start(f32[1,128]{1,0:T(1,128)} %add.219.refs_2_) | copy-start | bytes 1540
  788.1 65.2 %copy-start.9 = (f32[200,200]{1,0:T(8,128)S(1)}, f32[200,200]{1,0:T(8,128)}, u32[]{:S(2)}) copy-start(f32[200,200]{1,0:T(8,128)} %param.23) | copy-start | bytes 480004
  788.1 65.2 %copy-start.11 = (f32[200,200]{1,0:T(8,128)S(1)}, f32[200,200]{1,0:T(8,128)}, u32[]{:S(2)}) copy-start(f32[200,200]{1,0:T(8,128)} %param.24) | copy-start | bytes 480004
  788.1 65.2 %copy-start.12 = (f32[200,200]{1,0:T(8,128)S(1)}, f32[200,200]{1,0:T(8,128)}, u32[]{:S(2)}) copy-start(f32[200,200]{1,0:T(8,128)} %param.25) | copy-start | bytes 480004
  847.7 42.8 %all-to-all-start.3 = ((bf16[16,200,256]{2,1,0:T(8,128)(2,1)}), bf16[16,200,256]{2,1,0:T(8,128)(2,1)S(1)}, u32[]{:S(2)}, u32[]{:S(2)}) async-start(bf16[16,200,256]{2,1,0:T(8,128)(2,1)} %outgoing.6), calls=%async_computation.3 | async-start | bytes 3276800 | tf_op jit(solution)/shard_map/all_to_all | solution.py:824
  (14 other events, 44.4 us)
Sparse Core Ops, SparseCore 0:
  16.2 176.1 all-gather.4
  194.0 96.1 all-gather.6
  742.4 95.0 reduce-scatter.1

commit v6 on v5

--- a/solution.py
+++ b/solution.py
@@ -19,7 +19,8 @@
 LANES = 128
 UNROLL = 8
 PARTS = 4
-HALVES = 4
+HALVES = 2
+EARLY = 96
 TURN = 512
 REL_PAD = 256
 TERMS = 3
@@ -241,24 +242,27 @@
     return jnp.sum(values * values, axis=0, keepdims=True)
 
 
-def negatives_kernel(neg_ref, low_ref, norm_ref):
+def negatives_kernel(neg_ref, early_ref, late_ref, norm_ref):
     neg_t = neg_ref[...].T
-    low_ref[...] = neg_t[: low_ref.shape[0]].astype(BF16)
+    early_ref[...] = neg_t[:EARLY].astype(BF16)
+    late_ref[...] = neg_t[EARLY:].astype(BF16)
     norm_ref[...] = column_sum(neg_t)
 
 
-def negatives(fetched, depth, blocks, block_len):
+def negatives(fetched, blocks, block_len):
     count = blocks * block_len
     return pl.pallas_call(
         negatives_kernel,
         out_shape=[
-            jax.ShapeDtypeStruct((depth, count), BF16),
+            jax.ShapeDtypeStruct((EARLY, count), BF16),
+            jax.ShapeDtypeStruct((LANES - EARLY, count), BF16),
             jax.ShapeDtypeStruct((1, count), F32),
         ],
         grid=(blocks,),
         in_specs=[pl.BlockSpec((block_len, LANES), lambda b: (2 * blocks + b, 0))],
         out_specs=[
-            pl.BlockSpec((depth, block_len), lambda b: (0, b)),
+            pl.BlockSpec((EARLY, block_len), lambda b: (0, b)),
+            pl.BlockSpec((LANES - EARLY, block_len), lambda b: (0, b)),
             pl.BlockSpec((1, block_len), lambda b: (0, b)),
         ],
         compiler_params=params(),
@@ -279,14 +283,18 @@
     return shifted_t, column_sum((shifted - tail).T) - column_sum(shifted_t)
 
 
-def edges_kernel(depth, head_ref, tail_ref, rel_ref, off_ref, tail_out, low_ref, bias_ref):
+def edges_kernel(
+    depth, head_ref, tail_ref, rel_ref, late_ref, off_ref, tail_out, low_ref, bias_ref
+):
     shifted_t, bias = edge_parts(depth, head_ref, tail_ref, rel_ref, off_ref, tail_out)
-    low_ref[...] = shifted_t[:depth].astype(BF16)
+    low_ref[:depth] = shifted_t[:depth].astype(BF16)
+    low_ref[depth:] = late_ref[...]
     bias_ref[...] = bias
 
 
-def edges(fetched, rel_rows, depth, blocks, block_len):
+def edges(fetched, rel_rows, late, depth, blocks, block_len):
     count = blocks * block_len
+    tall = depth + late.shape[0]
 
     def rows(at):
         return pl.BlockSpec((block_len, LANES), lambda b: (at * blocks + b, 0))
@@ -296,21 +304,22 @@
         out_shape=[
             jax.ShapeDtypeStruct((count, LANES), F32),
             jax.ShapeDtypeStruct((count, LANES), BF16),
-            jax.ShapeDtypeStruct((depth, count), BF16),
+            jax.ShapeDtypeStruct((tall, count), BF16),
             jax.ShapeDtypeStruct((1, count), F32),
         ],
         grid=(blocks,),
-        in_specs=[rows(0), rows(1), rows(0)],
+        in_specs=[rows(0), rows(1), rows(0)]
+        + [pl.BlockSpec((tall - depth, block_len), lambda b: (0, b))],
         out_specs=[
             rows(0),
             rows(0),
-            pl.BlockSpec((depth, block_len), lambda b: (0, b)),
+            pl.BlockSpec((tall, block_len), lambda b: (0, b)),
             pl.BlockSpec((1, block_len), lambda b: (0, b)),
         ],
         compiler_params=params(),
         cost_estimate=cost(0, 30e6),
         name="edges",
-    )(fetched, fetched, rel_rows)
+    )(fetched, fetched, rel_rows, late)
 
 
 def last_rows(depth):
@@ -388,15 +397,18 @@
         slot = lax.rem(me + (n_col - k), n_col)
         for m, (start, depth) in enumerate(slices):
             if m < n - 1:
-                shift, neg = given[k][2 * m][...], given[k][2 * m + 1][...]
+                early, late = given[k][2 * m : 2 * m + 2]
+                shift_scr[slot, start : start + depth, :] = 2.0 * late[:depth, :]
+                neg_scr[slot, start : start + EARLY, :] = early[...]
+                neg_scr[slot, start + EARLY : start + depth, :] = late[depth:, :]
             else:
                 pair = given[k][-1]
                 shift, neg = pair[0, :depth, :], pair[1, :depth, :]
                 for row in range(2):
                     terms = pair[row, last_rows(depth) : last_rows(depth) + 8, :].astype(F32)
                     sums_scr[slot, row : row + 1] = jnp.sum(terms, axis=0, keepdims=True)
-            shift_scr[slot, start : start + depth, :] = 2.0 * shift
-            neg_scr[slot, start : start + depth, :] = neg
+                shift_scr[slot, start : start + depth, :] = 2.0 * shift
+                neg_scr[slot, start : start + depth, :] = neg
     bias = jnp.sum(sums_scr[:, 0, :], axis=0, keepdims=True) + MARGIN
     neg_norm = jnp.sum(sums_scr[:, 1, :], axis=0, keepdims=True)
     row_bias[...] = jnp.broadcast_to(bias, (LANES, length)).T
@@ -674,11 +686,6 @@
     )(weights, first, second, total)
 
 
-def add_across(value, groups, step):
-    turn = [(g, g ^ step) for g in range(groups)]
-    return value + lax.ppermute(value, "edge", turn)
-
-
 def chunk_bounds(capacity):
     units = capacity // LANES
     sizes = [3, 6, 5, 2] if units == 16 else [units // 4] * 3 + [units - 3 * (units // 4)]
@@ -729,8 +736,6 @@
         dense.append(lax.all_gather(sent, "edge", axis=0, tiled=False))
 
     place_list, row_list, counts = owner_lists(all_ids, groups, capacity, ent_rows)
-    asked = lax.all_to_all(row_list, "edge", split_axis=0, concat_axis=0, tiled=True)
-    asked_counts = jnp.sum((asked < ent_rows).astype(jnp.int32), axis=1)
     safe_places = jnp.minimum(place_list, id_count - 1)
     place_flat, row_flat = place_list.reshape(-1), row_list.reshape(-1)
 
@@ -748,23 +753,23 @@
     tails = [[] for _ in range(HALVES)]
     biases, norms, first_sent, rel_rows = [], [], [], None
     for k, (start, depth) in enumerate(slices):
-        early = first_sent if k > 0 else [asked]
-        fetched = fetch(counts, place_flat, row_flat, dense[k], id_count, ent_rows, early)
+        sent = first_sent if k > 0 else []
+        fetched = fetch(counts, place_flat, row_flat, dense[k], id_count, ent_rows, sent)
         if k < n - 1:
-            neg_low, norm = negatives(fetched, depth, blocks, block_len)
-            neg_all = [neg_low] + from_others(neg_low)
+            early, late, norm = negatives(fetched, blocks, block_len)
+            early_all = [early] + from_others(early)
             if rel_rows is None:
-                rel_rows = relation_rows(rel_places, dense[0], rel_scale, slices, [neg_low])
-            off, tail, low, bias = edges(fetched, rel_rows[k], depth, blocks, block_len)
+                rel_rows = relation_rows(rel_places, dense[0], rel_scale, slices, [early])
+            off, tail, low, bias = edges(fetched, rel_rows[k], late, depth, blocks, block_len)
             low_all = [low] + from_others(low)
-            first_sent = neg_all[1:]
+            first_sent = early_all[1:]
             biases.append(bias)
             norms.append(norm)
             for half in range(HALVES):
                 offs[half].append(off)
                 tails[half].append(tail)
                 for col in range(n_col):
-                    given[half][col] += [low_all[col], neg_all[col]]
+                    given[half][col] += [early_all[col], low_all[col]]
             continue
         if rel_rows is None:
             rel_rows = relation_rows(rel_places, dense[0], rel_scale, slices, [])
@@ -779,12 +784,13 @@
             given[half][col].append(piece)
 
     grad, loss_tiles = None, []
-    finish(0, [])
     for half in range(HALVES):
-        after = []
-        if half + 1 < HALVES:
-            finish(half + 1, [given[half][-1][-1]] + loss_tiles[-1:])
-            after = offs[half + 1][-1:]
+        finish(half, offs[half - 1][-1:] if half > 0 else [])
+    row_list, _ = lax.optimization_barrier((row_list, offs[-1][-1]))
+    asked = lax.all_to_all(row_list, "edge", split_axis=0, concat_axis=0, tiled=True)
+    asked_counts = jnp.sum((asked < ent_rows).astype(jnp.int32), axis=1)
+    for half in range(HALVES):
+        after = [asked] if half == 0 else []
         grad, loss_tile = block_math(
             me,
             live_counts,
@@ -800,34 +806,26 @@
         loss_tiles.append(loss_tile)
     live = jnp.sum(jnp.minimum(live_counts, block_len)).astype(F32)
     loss_own = jnp.sum(functools.reduce(jnp.add, loss_tiles))
-    lane = jnp.arange(LANES, dtype=jnp.int32)[None, :]
+    lane = jnp.arange(LANES, dtype=jnp.int32)
     loss_row = jnp.where(lane == 0, loss_own, jnp.where(lane == 1, live, 0.0))
-    step = 1
-    loss_rows = []
-    while step < groups:
-        loss_row = add_across(loss_row, groups, step)
-        loss_rows.append(loss_row)
-        step *= 2
-
-    def loss_step(k):
-        return loss_rows[min(k, len(loss_rows) - 1)]
+    loss_all = lax.all_to_all(
+        jnp.broadcast_to(loss_row, (groups, 1, LANES)), "edge", split_axis=0, concat_axis=0, tiled=True
+    )
+    loss_pair = jnp.sum(loss_all[:, 0, :2], axis=0)
 
     flat = grad.reshape(n * id_count, LANES)
     bounds = chunk_bounds(capacity)
     chunks = len(bounds) - 1
     arrived, total, after = [], None, []
     for k in range(chunks):
-        after = after + [loss_step(0)] if k == 1 else after
         sent = outgoing(
             counts, safe_places, flat, slices, bounds[k], bounds[k + 1] - bounds[k], after
         )
         arrived.append(lax.all_to_all(sent, "edge", split_axis=0, concat_axis=0, tiled=True))
         after = []
         if k == 1:
-            rel_terms = relation_sums(
-                relation_ids, grad, n, rel_total, [arrived[0], loss_step(1)]
-            )
-            after = [rel_terms, loss_step(2)]
+            rel_terms = relation_sums(relation_ids, grad, n, rel_total, [arrived[0], loss_all])
+            after = [rel_terms]
             rel_terms = rel_terms.reshape(rel_total, n * LANES)[:, :width]
             relation_grad = lax.psum_scatter(rel_terms, "edge", scatter_dimension=0, tiled=True)
         if k == chunks - 1:
@@ -836,10 +834,9 @@
             total = collect(
                 asked_counts, asked, arrived[k - 1], total, slices, bounds[k - 1], ent_rows, after
             )
-            after = [total, rel_terms, loss_step(3)]
+            after = [total, rel_terms]
     k = chunks - 1
     total = collect(asked_counts, asked, arrived[k], total, slices, bounds[k], ent_rows, [])
-    loss_pair = loss_step(groups)[0, :2]
 
     new_entity, new_entity_first, new_entity_second = update_entities(
         entity_table, total, entity_first, entity_second, slices

time: 935 us -> 832 us (0.89)
  waiting for transfers between devices: 330 us -> 260 us
  starting transfers between devices: 46.4 us -> 34.7 us
  Pallas kernels: 471 us -> 461 us
    ppermute x4 -> x0, waiting for transfers between devices: 96 us -> none  [add_across(): return value + lax.ppermute(value, 'edge', turn)]
    all_to_all x4, waiting for transfers between devices: 67.4 us -> 93.5 us  [shards(): lax.all_to_all(sent, 'edge', split_axis=0, concat_axis=0, tiled=True)]
    all_gather x2, waiting for transfers between devices: 138 us -> 149 us  [shards(): dense.append(lax.all_gather(sent, 'edge', axis=0, tiled=False))]
    ppermute x4 -> x0, starting transfers between devices: 10.1 us -> none  [add_across(): return value + lax.ppermute(value, 'edge', turn)]
    ppermute x6 -> x4, waiting for transfers between devices: 21 us -> 12.6 us  [from_others(): return [lax.ppermute(array, 'col', turn) for turn in turns]]
    pallas_call x4 -> x2, Pallas kernels: 59.6 us -> 52.2 us  [block_math(): pl.pallas_call(functools.partial(block_kernel, slices, n_col, half), out_...]
  transfers between devices with their start and end apart: 18 -> 13, of which waited for: 12 -> 9; matrix products, arithmetic and copies ran while one was open for 5% -> 5% of each run, Pallas kernels for 43% -> 49%
where the time goes in v6:
time: 832 us; the launch traced here: 828 us
  Pallas kernels  461 us (55%)
  waiting for transfers between devices  260 us (31%)
  starting transfers between devices  34.7 us (4%)
  other arithmetic  30.5 us (4%)
  between operations  15.4 us (2%)
  local copies, waits for them, and re-layouts  14.9 us (2%)
  matrix products  12.3 us (1%)
    all_gather x2, waiting for transfers between devices, shards(): dense.append(lax.all_gather(sent, 'edge', axis=0, tiled=False))  149 us
    pallas_call x4, Pallas kernels, collect(): pl.pallas_call(functools.partial(collect_kernel, slices, capacity, begin,...  115 us
    pallas_call x2, Pallas kernels, fetch(): pl.pallas_call(functools.partial(fetch_kernel, capacity, moves, ent_rows)...  98.8 us
    pallas_call x4, Pallas kernels, outgoing(): pl.pallas_call(functools.partial(outgoing_kernel, slices, capacity, begin...  96.1 us
    all_to_all x4, waiting for transfers between devices, shards(): lax.all_to_all(sent, 'edge', split_axis=0, concat_axis=0, tiled=True)  93.5 us
    pallas_call x2, Pallas kernels, block_math(): pl.pallas_call(functools.partial(block_kernel, slices, n_col, half), out_...  52.2 us
    pallas_call x1, Pallas kernels, relation_sums(): pl.pallas_call(functools.partial(relation_sums_kernel, n), out_shape=jax....  30.1 us
    pallas_call x1, Pallas kernels, relation_rows(): pl.pallas_call(functools.partial(relation_rows_kernel, slices), out_shape...  20.4 us
  transfers between devices with their start and end apart: 13, of which 9 were waited for; matrix products, arithmetic and copies ran while one was open for 5% of the time, Pallas kernels for 49%

profile of v6, /device:TPU:16, one launch (start us, length us, event | category | flops | bytes accessed | tf_op | source)
XLA Modules:
  0.0 828.2 jit_solution(5600465066069076332)
XLA Ops:
  22.3 8.8 %broadcast_multiply_fusion = bf16[4,128,24576]{2,1,0:T(8,128)(2,1)} fusion(bf16[128,24576]{1,0:T(8,128)(2,1)S(1)} %fusion.2, bf16[4,24576]{1,0:T(4,128)(2,1)S(1)} %pad_maximum_fusion), kind=kLoop, calls=%fused_computation.2 | loop fusion | flops 12582912 | bytes 31653888 | tf_op jit(solution)/shard_map/mul | solution.py:84
  31.1 11.8 %fusion.8 = s32[256,512]{1,0:T(8,128)S(1)} fusion(bf16[512,24576]{1,0:T(8,128)(2,1)} %bitcast.41, s32[24576]{0:T(1024)S(1)} %get-tuple-element.66), kind=kOutput, calls=%fused_computation.16 | convolution fusion | flops 6448873472 | bytes 25788416 | tf_op jit(solution)/shard_map/dot_general | solution.py:85
  46.3 141.2 %all-gather.5.cloned.1.call-done = bf16[2048,8448]{1,0:T(8,128)(2,1)} async-done(((bf16[128,8448]{1,0:T(8,128)(2,1)}), bf16[2048,8448]{1,0:T(8,128)(2,1)}) %all-gather.5.cloned.1.call-update) | async-done | bytes 34603024 | tf_op jit(solution)/shard_map/all_gather | solution.py:736
  187.4 49.1 %fetch_rows.2.neg_ref.head_ref.tail_ref = f32[24584,128]{1,0:T(8,128)} custom-call(s32[16]{0:T(128)} %convert_element_type.63.counts_ref, s32[32768]{0:T(1024)} %bitcast.47, s32[32768]{0:T(1024)} %bitcast.50, bf16[16,128,8448]{2,1,0:T(8,128)(2,1)} %bitcast.35), custom_call_target="tpu_custom_call" | custom-call | bytes 170000000 | tf_op jit(solution)/shard_map/fetch_rows/pallas_call | solution.py:222
  236.6 6.8 negatives.1
  246.2 20.4 %relation_rows.1 = (f32[8192,128]{1,0:T(8,128)}, f32[8192,128]{1,0:T(8,128)}) custom-call(s32[8192]{0:T(1024)} %fusion.28.ids_ref, f32[16,256]{1,0:T(8,128)} %pad.14.scale_ref, bf16[16,128,8448]{2,1,0:T(8,128)(2,1)} %bitcast.36, bf16[16,128,8448]{2,1,0:T(8,128)(2,1)} %bitcast.37, bf16[96,8192]{1,0:T(8,128)(2,1)} %get-tuple-element.30.refs_2_.refs_0_), custom_call_target="tpu_custom_call" | custom-call | bytes 80000000 | tf_op jit(solution)/shard_map/relation_rows/pallas_call | solution.py:130
  266.6 10.6 %edges.1 = (f32[8192,128]{1,0:T(8,128)}, bf16[8192,128]{1,0:T(8,128)(2,1)}, bf16[160,8192]{1,0:T(8,128)(2,1)}, f32[1,8192]{1,0:T(1,128)}) custom-call(f32[24584,128]{1,0:T(8,128)} %fetch_rows.2.neg_ref.head_ref.tail_ref, f32[24584,128]{1,0:T(8,128)} %fetch_rows.2.neg_ref.head_ref.tail_ref, f32[8192,128]{1,0:T(8,128)} %get-tuple-element.31.rel_ref, ...), custom_call_target="tpu_custom_call" | custom-call | bytes 30000000 | tf_op jit(solution)/shard_map/edges/pallas_call | solution.py:302
  277.7 7.6 all-gather.7.cloned.1.call-done
  286.4 49.6 %fetch_rows.3.head_ref.tail_ref.neg_ref = f32[24584,128]{1,0:T(8,128)} custom-call(s32[16]{0:T(128)} %convert_element_type.63.counts_ref, s32[32768]{0:T(1024)} %bitcast.48, s32[32768]{0:T(1024)} %bitcast.51, bf16[16,72,7936]{2,1,0:T(8,128)(2,1)} %bitcast.42, bf16[96,8192]{1,0:T(8,128)(2,1)} %copy-done.3), custom_call_target="tpu_custom_call" | custom-call | bytes 170000000 | tf_op jit(solution)/shard_map/fetch_rows/pallas_call | solution.py:222
  336.1 6.4 last_slice.2
  344.0 6.4 last_slice.3
  351.7 5.2 all-to-all-start
  363.1 11.3 %collective-permute-done.2.refs_5_ = bf16[2,80,4096]{2,1,0:T(8,128)(2,1)} collective-permute-done((bf16[2,80,4096]{2,1,0:T(8,128)(2,1)}, bf16[2,80,4096]{2,1,0:T(8,128)(2,1)}, u32[]{:S(2)}, u32[]{:S(2)}) %collective-permute-start.2) | collective-permute-done | bytes 1310752 | tf_op jit(solution)/shard_map/ppermute | solution.py:748
  374.4 26.0 %block_math.2 = (f32[3,16384,128]{2,1,0:T(8,128)}, f32[8,128]{1,0:T(8,128)}) custom-call(s32[1]{0:T(128)} %bitcast.me_ref, s32[8]{0:T(128)} %live_ref.3, bf16[96,8192]{1,0:T(8,128)(2,1)} %get-tuple-element.30.refs_2_.refs_0_, bf16[160,8192]{1,0:T(8,128)(2,1)} %get-tuple-element.33.refs_1_, bf16[2,80,4096]{2,1,0:T(8,128)(2,1)} %get-tuple-element.37.refs_2_, ...), custom_call_target="tpu_custom_call" | custom-call | flops 6710886400 | bytes 120000000 | tf_op jit(solution)/shard_map/block_math/pallas_call | solution.py:508
  402.8 26.2 %block_math.3 = (f32[3,16384,128]{2,1,0:T(8,128)}, f32[8,128]{1,0:T(8,128)}) custom-call(s32[1]{0:T(128)} %bitcast.me_ref, s32[8]{0:T(128)} %live_ref.3, bf16[96,8192]{1,0:T(8,128)(2,1)} %get-tuple-element.30.refs_2_.refs_0_, bf16[160,8192]{1,0:T(8,128)(2,1)} %get-tuple-element.33.refs_1_, ...), custom_call_target="tpu_custom_call", output_to_operand_aliasing={{0}: (12, {})} | custom-call | flops 6710886400 | bytes 120000000 | tf_op jit(solution)/shard_map/block_math/pallas_call | solution.py:508
  431.5 5.1 all-to-all-start.1
  437.3 23.5 %outgoing.5 = bf16[16,200,384]{2,1,0:T(8,128)(2,1)} custom-call(s32[16]{0:T(128)} %convert_element_type.63.counts_ref, s32[32768]{0:T(1024)} %broadcast_minimum_fusion.place_ref, f32[49152,128]{1,0:T(8,128)} %bitcast.31), custom_call_target="tpu_custom_call" | custom-call | bytes 80000000 | tf_op jit(solution)/shard_map/outgoing/pallas_call | solution.py:571
  460.8 6.0 all-to-all-start.3
  466.8 36.6 %outgoing.4 = bf16[16,200,768]{2,1,0:T(8,128)(2,1)} custom-call(s32[16]{0:T(128)} %convert_element_type.63.counts_ref, s32[32768]{0:T(1024)} %broadcast_minimum_fusion.place_ref, f32[49152,128]{1,0:T(8,128)} %bitcast.32), custom_call_target="tpu_custom_call" | custom-call | bytes 80000000 | tf_op jit(solution)/shard_map/outgoing/pallas_call | solution.py:571
  503.4 18.8 %all-to-all-done.3.refs_0_.came_ref = bf16[16,200,384]{2,1,0:T(8,128)(2,1)S(1)} async-done(((bf16[16,200,384]{2,1,0:T(8,128)(2,1)}), bf16[16,200,384]{2,1,0:T(8,128)(2,1)S(1)}, u32[]{:S(2)}, u32[]{:S(2)}) %all-to-all-start.3) | async-done | bytes 2457632 | tf_op jit(solution)/shard_map/all_to_all | solution.py:824
  523.7 4.9 all-to-all-start.2
  529.4 30.1 %relation_sums.1.refs_0_ = f32[6400,128]{1,0:T(8,128)} custom-call(s32[8192]{0:T(1024)} %ids_ref.1, f32[3,16384,128]{2,1,0:T(8,128)} %get-tuple-element.49.grad, bf16[16,200,384]{2,1,0:T(8,128)(2,1)} %copy-done, f32[16,1,128]{2,1,0:T(1,128)} %copy-done.13), custom_call_target="tpu_custom_call" | custom-call | bytes 120000000 | tf_op jit(solution)/shard_map/relation_sums/pallas_call | solution.py:647
  564.4 27.8 %collect.4.refs_0_ = f32[15888,128]{1,0:T(8,128)} custom-call(s32[16]{0:T(128)} %convert_reduce_fusion.2.counts_ref, s32[32768]{0:T(1024)} %bitcast.43, bf16[16,200,384]{2,1,0:T(8,128)(2,1)} %copy-done, f32[6400,128]{1,0:T(8,128)} %relation_sums.1.refs_0_), custom_call_target="tpu_custom_call" | custom-call | bytes 120000000 | tf_op jit(solution)/shard_map/collect/pallas_call | solution.py:617
  592.2 24.2 %outgoing.7 = bf16[16,200,640]{2,1,0:T(8,128)(2,1)} custom-call(s32[16]{0:T(128)} %convert_element_type.63.counts_ref, s32[32768]{0:T(1024)} %broadcast_minimum_fusion.place_ref, f32[49152,128]{1,0:T(8,128)} %bitcast.33, f32[15888,128]{1,0:T(8,128)} %collect.4.refs_0_, f32[3200,200]{1,0:T(8,128)} %bitcast.38), custom_call_target="tpu_custom_call" | custom-call | bytes 80000000 | tf_op jit(solution)/shard_map/outgoing/pallas_call | solution.py:571
  616.4 20.4 %all-to-all-done.2.came_ref = bf16[16,200,768]{2,1,0:T(8,128)(2,1)} async-done(((bf16[16,200,768]{2,1,0:T(8,128)(2,1)}), bf16[16,200,768]{2,1,0:T(8,128)(2,1)}, u32[]{:S(2)}, u32[]{:S(2)}) %all-to-all-start.2) | async-done | bytes 4915232 | tf_op jit(solution)/shard_map/all_to_all | solution.py:824
  642.2 50.2 %collect.5.refs_0_ = f32[15888,128]{1,0:T(8,128)} custom-call(s32[16]{0:T(128)} %convert_reduce_fusion.2.counts_ref, s32[32768]{0:T(1024)} %bitcast.44, bf16[16,200,768]{2,1,0:T(8,128)(2,1)} %all-to-all-done.2.came_ref, f32[15888,128]{1,0:T(8,128)} %collect.4.refs_0_), custom_call_target="tpu_custom_call" | custom-call | bytes 120000000 | tf_op jit(solution)/shard_map/collect/pallas_call | solution.py:617
  692.4 11.8 %outgoing.6 = bf16[16,200,256]{2,1,0:T(8,128)(2,1)} custom-call(s32[16]{0:T(128)} %convert_element_type.63.counts_ref, s32[32768]{0:T(1024)} %broadcast_minimum_fusion.place_ref, f32[49152,128]{1,0:T(8,128)} %bitcast.34, f32[15888,128]{1,0:T(8,128)} %collect.5.refs_0_, f32[3200,200]{1,0:T(8,128)} %bitcast.40), custom_call_target="tpu_custom_call" | custom-call | bytes 80000000 | tf_op jit(solution)/shard_map/outgoing/pallas_call | solution.py:571
  704.2 47.8 %all-to-all-done.5.came_ref = bf16[16,200,640]{2,1,0:T(8,128)(2,1)} async-done(((bf16[16,200,640]{2,1,0:T(8,128)(2,1)}), bf16[16,200,640]{2,1,0:T(8,128)(2,1)}, u32[]{:S(2)}, u32[]{:S(2)}) %all-to-all-start.5) | async-done | bytes 4096032 | tf_op jit(solution)/shard_map/all_to_all | solution.py:824
  759.1 28.9 %collect.6.refs_0_ = f32[15888,128]{1,0:T(8,128)} custom-call(s32[16]{0:T(128)} %convert_reduce_fusion.2.counts_ref, s32[32768]{0:T(1024)} %bitcast.45, bf16[16,200,640]{2,1,0:T(8,128)(2,1)} %all-to-all-done.5.came_ref, f32[15888,128]{1,0:T(8,128)} %collect.5.refs_0_, f32[200,200]{1,0:T(8,128)} %reduce-scatter.2.cloned.1.call-done.refs_1_), custom_call_target="tpu_custom_call" | custom-call | bytes 120000000 | tf_op jit(solution)/shard_map/collect/pallas_call | solution.py:617
  788.0 6.5 all-to-all-done.4.came_ref
  795.7 7.8 collect.7.total
  803.5 18.2 %update_entities.1 = (f32[200,7936]{1,0:T(8,128)}, f32[200,7936]{1,0:T(8,128)}, f32[200,7936]{1,0:T(8,128)}) custom-call(f32[200,7936]{1,0:T(8,128)} %weights_ref.1, f32[200,7936]{1,0:T(8,128)} %first_ref.1, f32[200,7936]{1,0:T(8,128)} %second_ref.1, f32[15888,128]{1,0:T(8,128)} %collect.7.total), custom_call_target="tpu_custom_call" | custom-call | bytes 60000000 | tf_op jit(solution)/shard_map/update_entities/pallas_call | solution.py:676
  (108 shorter events, 56.7 us)
Async XLA Ops:
  7.2 180.3 %all-gather.5.cloned.1.call-start = ((), (), s32[]{:S(2)}) async-start(), calls=%async_computation.8 | async-start | bytes 36765696 | tf_op jit(solution)/shard_map/all_gather | solution.py:736
  11.7 2.7 copy-start.11
  11.7 2.8 copy-start.9
  11.7 2.8 copy-start.10
  13.2 272.0 %all-gather.7.cloned.1.call-start = ((), (), s32[]{:S(2)}) async-start(), calls=%async_computation.9 | async-start | bytes 19427328 | tf_op jit(solution)/shard_map/all_gather | solution.py:736
  31.1 12.0 %copy-start.15 = (f32[3200]{0:T(1024)S(1)}, f32[3200]{0:T(1024)}, u32[]{:S(2)}) copy-start(f32[3200]{0:T(1024)} %param.18) | copy-start | bytes 38404
  236.6 8.3 %copy-start.16 = (s32[3200]{0:T(1024)S(1)}, s32[3200]{0:T(1024)}, u32[]{:S(2)}) copy-start(s32[3200]{0:T(1024)} %param.19) | copy-start | bytes 38404
  236.6 9.0 %copy-start.12 = (s32[8192]{0:T(1024)S(1)}, s32[8192]{0:T(1024)}, u32[]{:S(2)}) copy-start(s32[8192]{0:T(1024)} %ids_ref.1) | copy-start | bytes 98308
  243.4 41.9 %collective-permute-start = (bf16[96,8192]{1,0:T(8,128)(2,1)}, bf16[96,8192]{1,0:T(8,128)(2,1)S(1)}, u32[]{:S(2)}, u32[]{:S(2)}) collective-permute-start(bf16[96,8192]{1,0:T(8,128)(2,1)} %get-tuple-element.30.refs_2_.refs_0_), channel_id=1, source_target_pairs={{0,1},{1,0},{2,3},{3,2},{4,5},{5,4},{6,7},{7,6},{8,9},{9,8},{10,11... | collective-permute-start | bytes 4718600 | tf_op jit(solution)/shard_map/ppermute | solution.py:748
  277.2 85.9 %collective-permute-start.1 = (bf16[160,8192]{1,0:T(8,128)(2,1)}, bf16[160,8192]{1,0:T(8,128)(2,1)}, u32[]{:S(2)}, u32[]{:S(2)}) collective-permute-start(bf16[160,8192]{1,0:T(8,128)(2,1)} %get-tuple-element.33.refs_1_), channel_id=1, source_target_pairs={{0,1},{1,0},{2,3},{3,2},{4,5},{5,4},{6,7},{7,6},{8,9},{9,8},{10,11... | collective-permute-start | bytes 7864328 | tf_op jit(solution)/shard_map/ppermute | solution.py:748
  285.3 1.2 copy-start.3
  342.5 31.9 %collective-permute-start.2 = (bf16[2,80,4096]{2,1,0:T(8,128)(2,1)}, bf16[2,80,4096]{2,1,0:T(8,128)(2,1)}, u32[]{:S(2)}, u32[]{:S(2)}) collective-permute-start(bf16[2,80,4096]{2,1,0:T(8,128)(2,1)} %get-tuple-element.37.refs_2_), channel_id=1, source_target_pairs={{0,1},{1,0},{2,3},{3,2},{4,5},{5,4},{6,7},{7,6},{8,9},{9,8},{10,11... | collective-permute-start | bytes 3932168 | tf_op jit(solution)/shard_map/ppermute | solution.py:748
  344.0 12.9 %copy-start.18 = (s32[8]{0:T(128)S(1)}, s32[8]{0:T(128)}, u32[]{:S(2)}) copy-start(s32[8]{0:T(128)} %live_ref.3) | copy-start | bytes 100
  350.4 51.3 %collective-permute-start.3 = (bf16[2,80,4096]{2,1,0:T(8,128)(2,1)}, bf16[2,80,4096]{2,1,0:T(8,128)(2,1)S(1)}, u32[]{:S(2)}, u32[]{:S(2)}) collective-permute-start(bf16[2,80,4096]{2,1,0:T(8,128)(2,1)} %get-tuple-element.45.refs_2_), channel_id=1, source_target_pairs={{0,1},{1,0},{2,3},{3,2},{4,5},{5,4},{6,7},{7,6},{8,9},{9,8},{10,11... | collective-permute-start | bytes 3932168 | tf_op jit(solution)/shard_map/ppermute | solution.py:748
  351.7 10.7 %all-to-all-start = ((s32[16,1,2048]{2,1,0:T(1,128)}), s32[16,1,2048]{2,1,0:T(1,128)S(1)}, u32[]{:S(2)}, u32[]{:S(2)}) async-start(s32[16,1,2048]{2,1,0:T(1,128)} %all_to_all.22), calls=%async_computation | async-start | bytes 262144 | tf_op jit(solution)/shard_map/all_to_all | solution.py:790
  362.4 166.2 %copy-start.2 = (s32[16,1,2048]{2,1,0:T(1,128)}, s32[16,1,2048]{2,1,0:T(1,128)S(1)}, u32[]{:S(2)}) copy-start(s32[16,1,2048]{2,1,0:T(1,128)S(1)} %all-to-all-done) | copy-start | bytes 393220
  401.7 1.1 copy-start.5
  402.8 26.2 %copy-start.17 = (f32[8,128]{1,0:T(8,128)S(1)}, f32[8,128]{1,0:T(8,128)}, u32[]{:S(2)}) copy-start(f32[8,128]{1,0:T(8,128)} %get-tuple-element.44) | copy-start | bytes 12292
  402.8 33.8 %copy-start.4 = (s32[256,1,128]{2,1,0:T(1,128)S(1)}, s32[256,1,128]{2,1,0:T(1,128)}, u32[]{:S(2)}) copy-start(s32[256,1,128]{2,1,0:T(1,128)} %get-tuple-element.65) | copy-start | bytes 393220
  431.5 29.3 %all-to-all-start.1 = ((f32[16,1,128]{2,1,0:T(1,128)}), f32[16,1,128]{2,1,0:T(1,128)S(1)}, u32[]{:S(2)}, u32[]{:S(2)}) async-start(f32[16,1,128]{2,1,0:T(1,128)} %broadcast_in_dim.47), calls=%async_computation.1 | async-start | bytes 16384 | tf_op jit(solution)/shard_map/all_to_all | solution.py:811
  460.8 42.6 %copy-start.13 = (f32[16,1,128]{2,1,0:T(1,128)}, f32[16,1,128]{2,1,0:T(1,128)S(1)}, u32[]{:S(2)}) copy-start(f32[16,1,128]{2,1,0:T(1,128)S(1)} %all-to-all-done.1.refs_1_) | copy-start | bytes 24580
  460.8 61.4 %all-to-all-start.3 = ((bf16[16,200,384]{2,1,0:T(8,128)(2,1)}), bf16[16,200,384]{2,1,0:T(8,128)(2,1)S(1)}, u32[]{:S(2)}, u32[]{:S(2)}) async-start(bf16[16,200,384]{2,1,0:T(8,128)(2,1)} %outgoing.5), calls=%async_computation.3 | async-start | bytes 4915200 | tf_op jit(solution)/shard_map/all_to_all | solution.py:824
  522.2 1.5 copy-start
  523.7 113.1 %all-to-all-start.2 = ((bf16[16,200,768]{2,1,0:T(8,128)(2,1)}), bf16[16,200,768]{2,1,0:T(8,128)(2,1)}, u32[]{:S(2)}, u32[]{:S(2)}) async-start(bf16[16,200,768]{2,1,0:T(8,128)(2,1)} %outgoing.4), calls=%async_computation.2 | async-start | bytes 9830400 | tf_op jit(solution)/shard_map/all_to_all | solution.py:824
  636.8 115.2 %all-to-all-start.5 = ((bf16[16,200,640]{2,1,0:T(8,128)(2,1)}), bf16[16,200,640]{2,1,0:T(8,128)(2,1)}, u32[]{:S(2)}, u32[]{:S(2)}) async-start(bf16[16,200,640]{2,1,0:T(8,128)(2,1)} %outgoing.7), calls=%async_computation.5 | async-start | bytes 8192000 | tf_op jit(solution)/shard_map/all_to_all | solution.py:824
  641.5 115.8 %reduce-scatter.2.cloned.1.call-start = ((), (), s32[]{:S(2)}) async-start(), calls=%async_computation.7 | async-start | bytes 3481600 | tf_op jit(solution)/shard_map/reduce_scatter | solution.py:830
  692.4 64.3 %copy-start.14 = (f32[16,1,128]{2,1,0:T(1,128)S(1)}, f32[16,1,128]{2,1,0:T(1,128)}, u32[]{:S(2)}) copy-start(f32[16,1,128]{2,1,0:T(1,128)} %copy-done.13) | copy-start | bytes 24580
  692.4 64.9 %copy-start.6 = (f32[200,200]{1,0:T(8,128)S(1)}, f32[200,200]{1,0:T(8,128)}, u32[]{:S(2)}) copy-start(f32[200,200]{1,0:T(8,128)} %param.23) | copy-start | bytes 480004
  692.4 64.9 %copy-start.7 = (f32[200,200]{1,0:T(8,128)S(1)}, f32[200,200]{1,0:T(8,128)}, u32[]{:S(2)}) copy-start(f32[200,200]{1,0:T(8,128)} %param.24) | copy-start | bytes 480004
  692.4 64.9 %copy-start.8 = (f32[200,200]{1,0:T(8,128)S(1)}, f32[200,200]{1,0:T(8,128)}, u32[]{:S(2)}) copy-start(f32[200,200]{1,0:T(8,128)} %param.25) | copy-start | bytes 480004
  752.0 42.5 %all-to-all-start.4 = ((bf16[16,200,256]{2,1,0:T(8,128)(2,1)}), bf16[16,200,256]{2,1,0:T(8,128)(2,1)S(1)}, u32[]{:S(2)}, u32[]{:S(2)}) async-start(bf16[16,200,256]{2,1,0:T(8,128)(2,1)} %outgoing.6), calls=%async_computation.4 | async-start | bytes 3276800 | tf_op jit(solution)/shard_map/all_to_all | solution.py:824
  794.5 1.2 copy-start.1
Sparse Core Ops, SparseCore 0:
  13.3 174.0 all-gather.4
  189.0 96.1 all-gather.6
  646.7 96.0 reduce-scatter.1

commit v7 on v6

--- a/solution.py
+++ b/solution.py
@@ -33,8 +33,8 @@
 VMEM = pltpu.VMEM
 
 
-def params():
-    return pltpu.CompilerParams(vmem_limit_bytes=60 << 20)
+def params(mebibytes=60):
+    return pltpu.CompilerParams(vmem_limit_bytes=mebibytes << 20)
 
 
 def cost(flops, moved):
@@ -137,7 +137,7 @@
         out_specs=[whole(VMEM)] * n,
         scratch_shapes=[pltpu.VMEM((LANES, REL_PAD), F32)]
         + [pltpu.VMEM((groups * REL_PAD, LANES), F32)] * n,
-        compiler_params=params(),
+        compiler_params=params(28),
         cost_estimate=cost(0, 80e6),
         name="relation_rows",
     )(places, scale, *[dense] * n, *after)
@@ -232,7 +232,7 @@
         + [whole(pl.ANY)] * len(after),
         out_specs=whole(VMEM),
         scratch_shapes=[pltpu.VMEM((ent_rows + 8, LANES), F32)] * 2,
-        compiler_params=params(),
+        compiler_params=params(32),
         cost_estimate=cost(0, 170e6),
         name="fetch_rows",
     )(counts, place_list, row_list, dense, *after)
@@ -265,7 +265,7 @@
             pl.BlockSpec((LANES - EARLY, block_len), lambda b: (0, b)),
             pl.BlockSpec((1, block_len), lambda b: (0, b)),
         ],
-        compiler_params=params(),
+        compiler_params=params(12),
         cost_estimate=cost(0, 10e6),
         name="negatives",
     )(fetched)
@@ -316,7 +316,7 @@
             pl.BlockSpec((tall, block_len), lambda b: (0, b)),
             pl.BlockSpec((1, block_len), lambda b: (0, b)),
         ],
-        compiler_params=params(),
+        compiler_params=params(16),
         cost_estimate=cost(0, 30e6),
         name="edges",
     )(fetched, fetched, rel_rows, late)
@@ -376,7 +376,7 @@
             pl.BlockSpec((block_len, LANES), lambda b: (b, 0)),
             pl.BlockSpec((2, tall, block_len), lambda b: (0, 0, b)),
         ],
-        compiler_params=params(),
+        compiler_params=params(16),
         cost_estimate=cost(0, 20e6),
         name="last_slice",
     )(fetched, fetched, fetched, rel_rows, *biases, *norms, *after)
@@ -530,7 +530,7 @@
             pltpu.VMEM((block_len, LANES), F32),
             pltpu.VMEM((block_len, LANES), F32),
         ],
-        compiler_params=params(),
+        compiler_params=params(30),
         cost_estimate=cost(part * 8 * block_len * block_len * width, 120e6),
         name="block_math",
     )(me, live_counts, *flat, *offs, *tails, *kept, *after)
@@ -574,7 +574,7 @@
         in_specs=[whole(SMEM)] * 2 + [whole(VMEM)] + [whole(pl.ANY)] * len(after),
         out_specs=whole(VMEM),
         scratch_shapes=[pltpu.VMEM((n * chunk, LANES), F32)],
-        compiler_params=params(),
+        compiler_params=params(40),
         cost_estimate=cost(0, 80e6),
         name="outgoing",
     )(counts, place_list.reshape(-1), grad, *after)
@@ -622,7 +622,7 @@
         + [whole(pl.ANY)] * len(after),
         out_specs=whole(VMEM),
         scratch_shapes=[pltpu.VMEM((n * chunk, LANES), F32)],
-        compiler_params=params(),
+        compiler_params=params(30),
         cost_estimate=cost(0, 120e6),
         name="collect",
     )(counts, row_list.reshape(-1), came, *given, *after)
@@ -651,7 +651,7 @@
         in_specs=[whole(SMEM), pl.BlockSpec((1, n * count, LANES), lambda i: (0, 0, 0))]
         + [whole(pl.ANY)] * len(after),
         out_specs=whole(VMEM),
-        compiler_params=params(),
+        compiler_params=params(30),
         cost_estimate=cost(0, 120e6),
         name="relation_sums",
     )(relation_ids, grad, *after)
@@ -680,7 +680,7 @@
         in_specs=[table] * 3 + [pl.BlockSpec((n * cols, LANES), lambda i: (i, 0))],
         out_specs=[table] * 3,
         scratch_shapes=[pltpu.VMEM((width, cols), F32)],
-        compiler_params=params(),
+        compiler_params=params(20),
         cost_estimate=cost(0, 60e6),
         name="update_entities",
     )(weights, first, second, total)

time: 832 us -> 828 us (level)
  local copies, waits for them, and re-layouts: 14.9 us -> 65.5 us
  Pallas kernels: 461 us -> 413 us
  waiting for transfers between devices: 260 us -> 249 us
    unnamed x44 -> x110, local copies, waits for them, and re-layouts: 5.86 us -> 57.2 us
    all_to_all x4, waiting for transfers between devices: 93.5 us -> 70.2 us  [shards(): lax.all_to_all(sent, 'edge', split_axis=0, concat_axis=0, tiled=True)]
    all_gather x2, waiting for transfers between devices: 149 us -> 162 us  [shards(): dense.append(lax.all_gather(sent, 'edge', axis=0, tiled=False))]
    pallas_call x2, Pallas kernels: 98.8 us -> 89.7 us  [fetch(): pl.pallas_call(functools.partial(fetch_kernel, capacity, moves, ent_rows)...]
  transfers between devices with their start and end apart: 13 -> 13, of which waited for: 9 -> 8; matrix products, arithmetic and copies ran while one was open for 5% -> 5% of each run, Pallas kernels for 49% -> 46%
where the time goes in v7:
time: 828 us; the launch traced here: 818 us
  Pallas kernels  413 us (50%)
  waiting for transfers between devices  249 us (30%)
  local copies, waits for them, and re-layouts  65.5 us (8%)
  starting transfers between devices  34.8 us (4%)
  other arithmetic  27.5 us (3%)
  between operations  15.8 us (2%)
  matrix products  12.3 us (1%)
    all_gather x2, waiting for transfers between devices, shards(): dense.append(lax.all_gather(sent, 'edge', axis=0, tiled=False))  162 us
    pallas_call x4, Pallas kernels, collect(): pl.pallas_call(functools.partial(collect_kernel, slices, capacity, begin,...  111 us
    pallas_call x4, Pallas kernels, outgoing(): pl.pallas_call(functools.partial(outgoing_kernel, slices, capacity, begin...  90.4 us
    pallas_call x2, Pallas kernels, fetch(): pl.pallas_call(functools.partial(fetch_kernel, capacity, moves, ent_rows)...  89.7 us
    all_to_all x4, waiting for transfers between devices, shards(): lax.all_to_all(sent, 'edge', split_axis=0, concat_axis=0, tiled=True)  70.2 us
    unnamed x110, local copies, waits for them, and re-layouts  57.2 us
    pallas_call x2, Pallas kernels, block_math(): pl.pallas_call(functools.partial(block_kernel, slices, n_col, half), out_...  51 us
    pallas_call x1, Pallas kernels, relation_sums(): pl.pallas_call(functools.partial(relation_sums_kernel, n), out_shape=jax....  31.1 us
  transfers between devices with their start and end apart: 13, of which 8 were waited for; matrix products, arithmetic and copies ran while one was open for 5% of the time, Pallas kernels for 46%

profile of v7, /device:TPU:16, one launch (start us, length us, event | category | flops | bytes accessed | tf_op | source)
XLA Modules:
  0.0 817.7 jit_solution(376923599753212792)
XLA Ops:
  21.8 8.7 %broadcast_multiply_fusion = bf16[4,128,24576]{2,1,0:T(8,128)(2,1)} fusion(bf16[128,24576]{1,0:T(8,128)(2,1)S(1)} %fusion.2, bf16[4,24576]{1,0:T(4,128)(2,1)S(1)} %pad_maximum_fusion), kind=kLoop, calls=%fused_computation.2 | loop fusion | flops 12582912 | bytes 31653888 | tf_op jit(solution)/shard_map/mul | solution.py:84
  30.5 11.8 %fusion.8 = s32[256,512]{1,0:T(8,128)S(1)} fusion(bf16[512,24576]{1,0:T(8,128)(2,1)} %bitcast.53, s32[24576]{0:T(1024)S(1)} %get-tuple-element.66), kind=kOutput, calls=%fused_computation.16 | convolution fusion | flops 6448873472 | bytes 25788416 | tf_op jit(solution)/shard_map/dot_general | solution.py:85
  45.9 141.5 %all-gather.5.cloned.1.call-done = bf16[2048,8448]{1,0:T(8,128)(2,1)} async-done(((bf16[128,8448]{1,0:T(8,128)(2,1)}), bf16[2048,8448]{1,0:T(8,128)(2,1)}) %all-gather.5.cloned.1.call-update) | async-done | bytes 34603024 | tf_op jit(solution)/shard_map/all_gather | solution.py:736
  187.4 44.5 %fetch_rows.2.neg_ref.head_ref.tail_ref = f32[24584,128]{1,0:T(8,128)S(1)} custom-call(s32[16]{0:T(128)S(1)} %convert_element_type.63.counts_ref, s32[32768]{0:T(1024)S(1)} %bitcast.40, s32[32768]{0:T(1024)S(1)} %bitcast.43, bf16[16,128,8448]{2,1,0:T(8,128)(2,1)} %bitcast.50), custom_call_target="tpu_custom_call" | custom-call | bytes 170000000 | tf_op jit(solution)/shard_map/fetch_rows/pallas_call | solution.py:222
  239.0 16.6 %relation_rows.1 = (f32[8192,128]{1,0:T(8,128)S(1)}, f32[8192,128]{1,0:T(8,128)S(1)}) custom-call(s32[8192]{0:T(1024)S(1)} %fusion.28.ids_ref, f32[16,256]{1,0:T(8,128)S(1)} %pad.14.scale_ref, bf16[16,128,8448]{2,1,0:T(8,128)(2,1)} %bitcast.51, bf16[16,128,8448]{2,1,0:T(8,128)(2,1)} %bitcast.52, bf16[96,8192]{1,0:T(8,128)(2,1)S(1)} %get-tuple-element.30.refs_2_.refs_0_), custom_call_target="tpu_custom_call" | custom-call | bytes 80000000 | tf_op jit(solution)/shard_map/relation_rows/pallas_call | solution.py:130
  255.7 5.0 edges.1
  264.6 20.6 %all-gather.7.cloned.1.call-done = bf16[1152,7936]{1,0:T(8,128)(2,1)} async-done(((bf16[72,7936]{1,0:T(8,128)(2,1)}), bf16[1152,7936]{1,0:T(8,128)(2,1)}) %all-gather.7.cloned.1.call-update) | async-done | bytes 18284560 | tf_op jit(solution)/shard_map/all_gather | solution.py:736
  285.3 45.2 %fetch_rows.3.head_ref.tail_ref.neg_ref = f32[24584,128]{1,0:T(8,128)S(1)} custom-call(s32[16]{0:T(128)S(1)} %convert_element_type.63.counts_ref, s32[32768]{0:T(1024)S(1)} %bitcast.41, s32[32768]{0:T(1024)S(1)} %bitcast.44, bf16[16,72,7936]{2,1,0:T(8,128)(2,1)} %bitcast.54, bf16[96,8192]{1,0:T(8,128)(2,1)S(1)} %collective-permute-done.refs_0_.refs_3_), custom_call_target="tpu_custom_call" | custom-call | bytes 170000000 | tf_op jit(solution)/shard_map/fetch_rows/pallas_call | solution.py:222
  343.4 5.1 all-to-all-start
  349.9 4.2 all-to-all-done
  354.1 11.4 %collective-permute-done.2.refs_5_ = bf16[2,80,4096]{2,1,0:T(8,128)(2,1)} collective-permute-done((bf16[2,80,4096]{2,1,0:T(8,128)(2,1)}, bf16[2,80,4096]{2,1,0:T(8,128)(2,1)}, u32[]{:S(2)}, u32[]{:S(2)}) %collective-permute-start.2) | collective-permute-done | bytes 1310752 | tf_op jit(solution)/shard_map/ppermute | solution.py:748
  372.1 25.5 %block_math.2 = (f32[3,16384,128]{2,1,0:T(8,128)}, f32[8,128]{1,0:T(8,128)S(1)}) custom-call(s32[1]{0:T(128)} %bitcast.me_ref, s32[8]{0:T(128)S(1)} %copy-done.36, bf16[96,8192]{1,0:T(8,128)(2,1)S(1)} %get-tuple-element.30.refs_2_.refs_0_, bf16[160,8192]{1,0:T(8,128)(2,1)} %get-tuple-element.33.refs_1_, bf16[2,80,4096]{2,1,0:T(8,128)(2,1)} %get-tuple-element.37.refs_2_, ...), custom_call_target="tpu_custom_call" | custom-call | flops 6710886400 | bytes 120000000 | tf_op jit(solution)/shard_map/block_math/pallas_call | solution.py:508
  397.6 25.5 %block_math.3 = (f32[3,16384,128]{2,1,0:T(8,128)}, f32[8,128]{1,0:T(8,128)S(1)}) custom-call(s32[1]{0:T(128)} %bitcast.me_ref, s32[8]{0:T(128)S(1)} %copy-done.36, bf16[96,8192]{1,0:T(8,128)(2,1)S(1)} %get-tuple-element.30.refs_2_.refs_0_, bf16[160,8192]{1,0:T(8,128)(2,1)} %get-tuple-element.33.refs_1_, ...), custom_call_target="tpu_custom_call", output_to_operand_aliasing={{0}: (12, {})} | custom-call | flops 6710886400 | bytes 120000000 | tf_op jit(solution)/shard_map/block_math/pallas_call | solution.py:508
  425.0 5.1 all-to-all-start.1
  430.1 22.0 %outgoing.5 = bf16[16,200,384]{2,1,0:T(8,128)(2,1)S(1)} custom-call(s32[16]{0:T(128)S(1)} %convert_element_type.63.counts_ref, s32[32768]{0:T(1024)S(1)} %broadcast_minimum_fusion.place_ref, f32[49152,128]{1,0:T(8,128)} %bitcast.46), custom_call_target="tpu_custom_call" | custom-call | bytes 80000000 | tf_op jit(solution)/shard_map/outgoing/pallas_call | solution.py:571
  453.6 6.0 all-to-all-start.3
  459.7 34.3 %outgoing.4 = bf16[16,200,768]{2,1,0:T(8,128)(2,1)S(1)} custom-call(s32[16]{0:T(128)S(1)} %convert_element_type.63.counts_ref, s32[32768]{0:T(1024)S(1)} %broadcast_minimum_fusion.place_ref, f32[49152,128]{1,0:T(8,128)} %bitcast.47), custom_call_target="tpu_custom_call" | custom-call | bytes 80000000 | tf_op jit(solution)/shard_map/outgoing/pallas_call | solution.py:571
  496.2 18.8 %all-to-all-done.3.refs_0_.came_ref = bf16[16,200,384]{2,1,0:T(8,128)(2,1)S(1)} async-done(((bf16[16,200,384]{2,1,0:T(8,128)(2,1)}), bf16[16,200,384]{2,1,0:T(8,128)(2,1)S(1)}, u32[]{:S(2)}, u32[]{:S(2)}) %all-to-all-start.3) | async-done | bytes 2457632 | tf_op jit(solution)/shard_map/all_to_all | solution.py:824
  515.0 4.9 all-to-all-start.2
  520.1 31.1 %relation_sums.1.refs_0_ = f32[6400,128]{1,0:T(8,128)S(1)} custom-call(s32[8192]{0:T(1024)S(1)} %copy-done.35, f32[3,16384,128]{2,1,0:T(8,128)} %get-tuple-element.49.grad, bf16[16,200,384]{2,1,0:T(8,128)(2,1)S(1)} %all-to-all-done.3.refs_0_.came_ref, f32[16,1,128]{2,1,0:T(1,128)S(1)} %all-to-all-done.1.refs_1_), custom_call_target="tpu_custom_call" | custom-call | bytes 120000000 | tf_op jit(solution)/shard_map/relation_sums/pallas_call | solution.py:647
  560.9 26.2 %collect.4.refs_0_ = f32[15888,128]{1,0:T(8,128)S(1)} custom-call(s32[16]{0:T(128)S(1)} %convert_reduce_fusion.2.counts_ref, s32[32768]{0:T(1024)S(1)} %bitcast.36, bf16[16,200,384]{2,1,0:T(8,128)(2,1)S(1)} %copy-done.13, f32[6400,128]{1,0:T(8,128)S(1)} %copy-done.10), custom_call_target="tpu_custom_call" | custom-call | bytes 120000000 | tf_op jit(solution)/shard_map/collect/pallas_call | solution.py:617
  590.3 22.2 %outgoing.7 = bf16[16,200,640]{2,1,0:T(8,128)(2,1)S(1)} custom-call(s32[16]{0:T(128)S(1)} %convert_element_type.63.counts_ref, s32[32768]{0:T(1024)S(1)} %broadcast_minimum_fusion.place_ref, f32[49152,128]{1,0:T(8,128)} %bitcast.48, f32[15888,128]{1,0:T(8,128)} %copy-done.3, f32[3200,200]{1,0:T(8,128)S(1)} %bitcast.33), custom_call_target="tpu_custom_call" | custom-call | bytes 80000000 | tf_op jit(solution)/shard_map/outgoing/pallas_call | solution.py:571
  614.5 13.6 %all-to-all-done.2.came_ref = bf16[16,200,768]{2,1,0:T(8,128)(2,1)} async-done(((bf16[16,200,768]{2,1,0:T(8,128)(2,1)}), bf16[16,200,768]{2,1,0:T(8,128)(2,1)}, u32[]{:S(2)}, u32[]{:S(2)}) %all-to-all-start.2) | async-done | bytes 4915232 | tf_op jit(solution)/shard_map/all_to_all | solution.py:824
  628.1 4.7 all-to-all-start.5
  636.8 53.8 %collect.5.refs_0_ = f32[15888,128]{1,0:T(8,128)S(1)} custom-call(s32[16]{0:T(128)S(1)} %convert_reduce_fusion.2.counts_ref, s32[32768]{0:T(1024)S(1)} %bitcast.37, bf16[16,200,768]{2,1,0:T(8,128)(2,1)} %all-to-all-done.2.came_ref, f32[15888,128]{1,0:T(8,128)S(1)} %copy-done.4), custom_call_target="tpu_custom_call" | custom-call | bytes 120000000 | tf_op jit(solution)/shard_map/collect/pallas_call | solution.py:617
  690.7 11.8 %outgoing.6 = bf16[16,200,256]{2,1,0:T(8,128)(2,1)} custom-call(s32[16]{0:T(128)S(1)} %convert_element_type.63.counts_ref, s32[32768]{0:T(1024)S(1)} %broadcast_minimum_fusion.place_ref, f32[49152,128]{1,0:T(8,128)} %bitcast.49, f32[15888,128]{1,0:T(8,128)S(1)} %collect.5.refs_0_, f32[3200,200]{1,0:T(8,128)S(1)} %bitcast.35), custom_call_target="tpu_custom_call" | custom-call | bytes 80000000 | tf_op jit(solution)/shard_map/outgoing/pallas_call | solution.py:571
  705.7 37.6 %all-to-all-done.5.came_ref = bf16[16,200,640]{2,1,0:T(8,128)(2,1)} async-done(((bf16[16,200,640]{2,1,0:T(8,128)(2,1)}), bf16[16,200,640]{2,1,0:T(8,128)(2,1)}, u32[]{:S(2)}, u32[]{:S(2)}) %all-to-all-start.5) | async-done | bytes 4096032 | tf_op jit(solution)/shard_map/all_to_all | solution.py:824
  743.3 4.7 all-to-all-start.4
  754.7 27.7 %collect.6.refs_0_ = f32[15888,128]{1,0:T(8,128)S(1)} custom-call(s32[16]{0:T(128)S(1)} %convert_reduce_fusion.2.counts_ref, s32[32768]{0:T(1024)S(1)} %bitcast.38, bf16[16,200,640]{2,1,0:T(8,128)(2,1)} %all-to-all-done.5.came_ref, f32[15888,128]{1,0:T(8,128)S(1)} %copy-done.2, f32[200,200]{1,0:T(8,128)S(1)} %copy-done.31), custom_call_target="tpu_custom_call" | custom-call | bytes 120000000 | tf_op jit(solution)/shard_map/collect/pallas_call | solution.py:617
  785.8 3.3 copy-done.8
  789.2 3.5 collect.7.total
  801.0 10.1 %update_entities.1 = (f32[200,7936]{1,0:T(8,128)}, f32[200,7936]{1,0:T(8,128)}, f32[200,7936]{1,0:T(8,128)}) custom-call(f32[200,7936]{1,0:T(8,128)S(1)} %copy-done.11, f32[200,7936]{1,0:T(8,128)S(1)} %copy-done.19, f32[200,7936]{1,0:T(8,128)S(1)} %copy-done.20, f32[15888,128]{1,0:T(8,128)S(1)} %collect.7.total), custom_call_target="tpu_custom_call" | custom-call | bytes 60000000 | tf_op jit(solution)/shard_map/update_entities/pallas_call | solution.py:676
  (175 shorter events, 94.6 us)
Async XLA Ops:
  7.2 180.3 %all-gather.5.cloned.1.call-start = ((), (), s32[]{:S(2)}) async-start(), calls=%async_computation.8 | async-start | bytes 36765696 | tf_op jit(solution)/shard_map/all_gather | solution.py:736
  13.2 272.0 %all-gather.7.cloned.1.call-start = ((), (), s32[]{:S(2)}) async-start(), calls=%async_computation.9 | async-start | bytes 19427328 | tf_op jit(solution)/shard_map/all_gather | solution.py:736
  30.5 12.0 %copy-start.46 = (f32[3200]{0:T(1024)S(1)}, f32[3200]{0:T(1024)}, u32[]{:S(2)}) copy-start(f32[3200]{0:T(1024)} %param.18) | copy-start | bytes 38404
  232.0 6.8 copy-start.47
  232.0 6.9 copy-start.34
  237.3 47.9 %collective-permute-start = (bf16[96,8192]{1,0:T(8,128)(2,1)S(1)}, bf16[96,8192]{1,0:T(8,128)(2,1)S(1)}, u32[]{:S(2)}, u32[]{:S(2)}) collective-permute-start(bf16[96,8192]{1,0:T(8,128)(2,1)S(1)} %get-tuple-element.30.refs_2_.refs_0_), channel_id=1, source_target_pairs={{0,1},{1,0},{2,3},{3,2},{4,5},{5,4},{6,7},{7,6},{8,9},{9,8},{10,11... | collective-permute-start | bytes 4718600 | tf_op jit(solution)/shard_map/ppermute | solution.py:748
  238.9 16.7 %slice-start = ((s8[12587008]{0:T(1024)(128)(4,1)}), s8[4194304]{0:T(1024)(128)(4,1)S(1)}, s32[]{:S(2)}) async-start(s8[12587008]{0:T(1024)(128)(4,1)} %bitcast.31), calls=%async_computation.10 | async-start | bytes 8388608
  239.0 16.7 %slice-start.1 = ((s8[12587008]{0:T(1024)(128)(4,1)}), s8[4194304]{0:T(1024)(128)(4,1)S(1)}, s32[]{:S(2)}) async-start(s8[12587008]{0:T(1024)(128)(4,1)} %bitcast.31), calls=%async_computation.11 | async-start | bytes 8388608
  239.0 16.7 %slice-start.2 = ((s8[12587008]{0:T(1024)(128)(4,1)}), s8[4194304]{0:T(1024)(128)(4,1)S(1)}, s32[]{:S(2)}) async-start(s8[12587008]{0:T(1024)(128)(4,1)} %bitcast.31), calls=%async_computation.12 | async-start | bytes 8388608
  239.0 16.7 %slice-start.3 = ((s8[12587008]{0:T(1024)(128)(4,1)}), s8[4096]{0:T(1024)(128)(4,1)S(1)}, s32[]{:S(2)}) async-start(s8[12587008]{0:T(1024)(128)(4,1)} %bitcast.31), calls=%async_computation.13 | async-start | bytes 8192
  239.0 16.7 %copy-start.33 = (bf16[32,8192]{1,0:T(8,128)(2,1)S(1)}, bf16[32,8192]{1,0:T(8,128)(2,1)}, u32[]{:S(2)}) copy-start(bf16[32,8192]{1,0:T(8,128)(2,1)} %copy-done.32) | copy-start | bytes 1572868
  264.0 90.1 %collective-permute-start.1 = (bf16[160,8192]{1,0:T(8,128)(2,1)}, bf16[160,8192]{1,0:T(8,128)(2,1)}, u32[]{:S(2)}, u32[]{:S(2)}) collective-permute-start(bf16[160,8192]{1,0:T(8,128)(2,1)} %get-tuple-element.33.refs_1_), channel_id=1, source_target_pairs={{0,1},{1,0},{2,3},{3,2},{4,5},{5,4},{6,7},{7,6},{8,9},{9,8},{10,11... | collective-permute-start | bytes 7864328 | tf_op jit(solution)/shard_map/ppermute | solution.py:748
  285.3 45.2 %copy-start.16 = (f32[8192,128]{1,0:T(8,128)S(1)}, f32[8192,128]{1,0:T(8,128)}, u32[]{:S(2)}) copy-start(f32[8192,128]{1,0:T(8,128)} %copy-done.15) | copy-start | bytes 12582916
  333.6 31.9 %collective-permute-start.2 = (bf16[2,80,4096]{2,1,0:T(8,128)(2,1)}, bf16[2,80,4096]{2,1,0:T(8,128)(2,1)}, u32[]{:S(2)}, u32[]{:S(2)}) collective-permute-start(bf16[2,80,4096]{2,1,0:T(8,128)(2,1)} %get-tuple-element.37.refs_2_), channel_id=1, source_target_pairs={{0,1},{1,0},{2,3},{3,2},{4,5},{5,4},{6,7},{7,6},{8,9},{9,8},{10,11... | collective-permute-start | bytes 3932168 | tf_op jit(solution)/shard_map/ppermute | solution.py:748
  335.1 6.0 copy-start.40
  335.1 13.5 %copy-start.36 = (s32[8]{0:T(128)S(1)}, s32[8]{0:T(128)}, u32[]{:S(2)}) copy-start(s32[8]{0:T(128)} %live_ref.3) | copy-start | bytes 100
  340.5 57.1 %collective-permute-start.3 = (bf16[2,80,4096]{2,1,0:T(8,128)(2,1)}, bf16[2,80,4096]{2,1,0:T(8,128)(2,1)}, u32[]{:S(2)}, u32[]{:S(2)}) collective-permute-start(bf16[2,80,4096]{2,1,0:T(8,128)(2,1)} %get-tuple-element.45.refs_2_), channel_id=1, source_target_pairs={{0,1},{1,0},{2,3},{3,2},{4,5},{5,4},{6,7},{7,6},{8,9},{9,8},{10,11... | collective-permute-start | bytes 3932168 | tf_op jit(solution)/shard_map/ppermute | solution.py:748
  343.4 10.7 %all-to-all-start = ((s32[16,1,2048]{2,1,0:T(1,128)}), s32[16,1,2048]{2,1,0:T(1,128)S(1)}, u32[]{:S(2)}, u32[]{:S(2)}) async-start(s32[16,1,2048]{2,1,0:T(1,128)} %all_to_all.22), calls=%async_computation | async-start | bytes 262144 | tf_op jit(solution)/shard_map/all_to_all | solution.py:790
  372.1 25.5 %copy-start.26 = (f32[4096,128]{1,0:T(8,128)S(1)}, f32[4096,128]{1,0:T(8,128)}, u32[]{:S(2)}) copy-start(f32[4096,128]{1,0:T(8,128)} %copy-done.25) | copy-start | bytes 6291460
  372.1 25.5 %copy-start.30 = (bf16[4096,128]{1,0:T(8,128)(2,1)S(1)}, bf16[4096,128]{1,0:T(8,128)(2,1)}, u32[]{:S(2)}) copy-start(bf16[4096,128]{1,0:T(8,128)(2,1)} %copy-done.29) | copy-start | bytes 3145732
  425.0 28.6 %all-to-all-start.1 = ((f32[16,1,128]{2,1,0:T(1,128)}), f32[16,1,128]{2,1,0:T(1,128)S(1)}, u32[]{:S(2)}, u32[]{:S(2)}) async-start(f32[16,1,128]{2,1,0:T(1,128)} %broadcast_in_dim.47), calls=%async_computation.1 | async-start | bytes 16384 | tf_op jit(solution)/shard_map/all_to_all | solution.py:811
  453.6 61.4 %all-to-all-start.3 = ((bf16[16,200,384]{2,1,0:T(8,128)(2,1)}), bf16[16,200,384]{2,1,0:T(8,128)(2,1)S(1)}, u32[]{:S(2)}, u32[]{:S(2)}) async-start(bf16[16,200,384]{2,1,0:T(8,128)(2,1)} %copy-done.18), calls=%async_computation.3 | async-start | bytes 4915200 | tf_op jit(solution)/shard_map/all_to_all | solution.py:824
  496.2 23.9 %copy-start.35 = (s32[8192]{0:T(1024)S(1)}, s32[8192]{0:T(1024)}, u32[]{:S(2)}) copy-start(s32[8192]{0:T(1024)} %ids_ref.1) | copy-start | bytes 98308
  515.0 113.1 %all-to-all-start.2 = ((bf16[16,200,768]{2,1,0:T(8,128)(2,1)}), bf16[16,200,768]{2,1,0:T(8,128)(2,1)}, u32[]{:S(2)}, u32[]{:S(2)}) async-start(bf16[16,200,768]{2,1,0:T(8,128)(2,1)} %copy-done.14), calls=%async_computation.2 | async-start | bytes 9830400 | tf_op jit(solution)/shard_map/all_to_all | solution.py:824
  556.1 34.2 %copy-start.5 = (f32[3200,256]{1,0:T(8,128)}, f32[3200,256]{1,0:T(8,128)S(1)}, u32[]{:S(2)}) copy-start(f32[3200,256]{1,0:T(8,128)S(1)} %reshape.726) | copy-start | bytes 9830404
  628.1 115.2 %all-to-all-start.5 = ((bf16[16,200,640]{2,1,0:T(8,128)(2,1)}), bf16[16,200,640]{2,1,0:T(8,128)(2,1)}, u32[]{:S(2)}, u32[]{:S(2)}) async-start(bf16[16,200,640]{2,1,0:T(8,128)(2,1)} %copy-done.17), calls=%async_computation.5 | async-start | bytes 8192000 | tf_op jit(solution)/shard_map/all_to_all | solution.py:824
  632.8 115.8 %reduce-scatter.2.cloned.1.call-start = ((), (), s32[]{:S(2)}) async-start(), calls=%async_computation.7 | async-start | bytes 3481600 | tf_op jit(solution)/shard_map/reduce_scatter | solution.py:830
  636.8 53.8 %copy-start.6 = (f32[3200,256]{1,0:T(8,128)S(1)}, f32[3200,256]{1,0:T(8,128)}, u32[]{:S(2)}) copy-start(f32[3200,256]{1,0:T(8,128)} %copy-done.5) | copy-start | bytes 9830404
  690.7 57.9 %copy-start.39 = (f32[200,200]{1,0:T(8,128)S(1)}, f32[200,200]{1,0:T(8,128)}, u32[]{:S(2)}) copy-start(f32[200,200]{1,0:T(8,128)} %param.23) | copy-start | bytes 480004
  690.7 57.9 %copy-start.41 = (f32[200,200]{1,0:T(8,128)S(1)}, f32[200,200]{1,0:T(8,128)}, u32[]{:S(2)}) copy-start(f32[200,200]{1,0:T(8,128)} %param.24) | copy-start | bytes 480004
  690.7 57.9 %copy-start.42 = (f32[200,200]{1,0:T(8,128)S(1)}, f32[200,200]{1,0:T(8,128)}, u32[]{:S(2)}) copy-start(f32[200,200]{1,0:T(8,128)} %param.25) | copy-start | bytes 480004
  743.3 42.5 %all-to-all-start.4 = ((bf16[16,200,256]{2,1,0:T(8,128)(2,1)}), bf16[16,200,256]{2,1,0:T(8,128)(2,1)S(1)}, u32[]{:S(2)}, u32[]{:S(2)}) async-start(bf16[16,200,256]{2,1,0:T(8,128)(2,1)} %outgoing.6), calls=%async_computation.4 | async-start | bytes 3276800 | tf_op jit(solution)/shard_map/all_to_all | solution.py:824
  (33 other events, 86.3 us)
Sparse Core Ops, SparseCore 0:
  13.3 174.0 all-gather.4
  189.0 96.1 all-gather.6
  638.0 95.8 reduce-scatter.1

commit v8 on v7

--- a/solution.py
+++ b/solution.py
@@ -39,6 +39,14 @@
 
 def cost(flops, moved):
     return pl.CostEstimate(flops=int(flops), bytes_accessed=int(moved), transcendentals=0)
+
+
+def corner(array):
+    return array[(0,) * (array.ndim - 2) + (slice(0, 8), slice(0, LANES))]
+
+
+def token_shape():
+    return jax.ShapeDtypeStruct((8, LANES), F32)
 
 
 def whole(space):
@@ -574,17 +582,22 @@
         in_specs=[whole(SMEM)] * 2 + [whole(VMEM)] + [whole(pl.ANY)] * len(after),
         out_specs=whole(VMEM),
         scratch_shapes=[pltpu.VMEM((n * chunk, LANES), F32)],
-        compiler_params=params(40),
+        compiler_params=params(34),
         cost_estimate=cost(0, 80e6),
         name="outgoing",
     )(counts, place_list.reshape(-1), grad, *after)
 
 
 def collect_kernel(slices, capacity, begin, first, counts_ref, row_ref, came_ref, *refs):
+    total, token, tile = refs[-3:]
+    total[...] = jnp.zeros_like(total) if first else refs[0][...]
+    token[...] = jnp.zeros_like(token)
+    add_rows(slices, capacity, begin, counts_ref, row_ref, came_ref, total, tile)
+
+
+def add_rows(slices, capacity, begin, counts_ref, row_ref, came_ref, total, tile):
     n = len(slices)
-    total, tile = refs[-2:]
     groups, width, chunk = came_ref.shape
-    total[...] = jnp.zeros_like(total) if first else refs[0][...]
 
     def source(group, carry):
         wanted = jnp.clip(counts_ref[group] - begin, 0, chunk)
@@ -616,21 +629,23 @@
     given = [] if total is None else [total]
     return pl.pallas_call(
         functools.partial(collect_kernel, slices, capacity, begin, total is None),
-        out_shape=jax.ShapeDtypeStruct((n * (ent_rows + 8), LANES), F32),
+        out_shape=[jax.ShapeDtypeStruct((n * (ent_rows + 8), LANES), F32), token_shape()],
+        input_output_aliases={3: 0} if given else {},
         in_specs=[whole(SMEM)] * 2
         + [whole(VMEM)] * (1 + len(given))
         + [whole(pl.ANY)] * len(after),
-        out_specs=whole(VMEM),
+        out_specs=[whole(VMEM)] * 2,
         scratch_shapes=[pltpu.VMEM((n * chunk, LANES), F32)],
-        compiler_params=params(30),
+        compiler_params=params(26),
         cost_estimate=cost(0, 120e6),
         name="collect",
     )(counts, row_list.reshape(-1), came, *given, *after)
 
 
 def relation_sums_kernel(n, ids_ref, grad, *refs):
-    total = refs[-1]
+    total, token = refs[-2:]
     total[...] = jnp.zeros_like(total)
+    token[...] = jnp.zeros_like(token)
 
     def body(step, carry):
         for lane in range(UNROLL):
@@ -646,44 +661,71 @@
     count = relation_ids.shape[0]
     return pl.pallas_call(
         functools.partial(relation_sums_kernel, n),
-        out_shape=jax.ShapeDtypeStruct((n * rel_total, LANES), F32),
+        out_shape=[jax.ShapeDtypeStruct((n * rel_total, LANES), F32), token_shape()],
         grid=(1,),
         in_specs=[whole(SMEM), pl.BlockSpec((1, n * count, LANES), lambda i: (0, 0, 0))]
         + [whole(pl.ANY)] * len(after),
-        out_specs=whole(VMEM),
+        out_specs=[whole(VMEM)] * 2,
         compiler_params=params(30),
         cost_estimate=cost(0, 120e6),
         name="relation_sums",
     )(relation_ids, grad, *after)
 
 
-def update_kernel(slices, weights_ref, first_ref, second_ref, total, *refs):
+def finish_kernel(
+    slices,
+    capacity,
+    begin,
+    counts_ref,
+    row_ref,
+    came_ref,
+    total_ref,
+    weights_ref,
+    first_ref,
+    second_ref,
+    *refs,
+):
     n = len(slices)
-    outs, scr = refs[:3], refs[3]
+    outs, (total, tile, gradient) = refs[:3], refs[3:]
     cols = weights_ref.shape[1]
+    step = pl.program_id(0)
+
+    @pl.when(step == 0)
+    def _():
+        total[: total_ref.shape[0], :] = total_ref[...]
+        add_rows(slices, capacity, begin, counts_ref, row_ref, came_ref, total, tile)
+
     for m, (start, depth) in enumerate(slices):
-        scr[start : start + depth, :] = total[pl.ds(m, cols, stride=n), :].T[:depth]
-    results = adamw_update(weights_ref[...], scr[...], first_ref[...], second_ref[...])
+        part = total[pl.ds(step * (n * cols) + m, cols, stride=n), :]
+        gradient[start : start + depth, :] = part.T[:depth]
+    results = adamw_update(weights_ref[...], gradient[...], first_ref[...], second_ref[...])
     for out, result in zip(outs, results):
         out[...] = result
 
 
-def update_entities(weights, total, first, second, slices):
+def finish_entities(counts, row_list, came, total, begin, weights, first, second, slices):
     width, ent_rows = weights.shape
+    capacity = row_list.shape[1]
     cols = 1024
+    steps = pl.cdiv(ent_rows, cols)
     n = len(slices)
     table = pl.BlockSpec((width, cols), lambda i: (0, i))
+    tall = max(n * cols * steps, total.shape[0])
     return pl.pallas_call(
-        functools.partial(update_kernel, slices),
+        functools.partial(finish_kernel, slices, capacity, begin),
         out_shape=[jax.ShapeDtypeStruct((width, ent_rows), F32)] * 3,
-        grid=(pl.cdiv(ent_rows, cols),),
-        in_specs=[table] * 3 + [pl.BlockSpec((n * cols, LANES), lambda i: (i, 0))],
+        grid=(steps,),
+        in_specs=[whole(SMEM)] * 2 + [whole(VMEM)] * 2 + [table] * 3,
         out_specs=[table] * 3,
-        scratch_shapes=[pltpu.VMEM((width, cols), F32)],
-        compiler_params=params(20),
+        scratch_shapes=[
+            pltpu.VMEM((tall, LANES), F32),
+            pltpu.VMEM((n * came.shape[2], LANES), F32),
+            pltpu.VMEM((width, cols), F32),
+        ],
+        compiler_params=params(56),
         cost_estimate=cost(0, 60e6),
-        name="update_entities",
-    )(weights, first, second, total)
+        name="finish_entities",
+    )(counts, row_list.reshape(-1), came, total, weights, first, second)
 
 
 def chunk_bounds(capacity):
@@ -759,10 +801,10 @@
             early, late, norm = negatives(fetched, blocks, block_len)
             early_all = [early] + from_others(early)
             if rel_rows is None:
-                rel_rows = relation_rows(rel_places, dense[0], rel_scale, slices, [early])
+                rel_rows = relation_rows(rel_places, dense[0], rel_scale, slices, [norm])
             off, tail, low, bias = edges(fetched, rel_rows[k], late, depth, blocks, block_len)
             low_all = [low] + from_others(low)
-            first_sent = early_all[1:]
+            first_sent = [corner(piece) for piece in early_all[1:]]
             biases.append(bias)
             norms.append(norm)
             for half in range(HALVES):
@@ -785,12 +827,12 @@
 
     grad, loss_tiles = None, []
     for half in range(HALVES):
-        finish(half, offs[half - 1][-1:] if half > 0 else [])
-    row_list, _ = lax.optimization_barrier((row_list, offs[-1][-1]))
+        finish(half, [corner(offs[half - 1][-1])] if half > 0 else [])
+    row_list, _ = lax.optimization_barrier((row_list, corner(offs[-1][-1])))
     asked = lax.all_to_all(row_list, "edge", split_axis=0, concat_axis=0, tiled=True)
     asked_counts = jnp.sum((asked < ent_rows).astype(jnp.int32), axis=1)
     for half in range(HALVES):
-        after = [asked] if half == 0 else []
+        after = [corner(asked)] if half == 0 else []
         grad, loss_tile = block_math(
             me,
             live_counts,
@@ -824,22 +866,29 @@
         arrived.append(lax.all_to_all(sent, "edge", split_axis=0, concat_axis=0, tiled=True))
         after = []
         if k == 1:
-            rel_terms = relation_sums(relation_ids, grad, n, rel_total, [arrived[0], loss_all])
-            after = [rel_terms]
+            before = [corner(arrived[0]), corner(loss_all)]
+            rel_terms, token = relation_sums(relation_ids, grad, n, rel_total, before)
+            after = [token]
             rel_terms = rel_terms.reshape(rel_total, n * LANES)[:, :width]
             relation_grad = lax.psum_scatter(rel_terms, "edge", scatter_dimension=0, tiled=True)
         if k == chunks - 1:
-            after = [relation_grad]
+            after = [corner(relation_grad)]
         if k > 0:
-            total = collect(
+            total, token = collect(
                 asked_counts, asked, arrived[k - 1], total, slices, bounds[k - 1], ent_rows, after
             )
-            after = [total, rel_terms]
+            after = [token, corner(rel_terms)]
     k = chunks - 1
-    total = collect(asked_counts, asked, arrived[k], total, slices, bounds[k], ent_rows, [])
-
-    new_entity, new_entity_first, new_entity_second = update_entities(
-        entity_table, total, entity_first, entity_second, slices
+    new_entity, new_entity_first, new_entity_second = finish_entities(
+        asked_counts,
+        asked,
+        arrived[k],
+        total,
+        bounds[k],
+        entity_table,
+        entity_first,
+        entity_second,
+        slices,
     )
     new_relation, new_relation_first, new_relation_second = adamw_update(
         relation_table, relation_grad, relation_first, relation_second

time: 828 us -> 822 us (level)
  local copies, waits for them, and re-layouts: 65.5 us -> 50.2 us
  Pallas kernels: 413 us -> 422 us
    unnamed x110 -> x90, local copies, waits for them, and re-layouts: 57.2 us -> 39.7 us
    ppermute x4, waiting for transfers between devices: 11.4 us -> 23.6 us  [from_others(): return [lax.ppermute(array, 'col', turn) for turn in turns]]
    all_gather x2, waiting for transfers between devices: 162 us -> 151 us  [shards(): dense.append(lax.all_gather(sent, 'edge', axis=0, tiled=False))]
    pallas_call x2, Pallas kernels: 41.2 us -> 51.6 us  [the longest x1 31.1 us: relation_sums(): pl.pallas_call(functools.partial(relation_sums_kernel, n), out_shape=[jax...]
    pallas_call x4 -> x3, Pallas kernels: 111 us -> 107 us  [collect(): pl.pallas_call(functools.partial(collect_kernel, slices, capacity, begin,...]
  transfers between devices with their start and end apart: 13 -> 13, of which waited for: 8 -> 9; matrix products, arithmetic and copies ran while one was open for 5% -> 5% of each run, Pallas kernels for 46% -> 46%
where the time goes in v8:
time: 822 us; the launch traced here: 815 us
  Pallas kernels  422 us (51%)
  waiting for transfers between devices  253 us (31%)
  local copies, waits for them, and re-layouts  50.2 us (6%)
  starting transfers between devices  35 us (4%)
  other arithmetic  27.5 us (3%)
  between operations  15.8 us (2%)
  matrix products  12.3 us (1%)
    all_gather x2, waiting for transfers between devices, shards(): dense.append(lax.all_gather(sent, 'edge', axis=0, tiled=False))  151 us
    pallas_call x3, Pallas kernels, collect(): pl.pallas_call(functools.partial(collect_kernel, slices, capacity, begin,...  107 us
    pallas_call x4, Pallas kernels, outgoing(): pl.pallas_call(functools.partial(outgoing_kernel, slices, capacity, begin...  90.4 us
    pallas_call x2, Pallas kernels, fetch(): pl.pallas_call(functools.partial(fetch_kernel, capacity, moves, ent_rows)...  89.6 us
    all_to_all x4, waiting for transfers between devices, shards(): lax.all_to_all(sent, 'edge', split_axis=0, concat_axis=0, tiled=True)  73.3 us
    pallas_call x2, Pallas kernels, block_math(): pl.pallas_call(functools.partial(block_kernel, slices, n_col, half), out_...  51 us
    unnamed x90, local copies, waits for them, and re-layouts  39.7 us
    pallas_call x1, Pallas kernels, relation_sums(): pl.pallas_call(functools.partial(relation_sums_kernel, n), out_shape=[jax...  31.1 us
  transfers between devices with their start and end apart: 13, of which 9 were waited for; matrix products, arithmetic and copies ran while one was open for 5% of the time, Pallas kernels for 46%

profile of v8, /device:TPU:16, one launch (start us, length us, event | category | flops | bytes accessed | tf_op | source)
XLA Modules:
  0.0 815.1 jit_solution(3164500854714215562)
XLA Ops:
  21.8 8.8 %broadcast_multiply_fusion = bf16[4,128,24576]{2,1,0:T(8,128)(2,1)} fusion(bf16[128,24576]{1,0:T(8,128)(2,1)S(1)} %fusion.2, bf16[4,24576]{1,0:T(4,128)(2,1)S(1)} %pad_maximum_fusion), kind=kLoop, calls=%fused_computation.2 | loop fusion | flops 12582912 | bytes 31653888 | tf_op jit(solution)/shard_map/mul | solution.py:92
  30.6 11.8 %fusion.8 = s32[256,512]{1,0:T(8,128)S(1)} fusion(bf16[512,24576]{1,0:T(8,128)(2,1)} %bitcast.53, s32[24576]{0:T(1024)S(1)} %get-tuple-element.78), kind=kOutput, calls=%fused_computation.16 | convolution fusion | flops 6448873472 | bytes 25788416 | tf_op jit(solution)/shard_map/dot_general | solution.py:93
  46.0 141.5 %all-gather.5.cloned.1.call-done = bf16[2048,8448]{1,0:T(8,128)(2,1)} async-done(((bf16[128,8448]{1,0:T(8,128)(2,1)}), bf16[2048,8448]{1,0:T(8,128)(2,1)}) %all-gather.5.cloned.1.call-update) | async-done | bytes 34603024 | tf_op jit(solution)/shard_map/all_gather | solution.py:778
  187.4 44.5 %fetch_rows.2.neg_ref.head_ref.tail_ref = f32[24584,128]{1,0:T(8,128)S(1)} custom-call(s32[16]{0:T(128)S(1)} %convert_element_type.63.counts_ref, s32[32768]{0:T(1024)S(1)} %bitcast.41, s32[32768]{0:T(1024)S(1)} %bitcast.44, bf16[16,128,8448]{2,1,0:T(8,128)(2,1)} %bitcast.50), custom_call_target="tpu_custom_call" | custom-call | bytes 170000000 | tf_op jit(solution)/shard_map/fetch_rows/pallas_call | solution.py:230
  232.0 5.9 negatives.1
  239.5 16.6 %relation_rows.1 = (f32[8192,128]{1,0:T(8,128)S(1)}, f32[8192,128]{1,0:T(8,128)S(1)}) custom-call(s32[8192]{0:T(1024)S(1)} %fusion.28.ids_ref, f32[16,256]{1,0:T(8,128)S(1)} %pad.14.scale_ref, bf16[16,128,8448]{2,1,0:T(8,128)(2,1)} %bitcast.51, bf16[16,128,8448]{2,1,0:T(8,128)(2,1)} %bitcast.52, f32[1,8192]{1,0:T(1,128)S(1)} %get-tuple-element.37.refs_2_.refs_1_), custom_call_target="tpu_custom_call" | custom-call | bytes 80000000 | tf_op jit(solution)/shard_map/relation_rows/pallas_call | solution.py:138
  263.3 12.1 %collective-permute-done.refs_3_ = bf16[96,8192]{1,0:T(8,128)(2,1)} collective-permute-done((bf16[96,8192]{1,0:T(8,128)(2,1)}, bf16[96,8192]{1,0:T(8,128)(2,1)}, u32[]{:S(2)}, u32[]{:S(2)}) %collective-permute-start) | collective-permute-done | bytes 1572896 | tf_op jit(solution)/shard_map/ppermute | solution.py:790
  276.0 9.2 %all-gather.7.cloned.1.call-done = bf16[1152,7936]{1,0:T(8,128)(2,1)} async-done(((bf16[72,7936]{1,0:T(8,128)(2,1)}), bf16[1152,7936]{1,0:T(8,128)(2,1)}) %all-gather.7.cloned.1.call-update) | async-done | bytes 18284560 | tf_op jit(solution)/shard_map/all_gather | solution.py:778
  285.3 45.2 %fetch_rows.3.head_ref.tail_ref.neg_ref = f32[24584,128]{1,0:T(8,128)S(1)} custom-call(s32[16]{0:T(128)S(1)} %convert_element_type.63.counts_ref, s32[32768]{0:T(1024)S(1)} %bitcast.42, s32[32768]{0:T(1024)S(1)} %bitcast.45, bf16[16,72,7936]{2,1,0:T(8,128)(2,1)} %bitcast.54, bf16[8,128]{1,0:T(8,128)(2,1)S(1)} %slice.79.refs_0_), custom_call_target="tpu_custom_call" | custom-call | bytes 170000000 | tf_op jit(solution)/shard_map/fetch_rows/pallas_call | solution.py:230
  344.2 5.2 all-to-all-start
  350.7 4.2 all-to-all-done
  355.0 11.5 %collective-permute-done.2.refs_5_ = bf16[2,80,4096]{2,1,0:T(8,128)(2,1)} collective-permute-done((bf16[2,80,4096]{2,1,0:T(8,128)(2,1)}, bf16[2,80,4096]{2,1,0:T(8,128)(2,1)}, u32[]{:S(2)}, u32[]{:S(2)}) %collective-permute-start.2) | collective-permute-done | bytes 1310752 | tf_op jit(solution)/shard_map/ppermute | solution.py:790
  373.1 25.5 %block_math.2 = (f32[3,16384,128]{2,1,0:T(8,128)}, f32[8,128]{1,0:T(8,128)S(1)}) custom-call(s32[1]{0:T(128)} %bitcast.me_ref, s32[8]{0:T(128)S(1)} %copy-done.23, bf16[96,8192]{1,0:T(8,128)(2,1)} %get-tuple-element.36.refs_0_, bf16[160,8192]{1,0:T(8,128)(2,1)S(1)} %get-tuple-element.40.refs_1_, bf16[2,80,4096]{2,1,0:T(8,128)(2,1)} %get-tuple-element.43.refs_2_, ...), custom_call_target="tpu_custom_call" | custom-call | flops 6710886400 | bytes 120000000 | tf_op jit(solution)/shard_map/block_math/pallas_call | solution.py:516
  398.6 25.5 %block_math.3 = (f32[3,16384,128]{2,1,0:T(8,128)}, f32[8,128]{1,0:T(8,128)S(1)}) custom-call(s32[1]{0:T(128)} %bitcast.me_ref, s32[8]{0:T(128)S(1)} %copy-done.23, bf16[96,8192]{1,0:T(8,128)(2,1)} %get-tuple-element.36.refs_0_, bf16[160,8192]{1,0:T(8,128)(2,1)S(1)} %get-tuple-element.40.refs_1_, ...), custom_call_target="tpu_custom_call", output_to_operand_aliasing={{0}: (12, {})} | custom-call | flops 6710886400 | bytes 120000000 | tf_op jit(solution)/shard_map/block_math/pallas_call | solution.py:516
  426.0 5.2 all-to-all-start.1
  431.2 22.0 %outgoing.5 = bf16[16,200,384]{2,1,0:T(8,128)(2,1)S(1)} custom-call(s32[16]{0:T(128)S(1)} %convert_element_type.63.counts_ref, s32[32768]{0:T(1024)S(1)} %broadcast_minimum_fusion.place_ref, f32[49152,128]{1,0:T(8,128)} %bitcast.46), custom_call_target="tpu_custom_call" | custom-call | bytes 80000000 | tf_op jit(solution)/shard_map/outgoing/pallas_call | solution.py:579
  454.7 6.0 all-to-all-start.3
  460.7 34.3 %outgoing.4 = bf16[16,200,768]{2,1,0:T(8,128)(2,1)S(1)} custom-call(s32[16]{0:T(128)S(1)} %convert_element_type.63.counts_ref, s32[32768]{0:T(1024)S(1)} %broadcast_minimum_fusion.place_ref, f32[49152,128]{1,0:T(8,128)} %bitcast.47), custom_call_target="tpu_custom_call" | custom-call | bytes 80000000 | tf_op jit(solution)/shard_map/outgoing/pallas_call | solution.py:579
  497.3 18.8 %all-to-all-done.3.came_ref = bf16[16,200,384]{2,1,0:T(8,128)(2,1)S(1)} async-done(((bf16[16,200,384]{2,1,0:T(8,128)(2,1)}), bf16[16,200,384]{2,1,0:T(8,128)(2,1)S(1)}, u32[]{:S(2)}, u32[]{:S(2)}) %all-to-all-start.3) | async-done | bytes 2457632 | tf_op jit(solution)/shard_map/all_to_all | solution.py:866
  516.1 4.9 all-to-all-start.2
  521.2 31.1 %relation_sums.1 = (f32[6400,128]{1,0:T(8,128)S(1)}, f32[8,128]{1,0:T(8,128)S(1)}) custom-call(s32[8192]{0:T(1024)S(1)} %copy-done.21, f32[3,16384,128]{2,1,0:T(8,128)} %get-tuple-element.54.grad, bf16[8,128]{1,0:T(8,128)(2,1)S(1)} %slice_bitcast_fusion.refs_0_, f32[1,128]{1,0:T(1,128)S(1)} %slice_bitcast_fusion.1.refs_1_), custom_call_target="tpu_custom_call" | custom-call | bytes 120000000 | tf_op jit(solution)/shard_map/relation_sums/pallas_call | solution.py:662
  554.0 4.9 reshape.726
  559.6 26.2 %collect.3 = (f32[15888,128]{1,0:T(8,128)S(1)}, f32[8,128]{1,0:T(8,128)S(1)}) custom-call(s32[16]{0:T(128)S(1)} %convert_reduce_fusion.2.counts_ref, s32[32768]{0:T(1024)S(1)} %bitcast.37, bf16[16,200,384]{2,1,0:T(8,128)(2,1)S(1)} %all-to-all-done.3.came_ref, f32[8,128]{1,0:T(8,128)S(1)} %get-tuple-element.55.refs_0_), custom_call_target="tpu_custom_call" | custom-call | bytes 120000000 | tf_op jit(solution)/shard_map/collect/pallas_call | solution.py:630
  588.9 22.2 %outgoing.7 = bf16[16,200,640]{2,1,0:T(8,128)(2,1)S(1)} custom-call(s32[16]{0:T(128)S(1)} %convert_element_type.63.counts_ref, s32[32768]{0:T(1024)S(1)} %broadcast_minimum_fusion.place_ref, f32[49152,128]{1,0:T(8,128)} %bitcast.48, f32[8,128]{1,0:T(8,128)S(1)} %get-tuple-element.59.refs_0_, f32[8,128]{1,0:T(8,128)S(1)} %slice.84.refs_1_), custom_call_target="tpu_custom_call" | custom-call | bytes 80000000 | tf_op jit(solution)/shard_map/outgoing/pallas_call | solution.py:579
  613.1 16.1 %all-to-all-done.2.came_ref = bf16[16,200,768]{2,1,0:T(8,128)(2,1)} async-done(((bf16[16,200,768]{2,1,0:T(8,128)(2,1)}), bf16[16,200,768]{2,1,0:T(8,128)(2,1)}, u32[]{:S(2)}, u32[]{:S(2)}) %all-to-all-start.2) | async-done | bytes 4915232 | tf_op jit(solution)/shard_map/all_to_all | solution.py:866
  629.2 4.7 all-to-all-start.5
  637.9 54.3 %collect.4 = (f32[15888,128]{1,0:T(8,128)S(1)}, f32[8,128]{1,0:T(8,128)S(1)}) custom-call(s32[16]{0:T(128)S(1)} %convert_reduce_fusion.2.counts_ref, s32[32768]{0:T(1024)S(1)} %bitcast.38, bf16[16,200,768]{2,1,0:T(8,128)(2,1)} %all-to-all-done.2.came_ref, f32[15888,128]{1,0:T(8,128)S(1)} %copy-done.2), custom_call_target="tpu_custom_call", output_to_operand_aliasing={{0}: (3, {})} | custom-call | bytes 120000000 | tf_op jit(solution)/shard_map/collect/pallas_call | solution.py:630
  695.4 11.8 %outgoing.6 = bf16[16,200,256]{2,1,0:T(8,128)(2,1)} custom-call(s32[16]{0:T(128)S(1)} %convert_element_type.63.counts_ref, s32[32768]{0:T(1024)S(1)} %broadcast_minimum_fusion.place_ref, f32[49152,128]{1,0:T(8,128)} %bitcast.49, f32[8,128]{1,0:T(8,128)S(1)} %get-tuple-element.57.refs_0_, f32[8,128]{1,0:T(8,128)S(1)} %slice.84.refs_1_), custom_call_target="tpu_custom_call" | custom-call | bytes 80000000 | tf_op jit(solution)/shard_map/outgoing/pallas_call | solution.py:579
  707.2 37.2 %all-to-all-done.5.came_ref = bf16[16,200,640]{2,1,0:T(8,128)(2,1)} async-done(((bf16[16,200,640]{2,1,0:T(8,128)(2,1)}), bf16[16,200,640]{2,1,0:T(8,128)(2,1)}, u32[]{:S(2)}, u32[]{:S(2)}) %all-to-all-start.5) | async-done | bytes 4096032 | tf_op jit(solution)/shard_map/all_to_all | solution.py:866
  744.4 4.7 all-to-all-start.4
  755.5 27.0 %collect.5 = (f32[15888,128]{1,0:T(8,128)S(1)}, f32[8,128]{1,0:T(8,128)}) custom-call(s32[16]{0:T(128)S(1)} %convert_reduce_fusion.2.counts_ref, s32[32768]{0:T(1024)S(1)} %bitcast.39, bf16[16,200,640]{2,1,0:T(8,128)(2,1)} %all-to-all-done.5.came_ref, f32[15888,128]{1,0:T(8,128)S(1)} %copy-done.4, ...), custom_call_target="tpu_custom_call", output_to_operand_aliasing={{0}: (3, {})} | custom-call | bytes 120000000 | tf_op jit(solution)/shard_map/collect/pallas_call | solution.py:630
  788.1 20.5 %finish_entities.1 = (f32[200,7936]{1,0:T(8,128)}, f32[200,7936]{1,0:T(8,128)}, f32[200,7936]{1,0:T(8,128)}) custom-call(s32[16]{0:T(128)} %copy-done.22, s32[32768]{0:T(1024)} %bitcast.40, bf16[16,200,256]{2,1,0:T(8,128)(2,1)} %copy-done.28, f32[15888,128]{1,0:T(8,128)} %copy-done.5, f32[200,7936]{1,0:T(8,128)} %weights_ref.1, f32[200,7936]{1,0:T(8,128)} %first_ref.1, ...), custom_call_target="tpu_custom_call" | custom-call | bytes 60000000 | tf_op jit(solution)/shard_map/finish_entities/pallas_call | solution.py:714
  (161 shorter events, 80.0 us)
Async XLA Ops:
  7.2 180.3 %all-gather.5.cloned.1.call-start = ((), (), s32[]{:S(2)}) async-start(), calls=%async_computation.8 | async-start | bytes 36765696 | tf_op jit(solution)/shard_map/all_gather | solution.py:778
  13.2 272.0 %all-gather.7.cloned.1.call-start = ((), (), s32[]{:S(2)}) async-start(), calls=%async_computation.9 | async-start | bytes 19427328 | tf_op jit(solution)/shard_map/all_gather | solution.py:778
  30.6 12.0 %copy-start.36 = (f32[3200]{0:T(1024)S(1)}, f32[3200]{0:T(1024)}, u32[]{:S(2)}) copy-start(f32[3200]{0:T(1024)} %param.18) | copy-start | bytes 38404
  231.9 5.9 copy-start
  231.9 7.4 copy-start.37
  231.9 7.5 copy-start.21
  237.8 37.5 %collective-permute-start = (bf16[96,8192]{1,0:T(8,128)(2,1)}, bf16[96,8192]{1,0:T(8,128)(2,1)}, u32[]{:S(2)}, u32[]{:S(2)}) collective-permute-start(bf16[96,8192]{1,0:T(8,128)(2,1)} %get-tuple-element.36.refs_0_), channel_id=1, source_target_pairs={{0,1},{1,0},{2,3},{3,2},{4,5},{5,4},{6,7},{7,6},{8,9},{9,8},{10,11... | collective-permute-start | bytes 4718600 | tf_op jit(solution)/shard_map/ppermute | solution.py:790
  239.5 16.6 %slice-start = ((s8[12587008]{0:T(1024)(128)(4,1)}), s8[4194304]{0:T(1024)(128)(4,1)S(1)}, s32[]{:S(2)}) async-start(s8[12587008]{0:T(1024)(128)(4,1)} %bitcast.35), calls=%async_computation.10 | async-start | bytes 8388608
  239.5 16.6 %slice-start.1 = ((s8[12587008]{0:T(1024)(128)(4,1)}), s8[4194304]{0:T(1024)(128)(4,1)S(1)}, s32[]{:S(2)}) async-start(s8[12587008]{0:T(1024)(128)(4,1)} %bitcast.35), calls=%async_computation.11 | async-start | bytes 8388608
  239.5 16.6 %slice-start.2 = ((s8[12587008]{0:T(1024)(128)(4,1)}), s8[4194304]{0:T(1024)(128)(4,1)S(1)}, s32[]{:S(2)}) async-start(s8[12587008]{0:T(1024)(128)(4,1)} %bitcast.35), calls=%async_computation.12 | async-start | bytes 8388608
  239.5 16.6 %slice-start.3 = ((s8[12587008]{0:T(1024)(128)(4,1)}), s8[4096]{0:T(1024)(128)(4,1)S(1)}, s32[]{:S(2)}) async-start(s8[12587008]{0:T(1024)(128)(4,1)} %bitcast.35), calls=%async_computation.13 | async-start | bytes 8192
  262.7 92.3 %collective-permute-start.1 = (bf16[160,8192]{1,0:T(8,128)(2,1)S(1)}, bf16[160,8192]{1,0:T(8,128)(2,1)}, u32[]{:S(2)}, u32[]{:S(2)}) collective-permute-start(bf16[160,8192]{1,0:T(8,128)(2,1)S(1)} %get-tuple-element.40.refs_1_), channel_id=1, source_target_pairs={{0,1},{1,0},{2,3},{3,2},{4,5},{5,4},{6,7},{7,6},{8,9},{9,8},{10,11... | collective-permute-start | bytes 7864328 | tf_op jit(solution)/shard_map/ppermute | solution.py:790
  285.3 45.2 %copy-start.8 = (f32[8192,128]{1,0:T(8,128)S(1)}, f32[8192,128]{1,0:T(8,128)}, u32[]{:S(2)}) copy-start(f32[8192,128]{1,0:T(8,128)} %copy-done.7) | copy-start | bytes 12582916
  334.6 31.9 %collective-permute-start.2 = (bf16[2,80,4096]{2,1,0:T(8,128)(2,1)}, bf16[2,80,4096]{2,1,0:T(8,128)(2,1)}, u32[]{:S(2)}, u32[]{:S(2)}) collective-permute-start(bf16[2,80,4096]{2,1,0:T(8,128)(2,1)} %get-tuple-element.43.refs_2_), channel_id=1, source_target_pairs={{0,1},{1,0},{2,3},{3,2},{4,5},{5,4},{6,7},{7,6},{8,9},{9,8},{10,11... | collective-permute-start | bytes 3932168 | tf_op jit(solution)/shard_map/ppermute | solution.py:790
  337.4 6.0 copy-start.30
  337.4 12.0 %copy-start.23 = (s32[8]{0:T(128)S(1)}, s32[8]{0:T(128)}, u32[]{:S(2)}) copy-start(s32[8]{0:T(128)} %live_ref.3) | copy-start | bytes 100
  342.8 55.7 %collective-permute-start.3 = (bf16[2,80,4096]{2,1,0:T(8,128)(2,1)}, bf16[2,80,4096]{2,1,0:T(8,128)(2,1)}, u32[]{:S(2)}, u32[]{:S(2)}) collective-permute-start(bf16[2,80,4096]{2,1,0:T(8,128)(2,1)} %get-tuple-element.49.refs_2_), channel_id=1, source_target_pairs={{0,1},{1,0},{2,3},{3,2},{4,5},{5,4},{6,7},{7,6},{8,9},{9,8},{10,11... | collective-permute-start | bytes 3932168 | tf_op jit(solution)/shard_map/ppermute | solution.py:790
  344.2 10.7 %all-to-all-start = ((s32[16,1,2048]{2,1,0:T(1,128)}), s32[16,1,2048]{2,1,0:T(1,128)S(1)}, u32[]{:S(2)}, u32[]{:S(2)}) async-start(s32[16,1,2048]{2,1,0:T(1,128)} %all_to_all.23), calls=%async_computation | async-start | bytes 262144 | tf_op jit(solution)/shard_map/all_to_all | solution.py:832
  354.9 397.3 %copy-start.11 = (s32[16,1,2048]{2,1,0:T(1,128)}, s32[16,1,2048]{2,1,0:T(1,128)S(1)}, u32[]{:S(2)}) copy-start(s32[16,1,2048]{2,1,0:T(1,128)S(1)} %all-to-all-done) | copy-start | bytes 393220
  373.1 25.5 %copy-start.18 = (f32[4096,128]{1,0:T(8,128)S(1)}, f32[4096,128]{1,0:T(8,128)}, u32[]{:S(2)}) copy-start(f32[4096,128]{1,0:T(8,128)} %copy-done.17) | copy-start | bytes 6291460
  373.1 25.5 %copy-start.20 = (bf16[4096,128]{1,0:T(8,128)(2,1)S(1)}, bf16[4096,128]{1,0:T(8,128)(2,1)}, u32[]{:S(2)}) copy-start(bf16[4096,128]{1,0:T(8,128)(2,1)} %copy-done.19) | copy-start | bytes 3145732
  426.0 28.7 %all-to-all-start.1 = ((f32[16,1,128]{2,1,0:T(1,128)}), f32[16,1,128]{2,1,0:T(1,128)S(1)}, u32[]{:S(2)}, u32[]{:S(2)}) async-start(f32[16,1,128]{2,1,0:T(1,128)} %broadcast_in_dim.47), calls=%async_computation.1 | async-start | bytes 16384 | tf_op jit(solution)/shard_map/all_to_all | solution.py:853
  454.7 61.4 %all-to-all-start.3 = ((bf16[16,200,384]{2,1,0:T(8,128)(2,1)}), bf16[16,200,384]{2,1,0:T(8,128)(2,1)S(1)}, u32[]{:S(2)}, u32[]{:S(2)}) async-start(bf16[16,200,384]{2,1,0:T(8,128)(2,1)} %copy-done.10), calls=%async_computation.3 | async-start | bytes 4915200 | tf_op jit(solution)/shard_map/all_to_all | solution.py:866
  516.1 113.1 %all-to-all-start.2 = ((bf16[16,200,768]{2,1,0:T(8,128)(2,1)}), bf16[16,200,768]{2,1,0:T(8,128)(2,1)}, u32[]{:S(2)}, u32[]{:S(2)}) async-start(bf16[16,200,768]{2,1,0:T(8,128)(2,1)} %copy-done.6), calls=%async_computation.2 | async-start | bytes 9830400 | tf_op jit(solution)/shard_map/all_to_all | solution.py:866
  521.2 231.0 %copy-start.22 = (s32[16]{0:T(128)}, s32[16]{0:T(128)S(1)}, u32[]{:S(2)}) copy-start(s32[16]{0:T(128)S(1)} %convert_reduce_fusion.2.counts_ref) | copy-start | bytes 196
  629.2 115.2 %all-to-all-start.5 = ((bf16[16,200,640]{2,1,0:T(8,128)(2,1)}), bf16[16,200,640]{2,1,0:T(8,128)(2,1)}, u32[]{:S(2)}, u32[]{:S(2)}) async-start(bf16[16,200,640]{2,1,0:T(8,128)(2,1)} %copy-done.9), calls=%async_computation.5 | async-start | bytes 8192000 | tf_op jit(solution)/shard_map/all_to_all | solution.py:866
  633.8 115.8 %reduce-scatter.2.cloned.1.call-start = ((), (), s32[]{:S(2)}) async-start(), calls=%async_computation.7 | async-start | bytes 3481600 | tf_op jit(solution)/shard_map/reduce_scatter | solution.py:873
  634.6 3.3 copy-start.2
  695.4 54.9 %copy-start.29 = (f32[200,200]{1,0:T(8,128)S(1)}, f32[200,200]{1,0:T(8,128)}, u32[]{:S(2)}) copy-start(f32[200,200]{1,0:T(8,128)} %param.23) | copy-start | bytes 480004
  695.4 54.9 %copy-start.31 = (f32[200,200]{1,0:T(8,128)S(1)}, f32[200,200]{1,0:T(8,128)}, u32[]{:S(2)}) copy-start(f32[200,200]{1,0:T(8,128)} %param.24) | copy-start | bytes 480004
  695.4 54.9 %copy-start.32 = (f32[200,200]{1,0:T(8,128)S(1)}, f32[200,200]{1,0:T(8,128)}, u32[]{:S(2)}) copy-start(f32[200,200]{1,0:T(8,128)} %param.25) | copy-start | bytes 480004
  744.4 42.5 %all-to-all-start.4 = ((bf16[16,200,256]{2,1,0:T(8,128)(2,1)}), bf16[16,200,256]{2,1,0:T(8,128)(2,1)S(1)}, u32[]{:S(2)}, u32[]{:S(2)}) async-start(bf16[16,200,256]{2,1,0:T(8,128)(2,1)} %outgoing.6), calls=%async_computation.4 | async-start | bytes 3276800 | tf_op jit(solution)/shard_map/all_to_all | solution.py:866
  (23 other events, 47.6 us)
Sparse Core Ops, SparseCore 0:
  13.3 174.0 all-gather.4
  189.0 96.1 all-gather.6
  639.1 95.8 reduce-scatter.1

commit v9 on v8

--- a/solution.py
+++ b/solution.py
@@ -19,8 +19,7 @@
 LANES = 128
 UNROLL = 8
 PARTS = 4
-HALVES = 2
-EARLY = 96
+EARLY = 48
 TURN = 512
 REL_PAD = 256
 TERMS = 3
@@ -62,6 +61,12 @@
         first_hat / (jnp.sqrt(second_hat) + EPSILON) + DECAY * weights
     )
     return (updated, new_first, new_second)
+
+
+def block_parts(blocks):
+    small = max(1, blocks // 4)
+    middle = (blocks - small) // 2
+    return [(0, small), (small, middle), (small + middle, blocks - small - middle)]
 
 
 def width_slices(width):
@@ -292,15 +297,16 @@
 
 
 def edges_kernel(
-    depth, head_ref, tail_ref, rel_ref, late_ref, off_ref, tail_out, low_ref, bias_ref
+    depth, head_ref, tail_ref, rel_ref, late_ref, *refs
 ):
+    off_ref, tail_out, low_ref, bias_ref = refs[-4:]
     shifted_t, bias = edge_parts(depth, head_ref, tail_ref, rel_ref, off_ref, tail_out)
     low_ref[:depth] = shifted_t[:depth].astype(BF16)
     low_ref[depth:] = late_ref[...]
     bias_ref[...] = bias
 
 
-def edges(fetched, rel_rows, late, depth, blocks, block_len):
+def edges(fetched, rel_rows, late, depth, blocks, block_len, after):
     count = blocks * block_len
     tall = depth + late.shape[0]
 
@@ -317,7 +323,8 @@
         ],
         grid=(blocks,),
         in_specs=[rows(0), rows(1), rows(0)]
-        + [pl.BlockSpec((tall - depth, block_len), lambda b: (0, b))],
+        + [pl.BlockSpec((tall - depth, block_len), lambda b: (0, b))]
+        + [whole(pl.ANY)] * len(after),
         out_specs=[
             rows(0),
             rows(0),
@@ -327,7 +334,7 @@
         compiler_params=params(16),
         cost_estimate=cost(0, 30e6),
         name="edges",
-    )(fetched, fetched, rel_rows, late)
+    )(fetched, fetched, rel_rows, late, *after)
 
 
 def last_rows(depth):
@@ -359,13 +366,13 @@
     pair_ref[1] = with_terms(neg_t, norm, depth)
 
 
-def last_slice(fetched, rel_rows, biases, norms, depth, blocks, block_len, half, after):
-    part = blocks // HALVES
-    count = part * block_len
+def last_slice(fetched, rel_rows, biases, norms, depth, blocks, block_len, part, after):
+    first, size = part
+    count = size * block_len
     tall = last_rows(depth) + 8
 
     def rows(at):
-        return pl.BlockSpec((block_len, LANES), lambda b: (at * blocks + half * part + b, 0))
+        return pl.BlockSpec((block_len, LANES), lambda b: (at * blocks + first + b, 0))
 
     return pl.pallas_call(
         functools.partial(last_kernel, depth, len(biases)),
@@ -374,9 +381,9 @@
             jax.ShapeDtypeStruct((count, LANES), BF16),
             jax.ShapeDtypeStruct((2, tall, count), BF16),
         ],
-        grid=(part,),
+        grid=(size,),
         in_specs=[rows(0), rows(1), rows(2), rows(0)]
-        + [pl.BlockSpec((1, block_len), lambda b: (0, half * part + b))]
+        + [pl.BlockSpec((1, block_len), lambda b: (0, first + b))]
         * (len(biases) + len(norms))
         + [whole(pl.ANY)] * len(after),
         out_specs=[
@@ -390,7 +397,7 @@
     )(fetched, fetched, fetched, rel_rows, *biases, *norms, *after)
 
 
-def block_kernel(slices, n_col, half, me_ref, live_ref, *refs):
+def block_kernel(slices, n_col, first_block, me_ref, live_ref, *refs):
     n = len(slices)
     per_col = 2 * n - 1
     given = [refs[k * per_col : (k + 1) * per_col] for k in range(n_col)]
@@ -421,7 +428,7 @@
     neg_norm = jnp.sum(sums_scr[:, 1, :], axis=0, keepdims=True)
     row_bias[...] = jnp.broadcast_to(bias, (LANES, length)).T
 
-    live = live_ref[half * pl.num_programs(0) + block]
+    live = live_ref[first_block + block]
     tile = 256
     small = 128
     lane_tiles = [slice(at, at + LANES) for at in range(0, length, LANES)]
@@ -495,10 +502,10 @@
         grad[2, pl.ds(m, length, stride=n), :depth] = moved[start : start + depth, :].T
 
 
-def block_math(me, live_counts, given, offs, tails, old, slices, block_len, half, after):
+def block_math(me, live_counts, given, offs, tails, old, slices, block_len, part, after):
     n, n_col = len(slices), len(given)
     blocks = live_counts.shape[0]
-    part = blocks // HALVES
+    begin, size = part
     width = sum(depth for _, depth in slices)
     flat = [piece for per_col in given for piece in per_col]
     kept = [] if old is None else [old]
@@ -506,26 +513,26 @@
     def columns(piece):
         if piece.ndim == 3:
             return pl.BlockSpec((2, piece.shape[1], block_len), lambda b: (0, 0, b))
-        return pl.BlockSpec((piece.shape[0], block_len), lambda b: (0, half * part + b))
+        return pl.BlockSpec((piece.shape[0], block_len), lambda b: (0, begin + b))
 
     def rows(array):
-        first = half * part if array.shape[0] > part * block_len else 0
+        first = begin if array.shape[0] > size * block_len else 0
         return pl.BlockSpec((block_len, LANES), lambda b: (first + b, 0))
 
     first_old = 2 + len(flat) + 2 * n
     return pl.pallas_call(
-        functools.partial(block_kernel, slices, n_col, half),
+        functools.partial(block_kernel, slices, n_col, begin),
         out_shape=[
             jax.ShapeDtypeStruct((3, n * blocks * block_len, LANES), F32),
             jax.ShapeDtypeStruct((8, LANES), F32),
         ],
-        grid=(part,),
+        grid=(size,),
         in_specs=[whole(SMEM)] * 2
         + [columns(piece) for piece in flat]
         + [rows(array) for array in offs + tails]
         + [whole(pl.ANY)] * len(kept + after),
         out_specs=[
-            pl.BlockSpec((3, n * block_len, LANES), lambda b: (0, half * part + b, 0)),
+            pl.BlockSpec((3, n * block_len, LANES), lambda b: (0, begin + b, 0)),
             pl.BlockSpec((8, LANES), lambda b: (0, 0)),
         ],
         input_output_aliases={first_old + k: k for k in range(len(kept))},
@@ -538,8 +545,8 @@
             pltpu.VMEM((block_len, LANES), F32),
             pltpu.VMEM((block_len, LANES), F32),
         ],
-        compiler_params=params(30),
-        cost_estimate=cost(part * 8 * block_len * block_len * width, 120e6),
+        compiler_params=params(60),
+        cost_estimate=cost(size * 8 * block_len * block_len * width, 120e6),
         name="block_math",
     )(me, live_counts, *flat, *offs, *tails, *kept, *after)
 
@@ -790,24 +797,26 @@
         return [lax.ppermute(array, "col", turn) for turn in turns]
 
     me = lax.axis_index("col").astype(jnp.int32).reshape(1)
-    given = [[[] for _ in range(n_col)] for _ in range(HALVES)]
-    offs = [[] for _ in range(HALVES)]
-    tails = [[] for _ in range(HALVES)]
-    biases, norms, first_sent, rel_rows = [], [], [], None
+    parts = block_parts(blocks)
+    given = [[[] for _ in range(n_col)] for _ in range(len(parts))]
+    offs = [[] for _ in range(len(parts))]
+    tails = [[] for _ in range(len(parts))]
+    biases, norms, rel_rows = [], [], None
     for k, (start, depth) in enumerate(slices):
-        sent = first_sent if k > 0 else []
-        fetched = fetch(counts, place_flat, row_flat, dense[k], id_count, ent_rows, sent)
+        fetched = fetch(counts, place_flat, row_flat, dense[k], id_count, ent_rows, [])
         if k < n - 1:
             early, late, norm = negatives(fetched, blocks, block_len)
             early_all = [early] + from_others(early)
+            first_sent = [corner(piece) for piece in early_all[1:]]
             if rel_rows is None:
                 rel_rows = relation_rows(rel_places, dense[0], rel_scale, slices, [norm])
-            off, tail, low, bias = edges(fetched, rel_rows[k], late, depth, blocks, block_len)
+            off, tail, low, bias = edges(
+                fetched, rel_rows[k], late, depth, blocks, block_len, first_sent
+            )
             low_all = [low] + from_others(low)
-            first_sent = [corner(piece) for piece in early_all[1:]]
             biases.append(bias)
             norms.append(norm)
-            for half in range(HALVES):
+            for half in range(len(parts)):
                 offs[half].append(off)
                 tails[half].append(tail)
                 for col in range(n_col):
@@ -818,7 +827,7 @@
 
     def finish(half, after):
         off, tail, pair = last_slice(
-            fetched, rel_rows[-1], biases, norms, slices[-1][1], blocks, block_len, half, after
+            fetched, rel_rows[-1], biases, norms, slices[-1][1], blocks, block_len, parts[half], after
         )
         offs[half].append(off)
         tails[half].append(tail)
@@ -826,13 +835,14 @@
             given[half][col].append(piece)
 
     grad, loss_tiles = None, []
-    for half in range(HALVES):
-        finish(half, [corner(offs[half - 1][-1])] if half > 0 else [])
-    row_list, _ = lax.optimization_barrier((row_list, corner(offs[-1][-1])))
+    finish(0, [])
+    finish(1, [corner(offs[0][-1])])
+    finish(2, [corner(piece) for piece in given[0][-1][-1:]])
+    row_list, _ = lax.optimization_barrier((row_list, corner(offs[1][-1])))
     asked = lax.all_to_all(row_list, "edge", split_axis=0, concat_axis=0, tiled=True)
     asked_counts = jnp.sum((asked < ent_rows).astype(jnp.int32), axis=1)
-    for half in range(HALVES):
-        after = [corner(asked)] if half == 0 else []
+    for half in range(len(parts)):
+        after = [corner(asked), corner(offs[2][-1])] if half == 0 else []
         grad, loss_tile = block_math(
             me,
             live_counts,
@@ -842,7 +852,7 @@
             grad,
             slices,
             block_len,
-            half,
+            parts[half],
             after,
         )
         loss_tiles.append(loss_tile)
@@ -869,8 +879,8 @@
             before = [corner(arrived[0]), corner(loss_all)]
             rel_terms, token = relation_sums(relation_ids, grad, n, rel_total, before)
             after = [token]
-            rel_terms = rel_terms.reshape(rel_total, n * LANES)[:, :width]
             relation_grad = lax.psum_scatter(rel_terms, "edge", scatter_dimension=0, tiled=True)
+            relation_grad = relation_grad.reshape(rel_own, n * LANES)[:, :width]
         if k == chunks - 1:
             after = [corner(relation_grad)]
         if k > 0:

time: 822 us -> 839 us (1.021)
  local copies, waits for them, and re-layouts: 50.2 us -> 60 us
    ppermute x4 -> x5, waiting for transfers between devices: 23.6 us -> 8.31 us  [from_others(): return [lax.ppermute(array, 'col', turn) for turn in turns]]
    unnamed x90 -> x122, local copies, waits for them, and re-layouts: 39.7 us -> 49.3 us
    all_gather x2, waiting for transfers between devices: 151 us -> 159 us  [shards(): dense.append(lax.all_gather(sent, 'edge', axis=0, tiled=False))]
    pallas_call x2 -> x3, Pallas kernels: 51 us -> 56 us  [block_math(): pl.pallas_call(functools.partial(block_kernel, slices, n_col, begin), out...]
  transfers between devices with their start and end apart: 13 -> 14, of which waited for: 9 -> 6; matrix products, arithmetic and copies ran while one was open for 5% -> 5% of each run, Pallas kernels for 46% -> 46%
where the time goes in v9:
time: 839 us; the launch traced here: 829 us
  Pallas kernels  427 us (51%)
  waiting for transfers between devices  248 us (30%)
  local copies, waits for them, and re-layouts  60 us (7%)
  starting transfers between devices  36.5 us (4%)
  other arithmetic  28.9 us (3%)
  between operations  16.4 us (2%)
  matrix products  12.3 us (1%)
    all_gather x2, waiting for transfers between devices, shards(): dense.append(lax.all_gather(sent, 'edge', axis=0, tiled=False))  159 us
    pallas_call x3, Pallas kernels, collect(): pl.pallas_call(functools.partial(collect_kernel, slices, capacity, begin,...  109 us
    pallas_call x4, Pallas kernels, outgoing(): pl.pallas_call(functools.partial(outgoing_kernel, slices, capacity, begin...  90.4 us
    pallas_call x2, Pallas kernels, fetch(): pl.pallas_call(functools.partial(fetch_kernel, capacity, moves, ent_rows)...  89.8 us
    all_to_all x4, waiting for transfers between devices, shards(): lax.all_to_all(sent, 'edge', split_axis=0, concat_axis=0, tiled=True)  79.5 us
    pallas_call x3, Pallas kernels, block_math(): pl.pallas_call(functools.partial(block_kernel, slices, n_col, begin), out...  56 us
    unnamed x122, local copies, waits for them, and re-layouts  49.3 us
    pallas_call x1, Pallas kernels, relation_sums(): pl.pallas_call(functools.partial(relation_sums_kernel, n), out_shape=[jax...  30.1 us
  transfers between devices with their start and end apart: 14, of which 6 were waited for; matrix products, arithmetic and copies ran while one was open for 5% of the time, Pallas kernels for 46%

profile of v9, /device:TPU:16, one launch (start us, length us, event | category | flops | bytes accessed | tf_op | source)
XLA Modules:
  0.0 829.4 jit_solution(2029614409887764670)
XLA Ops:
  24.6 8.8 %broadcast_multiply_fusion = bf16[4,128,24576]{2,1,0:T(8,128)(2,1)} fusion(bf16[128,24576]{1,0:T(8,128)(2,1)S(1)} %fusion.2, bf16[4,24576]{1,0:T(4,128)(2,1)S(1)} %pad_maximum_fusion), kind=kLoop, calls=%fused_computation.2 | loop fusion | flops 12582912 | bytes 31653888 | tf_op jit(solution)/shard_map/mul | solution.py:97
  33.4 11.8 %fusion.8 = s32[256,512]{1,0:T(8,128)S(1)} fusion(bf16[512,24576]{1,0:T(8,128)(2,1)} %bitcast.54, s32[24576]{0:T(1024)S(1)} %get-tuple-element.88), kind=kOutput, calls=%fused_computation.16 | convolution fusion | flops 6448873472 | bytes 25788416 | tf_op jit(solution)/shard_map/dot_general | solution.py:98
  47.5 142.8 %all-gather.5.cloned.1.call-done = bf16[2048,8448]{1,0:T(8,128)(2,1)} async-done(((bf16[128,8448]{1,0:T(8,128)(2,1)}), bf16[2048,8448]{1,0:T(8,128)(2,1)}) %all-gather.5.cloned.1.call-update) | async-done | bytes 34603024 | tf_op jit(solution)/shard_map/all_gather | solution.py:785
  190.3 44.5 %fetch_rows.2.neg_ref.head_ref.tail_ref = f32[24584,128]{1,0:T(8,128)S(1)} custom-call(s32[16]{0:T(128)S(1)} %convert_element_type.63.counts_ref, s32[32768]{0:T(1024)S(1)} %bitcast.42, s32[32768]{0:T(1024)S(1)} %bitcast.45, bf16[16,128,8448]{2,1,0:T(8,128)(2,1)} %bitcast.51), custom_call_target="tpu_custom_call" | custom-call | bytes 170000000 | tf_op jit(solution)/shard_map/fetch_rows/pallas_call | solution.py:235
  244.1 16.6 %relation_rows.1 = (f32[8192,128]{1,0:T(8,128)S(1)}, f32[8192,128]{1,0:T(8,128)S(1)}) custom-call(s32[8192]{0:T(1024)S(1)} %fusion.28.ids_ref, f32[16,256]{1,0:T(8,128)S(1)} %pad.14.scale_ref, bf16[16,128,8448]{2,1,0:T(8,128)(2,1)} %bitcast.52, bf16[16,128,8448]{2,1,0:T(8,128)(2,1)} %bitcast.53, f32[1,8192]{1,0:T(1,128)S(1)} %get-tuple-element.42.refs_2_.refs_1_), custom_call_target="tpu_custom_call" | custom-call | bytes 80000000 | tf_op jit(solution)/shard_map/relation_rows/pallas_call | solution.py:143
  271.4 16.7 %all-gather.7.cloned.1.call-done = bf16[1152,7936]{1,0:T(8,128)(2,1)} async-done(((bf16[72,7936]{1,0:T(8,128)(2,1)}), bf16[1152,7936]{1,0:T(8,128)(2,1)}) %all-gather.7.cloned.1.call-update) | async-done | bytes 18284560 | tf_op jit(solution)/shard_map/all_gather | solution.py:785
  289.0 45.2 %fetch_rows.3.head_ref.tail_ref.neg_ref = f32[24584,128]{1,0:T(8,128)S(1)} custom-call(s32[16]{0:T(128)S(1)} %convert_element_type.63.counts_ref, s32[32768]{0:T(1024)S(1)} %bitcast.43, s32[32768]{0:T(1024)S(1)} %bitcast.46, bf16[16,72,7936]{2,1,0:T(8,128)(2,1)} %bitcast.55), custom_call_target="tpu_custom_call" | custom-call | bytes 170000000 | tf_op jit(solution)/shard_map/fetch_rows/pallas_call | solution.py:235
  347.9 5.4 all-to-all-start
  353.3 8.3 %collective-permute-done.2.refs_5_ = bf16[2,80,2048]{2,1,0:T(8,128)(2,1)} collective-permute-done((bf16[2,80,2048]{2,1,0:T(8,128)(2,1)}, bf16[2,80,2048]{2,1,0:T(8,128)(2,1)}, u32[]{:S(2)}, u32[]{:S(2)}) %collective-permute-start.2) | collective-permute-done | bytes 655392 | tf_op jit(solution)/shard_map/ppermute | solution.py:797
  362.3 4.6 copy-done.1
  378.9 14.8 %block_math.3 = (f32[3,16384,128]{2,1,0:T(8,128)}, f32[8,128]{1,0:T(8,128)}) custom-call(s32[1]{0:T(128)} %bitcast.me_ref, s32[8]{0:T(128)} %live_ref.5, bf16[48,8192]{1,0:T(8,128)(2,1)} %copy-done.17, bf16[208,8192]{1,0:T(8,128)(2,1)} %copy-done.12, bf16[2,80,2048]{2,1,0:T(8,128)(2,1)} %get-tuple-element.48.refs_2_, bf16[48,8192]{1,0:T(8,128)(2,1)} %copy-done.40, ...), custom_call_target="tpu_custom_call" | custom-call | flops 3355443200 | bytes 120000000 | tf_op jit(solution)/shard_map/block_math/pallas_call | solution.py:523
  393.7 20.4 %block_math.4 = (f32[3,16384,128]{2,1,0:T(8,128)}, f32[8,128]{1,0:T(8,128)}) custom-call(s32[1]{0:T(128)} %bitcast.me_ref, s32[8]{0:T(128)} %live_ref.5, bf16[48,8192]{1,0:T(8,128)(2,1)} %copy-done.17, bf16[208,8192]{1,0:T(8,128)(2,1)} %copy-done.12, bf16[2,80,3072]{2,1,0:T(8,128)(2,1)} %get-tuple-element.55.refs_2_, ...), custom_call_target="tpu_custom_call", output_to_operand_aliasing={{0}: (12, {})} | custom-call | flops 5033164800 | bytes 120000000 | tf_op jit(solution)/shard_map/block_math/pallas_call | solution.py:523
  414.2 20.8 %block_math.5 = (f32[3,16384,128]{2,1,0:T(8,128)}, f32[8,128]{1,0:T(8,128)}) custom-call(s32[1]{0:T(128)} %bitcast.me_ref, s32[8]{0:T(128)} %live_ref.5, bf16[48,8192]{1,0:T(8,128)(2,1)} %copy-done.17, bf16[208,8192]{1,0:T(8,128)(2,1)} %copy-done.12, bf16[2,80,3072]{2,1,0:T(8,128)(2,1)} %get-tuple-element.60.refs_2_, ...), custom_call_target="tpu_custom_call", output_to_operand_aliasing={{0}: (12, {})} | custom-call | flops 5033164800 | bytes 120000000 | tf_op jit(solution)/shard_map/block_math/pallas_call | solution.py:523
  437.5 5.1 all-to-all-start.1
  442.7 22.0 %outgoing.5 = bf16[16,200,384]{2,1,0:T(8,128)(2,1)S(1)} custom-call(s32[16]{0:T(128)S(1)} %convert_element_type.63.counts_ref, s32[32768]{0:T(1024)S(1)} %broadcast_minimum_fusion.place_ref, f32[49152,128]{1,0:T(8,128)} %bitcast.47), custom_call_target="tpu_custom_call" | custom-call | bytes 80000000 | tf_op jit(solution)/shard_map/outgoing/pallas_call | solution.py:586
  466.2 6.0 all-to-all-start.3
  472.2 34.3 %outgoing.4 = bf16[16,200,768]{2,1,0:T(8,128)(2,1)S(1)} custom-call(s32[16]{0:T(128)S(1)} %convert_element_type.63.counts_ref, s32[32768]{0:T(1024)S(1)} %broadcast_minimum_fusion.place_ref, f32[49152,128]{1,0:T(8,128)} %bitcast.48), custom_call_target="tpu_custom_call" | custom-call | bytes 80000000 | tf_op jit(solution)/shard_map/outgoing/pallas_call | solution.py:586
  508.8 18.8 %all-to-all-done.3.came_ref = bf16[16,200,384]{2,1,0:T(8,128)(2,1)S(1)} async-done(((bf16[16,200,384]{2,1,0:T(8,128)(2,1)}), bf16[16,200,384]{2,1,0:T(8,128)(2,1)S(1)}, u32[]{:S(2)}, u32[]{:S(2)}) %all-to-all-start.3) | async-done | bytes 2457632 | tf_op jit(solution)/shard_map/all_to_all | solution.py:876
  527.6 4.7 all-to-all-start.2
  532.4 30.1 %relation_sums.1 = (f32[6400,128]{1,0:T(8,128)}, f32[8,128]{1,0:T(8,128)S(1)}) custom-call(s32[8192]{0:T(1024)S(1)} %copy-done.38, f32[3,16384,128]{2,1,0:T(8,128)} %get-tuple-element.64.grad, bf16[8,128]{1,0:T(8,128)(2,1)S(1)} %slice_bitcast_fusion.refs_0_, f32[1,128]{1,0:T(1,128)S(1)} %slice_bitcast_fusion.2.refs_1_), custom_call_target="tpu_custom_call" | custom-call | bytes 120000000 | tf_op jit(solution)/shard_map/relation_sums/pallas_call | solution.py:669
  563.3 26.2 %collect.3 = (f32[15888,128]{1,0:T(8,128)S(1)}, f32[8,128]{1,0:T(8,128)S(1)}) custom-call(s32[16]{0:T(128)S(1)} %convert_reduce_fusion.2.counts_ref, s32[32768]{0:T(1024)S(1)} %bitcast.38, bf16[16,200,384]{2,1,0:T(8,128)(2,1)S(1)} %all-to-all-done.3.came_ref, f32[8,128]{1,0:T(8,128)S(1)} %get-tuple-element.65.refs_0_), custom_call_target="tpu_custom_call" | custom-call | bytes 120000000 | tf_op jit(solution)/shard_map/collect/pallas_call | solution.py:637
  592.6 22.2 %outgoing.7 = bf16[16,200,640]{2,1,0:T(8,128)(2,1)S(1)} custom-call(s32[16]{0:T(128)S(1)} %convert_element_type.63.counts_ref, s32[32768]{0:T(1024)S(1)} %broadcast_minimum_fusion.place_ref, f32[49152,128]{1,0:T(8,128)} %bitcast.49, f32[8,128]{1,0:T(8,128)S(1)} %get-tuple-element.69.refs_0_, f32[8,128]{1,0:T(8,128)S(1)} %slice.78.refs_1_), custom_call_target="tpu_custom_call" | custom-call | bytes 80000000 | tf_op jit(solution)/shard_map/outgoing/pallas_call | solution.py:586
  616.8 23.5 %all-to-all-done.2.came_ref = bf16[16,200,768]{2,1,0:T(8,128)(2,1)} async-done(((bf16[16,200,768]{2,1,0:T(8,128)(2,1)}), bf16[16,200,768]{2,1,0:T(8,128)(2,1)}, u32[]{:S(2)}, u32[]{:S(2)}) %all-to-all-start.2) | async-done | bytes 4915232 | tf_op jit(solution)/shard_map/all_to_all | solution.py:876
  640.4 4.7 all-to-all-start.5
  645.8 3.3 copy-done.4
  649.1 54.3 %collect.4 = (f32[15888,128]{1,0:T(8,128)S(1)}, f32[8,128]{1,0:T(8,128)S(1)}) custom-call(s32[16]{0:T(128)S(1)} %convert_reduce_fusion.2.counts_ref, s32[32768]{0:T(1024)S(1)} %bitcast.39, bf16[16,200,768]{2,1,0:T(8,128)(2,1)} %all-to-all-done.2.came_ref, f32[15888,128]{1,0:T(8,128)S(1)} %copy-done.4), custom_call_target="tpu_custom_call", output_to_operand_aliasing={{0}: (3, {})} | custom-call | bytes 120000000 | tf_op jit(solution)/shard_map/collect/pallas_call | solution.py:637
  706.6 11.8 %outgoing.6 = bf16[16,200,256]{2,1,0:T(8,128)(2,1)} custom-call(s32[16]{0:T(128)S(1)} %convert_element_type.63.counts_ref, s32[32768]{0:T(1024)S(1)} %broadcast_minimum_fusion.place_ref, f32[49152,128]{1,0:T(8,128)} %bitcast.50, f32[8,128]{1,0:T(8,128)S(1)} %get-tuple-element.67.refs_0_, f32[8,128]{1,0:T(8,128)S(1)} %slice.78.refs_1_), custom_call_target="tpu_custom_call" | custom-call | bytes 80000000 | tf_op jit(solution)/shard_map/outgoing/pallas_call | solution.py:586
  718.4 37.1 %all-to-all-done.5.came_ref = bf16[16,200,640]{2,1,0:T(8,128)(2,1)} async-done(((bf16[16,200,640]{2,1,0:T(8,128)(2,1)}), bf16[16,200,640]{2,1,0:T(8,128)(2,1)}, u32[]{:S(2)}, u32[]{:S(2)}) %all-to-all-start.5) | async-done | bytes 4096032 | tf_op jit(solution)/shard_map/all_to_all | solution.py:876
  755.6 5.1 all-to-all-start.4
  763.2 3.3 copy-done.6
  766.5 28.8 %collect.5 = (f32[15888,128]{1,0:T(8,128)S(1)}, f32[8,128]{1,0:T(8,128)}) custom-call(s32[16]{0:T(128)S(1)} %convert_reduce_fusion.2.counts_ref, s32[32768]{0:T(1024)S(1)} %bitcast.40, bf16[16,200,640]{2,1,0:T(8,128)(2,1)} %all-to-all-done.5.came_ref, f32[15888,128]{1,0:T(8,128)S(1)} %copy-done.6, ...), custom_call_target="tpu_custom_call", output_to_operand_aliasing={{0}: (3, {})} | custom-call | bytes 120000000 | tf_op jit(solution)/shard_map/collect/pallas_call | solution.py:637
  799.7 22.7 %finish_entities.1 = (f32[200,7936]{1,0:T(8,128)}, f32[200,7936]{1,0:T(8,128)}, f32[200,7936]{1,0:T(8,128)}) custom-call(s32[16]{0:T(128)} %copy-done.39, s32[32768]{0:T(1024)} %bitcast.41, bf16[16,200,256]{2,1,0:T(8,128)(2,1)} %copy-done.41, f32[15888,128]{1,0:T(8,128)} %copy-done.7, f32[200,7936]{1,0:T(8,128)} %weights_ref.1, f32[200,7936]{1,0:T(8,128)} %first_ref.1, ...), custom_call_target="tpu_custom_call" | custom-call | bytes 60000000 | tf_op jit(solution)/shard_map/finish_entities/pallas_call | solution.py:721
  (199 shorter events, 88.2 us)
Async XLA Ops:
  7.2 183.1 %all-gather.5.cloned.1.call-start = ((), (), s32[]{:S(2)}) async-start(), calls=%async_computation.8 | async-start | bytes 36765696 | tf_op jit(solution)/shard_map/all_gather | solution.py:785
  16.1 272.0 %all-gather.7.cloned.1.call-start = ((), (), s32[]{:S(2)}) async-start(), calls=%async_computation.9 | async-start | bytes 19427328 | tf_op jit(solution)/shard_map/all_gather | solution.py:785
  47.5 240.6 %copy-start.19 = (s32[256,1,128]{2,1,0:T(1,128)}, s32[256,1,128]{2,1,0:T(1,128)S(1)}, u32[]{:S(2)}) copy-start(s32[256,1,128]{2,1,0:T(1,128)S(1)} %get-tuple-element.87) | copy-start | bytes 393220
  241.1 19.6 %copy-start.17 = (bf16[48,8192]{1,0:T(8,128)(2,1)}, bf16[48,8192]{1,0:T(8,128)(2,1)S(1)}, u32[]{:S(2)}) copy-start(bf16[48,8192]{1,0:T(8,128)(2,1)S(1)} %get-tuple-element.41.refs_0_) | copy-start | bytes 2359300
  241.1 19.6 %copy-start.30 = (f32[1,8192]{1,0:T(1,128)}, f32[1,8192]{1,0:T(1,128)S(1)}, u32[]{:S(2)}) copy-start(f32[1,8192]{1,0:T(1,128)S(1)} %get-tuple-element.42.refs_2_.refs_1_) | copy-start | bytes 98308
  241.1 21.7 %collective-permute-start = (bf16[48,8192]{1,0:T(8,128)(2,1)S(1)}, bf16[48,8192]{1,0:T(8,128)(2,1)S(1)}, u32[]{:S(2)}, u32[]{:S(2)}) collective-permute-start(bf16[48,8192]{1,0:T(8,128)(2,1)S(1)} %get-tuple-element.41.refs_0_), channel_id=1, source_target_pairs={{0,1},{1,0},{2,3},{3,2},{4,5},{5,4},{6,7},{7,6},{8,9},{9,8},{10,11... | collective-permute-start | bytes 2359304 | tf_op jit(solution)/shard_map/ppermute | solution.py:797
  244.1 19.6 %slice-start = ((s8[12587008]{0:T(1024)(128)(4,1)}), s8[4194304]{0:T(1024)(128)(4,1)S(1)}, s32[]{:S(2)}) async-start(s8[12587008]{0:T(1024)(128)(4,1)} %bitcast.36), calls=%async_computation.10 | async-start | bytes 8388608
  244.1 19.6 %slice-start.1 = ((s8[12587008]{0:T(1024)(128)(4,1)}), s8[4194304]{0:T(1024)(128)(4,1)S(1)}, s32[]{:S(2)}) async-start(s8[12587008]{0:T(1024)(128)(4,1)} %bitcast.36), calls=%async_computation.11 | async-start | bytes 8388608
  270.9 63.4 %copy-start.12 = (bf16[208,8192]{1,0:T(8,128)(2,1)}, bf16[208,8192]{1,0:T(8,128)(2,1)S(1)}, u32[]{:S(2)}) copy-start(bf16[208,8192]{1,0:T(8,128)(2,1)S(1)} %get-tuple-element.45.refs_1_) | copy-start | bytes 10223620
  270.9 108.1 %collective-permute-start.1 = (bf16[208,8192]{1,0:T(8,128)(2,1)S(1)}, bf16[208,8192]{1,0:T(8,128)(2,1)}, u32[]{:S(2)}, u32[]{:S(2)}) collective-permute-start(bf16[208,8192]{1,0:T(8,128)(2,1)S(1)} %get-tuple-element.45.refs_1_), channel_id=1, source_target_pairs={{0,1},{1,0},{2,3},{3,2},{4,5},{5,4},{6,7},{7,6},{8,9},{9,8},{10,11... | collective-permute-start | bytes 10223624 | tf_op jit(solution)/shard_map/ppermute | solution.py:797
  289.0 45.3 %copy-start.9 = (f32[8192,128]{1,0:T(8,128)S(1)}, f32[8192,128]{1,0:T(8,128)}, u32[]{:S(2)}) copy-start(f32[8192,128]{1,0:T(8,128)} %copy-done.8) | copy-start | bytes 12582916
  289.0 45.3 %copy-start.31 = (f32[1,8192]{1,0:T(1,128)S(1)}, f32[1,8192]{1,0:T(1,128)}, u32[]{:S(2)}) copy-start(f32[1,8192]{1,0:T(1,128)} %copy-done.30) | copy-start | bytes 98308
  289.0 45.3 %copy-start.35 = (f32[1,8192]{1,0:T(1,128)S(1)}, f32[1,8192]{1,0:T(1,128)}, u32[]{:S(2)}) copy-start(f32[1,8192]{1,0:T(1,128)} %copy-done.34) | copy-start | bytes 98308
  338.2 23.4 %collective-permute-start.2 = (bf16[2,80,2048]{2,1,0:T(8,128)(2,1)}, bf16[2,80,2048]{2,1,0:T(8,128)(2,1)}, u32[]{:S(2)}, u32[]{:S(2)}) collective-permute-start(bf16[2,80,2048]{2,1,0:T(8,128)(2,1)} %get-tuple-element.48.refs_2_), channel_id=1, source_target_pairs={{0,1},{1,0},{2,3},{3,2},{4,5},{5,4},{6,7},{7,6},{8,9},{9,8},{10,11... | collective-permute-start | bytes 1966088 | tf_op jit(solution)/shard_map/ppermute | solution.py:797
  344.2 49.5 %collective-permute-start.3 = (bf16[2,80,3072]{2,1,0:T(8,128)(2,1)}, bf16[2,80,3072]{2,1,0:T(8,128)(2,1)}, u32[]{:S(2)}, u32[]{:S(2)}) collective-permute-start(bf16[2,80,3072]{2,1,0:T(8,128)(2,1)} %get-tuple-element.55.refs_2_), channel_id=1, source_target_pairs={{0,1},{1,0},{2,3},{3,2},{4,5},{5,4},{6,7},{7,6},{8,9},{9,8},{10,11... | collective-permute-start | bytes 2949128 | tf_op jit(solution)/shard_map/ppermute | solution.py:797
  347.9 29.1 %all-to-all-start = ((s32[16,1,2048]{2,1,0:T(1,128)}), s32[16,1,2048]{2,1,0:T(1,128)S(1)}, u32[]{:S(2)}, u32[]{:S(2)}) async-start(s32[16,1,2048]{2,1,0:T(1,128)} %all_to_all.23), calls=%async_computation | async-start | bytes 262144 | tf_op jit(solution)/shard_map/all_to_all | solution.py:842
  375.2 39.0 %collective-permute-start.4 = (bf16[2,80,3072]{2,1,0:T(8,128)(2,1)}, bf16[2,80,3072]{2,1,0:T(8,128)(2,1)}, u32[]{:S(2)}, u32[]{:S(2)}) collective-permute-start(bf16[2,80,3072]{2,1,0:T(8,128)(2,1)} %get-tuple-element.60.refs_2_), channel_id=1, source_target_pairs={{0,1},{1,0},{2,3},{3,2},{4,5},{5,4},{6,7},{7,6},{8,9},{9,8},{10,11... | collective-permute-start | bytes 2949128 | tf_op jit(solution)/shard_map/ppermute | solution.py:797
  377.0 386.2 %copy-start.18 = (s32[16,1,2048]{2,1,0:T(1,128)}, s32[16,1,2048]{2,1,0:T(1,128)S(1)}, u32[]{:S(2)}) copy-start(s32[16,1,2048]{2,1,0:T(1,128)S(1)} %all-to-all-done) | copy-start | bytes 393220
  414.2 20.8 %copy-start.52 = (f32[8,128]{1,0:T(8,128)S(1)}, f32[8,128]{1,0:T(8,128)}, u32[]{:S(2)}) copy-start(f32[8,128]{1,0:T(8,128)} %get-tuple-element.54) | copy-start | bytes 12292
  414.2 20.8 %copy-start.53 = (f32[8,128]{1,0:T(8,128)S(1)}, f32[8,128]{1,0:T(8,128)}, u32[]{:S(2)}) copy-start(f32[8,128]{1,0:T(8,128)} %get-tuple-element.59) | copy-start | bytes 12292
  414.2 28.5 %copy-start.20 = (s32[256,1,128]{2,1,0:T(1,128)S(1)}, s32[256,1,128]{2,1,0:T(1,128)}, u32[]{:S(2)}) copy-start(s32[256,1,128]{2,1,0:T(1,128)} %copy-done.19) | copy-start | bytes 393220
  437.5 28.6 %all-to-all-start.1 = ((f32[16,1,128]{2,1,0:T(1,128)}), f32[16,1,128]{2,1,0:T(1,128)S(1)}, u32[]{:S(2)}, u32[]{:S(2)}) async-start(f32[16,1,128]{2,1,0:T(1,128)} %broadcast_in_dim.47), calls=%async_computation.1 | async-start | bytes 16384 | tf_op jit(solution)/shard_map/all_to_all | solution.py:863
  466.2 61.4 %all-to-all-start.3 = ((bf16[16,200,384]{2,1,0:T(8,128)(2,1)}), bf16[16,200,384]{2,1,0:T(8,128)(2,1)S(1)}, u32[]{:S(2)}, u32[]{:S(2)}) async-start(bf16[16,200,384]{2,1,0:T(8,128)(2,1)} %copy-done.16), calls=%async_computation.3 | async-start | bytes 4915200 | tf_op jit(solution)/shard_map/all_to_all | solution.py:876
  508.8 23.6 %copy-start.38 = (s32[8192]{0:T(1024)S(1)}, s32[8192]{0:T(1024)}, u32[]{:S(2)}) copy-start(s32[8192]{0:T(1024)} %ids_ref.1) | copy-start | bytes 98308
  527.6 112.8 %all-to-all-start.2 = ((bf16[16,200,768]{2,1,0:T(8,128)(2,1)}), bf16[16,200,768]{2,1,0:T(8,128)(2,1)}, u32[]{:S(2)}, u32[]{:S(2)}) async-start(bf16[16,200,768]{2,1,0:T(8,128)(2,1)} %copy-done.13), calls=%async_computation.2 | async-start | bytes 9830400 | tf_op jit(solution)/shard_map/all_to_all | solution.py:876
  532.4 230.8 %copy-start.39 = (s32[16]{0:T(128)}, s32[16]{0:T(128)S(1)}, u32[]{:S(2)}) copy-start(s32[16]{0:T(128)S(1)} %convert_reduce_fusion.2.counts_ref) | copy-start | bytes 196
  640.4 115.2 %all-to-all-start.5 = ((bf16[16,200,640]{2,1,0:T(8,128)(2,1)}), bf16[16,200,640]{2,1,0:T(8,128)(2,1)}, u32[]{:S(2)}, u32[]{:S(2)}) async-start(bf16[16,200,640]{2,1,0:T(8,128)(2,1)} %copy-done.15), calls=%async_computation.5 | async-start | bytes 8192000 | tf_op jit(solution)/shard_map/all_to_all | solution.py:876
  645.1 116.2 %reduce-scatter.2.cloned.1.call-start = ((), (), s32[]{:S(2)}) async-start(), calls=%async_computation.7 | async-start | bytes 3481600 | tf_op jit(solution)/shard_map/reduce_scatter | solution.py:882
  706.6 55.6 %copy-start.42 = (f32[200,200]{1,0:T(8,128)S(1)}, f32[200,200]{1,0:T(8,128)}, u32[]{:S(2)}) copy-start(f32[200,200]{1,0:T(8,128)} %param.23) | copy-start | bytes 480004
  706.6 55.6 %copy-start.44 = (f32[200,200]{1,0:T(8,128)S(1)}, f32[200,200]{1,0:T(8,128)}, u32[]{:S(2)}) copy-start(f32[200,200]{1,0:T(8,128)} %param.24) | copy-start | bytes 480004
  706.6 55.6 %copy-start.45 = (f32[200,200]{1,0:T(8,128)S(1)}, f32[200,200]{1,0:T(8,128)}, u32[]{:S(2)}) copy-start(f32[200,200]{1,0:T(8,128)} %param.25) | copy-start | bytes 480004
  755.6 42.9 %all-to-all-start.4 = ((bf16[16,200,256]{2,1,0:T(8,128)(2,1)}), bf16[16,200,256]{2,1,0:T(8,128)(2,1)S(1)}, u32[]{:S(2)}, u32[]{:S(2)}) async-start(bf16[16,200,256]{2,1,0:T(8,128)(2,1)} %outgoing.6), calls=%async_computation.4 | async-start | bytes 3276800 | tf_op jit(solution)/shard_map/all_to_all | solution.py:876
  (40 other events, 164.7 us)
Sparse Core Ops, SparseCore 0:
  16.2 174.0 all-gather.4
  191.9 96.1 all-gather.6
  650.3 95.8 reduce-scatter.1

commit v10 on v8

--- a/solution.py
+++ b/solution.py
@@ -538,7 +538,7 @@
             pltpu.VMEM((block_len, LANES), F32),
             pltpu.VMEM((block_len, LANES), F32),
         ],
-        compiler_params=params(30),
+        compiler_params=params(60),
         cost_estimate=cost(part * 8 * block_len * block_len * width, 120e6),
         name="block_math",
     )(me, live_counts, *flat, *offs, *tails, *kept, *after)
@@ -730,7 +730,7 @@
 
 def chunk_bounds(capacity):
     units = capacity // LANES
-    sizes = [3, 6, 5, 2] if units == 16 else [units // 4] * 3 + [units - 3 * (units // 4)]
+    sizes = [4, 6, 3, 3] if units == 16 else [units // 4] * 3 + [units - 3 * (units // 4)]
     bounds = [0]
     for size in sizes:
         bounds.append(bounds[-1] + size * LANES)
@@ -829,7 +829,14 @@
     for half in range(HALVES):
         finish(half, [corner(offs[half - 1][-1])] if half > 0 else [])
     row_list, _ = lax.optimization_barrier((row_list, corner(offs[-1][-1])))
-    asked = lax.all_to_all(row_list, "edge", split_axis=0, concat_axis=0, tiled=True)
+    bounds = chunk_bounds(capacity)
+    few = jnp.sum((counts > bounds[-2]).astype(jnp.int32)) <= 1
+    flag = jnp.broadcast_to(few.astype(jnp.int32), (groups, LANES))
+    asked = lax.all_to_all(
+        jnp.concatenate([row_list, flag], axis=1), "edge", split_axis=0, concat_axis=0, tiled=True
+    )
+    all_few = jnp.min(asked[:, capacity]) > 0
+    asked = asked[:, :capacity]
     asked_counts = jnp.sum((asked < ent_rows).astype(jnp.int32), axis=1)
     for half in range(HALVES):
         after = [corner(asked)] if half == 0 else []
@@ -856,10 +863,13 @@
     loss_pair = jnp.sum(loss_all[:, 0, :2], axis=0)
 
     flat = grad.reshape(n * id_count, LANES)
-    bounds = chunk_bounds(capacity)
     chunks = len(bounds) - 1
+    begin, size = bounds[-2], bounds[-1] - bounds[-2]
+    most = jnp.argmax(counts)
+    most_places = lax.dynamic_slice_in_dim(safe_places, most, 1, axis=0)
+    most_count = lax.dynamic_slice_in_dim(counts, most, 1, axis=0)
     arrived, total, after = [], None, []
-    for k in range(chunks):
+    for k in range(chunks - 1):
         sent = outgoing(
             counts, safe_places, flat, slices, bounds[k], bounds[k + 1] - bounds[k], after
         )
@@ -867,24 +877,42 @@
         after = []
         if k == 1:
             before = [corner(arrived[0]), corner(loss_all)]
+            excess = outgoing(most_count, most_places, flat, slices, begin, size, before)
+            gathered = lax.all_gather(excess, "edge", axis=0, tiled=True)
+            before = [corner(excess)]
             rel_terms, token = relation_sums(relation_ids, grad, n, rel_total, before)
             after = [token]
             rel_terms = rel_terms.reshape(rel_total, n * LANES)[:, :width]
             relation_grad = lax.psum_scatter(rel_terms, "edge", scatter_dimension=0, tiled=True)
-        if k == chunks - 1:
-            after = [corner(relation_grad)]
         if k > 0:
             total, token = collect(
                 asked_counts, asked, arrived[k - 1], total, slices, bounds[k - 1], ent_rows, after
             )
-            after = [token, corner(rel_terms)]
-    k = chunks - 1
-    new_entity, new_entity_first, new_entity_second = finish_entities(
+            after = [token, corner(rel_terms), corner(gathered)]
+
+    def by_all_to_all():
+        sent = outgoing(counts, safe_places, flat, slices, begin, size, [])
+        return lax.all_to_all(sent, "edge", split_axis=0, concat_axis=0, tiled=True)
+
+    k = chunks - 2
+    total, token = collect(
         asked_counts,
         asked,
         arrived[k],
         total,
+        slices,
         bounds[k],
+        ent_rows,
+        [],
+    )
+    ordered = (token[0, 0] == 0.0) & (relation_grad[0, 0] == relation_grad[0, 0])
+    came = lax.cond(all_few & ordered, lambda: gathered, by_all_to_all)
+    new_entity, new_entity_first, new_entity_second = finish_entities(
+        asked_counts,
+        asked,
+        came,
+        total,
+        begin,
         entity_table,
         entity_first,
         entity_second,

time: 822 us -> 812 us (0.988)
    all_to_all x4 -> x3, waiting for transfers between devices: 73.3 us -> 37.1 us  [shards(): lax.all_to_all(sent, 'edge', split_axis=0, concat_axis=0, tiled=True)]
    reduce_scatter x1, waiting for transfers between devices: 0.01 us -> 21.2 us  [shards(): lax.psum_scatter(rel_terms, 'edge', scatter_dimension=0, tiled=True)]
    all_gather x0 -> x1, waiting for transfers between devices: none -> 10.8 us  [shards(): gathered = lax.all_gather(excess, 'edge', axis=0, tiled=True)]
    unnamed x90 -> x97, local copies, waits for them, and re-layouts: 39.7 us -> 30.2 us
    all_to_all x4 -> x3, starting transfers between devices: 20.4 us -> 15.4 us  [shards(): lax.all_to_all(sent, 'edge', split_axis=0, concat_axis=0, tiled=True)]
  transfers between devices with their start and end apart: 13 -> 13, of which waited for: 9 -> 10; matrix products, arithmetic and copies ran while one was open for 5% -> 6% of each run, Pallas kernels for 46% -> 43%
where the time goes in v10:
time: 812 us; the launch traced here: 810 us
  Pallas kernels  419 us (52%)
  waiting for transfers between devices  248 us (31%)
  local copies, waits for them, and re-layouts  47 us (6%)
  other arithmetic  32 us (4%)
  starting transfers between devices  30.6 us (4%)
  between operations  21.1 us (3%)
  matrix products  12.3 us (2%)
    all_gather x2, waiting for transfers between devices, shards(): dense.append(lax.all_gather(sent, 'edge', axis=0, tiled=False))  150 us
    pallas_call x3, Pallas kernels, collect(): pl.pallas_call(functools.partial(collect_kernel, slices, capacity, begin,...  102 us
    pallas_call x2, Pallas kernels, fetch(): pl.pallas_call(functools.partial(fetch_kernel, capacity, moves, ent_rows)...  89.7 us
    pallas_call x4, Pallas kernels, outgoing(): pl.pallas_call(functools.partial(outgoing_kernel, slices, capacity, begin...  88.9 us
    pallas_call x2, Pallas kernels, block_math(): pl.pallas_call(functools.partial(block_kernel, slices, n_col, half), out_...  52.1 us
    all_to_all x3, waiting for transfers between devices, shards(): lax.all_to_all(sent, 'edge', split_axis=0, concat_axis=0, tiled=True)  37.1 us
    pallas_call x1, Pallas kernels, relation_sums(): pl.pallas_call(functools.partial(relation_sums_kernel, n), out_shape=[jax...  31.1 us
    unnamed x97, local copies, waits for them, and re-layouts  30.2 us
  transfers between devices with their start and end apart: 13, of which 10 were waited for; matrix products, arithmetic and copies ran while one was open for 6% of the time, Pallas kernels for 43%

profile of v10, /device:TPU:16, one launch (start us, length us, event | category | flops | bytes accessed | tf_op | source)
XLA Modules:
  0.0 809.8 jit_solution(11300855266296396248)
XLA Ops:
  21.8 8.8 %broadcast_multiply_fusion = bf16[4,128,24576]{2,1,0:T(8,128)(2,1)} fusion(bf16[128,24576]{1,0:T(8,128)(2,1)S(1)} %fusion.2, bf16[4,24576]{1,0:T(4,128)(2,1)S(1)} %pad_maximum_fusion), kind=kLoop, calls=%fused_computation.2 | loop fusion | flops 12582912 | bytes 31653888 | tf_op jit(solution)/shard_map/mul | solution.py:92
  30.6 11.8 %fusion.8 = s32[256,512]{1,0:T(8,128)S(1)} fusion(bf16[512,24576]{1,0:T(8,128)(2,1)} %bitcast.64, s32[24576]{0:T(1024)S(1)} %get-tuple-element.98), kind=kOutput, calls=%fused_computation.16 | convolution fusion | flops 6448873472 | bytes 25788416 | tf_op jit(solution)/shard_map/dot_general | solution.py:93
  46.3 141.1 %all-gather.8.cloned.1.call-done = bf16[2048,8448]{1,0:T(8,128)(2,1)} async-done(((bf16[128,8448]{1,0:T(8,128)(2,1)}), bf16[2048,8448]{1,0:T(8,128)(2,1)}) %all-gather.8.cloned.1.call-update) | async-done | bytes 34603024 | tf_op jit(solution)/shard_map/all_gather | solution.py:778
  187.4 44.5 %fetch_rows.2.neg_ref.head_ref.tail_ref = f32[24584,128]{1,0:T(8,128)S(1)} custom-call(s32[16]{0:T(128)S(1)} %convert_element_type.72.counts_ref, s32[32768]{0:T(1024)S(1)} %bitcast.49, s32[32768]{0:T(1024)S(1)} %bitcast.52, bf16[16,128,8448]{2,1,0:T(8,128)(2,1)} %bitcast.61), custom_call_target="tpu_custom_call" | custom-call | bytes 170000000 | tf_op jit(solution)/shard_map/fetch_rows/pallas_call | solution.py:230
  232.0 5.8 negatives.1
  239.5 16.6 %relation_rows.1 = (f32[8192,128]{1,0:T(8,128)S(1)}, f32[8192,128]{1,0:T(8,128)S(1)}) custom-call(s32[8192]{0:T(1024)S(1)} %fusion.28.ids_ref, f32[16,256]{1,0:T(8,128)S(1)} %pad.15.scale_ref, bf16[16,128,8448]{2,1,0:T(8,128)(2,1)} %bitcast.62, bf16[16,128,8448]{2,1,0:T(8,128)(2,1)} %bitcast.63, f32[1,8192]{1,0:T(1,128)S(1)} %get-tuple-element.51.refs_2_.refs_1_), custom_call_target="tpu_custom_call" | custom-call | bytes 80000000 | tf_op jit(solution)/shard_map/relation_rows/pallas_call | solution.py:138
  263.3 12.0 %collective-permute-done.refs_3_ = bf16[96,8192]{1,0:T(8,128)(2,1)} collective-permute-done((bf16[96,8192]{1,0:T(8,128)(2,1)}, bf16[96,8192]{1,0:T(8,128)(2,1)}, u32[]{:S(2)}, u32[]{:S(2)}) %collective-permute-start) | collective-permute-done | bytes 1572896 | tf_op jit(solution)/shard_map/ppermute | solution.py:790
  276.0 9.2 %all-gather.10.cloned.1.call-done = bf16[1152,7936]{1,0:T(8,128)(2,1)} async-done(((bf16[72,7936]{1,0:T(8,128)(2,1)}), bf16[1152,7936]{1,0:T(8,128)(2,1)}) %all-gather.10.cloned.1.call-update) | async-done | bytes 18284560 | tf_op jit(solution)/shard_map/all_gather | solution.py:778
  285.2 45.2 %fetch_rows.3.head_ref.tail_ref.neg_ref = f32[24584,128]{1,0:T(8,128)S(1)} custom-call(s32[16]{0:T(128)S(1)} %convert_element_type.72.counts_ref, s32[32768]{0:T(1024)S(1)} %bitcast.50, s32[32768]{0:T(1024)S(1)} %bitcast.53, bf16[16,72,7936]{2,1,0:T(8,128)(2,1)} %bitcast.65, bf16[8,128]{1,0:T(8,128)(2,1)S(1)} %slice.100.refs_0_), custom_call_target="tpu_custom_call" | custom-call | bytes 170000000 | tf_op jit(solution)/shard_map/fetch_rows/pallas_call | solution.py:230
  344.8 5.1 all-to-all-start.1
  351.2 4.4 all-to-all-done.1
  356.3 10.2 %collective-permute-done.2.refs_5_ = bf16[2,80,4096]{2,1,0:T(8,128)(2,1)} collective-permute-done((bf16[2,80,4096]{2,1,0:T(8,128)(2,1)}, bf16[2,80,4096]{2,1,0:T(8,128)(2,1)}, u32[]{:S(2)}, u32[]{:S(2)}) %collective-permute-start.2) | collective-permute-done | bytes 1310752 | tf_op jit(solution)/shard_map/ppermute | solution.py:790
  366.5 26.0 %block_math.2 = (f32[3,16384,128]{2,1,0:T(8,128)}, f32[8,128]{1,0:T(8,128)}) custom-call(s32[1]{0:T(128)} %bitcast.me_ref, s32[8]{0:T(128)} %live_ref.3, bf16[96,8192]{1,0:T(8,128)(2,1)} %get-tuple-element.50.refs_0_, bf16[160,8192]{1,0:T(8,128)(2,1)} %copy-done.13, bf16[2,80,4096]{2,1,0:T(8,128)(2,1)} %get-tuple-element.57.refs_2_, ...), custom_call_target="tpu_custom_call" | custom-call | flops 6710886400 | bytes 120000000 | tf_op jit(solution)/shard_map/block_math/pallas_call | solution.py:516
  393.9 26.1 %block_math.3 = (f32[3,16384,128]{2,1,0:T(8,128)}, f32[8,128]{1,0:T(8,128)}) custom-call(s32[1]{0:T(128)} %bitcast.me_ref, s32[8]{0:T(128)} %live_ref.3, bf16[96,8192]{1,0:T(8,128)(2,1)} %get-tuple-element.50.refs_0_, bf16[160,8192]{1,0:T(8,128)(2,1)} %copy-done.13, ...), custom_call_target="tpu_custom_call", output_to_operand_aliasing={{0}: (12, {})} | custom-call | flops 6710886400 | bytes 120000000 | tf_op jit(solution)/shard_map/block_math/pallas_call | solution.py:516
  422.6 5.1 all-to-all-start.2
  427.7 26.0 %outgoing.6 = bf16[16,200,512]{2,1,0:T(8,128)(2,1)S(1)} custom-call(s32[16]{0:T(128)S(1)} %convert_element_type.72.counts_ref, s32[32768]{0:T(1024)S(1)} %broadcast_minimum_fusion.place_ref, f32[49152,128]{1,0:T(8,128)} %bitcast.56), custom_call_target="tpu_custom_call" | custom-call | bytes 80000000 | tf_op jit(solution)/shard_map/outgoing/pallas_call | solution.py:579
  455.4 6.0 all-to-all-start.3
  461.4 34.3 %outgoing.9 = bf16[16,200,768]{2,1,0:T(8,128)(2,1)S(1)} custom-call(s32[16]{0:T(128)S(1)} %convert_element_type.72.counts_ref, s32[32768]{0:T(1024)S(1)} %broadcast_minimum_fusion.place_ref, f32[49152,128]{1,0:T(8,128)} %bitcast.57), custom_call_target="tpu_custom_call" | custom-call | bytes 80000000 | tf_op jit(solution)/shard_map/outgoing/pallas_call | solution.py:579
  498.0 36.3 %all-to-all-done.3.came_ref = bf16[16,200,512]{2,1,0:T(8,128)(2,1)S(1)} async-done(((bf16[16,200,512]{2,1,0:T(8,128)(2,1)}), bf16[16,200,512]{2,1,0:T(8,128)(2,1)S(1)}, u32[]{:S(2)}, u32[]{:S(2)}) %all-to-all-start.3) | async-done | bytes 3276832 | tf_op jit(solution)/shard_map/all_to_all | solution.py:876
  534.4 4.7 all-to-all-start.5
  543.4 9.6 %outgoing.7 = bf16[1,200,384]{2,1,0:T(8,128)(2,1)S(1)} custom-call(s32[1]{0:T(128)} %dynamic_slice.6.counts_ref, s32[2048]{0:T(1024)S(1)} %bitcast.55, f32[49152,128]{1,0:T(8,128)} %bitcast.58, bf16[8,128]{1,0:T(8,128)(2,1)S(1)} %slice_bitcast_fusion.3.refs_0_, f32[1,128]{1,0:T(1,128)S(1)} %slice_bitcast_fusion.4.refs_1_), custom_call_target="tpu_custom_call" | custom-call | bytes 80000000 | tf_op jit(solution)/shard_map/outgoing/pallas_call | solution.py:579
  556.2 31.1 %relation_sums.1 = (f32[6400,128]{1,0:T(8,128)S(1)}, f32[8,128]{1,0:T(8,128)S(1)}) custom-call(s32[8192]{0:T(1024)S(1)} %copy-done.19, f32[3,16384,128]{2,1,0:T(8,128)} %get-tuple-element.68.grad, bf16[8,128]{1,0:T(8,128)(2,1)S(1)} %slice_bitcast_fusion.2.refs_0_), custom_call_target="tpu_custom_call" | custom-call | bytes 120000000 | tf_op jit(solution)/shard_map/relation_sums/pallas_call | solution.py:662
  589.0 4.9 reshape.739
  594.6 33.0 %collect.3 = (f32[15888,128]{1,0:T(8,128)S(1)}, f32[8,128]{1,0:T(8,128)S(1)}) custom-call(s32[16]{0:T(128)S(1)} %get-tuple-element.97.counts_ref, s32[32768]{0:T(1024)S(1)} %bitcast.45, bf16[16,200,512]{2,1,0:T(8,128)(2,1)S(1)} %all-to-all-done.3.came_ref, f32[8,128]{1,0:T(8,128)S(1)} %get-tuple-element.70.refs_0_), custom_call_target="tpu_custom_call" | custom-call | bytes 120000000 | tf_op jit(solution)/shard_map/collect/pallas_call | solution.py:630
  630.8 10.8 %all-gather.6.cloned.1.call-done = bf16[16,200,384]{2,1,0:T(8,128)(2,1)} async-done(((bf16[1,200,384]{2,1,0:T(8,128)(2,1)}), bf16[16,200,384]{2,1,0:T(8,128)(2,1)}) %all-gather.6.cloned.1.call-update) | async-done | bytes 2457616 | tf_op jit(solution)/shard_map/all_gather | solution.py:881
  642.3 19.0 %outgoing.8 = bf16[16,200,384]{2,1,0:T(8,128)(2,1)} custom-call(s32[16]{0:T(128)} %copy-done.36, s32[32768]{0:T(1024)S(1)} %broadcast_minimum_fusion.place_ref, f32[49152,128]{1,0:T(8,128)} %bitcast.59, f32[8,128]{1,0:T(8,128)S(1)} %get-tuple-element.71.refs_0_, f32[8,128]{1,0:T(8,128)S(1)} %slice.108.refs_1_, bf16[8,128]{1,0:T(8,128)(2,1)S(1)} %slice_bitcast_fusion.1.refs_2_), custom_call_target="tpu_custom_call" | custom-call | bytes 80000000 | tf_op jit(solution)/shard_map/outgoing/pallas_call | solution.py:579
  662.0 4.7 all-to-all-start.4
  669.8 3.3 copy-done.2
  673.1 49.3 %collect.4 = (f32[15888,128]{1,0:T(8,128)S(1)}, f32[8,128]{1,0:T(8,128)}) custom-call(s32[16]{0:T(128)S(1)} %get-tuple-element.97.counts_ref, s32[32768]{0:T(1024)S(1)} %bitcast.46, bf16[16,200,768]{2,1,0:T(8,128)(2,1)} %all-to-all-done.5.came_ref, f32[15888,128]{1,0:T(8,128)S(1)} %copy-done.2), custom_call_target="tpu_custom_call", output_to_operand_aliasing={{0}: (3, {})} | custom-call | bytes 120000000 | tf_op jit(solution)/shard_map/collect/pallas_call | solution.py:630
  725.5 21.2 %reduce-scatter.2.cloned.1.call-done = f32[200,200]{1,0:T(8,128)} async-done(((f32[3200,200]{1,0:T(8,128)}), f32[200,200]{1,0:T(8,128)}) %reduce-scatter.2.cloned.1.call-update) | async-done | bytes 160016 | tf_op jit(solution)/shard_map/reduce_scatter | solution.py:886
  754.4 19.5 %collect.5 = (f32[15888,128]{1,0:T(8,128)S(1)}, f32[8,128]{1,0:T(8,128)S(1)}) custom-call(s32[16]{0:T(128)S(1)} %get-tuple-element.97.counts_ref, s32[32768]{0:T(1024)S(1)} %bitcast.47, bf16[16,200,384]{2,1,0:T(8,128)(2,1)S(1)} %all-to-all-done.4.came_ref, f32[15888,128]{1,0:T(8,128)S(1)} %copy-done.4), custom_call_target="tpu_custom_call", output_to_operand_aliasing={{0}: (3, {})} | custom-call | bytes 120000000 | tf_op jit(solution)/shard_map/collect/pallas_call | solution.py:630
  780.0 23.3 %finish_entities.1 = (f32[200,7936]{1,0:T(8,128)}, f32[200,7936]{1,0:T(8,128)}, f32[200,7936]{1,0:T(8,128)}) custom-call(s32[16]{0:T(128)} %copy-done.20, s32[32768]{0:T(1024)} %bitcast.48, bf16[16,200,384]{2,1,0:T(8,128)(2,1)S(1)} %get-tuple-element.102.came_ref, f32[15888,128]{1,0:T(8,128)} %copy-done.5, f32[200,7936]{1,0:T(8,128)} %weights_ref.1, ...), custom_call_target="tpu_custom_call" | custom-call | bytes 60000000 | tf_op jit(solution)/shard_map/finish_entities/pallas_call | solution.py:714
  (181 shorter events, 81.5 us)
Async XLA Ops:
  7.2 180.2 %all-gather.8.cloned.1.call-start = ((), (), s32[]{:S(2)}) async-start(), calls=%async_computation.9 | async-start | bytes 36765696 | tf_op jit(solution)/shard_map/all_gather | solution.py:778
  13.2 272.0 %all-gather.10.cloned.1.call-start = ((), (), s32[]{:S(2)}) async-start(), calls=%async_computation.10 | async-start | bytes 19427328 | tf_op jit(solution)/shard_map/all_gather | solution.py:778
  18.0 523.8 %copy-start.36 = (s32[16]{0:T(128)}, s32[16]{0:T(128)S(1)}, u32[]{:S(2)}) copy-start(s32[16]{0:T(128)S(1)} %convert_element_type.72.counts_ref) | copy-start | bytes 196
  30.6 12.0 %copy-start.33 = (f32[3200]{0:T(1024)S(1)}, f32[3200]{0:T(1024)}, u32[]{:S(2)}) copy-start(f32[3200]{0:T(1024)} %param.20) | copy-start | bytes 38404
  237.8 37.5 %collective-permute-start = (bf16[96,8192]{1,0:T(8,128)(2,1)}, bf16[96,8192]{1,0:T(8,128)(2,1)}, u32[]{:S(2)}, u32[]{:S(2)}) collective-permute-start(bf16[96,8192]{1,0:T(8,128)(2,1)} %get-tuple-element.50.refs_0_), channel_id=1, source_target_pairs={{0,1},{1,0},{2,3},{3,2},{4,5},{5,4},{6,7},{7,6},{8,9},{9,8},{10,11... | collective-permute-start | bytes 4718600 | tf_op jit(solution)/shard_map/ppermute | solution.py:790
  239.4 16.6 %slice-start = ((s8[12587008]{0:T(1024)(128)(4,1)}), s8[4194304]{0:T(1024)(128)(4,1)S(1)}, s32[]{:S(2)}) async-start(s8[12587008]{0:T(1024)(128)(4,1)} %bitcast.43), calls=%async_computation.11 | async-start | bytes 8388608
  239.4 16.6 %slice-start.1 = ((s8[12587008]{0:T(1024)(128)(4,1)}), s8[4194304]{0:T(1024)(128)(4,1)S(1)}, s32[]{:S(2)}) async-start(s8[12587008]{0:T(1024)(128)(4,1)} %bitcast.43), calls=%async_computation.12 | async-start | bytes 8388608
  239.4 16.6 %slice-start.2 = ((s8[12587008]{0:T(1024)(128)(4,1)}), s8[4194304]{0:T(1024)(128)(4,1)S(1)}, s32[]{:S(2)}) async-start(s8[12587008]{0:T(1024)(128)(4,1)} %bitcast.43), calls=%async_computation.13 | async-start | bytes 8388608
  239.5 16.6 %slice-start.3 = ((s8[12587008]{0:T(1024)(128)(4,1)}), s8[4096]{0:T(1024)(128)(4,1)S(1)}, s32[]{:S(2)}) async-start(s8[12587008]{0:T(1024)(128)(4,1)} %bitcast.43), calls=%async_computation.14 | async-start | bytes 8192
  262.7 67.7 %copy-start.13 = (bf16[160,8192]{1,0:T(8,128)(2,1)}, bf16[160,8192]{1,0:T(8,128)(2,1)S(1)}, u32[]{:S(2)}) copy-start(bf16[160,8192]{1,0:T(8,128)(2,1)S(1)} %get-tuple-element.54.refs_1_) | copy-start | bytes 7864324
  262.7 93.6 %collective-permute-start.1 = (bf16[160,8192]{1,0:T(8,128)(2,1)S(1)}, bf16[160,8192]{1,0:T(8,128)(2,1)}, u32[]{:S(2)}, u32[]{:S(2)}) collective-permute-start(bf16[160,8192]{1,0:T(8,128)(2,1)S(1)} %get-tuple-element.54.refs_1_), channel_id=1, source_target_pairs={{0,1},{1,0},{2,3},{3,2},{4,5},{5,4},{6,7},{7,6},{8,9},{9,8},{10,11... | collective-permute-start | bytes 7864328 | tf_op jit(solution)/shard_map/ppermute | solution.py:790
  285.2 45.2 %copy-start.8 = (f32[8192,128]{1,0:T(8,128)S(1)}, f32[8192,128]{1,0:T(8,128)}, u32[]{:S(2)}) copy-start(f32[8192,128]{1,0:T(8,128)} %copy-done.7) | copy-start | bytes 12582916
  334.6 31.9 %collective-permute-start.2 = (bf16[2,80,4096]{2,1,0:T(8,128)(2,1)}, bf16[2,80,4096]{2,1,0:T(8,128)(2,1)}, u32[]{:S(2)}, u32[]{:S(2)}) collective-permute-start(bf16[2,80,4096]{2,1,0:T(8,128)(2,1)} %get-tuple-element.57.refs_2_), channel_id=1, source_target_pairs={{0,1},{1,0},{2,3},{3,2},{4,5},{5,4},{6,7},{7,6},{8,9},{9,8},{10,11... | collective-permute-start | bytes 3932168 | tf_op jit(solution)/shard_map/ppermute | solution.py:790
  336.0 13.9 %copy-start.40 = (s32[8]{0:T(128)S(1)}, s32[8]{0:T(128)}, u32[]{:S(2)}) copy-start(s32[8]{0:T(128)} %live_ref.3) | copy-start | bytes 100
  341.4 52.5 %collective-permute-start.3 = (bf16[2,80,4096]{2,1,0:T(8,128)(2,1)}, bf16[2,80,4096]{2,1,0:T(8,128)(2,1)}, u32[]{:S(2)}, u32[]{:S(2)}) collective-permute-start(bf16[2,80,4096]{2,1,0:T(8,128)(2,1)} %get-tuple-element.63.refs_2_), channel_id=1, source_target_pairs={{0,1},{1,0},{2,3},{3,2},{4,5},{5,4},{6,7},{7,6},{8,9},{9,8},{10,11... | collective-permute-start | bytes 3932168 | tf_op jit(solution)/shard_map/ppermute | solution.py:790
  344.8 10.8 %all-to-all-start.1 = ((s32[16,1,2176]{2,1,0:T(1,128)}), s32[16,1,2176]{2,1,0:T(1,128)S(1)}, u32[]{:S(2)}, u32[]{:S(2)}) async-start(s32[16,1,2176]{2,1,0:T(1,128)} %all_to_all.23), calls=%async_computation.1 | async-start | bytes 278528 | tf_op jit(solution)/shard_map/all_to_all | solution.py:835
  393.9 26.1 %copy-start.39 = (f32[8,128]{1,0:T(8,128)S(1)}, f32[8,128]{1,0:T(8,128)}, u32[]{:S(2)}) copy-start(f32[8,128]{1,0:T(8,128)} %get-tuple-element.62) | copy-start | bytes 12292
  422.6 32.8 %all-to-all-start.2 = ((f32[16,1,128]{2,1,0:T(1,128)}), f32[16,1,128]{2,1,0:T(1,128)S(1)}, u32[]{:S(2)}, u32[]{:S(2)}) async-start(f32[16,1,128]{2,1,0:T(1,128)} %broadcast_in_dim.48), calls=%async_computation.2 | async-start | bytes 16384 | tf_op jit(solution)/shard_map/all_to_all | solution.py:860
  455.4 87.9 %copy-start.34 = (f32[16,1,128]{2,1,0:T(1,128)}, f32[16,1,128]{2,1,0:T(1,128)S(1)}, u32[]{:S(2)}) copy-start(f32[16,1,128]{2,1,0:T(1,128)S(1)} %all-to-all-done.2) | copy-start | bytes 24580
  455.4 78.9 %all-to-all-start.3 = ((bf16[16,200,512]{2,1,0:T(8,128)(2,1)}), bf16[16,200,512]{2,1,0:T(8,128)(2,1)S(1)}, u32[]{:S(2)}, u32[]{:S(2)}) async-start(bf16[16,200,512]{2,1,0:T(8,128)(2,1)} %copy-done.9), calls=%async_computation.3 | async-start | bytes 6553600 | tf_op jit(solution)/shard_map/all_to_all | solution.py:876
  534.4 127.6 %all-to-all-start.5 = ((bf16[16,200,768]{2,1,0:T(8,128)(2,1)}), bf16[16,200,768]{2,1,0:T(8,128)(2,1)}, u32[]{:S(2)}, u32[]{:S(2)}) async-start(bf16[16,200,768]{2,1,0:T(8,128)(2,1)} %copy-done.6), calls=%async_computation.5 | async-start | bytes 9830400 | tf_op jit(solution)/shard_map/all_to_all | solution.py:876
  539.1 102.5 %all-gather.6.cloned.1.call-start = ((), (), s32[]{:S(2)}) async-start(), calls=%async_computation.7 | async-start | bytes 2611200 | tf_op jit(solution)/shard_map/all_gather | solution.py:881
  543.3 9.7 %copy-start.25 = (s32[16,2048]{1,0:T(8,128)}, s32[16,2048]{1,0:T(8,128)S(1)}, u32[]{:S(2)}) copy-start(s32[16,2048]{1,0:T(8,128)S(1)} %reshape.741) | copy-start | bytes 393220
  554.7 196.4 %copy-start.20 = (s32[16]{0:T(128)}, s32[16]{0:T(128)S(1)}, u32[]{:S(2)}) copy-start(s32[16]{0:T(128)S(1)} %get-tuple-element.97.counts_ref) | copy-start | bytes 196
  554.7 196.4 %copy-start.11 = (s32[2,16,8,128]{3,1,2,0:T(8,128)}, s32[2,16,8,128]{3,1,2,0:T(8,128)S(1)}, u32[]{:S(2)}) copy-start(s32[2,16,8,128]{3,1,2,0:T(8,128)S(1)} %copy.37) | copy-start | bytes 393220
  662.0 89.1 %all-to-all-start.4 = ((bf16[16,200,384]{2,1,0:T(8,128)(2,1)}), bf16[16,200,384]{2,1,0:T(8,128)(2,1)S(1)}, u32[]{:S(2)}, u32[]{:S(2)}) async-start(bf16[16,200,384]{2,1,0:T(8,128)(2,1)} %outgoing.8), calls=%async_computation.4 | async-start | bytes 4915200 | tf_op jit(solution)/shard_map/all_to_all | solution.py:876
  666.7 80.1 %reduce-scatter.2.cloned.1.call-start = ((), (), s32[]{:S(2)}) async-start(), calls=%async_computation.8 | async-start | bytes 3481600 | tf_op jit(solution)/shard_map/reduce_scatter | solution.py:886
  673.1 76.1 %copy-start.23 = (f32[200,200]{1,0:T(8,128)S(1)}, f32[200,200]{1,0:T(8,128)}, u32[]{:S(2)}) copy-start(f32[200,200]{1,0:T(8,128)} %param.25) | copy-start | bytes 480004
  673.1 76.1 %copy-start.28 = (f32[200,200]{1,0:T(8,128)S(1)}, f32[200,200]{1,0:T(8,128)}, u32[]{:S(2)}) copy-start(f32[200,200]{1,0:T(8,128)} %param.26) | copy-start | bytes 480004
  673.1 76.1 %copy-start.29 = (f32[200,200]{1,0:T(8,128)S(1)}, f32[200,200]{1,0:T(8,128)}, u32[]{:S(2)}) copy-start(f32[200,200]{1,0:T(8,128)} %param.27) | copy-start | bytes 480004
  754.4 23.8 %copy-start.26 = (s32[16,2048]{1,0:T(8,128)S(1)}, s32[16,2048]{1,0:T(8,128)}, u32[]{:S(2)}) copy-start(s32[16,2048]{1,0:T(8,128)} %copy-done.25) | copy-start | bytes 393220
  754.4 23.8 %copy-start.37 = (s32[16]{0:T(128)S(1)}, s32[16]{0:T(128)}, u32[]{:S(2)}) copy-start(s32[16]{0:T(128)} %copy-done.36) | copy-start | bytes 196
  (26 other events, 74.4 us)
Sparse Core Ops, SparseCore 0:
  13.3 174.0 all-gather.7
  189.0 96.1 all-gather.9
  553.8 87.7 all-gather.5
  671.6 75.0 reduce-scatter.1

commit v11 on v10

--- a/solution.py
+++ b/solution.py
@@ -875,20 +875,25 @@
         )
         arrived.append(lax.all_to_all(sent, "edge", split_axis=0, concat_axis=0, tiled=True))
         after = []
+        if k == 0:
+            excess = outgoing(
+                most_count, most_places, flat, slices, begin, size, [corner(sent), corner(loss_all)]
+            )
+            gathered = lax.all_gather(excess, "edge", axis=0, tiled=True)
+            after = [corner(excess)]
         if k == 1:
-            before = [corner(arrived[0]), corner(loss_all)]
-            excess = outgoing(most_count, most_places, flat, slices, begin, size, before)
-            gathered = lax.all_gather(excess, "edge", axis=0, tiled=True)
-            before = [corner(excess)]
+            before = [corner(arrived[0]), corner(loss_all), corner(excess)]
             rel_terms, token = relation_sums(relation_ids, grad, n, rel_total, before)
             after = [token]
             rel_terms = rel_terms.reshape(rel_total, n * LANES)[:, :width]
             relation_grad = lax.psum_scatter(rel_terms, "edge", scatter_dimension=0, tiled=True)
+        if k == 2:
+            after = [corner(relation_grad)]
         if k > 0:
             total, token = collect(
                 asked_counts, asked, arrived[k - 1], total, slices, bounds[k - 1], ent_rows, after
             )
-            after = [token, corner(rel_terms), corner(gathered)]
+            after = [token, corner(rel_terms)]
 
     def by_all_to_all():
         sent = outgoing(counts, safe_places, flat, slices, begin, size, [])
@@ -905,8 +910,7 @@
         ent_rows,
         [],
     )
-    ordered = (token[0, 0] == 0.0) & (relation_grad[0, 0] == relation_grad[0, 0])
-    came = lax.cond(all_few & ordered, lambda: gathered, by_all_to_all)
+    came = lax.cond(all_few & (token[0, 0] == 0.0), lambda: gathered, by_all_to_all)
     new_entity, new_entity_first, new_entity_second = finish_entities(
         asked_counts,
         asked,

time: 812 us -> 801 us (0.986)
    all_to_all x3, waiting for transfers between devices: 37.1 us -> 63.2 us  [shards(): lax.all_to_all(sent, 'edge', split_axis=0, concat_axis=0, tiled=True)]
    reduce_scatter x1, waiting for transfers between devices: 21.2 us -> 0.01 us  [shards(): lax.psum_scatter(rel_terms, 'edge', scatter_dimension=0, tiled=True)]
    all_gather x1, waiting for transfers between devices: 10.8 us -> 0.02 us  [shards(): gathered = lax.all_gather(excess, 'edge', axis=0, tiled=True)]
  transfers between devices with their start and end apart: 13 -> 13, of which waited for: 10 -> 9; matrix products, arithmetic and copies ran while one was open for 6% -> 6% of each run, Pallas kernels for 43% -> 46%
where the time goes in v11:
time: 801 us; the launch traced here: 802 us
  Pallas kernels  420 us (52%)
  waiting for transfers between devices  242 us (30%)
  local copies, waits for them, and re-layouts  45.7 us (6%)
  other arithmetic  31.1 us (4%)
  starting transfers between devices  30.6 us (4%)
  between operations  19.7 us (2%)
  matrix products  12.3 us (2%)
    all_gather x2, waiting for transfers between devices, shards(): dense.append(lax.all_gather(sent, 'edge', axis=0, tiled=False))  150 us
    pallas_call x3, Pallas kernels, collect(): pl.pallas_call(functools.partial(collect_kernel, slices, capacity, begin,...  102 us
    pallas_call x2, Pallas kernels, fetch(): pl.pallas_call(functools.partial(fetch_kernel, capacity, moves, ent_rows)...  89.7 us
    pallas_call x4, Pallas kernels, outgoing(): pl.pallas_call(functools.partial(outgoing_kernel, slices, capacity, begin...  88.5 us
    all_to_all x3, waiting for transfers between devices, shards(): lax.all_to_all(sent, 'edge', split_axis=0, concat_axis=0, tiled=True)  63.2 us
    pallas_call x2, Pallas kernels, block_math(): pl.pallas_call(functools.partial(block_kernel, slices, n_col, half), out_...  52.1 us
    pallas_call x1, Pallas kernels, relation_sums(): pl.pallas_call(functools.partial(relation_sums_kernel, n), out_shape=[jax...  31.1 us
    unnamed x97, local copies, waits for them, and re-layouts  29.3 us
  transfers between devices with their start and end apart: 13, of which 9 were waited for; matrix products, arithmetic and copies ran while one was open for 6% of the time, Pallas kernels for 46%

profile of v11, /device:TPU:16, one launch (start us, length us, event | category | flops | bytes accessed | tf_op | source)
XLA Modules:
  0.0 801.8 jit_solution(4048188290942824313)
XLA Ops:
  21.8 8.8 %broadcast_multiply_fusion = bf16[4,128,24576]{2,1,0:T(8,128)(2,1)} fusion(bf16[128,24576]{1,0:T(8,128)(2,1)S(1)} %fusion.2, bf16[4,24576]{1,0:T(4,128)(2,1)S(1)} %pad_maximum_fusion), kind=kLoop, calls=%fused_computation.2 | loop fusion | flops 12582912 | bytes 31653888 | tf_op jit(solution)/shard_map/mul | solution.py:92
  30.6 11.8 %fusion.8 = s32[256,512]{1,0:T(8,128)S(1)} fusion(bf16[512,24576]{1,0:T(8,128)(2,1)} %bitcast.64, s32[24576]{0:T(1024)S(1)} %get-tuple-element.98), kind=kOutput, calls=%fused_computation.16 | convolution fusion | flops 6448873472 | bytes 25788416 | tf_op jit(solution)/shard_map/dot_general | solution.py:93
  46.3 141.1 %all-gather.8.cloned.1.call-done = bf16[2048,8448]{1,0:T(8,128)(2,1)} async-done(((bf16[128,8448]{1,0:T(8,128)(2,1)}), bf16[2048,8448]{1,0:T(8,128)(2,1)}) %all-gather.8.cloned.1.call-update) | async-done | bytes 34603024 | tf_op jit(solution)/shard_map/all_gather | solution.py:778
  187.4 44.5 %fetch_rows.2.neg_ref.head_ref.tail_ref = f32[24584,128]{1,0:T(8,128)S(1)} custom-call(s32[16]{0:T(128)S(1)} %convert_element_type.72.counts_ref, s32[32768]{0:T(1024)S(1)} %bitcast.49, s32[32768]{0:T(1024)S(1)} %bitcast.52, bf16[16,128,8448]{2,1,0:T(8,128)(2,1)} %bitcast.61), custom_call_target="tpu_custom_call" | custom-call | bytes 170000000 | tf_op jit(solution)/shard_map/fetch_rows/pallas_call | solution.py:230
  232.0 5.8 negatives.1
  239.5 16.6 %relation_rows.1 = (f32[8192,128]{1,0:T(8,128)S(1)}, f32[8192,128]{1,0:T(8,128)S(1)}) custom-call(s32[8192]{0:T(1024)S(1)} %fusion.28.ids_ref, f32[16,256]{1,0:T(8,128)S(1)} %pad.15.scale_ref, bf16[16,128,8448]{2,1,0:T(8,128)(2,1)} %bitcast.62, bf16[16,128,8448]{2,1,0:T(8,128)(2,1)} %bitcast.63, f32[1,8192]{1,0:T(1,128)S(1)} %get-tuple-element.51.refs_2_.refs_1_), custom_call_target="tpu_custom_call" | custom-call | bytes 80000000 | tf_op jit(solution)/shard_map/relation_rows/pallas_call | solution.py:138
  263.3 12.0 %collective-permute-done.refs_3_ = bf16[96,8192]{1,0:T(8,128)(2,1)} collective-permute-done((bf16[96,8192]{1,0:T(8,128)(2,1)}, bf16[96,8192]{1,0:T(8,128)(2,1)}, u32[]{:S(2)}, u32[]{:S(2)}) %collective-permute-start) | collective-permute-done | bytes 1572896 | tf_op jit(solution)/shard_map/ppermute | solution.py:790
  276.0 9.2 %all-gather.10.cloned.1.call-done = bf16[1152,7936]{1,0:T(8,128)(2,1)} async-done(((bf16[72,7936]{1,0:T(8,128)(2,1)}), bf16[1152,7936]{1,0:T(8,128)(2,1)}) %all-gather.10.cloned.1.call-update) | async-done | bytes 18284560 | tf_op jit(solution)/shard_map/all_gather | solution.py:778
  285.2 45.2 %fetch_rows.3.head_ref.tail_ref.neg_ref = f32[24584,128]{1,0:T(8,128)S(1)} custom-call(s32[16]{0:T(128)S(1)} %convert_element_type.72.counts_ref, s32[32768]{0:T(1024)S(1)} %bitcast.50, s32[32768]{0:T(1024)S(1)} %bitcast.53, bf16[16,72,7936]{2,1,0:T(8,128)(2,1)} %bitcast.65, bf16[8,128]{1,0:T(8,128)(2,1)S(1)} %slice.101.refs_0_), custom_call_target="tpu_custom_call" | custom-call | bytes 170000000 | tf_op jit(solution)/shard_map/fetch_rows/pallas_call | solution.py:230
  343.9 5.1 all-to-all-start.1
  350.3 4.4 all-to-all-done.1
  355.4 10.2 %collective-permute-done.2.refs_5_ = bf16[2,80,4096]{2,1,0:T(8,128)(2,1)} collective-permute-done((bf16[2,80,4096]{2,1,0:T(8,128)(2,1)}, bf16[2,80,4096]{2,1,0:T(8,128)(2,1)}, u32[]{:S(2)}, u32[]{:S(2)}) %collective-permute-start.2) | collective-permute-done | bytes 1310752 | tf_op jit(solution)/shard_map/ppermute | solution.py:790
  365.5 26.0 %block_math.2 = (f32[3,16384,128]{2,1,0:T(8,128)}, f32[8,128]{1,0:T(8,128)}) custom-call(s32[1]{0:T(128)} %bitcast.me_ref, s32[8]{0:T(128)} %live_ref.3, bf16[96,8192]{1,0:T(8,128)(2,1)} %get-tuple-element.50.refs_0_, bf16[160,8192]{1,0:T(8,128)(2,1)} %copy-done.14, bf16[2,80,4096]{2,1,0:T(8,128)(2,1)} %get-tuple-element.57.refs_2_, ...), custom_call_target="tpu_custom_call" | custom-call | flops 6710886400 | bytes 120000000 | tf_op jit(solution)/shard_map/block_math/pallas_call | solution.py:516
  393.0 26.1 %block_math.3 = (f32[3,16384,128]{2,1,0:T(8,128)}, f32[8,128]{1,0:T(8,128)}) custom-call(s32[1]{0:T(128)} %bitcast.me_ref, s32[8]{0:T(128)} %live_ref.3, bf16[96,8192]{1,0:T(8,128)(2,1)} %get-tuple-element.50.refs_0_, bf16[160,8192]{1,0:T(8,128)(2,1)} %copy-done.14, ...), custom_call_target="tpu_custom_call", output_to_operand_aliasing={{0}: (12, {})} | custom-call | flops 6710886400 | bytes 120000000 | tf_op jit(solution)/shard_map/block_math/pallas_call | solution.py:516
  421.7 5.1 all-to-all-start.2
  426.8 26.0 %outgoing.6 = bf16[16,200,512]{2,1,0:T(8,128)(2,1)S(1)} custom-call(s32[16]{0:T(128)S(1)} %convert_element_type.72.counts_ref, s32[32768]{0:T(1024)S(1)} %broadcast_minimum_fusion.place_ref, f32[49152,128]{1,0:T(8,128)} %bitcast.56), custom_call_target="tpu_custom_call" | custom-call | bytes 80000000 | tf_op jit(solution)/shard_map/outgoing/pallas_call | solution.py:579
  454.5 6.0 all-to-all-start.3
  465.4 10.5 %outgoing.7 = bf16[1,200,384]{2,1,0:T(8,128)(2,1)} custom-call(s32[1]{0:T(128)} %dynamic_slice.6.counts_ref, s32[2048]{0:T(1024)S(1)} %bitcast.55, f32[49152,128]{1,0:T(8,128)} %bitcast.57, bf16[8,128]{1,0:T(8,128)(2,1)S(1)} %slice_bitcast_fusion.2.refs_0_, f32[1,128]{1,0:T(1,128)S(1)} %slice_bitcast_fusion.4.refs_1_), custom_call_target="tpu_custom_call" | custom-call | bytes 80000000 | tf_op jit(solution)/shard_map/outgoing/pallas_call | solution.py:579
  476.6 34.3 %outgoing.9 = bf16[16,200,768]{2,1,0:T(8,128)(2,1)S(1)} custom-call(s32[16]{0:T(128)S(1)} %convert_element_type.72.counts_ref, s32[32768]{0:T(1024)S(1)} %broadcast_minimum_fusion.place_ref, f32[49152,128]{1,0:T(8,128)} %bitcast.58, bf16[8,128]{1,0:T(8,128)(2,1)S(1)} %slice_bitcast_fusion.1.refs_2_.refs_0_), custom_call_target="tpu_custom_call" | custom-call | bytes 80000000 | tf_op jit(solution)/shard_map/outgoing/pallas_call | solution.py:579
  513.2 20.3 %all-to-all-done.3.came_ref = bf16[16,200,512]{2,1,0:T(8,128)(2,1)S(1)} async-done(((bf16[16,200,512]{2,1,0:T(8,128)(2,1)}), bf16[16,200,512]{2,1,0:T(8,128)(2,1)S(1)}, u32[]{:S(2)}, u32[]{:S(2)}) %all-to-all-start.3) | async-done | bytes 3276832 | tf_op jit(solution)/shard_map/all_to_all | solution.py:876
  533.4 4.7 all-to-all-start.5
  538.2 31.1 %relation_sums.1 = (f32[6400,128]{1,0:T(8,128)S(1)}, f32[8,128]{1,0:T(8,128)S(1)}) custom-call(s32[8192]{0:T(1024)S(1)} %copy-done.19, f32[3,16384,128]{2,1,0:T(8,128)} %get-tuple-element.68.grad, bf16[8,128]{1,0:T(8,128)(2,1)S(1)} %slice_bitcast_fusion.3.refs_0_, f32[1,128]{1,0:T(1,128)S(1)} %slice_bitcast_fusion.4.refs_1_, ...), custom_call_target="tpu_custom_call" | custom-call | bytes 120000000 | tf_op jit(solution)/shard_map/relation_sums/pallas_call | solution.py:662
  571.0 4.9 reshape.737
  577.7 33.0 %collect.3 = (f32[15888,128]{1,0:T(8,128)S(1)}, f32[8,128]{1,0:T(8,128)S(1)}) custom-call(s32[16]{0:T(128)S(1)} %get-tuple-element.97.counts_ref, s32[32768]{0:T(1024)S(1)} %bitcast.45, bf16[16,200,512]{2,1,0:T(8,128)(2,1)S(1)} %all-to-all-done.3.came_ref, f32[8,128]{1,0:T(8,128)S(1)} %get-tuple-element.70.refs_0_), custom_call_target="tpu_custom_call" | custom-call | bytes 120000000 | tf_op jit(solution)/shard_map/collect/pallas_call | solution.py:630
  613.9 17.6 %outgoing.8 = bf16[16,200,384]{2,1,0:T(8,128)(2,1)S(1)} custom-call(s32[16]{0:T(128)S(1)} %copy-done.36, s32[32768]{0:T(1024)S(1)} %broadcast_minimum_fusion.place_ref, f32[49152,128]{1,0:T(8,128)} %bitcast.59, f32[8,128]{1,0:T(8,128)S(1)} %get-tuple-element.71.refs_0_, f32[8,128]{1,0:T(8,128)S(1)} %slice.110.refs_1_), custom_call_target="tpu_custom_call" | custom-call | bytes 80000000 | tf_op jit(solution)/shard_map/outgoing/pallas_call | solution.py:579
  632.9 33.2 %all-to-all-done.5.came_ref = bf16[16,200,768]{2,1,0:T(8,128)(2,1)} async-done(((bf16[16,200,768]{2,1,0:T(8,128)(2,1)}), bf16[16,200,768]{2,1,0:T(8,128)(2,1)}, u32[]{:S(2)}, u32[]{:S(2)}) %all-to-all-start.5) | async-done | bytes 4915232 | tf_op jit(solution)/shard_map/all_to_all | solution.py:876
  666.2 4.7 all-to-all-start.4
  678.0 49.3 %collect.4 = (f32[15888,128]{1,0:T(8,128)S(1)}, f32[8,128]{1,0:T(8,128)}) custom-call(s32[16]{0:T(128)S(1)} %get-tuple-element.97.counts_ref, s32[32768]{0:T(1024)S(1)} %bitcast.46, bf16[16,200,768]{2,1,0:T(8,128)(2,1)} %all-to-all-done.5.came_ref, f32[15888,128]{1,0:T(8,128)S(1)} %copy-done.2, ...), custom_call_target="tpu_custom_call", output_to_operand_aliasing={{0}: (3, {})} | custom-call | bytes 120000000 | tf_op jit(solution)/shard_map/collect/pallas_call | solution.py:630
  731.4 9.7 %all-to-all-done.4.came_ref = bf16[16,200,384]{2,1,0:T(8,128)(2,1)S(1)} async-done(((bf16[16,200,384]{2,1,0:T(8,128)(2,1)}), bf16[16,200,384]{2,1,0:T(8,128)(2,1)S(1)}, u32[]{:S(2)}, u32[]{:S(2)}) %all-to-all-start.4) | async-done | bytes 2457632 | tf_op jit(solution)/shard_map/all_to_all | solution.py:876
  741.1 3.3 copy-done.4
  744.4 19.8 %collect.5 = (f32[15888,128]{1,0:T(8,128)S(1)}, f32[8,128]{1,0:T(8,128)S(1)}) custom-call(s32[16]{0:T(128)S(1)} %get-tuple-element.97.counts_ref, s32[32768]{0:T(1024)S(1)} %bitcast.47, bf16[16,200,384]{2,1,0:T(8,128)(2,1)S(1)} %all-to-all-done.4.came_ref, f32[15888,128]{1,0:T(8,128)S(1)} %copy-done.4), custom_call_target="tpu_custom_call", output_to_operand_aliasing={{0}: (3, {})} | custom-call | bytes 120000000 | tf_op jit(solution)/shard_map/collect/pallas_call | solution.py:630
  770.3 24.9 %finish_entities.1 = (f32[200,7936]{1,0:T(8,128)}, f32[200,7936]{1,0:T(8,128)}, f32[200,7936]{1,0:T(8,128)}) custom-call(s32[16]{0:T(128)} %copy-done.20, s32[32768]{0:T(1024)} %bitcast.48, bf16[16,200,384]{2,1,0:T(8,128)(2,1)S(1)} %get-tuple-element.102.came_ref, f32[15888,128]{1,0:T(8,128)} %copy-done.5, f32[200,7936]{1,0:T(8,128)} %weights_ref.1, ...), custom_call_target="tpu_custom_call" | custom-call | bytes 60000000 | tf_op jit(solution)/shard_map/finish_entities/pallas_call | solution.py:714
  (181 shorter events, 78.5 us)
Async XLA Ops:
  7.2 180.2 %all-gather.8.cloned.1.call-start = ((), (), s32[]{:S(2)}) async-start(), calls=%async_computation.9 | async-start | bytes 36765696 | tf_op jit(solution)/shard_map/all_gather | solution.py:778
  13.2 272.0 %all-gather.10.cloned.1.call-start = ((), (), s32[]{:S(2)}) async-start(), calls=%async_computation.10 | async-start | bytes 19427328 | tf_op jit(solution)/shard_map/all_gather | solution.py:778
  18.0 458.6 %copy-start.35 = (s32[16]{0:T(128)}, s32[16]{0:T(128)S(1)}, u32[]{:S(2)}) copy-start(s32[16]{0:T(128)S(1)} %convert_element_type.72.counts_ref) | copy-start | bytes 196
  237.8 37.5 %collective-permute-start = (bf16[96,8192]{1,0:T(8,128)(2,1)}, bf16[96,8192]{1,0:T(8,128)(2,1)}, u32[]{:S(2)}, u32[]{:S(2)}) collective-permute-start(bf16[96,8192]{1,0:T(8,128)(2,1)} %get-tuple-element.50.refs_0_), channel_id=1, source_target_pairs={{0,1},{1,0},{2,3},{3,2},{4,5},{5,4},{6,7},{7,6},{8,9},{9,8},{10,11... | collective-permute-start | bytes 4718600 | tf_op jit(solution)/shard_map/ppermute | solution.py:790
  239.4 16.6 %slice-start = ((s8[12587008]{0:T(1024)(128)(4,1)}), s8[4194304]{0:T(1024)(128)(4,1)S(1)}, s32[]{:S(2)}) async-start(s8[12587008]{0:T(1024)(128)(4,1)} %bitcast.43), calls=%async_computation.11 | async-start | bytes 8388608
  239.4 16.6 %slice-start.1 = ((s8[12587008]{0:T(1024)(128)(4,1)}), s8[4194304]{0:T(1024)(128)(4,1)S(1)}, s32[]{:S(2)}) async-start(s8[12587008]{0:T(1024)(128)(4,1)} %bitcast.43), calls=%async_computation.12 | async-start | bytes 8388608
  239.4 16.6 %slice-start.2 = ((s8[12587008]{0:T(1024)(128)(4,1)}), s8[4194304]{0:T(1024)(128)(4,1)S(1)}, s32[]{:S(2)}) async-start(s8[12587008]{0:T(1024)(128)(4,1)} %bitcast.43), calls=%async_computation.13 | async-start | bytes 8388608
  239.5 16.6 %slice-start.3 = ((s8[12587008]{0:T(1024)(128)(4,1)}), s8[4096]{0:T(1024)(128)(4,1)S(1)}, s32[]{:S(2)}) async-start(s8[12587008]{0:T(1024)(128)(4,1)} %bitcast.43), calls=%async_computation.14 | async-start | bytes 8192
  262.7 67.7 %copy-start.14 = (bf16[160,8192]{1,0:T(8,128)(2,1)}, bf16[160,8192]{1,0:T(8,128)(2,1)S(1)}, u32[]{:S(2)}) copy-start(bf16[160,8192]{1,0:T(8,128)(2,1)S(1)} %get-tuple-element.54.refs_1_) | copy-start | bytes 7864324
  262.7 92.6 %collective-permute-start.1 = (bf16[160,8192]{1,0:T(8,128)(2,1)S(1)}, bf16[160,8192]{1,0:T(8,128)(2,1)}, u32[]{:S(2)}, u32[]{:S(2)}) collective-permute-start(bf16[160,8192]{1,0:T(8,128)(2,1)S(1)} %get-tuple-element.54.refs_1_), channel_id=1, source_target_pairs={{0,1},{1,0},{2,3},{3,2},{4,5},{5,4},{6,7},{7,6},{8,9},{9,8},{10,11... | collective-permute-start | bytes 7864328 | tf_op jit(solution)/shard_map/ppermute | solution.py:790
  285.2 45.2 %copy-start.8 = (f32[8192,128]{1,0:T(8,128)S(1)}, f32[8192,128]{1,0:T(8,128)}, u32[]{:S(2)}) copy-start(f32[8192,128]{1,0:T(8,128)} %copy-done.7) | copy-start | bytes 12582916
  333.6 31.9 %collective-permute-start.2 = (bf16[2,80,4096]{2,1,0:T(8,128)(2,1)}, bf16[2,80,4096]{2,1,0:T(8,128)(2,1)}, u32[]{:S(2)}, u32[]{:S(2)}) collective-permute-start(bf16[2,80,4096]{2,1,0:T(8,128)(2,1)} %get-tuple-element.57.refs_2_), channel_id=1, source_target_pairs={{0,1},{1,0},{2,3},{3,2},{4,5},{5,4},{6,7},{7,6},{8,9},{9,8},{10,11... | collective-permute-start | bytes 3932168 | tf_op jit(solution)/shard_map/ppermute | solution.py:790
  335.1 13.9 %copy-start.40 = (s32[8]{0:T(128)S(1)}, s32[8]{0:T(128)}, u32[]{:S(2)}) copy-start(s32[8]{0:T(128)} %live_ref.3) | copy-start | bytes 100
  340.5 52.5 %collective-permute-start.3 = (bf16[2,80,4096]{2,1,0:T(8,128)(2,1)}, bf16[2,80,4096]{2,1,0:T(8,128)(2,1)}, u32[]{:S(2)}, u32[]{:S(2)}) collective-permute-start(bf16[2,80,4096]{2,1,0:T(8,128)(2,1)} %get-tuple-element.63.refs_2_), channel_id=1, source_target_pairs={{0,1},{1,0},{2,3},{3,2},{4,5},{5,4},{6,7},{7,6},{8,9},{9,8},{10,11... | collective-permute-start | bytes 3932168 | tf_op jit(solution)/shard_map/ppermute | solution.py:790
  343.9 10.8 %all-to-all-start.1 = ((s32[16,1,2176]{2,1,0:T(1,128)}), s32[16,1,2176]{2,1,0:T(1,128)S(1)}, u32[]{:S(2)}, u32[]{:S(2)}) async-start(s32[16,1,2176]{2,1,0:T(1,128)} %all_to_all.23), calls=%async_computation.1 | async-start | bytes 278528 | tf_op jit(solution)/shard_map/all_to_all | solution.py:835
  393.0 26.1 %copy-start.39 = (f32[8,128]{1,0:T(8,128)S(1)}, f32[8,128]{1,0:T(8,128)}, u32[]{:S(2)}) copy-start(f32[8,128]{1,0:T(8,128)} %get-tuple-element.62) | copy-start | bytes 12292
  421.7 32.8 %all-to-all-start.2 = ((f32[16,1,128]{2,1,0:T(1,128)}), f32[16,1,128]{2,1,0:T(1,128)S(1)}, u32[]{:S(2)}, u32[]{:S(2)}) async-start(f32[16,1,128]{2,1,0:T(1,128)} %broadcast_in_dim.48), calls=%async_computation.2 | async-start | bytes 16384 | tf_op jit(solution)/shard_map/all_to_all | solution.py:860
  454.5 78.9 %all-to-all-start.3 = ((bf16[16,200,512]{2,1,0:T(8,128)(2,1)}), bf16[16,200,512]{2,1,0:T(8,128)(2,1)S(1)}, u32[]{:S(2)}, u32[]{:S(2)}) async-start(bf16[16,200,512]{2,1,0:T(8,128)(2,1)} %copy-done.9), calls=%async_computation.3 | async-start | bytes 6553600 | tf_op jit(solution)/shard_map/all_to_all | solution.py:876
  513.2 25.0 %copy-start.19 = (s32[8192]{0:T(1024)S(1)}, s32[8192]{0:T(1024)}, u32[]{:S(2)}) copy-start(s32[8192]{0:T(1024)} %ids_ref.1) | copy-start | bytes 98308
  533.4 132.7 %all-to-all-start.5 = ((bf16[16,200,768]{2,1,0:T(8,128)(2,1)}), bf16[16,200,768]{2,1,0:T(8,128)(2,1)}, u32[]{:S(2)}, u32[]{:S(2)}) async-start(bf16[16,200,768]{2,1,0:T(8,128)(2,1)} %copy-done.6), calls=%async_computation.5 | async-start | bytes 9830400 | tf_op jit(solution)/shard_map/all_to_all | solution.py:876
  538.1 135.9 %reduce-scatter.2.cloned.1.call-start = ((), (), s32[]{:S(2)}) async-start(), calls=%async_computation.7 | async-start | bytes 3481600 | tf_op jit(solution)/shard_map/reduce_scatter | solution.py:889
  575.9 38.0 %copy-start.36 = (s32[16]{0:T(128)S(1)}, s32[16]{0:T(128)}, u32[]{:S(2)}) copy-start(s32[16]{0:T(128)} %copy-done.35) | copy-start | bytes 196
  576.9 164.2 %copy-start.20 = (s32[16]{0:T(128)}, s32[16]{0:T(128)S(1)}, u32[]{:S(2)}) copy-start(s32[16]{0:T(128)S(1)} %get-tuple-element.97.counts_ref) | copy-start | bytes 196
  576.9 164.1 %copy-start.12 = (s32[2,16,8,128]{3,1,2,0:T(8,128)}, s32[2,16,8,128]{3,1,2,0:T(8,128)S(1)}, u32[]{:S(2)}) copy-start(s32[2,16,8,128]{3,1,2,0:T(8,128)S(1)} %copy.37) | copy-start | bytes 393220
  666.2 74.9 %all-to-all-start.4 = ((bf16[16,200,384]{2,1,0:T(8,128)(2,1)}), bf16[16,200,384]{2,1,0:T(8,128)(2,1)S(1)}, u32[]{:S(2)}, u32[]{:S(2)}) async-start(bf16[16,200,384]{2,1,0:T(8,128)(2,1)} %copy-done.10), calls=%async_computation.4 | async-start | bytes 4915200 | tf_op jit(solution)/shard_map/all_to_all | solution.py:876
  670.9 97.7 %all-gather.6.cloned.1.call-start = ((), (), s32[]{:S(2)}) async-start(), calls=%async_computation.8 | async-start | bytes 2611200 | tf_op jit(solution)/shard_map/all_gather | solution.py:882
  678.0 52.4 %copy-start.23 = (f32[200,200]{1,0:T(8,128)S(1)}, f32[200,200]{1,0:T(8,128)}, u32[]{:S(2)}) copy-start(f32[200,200]{1,0:T(8,128)} %param.25) | copy-start | bytes 480004
  678.0 52.4 %copy-start.28 = (f32[200,200]{1,0:T(8,128)S(1)}, f32[200,200]{1,0:T(8,128)}, u32[]{:S(2)}) copy-start(f32[200,200]{1,0:T(8,128)} %reduce-scatter.2.cloned.1.call-done) | copy-start | bytes 480004
  678.0 52.4 %copy-start.29 = (f32[200,200]{1,0:T(8,128)S(1)}, f32[200,200]{1,0:T(8,128)}, u32[]{:S(2)}) copy-start(f32[200,200]{1,0:T(8,128)} %param.26) | copy-start | bytes 480004
  678.0 52.4 %copy-start.30 = (f32[200,200]{1,0:T(8,128)S(1)}, f32[200,200]{1,0:T(8,128)}, u32[]{:S(2)}) copy-start(f32[200,200]{1,0:T(8,128)} %param.27) | copy-start | bytes 480004
  744.4 24.1 %copy-start.26 = (s32[16,2048]{1,0:T(8,128)S(1)}, s32[16,2048]{1,0:T(8,128)}, u32[]{:S(2)}) copy-start(s32[16,2048]{1,0:T(8,128)} %copy-done.25) | copy-start | bytes 393220
  744.4 24.2 %copy-start.37 = (s32[16]{0:T(128)S(1)}, s32[16]{0:T(128)}, u32[]{:S(2)}) copy-start(s32[16]{0:T(128)} %copy-done.35) | copy-start | bytes 196
  (26 other events, 93.4 us)
Sparse Core Ops, SparseCore 0:
  13.3 174.0 all-gather.7
  189.0 96.1 all-gather.9
  576.0 83.1 reduce-scatter.1
  673.8 62.6 all-gather.5

commit v12 on v11

--- a/solution.py
+++ b/solution.py
@@ -24,6 +24,7 @@
 TURN = 512
 REL_PAD = 256
 TERMS = 3
+SPARE = 8
 NN = (((1,), (0,)), ((), ()))
 NT = (((1,), (1,)), ((), ()))
 TN = (((0,), (0,)), ((), ()))
@@ -335,14 +336,19 @@
 
 
 def with_terms(columns, total, depth):
+    terms = term_rows(total, 0)
+    return jnp.concatenate([columns[: last_rows(depth)], terms], axis=0).astype(BF16)
+
+
+def term_rows(total, first):
     place = lax.broadcasted_iota(jnp.int32, (8, total.shape[1]), 0)
     left = total
     terms = jnp.zeros(place.shape, F32)
     for k in range(TERMS):
         term = left.astype(BF16).astype(F32)
         left = left - term
-        terms = jnp.where(place == k, term, terms)
-    return jnp.concatenate([columns[: last_rows(depth)], terms], axis=0).astype(BF16)
+        terms = jnp.where(place == first + k, term, terms)
+    return terms
 
 
 def last_kernel(depth, n_given, head_ref, tail_ref, neg_ref, rel_ref, *refs):
@@ -550,8 +556,9 @@
 
 def outgoing_kernel(slices, capacity, begin, counts_ref, place_ref, grad, *refs):
     n = len(slices)
-    out_ref, tile = refs[-2:]
-    groups, width, chunk = out_ref.shape
+    out_ref, token, tile = refs[-3:]
+    groups, _, chunk = out_ref.shape
+    token[...] = jnp.zeros_like(token)
 
     def owner(group, carry):
         wanted = jnp.clip(counts_ref[group] - begin, 0, chunk)
@@ -572,15 +579,47 @@
     lax.fori_loop(0, groups, owner, 0)
 
 
-def outgoing(counts, place_list, grad, slices, begin, chunk, after):
-    groups, capacity = place_list.shape
+def excess_kernel(slices, capacity, begin, counts_ref, place_ref, live_ref, grad, loss_ref, *refs):
+    outgoing_kernel(slices, capacity, begin, counts_ref, place_ref, grad, *refs)
+    out_ref = refs[-3]
+    loss = jnp.sum(jnp.sum(loss_ref[...], axis=0, keepdims=True), axis=1, keepdims=True)
+    live = live_ref[0]
+    for block in range(1, live_ref.shape[0]):
+        live = live + live_ref[block]
+    count = jnp.full((1, LANES), live.astype(F32))
+    terms = term_rows(jnp.broadcast_to(loss, (1, LANES)), 0) + term_rows(count, TERMS)
+    width = sum(depth for _, depth in slices)
+    for at in range(0, out_ref.shape[2], LANES):
+        out_ref[0, last_rows(width) :, at : at + LANES] = terms.astype(BF16)
+
+
+def excess_rows(count, places, live, grad, loss, slices, begin, chunk, after):
     n = len(slices)
     width = sum(depth for _, depth in slices)
     return pl.pallas_call(
+        functools.partial(excess_kernel, slices, places.shape[1], begin),
+        out_shape=[
+            jax.ShapeDtypeStruct((1, last_rows(width) + SPARE, chunk), BF16),
+            token_shape(),
+        ],
+        in_specs=[whole(SMEM)] * 3 + [whole(VMEM)] * 2 + [whole(pl.ANY)] * len(after),
+        out_specs=[whole(VMEM)] * 2,
+        scratch_shapes=[pltpu.VMEM((n * chunk, LANES), F32)],
+        compiler_params=params(34),
+        cost_estimate=cost(0, 80e6),
+        name="excess_rows",
+    )(count, places.reshape(-1), live, grad, loss, *after)
+
+
+def outgoing(counts, place_list, grad, slices, begin, chunk, after, spare=0):
+    groups, capacity = place_list.shape
+    n = len(slices)
+    width = sum(depth for _, depth in slices) + spare
+    return pl.pallas_call(
         functools.partial(outgoing_kernel, slices, capacity, begin),
-        out_shape=jax.ShapeDtypeStruct((groups, width, chunk), BF16),
+        out_shape=[jax.ShapeDtypeStruct((groups, width, chunk), BF16), token_shape()],
         in_specs=[whole(SMEM)] * 2 + [whole(VMEM)] + [whole(pl.ANY)] * len(after),
-        out_specs=whole(VMEM),
+        out_specs=[whole(VMEM)] * 2,
         scratch_shapes=[pltpu.VMEM((n * chunk, LANES), F32)],
         compiler_params=params(34),
         cost_estimate=cost(0, 80e6),
@@ -597,7 +636,7 @@
 
 def add_rows(slices, capacity, begin, counts_ref, row_ref, came_ref, total, tile):
     n = len(slices)
-    groups, width, chunk = came_ref.shape
+    groups, _, chunk = came_ref.shape
 
     def source(group, carry):
         wanted = jnp.clip(counts_ref[group] - begin, 0, chunk)
@@ -698,9 +737,16 @@
     for m, (start, depth) in enumerate(slices):
         part = total[pl.ds(step * (n * cols) + m, cols, stride=n), :]
         gradient[start : start + depth, :] = part.T[:depth]
-    results = adamw_update(weights_ref[...], gradient[...], first_ref[...], second_ref[...])
-    for out, result in zip(outs, results):
-        out[...] = result
+    grad = gradient[...]
+    new_first = BETA_ONE * first_ref[...] + (1.0 - BETA_ONE) * grad
+    new_second = BETA_TWO * second_ref[...] + (1.0 - BETA_TWO) * grad * grad
+    under = jnp.sqrt(new_second * (1.0 / (1.0 - BETA_TWO**STEP))) + EPSILON
+    guess = pl.reciprocal(under, approx=True)
+    inverse = guess * (2.0 - under * guess)
+    pace = LEARN_RATE / (1.0 - BETA_ONE**STEP)
+    outs[0][...] = (1.0 - LEARN_RATE * DECAY) * weights_ref[...] - (pace * new_first) * inverse
+    outs[1][...] = new_first
+    outs[2][...] = new_second
 
 
 def finish_entities(counts, row_list, came, total, begin, weights, first, second, slices):
@@ -730,7 +776,7 @@
 
 def chunk_bounds(capacity):
     units = capacity // LANES
-    sizes = [4, 6, 3, 3] if units == 16 else [units // 4] * 3 + [units - 3 * (units // 4)]
+    sizes = [3, 7, 3, 3] if units == 16 else [units // 4] * 3 + [units - 3 * (units // 4)]
     bounds = [0]
     for size in sizes:
         bounds.append(bounds[-1] + size * LANES)
@@ -853,14 +899,8 @@
             after,
         )
         loss_tiles.append(loss_tile)
-    live = jnp.sum(jnp.minimum(live_counts, block_len)).astype(F32)
-    loss_own = jnp.sum(functools.reduce(jnp.add, loss_tiles))
-    lane = jnp.arange(LANES, dtype=jnp.int32)
-    loss_row = jnp.where(lane == 0, loss_own, jnp.where(lane == 1, live, 0.0))
-    loss_all = lax.all_to_all(
-        jnp.broadcast_to(loss_row, (groups, 1, LANES)), "edge", split_axis=0, concat_axis=0, tiled=True
-    )
-    loss_pair = jnp.sum(loss_all[:, 0, :2], axis=0)
+    live = jnp.minimum(live_counts, block_len)
+    loss_tile = functools.reduce(jnp.add, loss_tiles)
 
     flat = grad.reshape(n * id_count, LANES)
     chunks = len(bounds) - 1
@@ -870,24 +910,34 @@
     most_count = lax.dynamic_slice_in_dim(counts, most, 1, axis=0)
     arrived, total, after = [], None, []
     for k in range(chunks - 1):
-        sent = outgoing(
+        sent, sent_token = outgoing(
             counts, safe_places, flat, slices, bounds[k], bounds[k + 1] - bounds[k], after
         )
         arrived.append(lax.all_to_all(sent, "edge", split_axis=0, concat_axis=0, tiled=True))
         after = []
         if k == 0:
-            excess = outgoing(
-                most_count, most_places, flat, slices, begin, size, [corner(sent), corner(loss_all)]
+            excess, excess_token = excess_rows(
+                most_count,
+                most_places,
+                live,
+                flat,
+                loss_tile,
+                slices,
+                begin,
+                size,
+                [sent_token],
             )
-            gathered = lax.all_gather(excess, "edge", axis=0, tiled=True)
-            after = [corner(excess)]
+            after = [excess_token]
         if k == 1:
-            before = [corner(arrived[0]), corner(loss_all), corner(excess)]
+            before = [corner(arrived[0]), excess_token]
             rel_terms, token = relation_sums(relation_ids, grad, n, rel_total, before)
             after = [token]
             rel_terms = rel_terms.reshape(rel_total, n * LANES)[:, :width]
             relation_grad = lax.psum_scatter(rel_terms, "edge", scatter_dimension=0, tiled=True)
         if k == 2:
+            ready = (relation_grad[0, 0] == relation_grad[0, 0]) & (sent_token[0, 0] == 0.0)
+            excess = jnp.where(ready, excess, jnp.zeros_like(excess))
+            gathered = lax.all_gather(excess, "edge", axis=0, tiled=True)
             after = [corner(relation_grad)]
         if k > 0:
             total, token = collect(
@@ -896,7 +946,8 @@
             after = [token, corner(rel_terms)]
 
     def by_all_to_all():
-        sent = outgoing(counts, safe_places, flat, slices, begin, size, [])
+        spare = last_rows(width) + SPARE - width
+        sent, _ = outgoing(counts, safe_places, flat, slices, begin, size, [], spare)
         return lax.all_to_all(sent, "edge", split_axis=0, concat_axis=0, tiled=True)
 
     k = chunks - 2
@@ -911,6 +962,13 @@
         [],
     )
     came = lax.cond(all_few & (token[0, 0] == 0.0), lambda: gathered, by_all_to_all)
+    own_sums = gathered[:, last_rows(width) :, 0].astype(F32)
+    loss_pair = jnp.stack(
+        [
+            jnp.sum(jnp.sum(own_sums[:, :TERMS], axis=1)),
+            jnp.sum(jnp.sum(own_sums[:, TERMS : 2 * TERMS], axis=1)),
+        ]
+    )
     new_entity, new_entity_first, new_entity_second = finish_entities(
         asked_counts,
         asked,

time: 801 us -> 798 us (level)
  waiting for transfers between devices: 242 us -> 228 us
  local copies, waits for them, and re-layouts: 45.7 us -> 56.6 us
    all_to_all x3, waiting for transfers between devices: 63.2 us -> 10.8 us  [shards(): lax.all_to_all(sent, 'edge', split_axis=0, concat_axis=0, tiled=True)]
    reduce_scatter x1, waiting for transfers between devices: 0.01 us -> 46.2 us  [shards(): lax.psum_scatter(rel_terms, 'edge', scatter_dimension=0, tiled=True)]
    unnamed x97 -> x90, local copies, waits for them, and re-layouts: 29.3 us -> 40.7 us
    pallas_call x4 -> x3, Pallas kernels: 88.5 us -> 78.7 us  [outgoing(): pl.pallas_call(functools.partial(outgoing_kernel, slices, capacity, begin...]
    pallas_call x0 -> x1, Pallas kernels: none -> 9.63 us  [excess_rows(): pl.pallas_call(functools.partial(excess_kernel, slices, places.shape[1],...]
  transfers between devices with their start and end apart: 13 -> 12, of which waited for: 9 -> 9; matrix products, arithmetic and copies ran while one was open for 6% -> 6% of each run, Pallas kernels for 46% -> 44%
where the time goes in v12:
time: 798 us
  Pallas kernels  425 us (53%)
  waiting for transfers between devices  228 us (29%)
  local copies, waits for them, and re-layouts  56.6 us (7%)
  other arithmetic  30.6 us (4%)
  starting transfers between devices  24.6 us (3%)
  between operations  21 us (3%)
  matrix products  12.3 us (2%)
    all_gather x2, waiting for transfers between devices, shards(): dense.append(lax.all_gather(sent, 'edge', axis=0, tiled=False))  150 us
    pallas_call x3, Pallas kernels, collect(): pl.pallas_call(functools.partial(collect_kernel, slices, capacity, begin,...  104 us
    pallas_call x2, Pallas kernels, fetch(): pl.pallas_call(functools.partial(fetch_kernel, capacity, moves, ent_rows)...  89.6 us
    pallas_call x3, Pallas kernels, outgoing(): pl.pallas_call(functools.partial(outgoing_kernel, slices, capacity, begin...  78.7 us
    pallas_call x2, Pallas kernels, block_math(): pl.pallas_call(functools.partial(block_kernel, slices, n_col, half), out_...  52.2 us
    reduce_scatter x1, waiting for transfers between devices, shards(): lax.psum_scatter(rel_terms, 'edge', scatter_dimension=0, tiled=True)  46.2 us
    unnamed x90, local copies, waits for them, and re-layouts  40.7 us
    pallas_call x1, Pallas kernels, relation_sums(): pl.pallas_call(functools.partial(relation_sums_kernel, n), out_shape=[jax...  31.1 us
  transfers between devices with their start and end apart: 12, of which 9 were waited for; matrix products, arithmetic and copies ran while one was open for 6% of the time, Pallas kernels for 44%

profile of v12, /device:TPU:16, one launch (start us, length us, event | category | flops | bytes accessed | tf_op | source)
XLA Modules:
  0.0 798.3 jit_solution(11691461348150186203)
XLA Ops:
  21.8 8.7 %broadcast_multiply_fusion = bf16[4,128,24576]{2,1,0:T(8,128)(2,1)} fusion(bf16[128,24576]{1,0:T(8,128)(2,1)S(1)} %fusion.2, bf16[4,24576]{1,0:T(4,128)(2,1)S(1)} %pad_maximum_fusion), kind=kLoop, calls=%fused_computation.2 | loop fusion | flops 12582912 | bytes 31653888 | tf_op jit(solution)/shard_map/mul | solution.py:93
  30.5 11.8 %fusion.8 = s32[256,512]{1,0:T(8,128)S(1)} fusion(bf16[512,24576]{1,0:T(8,128)(2,1)} %bitcast.64, s32[24576]{0:T(1024)S(1)} %get-tuple-element.115), kind=kOutput, calls=%fused_computation.16 | convolution fusion | flops 6448873472 | bytes 25788416 | tf_op jit(solution)/shard_map/dot_general | solution.py:94
  46.3 141.2 %all-gather.8.cloned.1.call-done = bf16[2048,8448]{1,0:T(8,128)(2,1)} async-done(((bf16[128,8448]{1,0:T(8,128)(2,1)}), bf16[2048,8448]{1,0:T(8,128)(2,1)}) %all-gather.8.cloned.1.call-update) | async-done | bytes 34603024 | tf_op jit(solution)/shard_map/all_gather | solution.py:824
  187.4 44.5 %fetch_rows.2.neg_ref.head_ref.tail_ref = f32[24584,128]{1,0:T(8,128)S(1)} custom-call(s32[16]{0:T(128)S(1)} %convert_element_type.75.counts_ref, s32[32768]{0:T(1024)S(1)} %bitcast.49, s32[32768]{0:T(1024)S(1)} %bitcast.52, bf16[16,128,8448]{2,1,0:T(8,128)(2,1)} %bitcast.61), custom_call_target="tpu_custom_call" | custom-call | bytes 170000000 | tf_op jit(solution)/shard_map/fetch_rows/pallas_call | solution.py:231
  231.9 5.8 negatives.1
  239.4 16.6 %relation_rows.1 = (f32[8192,128]{1,0:T(8,128)S(1)}, f32[8192,128]{1,0:T(8,128)S(1)}) custom-call(s32[8192]{0:T(1024)S(1)} %fusion.28.ids_ref, f32[16,256]{1,0:T(8,128)S(1)} %pad.15.scale_ref, bf16[16,128,8448]{2,1,0:T(8,128)(2,1)} %bitcast.62, bf16[16,128,8448]{2,1,0:T(8,128)(2,1)} %bitcast.63, f32[1,8192]{1,0:T(1,128)S(1)} %get-tuple-element.59.refs_2_.refs_1_), custom_call_target="tpu_custom_call" | custom-call | bytes 80000000 | tf_op jit(solution)/shard_map/relation_rows/pallas_call | solution.py:139
  265.3 10.0 %collective-permute-done.refs_3_ = bf16[96,8192]{1,0:T(8,128)(2,1)} collective-permute-done((bf16[96,8192]{1,0:T(8,128)(2,1)}, bf16[96,8192]{1,0:T(8,128)(2,1)}, u32[]{:S(2)}, u32[]{:S(2)}) %collective-permute-start) | collective-permute-done | bytes 1572896 | tf_op jit(solution)/shard_map/ppermute | solution.py:836
  276.0 9.3 %all-gather.10.cloned.1.call-done = bf16[1152,7936]{1,0:T(8,128)(2,1)} async-done(((bf16[72,7936]{1,0:T(8,128)(2,1)}), bf16[1152,7936]{1,0:T(8,128)(2,1)}) %all-gather.10.cloned.1.call-update) | async-done | bytes 18284560 | tf_op jit(solution)/shard_map/all_gather | solution.py:824
  285.2 45.2 %fetch_rows.3.head_ref.tail_ref.neg_ref = f32[24584,128]{1,0:T(8,128)S(1)} custom-call(s32[16]{0:T(128)S(1)} %convert_element_type.75.counts_ref, s32[32768]{0:T(1024)S(1)} %bitcast.50, s32[32768]{0:T(1024)S(1)} %bitcast.53, bf16[16,72,7936]{2,1,0:T(8,128)(2,1)} %bitcast.65, bf16[8,128]{1,0:T(8,128)(2,1)S(1)} %slice.104.refs_0_), custom_call_target="tpu_custom_call" | custom-call | bytes 170000000 | tf_op jit(solution)/shard_map/fetch_rows/pallas_call | solution.py:231
  330.5 4.6 last_slice.2
  341.2 5.2 all-to-all-start.1
  347.0 4.6 copy-done.1
  360.4 9.1 %collective-permute-done.3.refs_5_ = bf16[2,80,4096]{2,1,0:T(8,128)(2,1)} collective-permute-done((bf16[2,80,4096]{2,1,0:T(8,128)(2,1)}, bf16[2,80,4096]{2,1,0:T(8,128)(2,1)}, u32[]{:S(2)}, u32[]{:S(2)}) %collective-permute-start.3) | collective-permute-done | bytes 1310752 | tf_op jit(solution)/shard_map/ppermute | solution.py:836
  369.5 26.0 %block_math.2 = (f32[3,16384,128]{2,1,0:T(8,128)}, f32[8,128]{1,0:T(8,128)}) custom-call(s32[1]{0:T(128)} %bitcast.me_ref, s32[8]{0:T(128)} %live_ref.3, bf16[96,8192]{1,0:T(8,128)(2,1)} %get-tuple-element.58.refs_0_, bf16[160,8192]{1,0:T(8,128)(2,1)} %copy-done.15, bf16[2,80,4096]{2,1,0:T(8,128)(2,1)} %get-tuple-element.71.refs_2_, ...), custom_call_target="tpu_custom_call" | custom-call | flops 6710886400 | bytes 120000000 | tf_op jit(solution)/shard_map/block_math/pallas_call | solution.py:522
  397.0 26.2 %block_math.3 = (f32[3,16384,128]{2,1,0:T(8,128)}, f32[8,128]{1,0:T(8,128)}) custom-call(s32[1]{0:T(128)} %bitcast.me_ref, s32[8]{0:T(128)} %live_ref.3, bf16[96,8192]{1,0:T(8,128)(2,1)} %get-tuple-element.58.refs_0_, bf16[160,8192]{1,0:T(8,128)(2,1)} %copy-done.15, ...), custom_call_target="tpu_custom_call", output_to_operand_aliasing={{0}: (12, {})} | custom-call | flops 6710886400 | bytes 120000000 | tf_op jit(solution)/shard_map/block_math/pallas_call | solution.py:522
  423.2 22.0 %outgoing.5 = (bf16[16,200,384]{2,1,0:T(8,128)(2,1)S(1)}, f32[8,128]{1,0:T(8,128)S(1)}) custom-call(s32[16]{0:T(128)S(1)} %convert_element_type.75.counts_ref, s32[32768]{0:T(1024)S(1)} %broadcast_minimum_fusion.place_ref, f32[49152,128]{1,0:T(8,128)} %bitcast.56), custom_call_target="tpu_custom_call" | custom-call | bytes 80000000 | tf_op jit(solution)/shard_map/outgoing/pallas_call | solution.py:618
  446.7 5.2 all-to-all-start.2
  455.2 9.6 %excess_rows.1 = (bf16[1,208,384]{2,1,0:T(8,128)(2,1)S(1)}, f32[8,128]{1,0:T(8,128)S(1)}) custom-call(s32[1]{0:T(128)} %dynamic_slice.6.counts_ref, s32[2048]{0:T(1024)S(1)} %bitcast.55, s32[8]{0:T(128)S(1)} %broadcast_minimum_fusion.1.live_ref, f32[49152,128]{1,0:T(8,128)} %bitcast.57, f32[8,128]{1,0:T(8,128)S(1)} %add.189.loss_ref, ...), custom_call_target="tpu_custom_call" | custom-call | bytes 80000000 | tf_op jit(solution)/shard_map/excess_rows/pallas_call | solution.py:599
  464.8 39.2 %outgoing.7 = (bf16[16,200,896]{2,1,0:T(8,128)(2,1)S(1)}, f32[8,128]{1,0:T(8,128)}) custom-call(s32[16]{0:T(128)S(1)} %convert_element_type.75.counts_ref, s32[32768]{0:T(1024)S(1)} %broadcast_minimum_fusion.place_ref, f32[49152,128]{1,0:T(8,128)} %bitcast.58, f32[8,128]{1,0:T(8,128)S(1)} %get-tuple-element.80.refs_1_.refs_0_), custom_call_target="tpu_custom_call" | custom-call | bytes 80000000 | tf_op jit(solution)/shard_map/outgoing/pallas_call | solution.py:618
  507.3 5.3 all-to-all-start.4
  512.6 31.1 %relation_sums.1 = (f32[6400,128]{1,0:T(8,128)S(1)}, f32[8,128]{1,0:T(8,128)S(1)}) custom-call(s32[8192]{0:T(1024)S(1)} %copy-done.21, f32[3,16384,128]{2,1,0:T(8,128)} %get-tuple-element.74.grad, bf16[8,128]{1,0:T(8,128)(2,1)S(1)} %slice_bitcast_fusion.1.refs_0_, f32[8,128]{1,0:T(8,128)S(1)} %get-tuple-element.80.refs_1_.refs_0_), custom_call_target="tpu_custom_call" | custom-call | bytes 120000000 | tf_op jit(solution)/shard_map/relation_sums/pallas_call | solution.py:701
  545.4 4.9 reshape.742
  551.3 26.2 %collect.3 = (f32[15888,128]{1,0:T(8,128)S(1)}, f32[8,128]{1,0:T(8,128)S(1)}) custom-call(s32[16]{0:T(128)S(1)} %get-tuple-element.114.counts_ref, s32[32768]{0:T(1024)S(1)} %bitcast.45, bf16[16,200,384]{2,1,0:T(8,128)(2,1)S(1)} %all-to-all-done.2.came_ref, f32[8,128]{1,0:T(8,128)S(1)} %get-tuple-element.82.refs_0_), custom_call_target="tpu_custom_call" | custom-call | bytes 120000000 | tf_op jit(solution)/shard_map/collect/pallas_call | solution.py:669
  580.6 17.5 %outgoing.6 = (bf16[16,200,384]{2,1,0:T(8,128)(2,1)S(1)}, f32[8,128]{1,0:T(8,128)S(1)}) custom-call(s32[16]{0:T(128)S(1)} %convert_element_type.75.counts_ref, s32[32768]{0:T(1024)S(1)} %broadcast_minimum_fusion.place_ref, f32[49152,128]{1,0:T(8,128)} %bitcast.59, f32[8,128]{1,0:T(8,128)S(1)} %get-tuple-element.83.refs_0_, f32[8,128]{1,0:T(8,128)S(1)} %slice.110.refs_1_), custom_call_target="tpu_custom_call" | custom-call | bytes 80000000 | tf_op jit(solution)/shard_map/outgoing/pallas_call | solution.py:618
  600.7 46.2 %reduce-scatter.2.cloned.1.call-done = f32[200,200]{1,0:T(8,128)} async-done(((f32[3200,200]{1,0:T(8,128)}), f32[200,200]{1,0:T(8,128)}) %reduce-scatter.2.cloned.1.call-update) | async-done | bytes 160016 | tf_op jit(solution)/shard_map/reduce_scatter | solution.py:936
  650.2 8.0 %all-to-all-done.4.came_ref = bf16[16,200,896]{2,1,0:T(8,128)(2,1)} async-done(((bf16[16,200,896]{2,1,0:T(8,128)(2,1)}), bf16[16,200,896]{2,1,0:T(8,128)(2,1)}, u32[]{:S(2)}, u32[]{:S(2)}) %all-to-all-start.4) | async-done | bytes 5734432 | tf_op jit(solution)/shard_map/all_to_all | solution.py:916
  658.2 4.7 all-to-all-start.3
  666.1 3.3 copy-done.4
  669.5 56.8 %collect.4 = (f32[15888,128]{1,0:T(8,128)S(1)}, f32[8,128]{1,0:T(8,128)}) custom-call(s32[16]{0:T(128)S(1)} %get-tuple-element.114.counts_ref, s32[32768]{0:T(1024)S(1)} %bitcast.46, bf16[16,200,896]{2,1,0:T(8,128)(2,1)} %all-to-all-done.4.came_ref, f32[15888,128]{1,0:T(8,128)S(1)} %copy-done.4, ...), custom_call_target="tpu_custom_call", output_to_operand_aliasing={{0}: (3, {})} | custom-call | bytes 120000000 | tf_op jit(solution)/shard_map/collect/pallas_call | solution.py:669
  731.5 3.3 copy-done.6
  734.8 20.8 %collect.5 = (f32[15888,128]{1,0:T(8,128)S(1)}, f32[8,128]{1,0:T(8,128)S(1)}) custom-call(s32[16]{0:T(128)S(1)} %get-tuple-element.114.counts_ref, s32[32768]{0:T(1024)S(1)} %bitcast.47, bf16[16,200,384]{2,1,0:T(8,128)(2,1)S(1)} %all-to-all-done.3.came_ref, f32[15888,128]{1,0:T(8,128)S(1)} %copy-done.6), custom_call_target="tpu_custom_call", output_to_operand_aliasing={{0}: (3, {})} | custom-call | bytes 120000000 | tf_op jit(solution)/shard_map/collect/pallas_call | solution.py:669
  765.1 26.7 %finish_entities.1 = (f32[200,7936]{1,0:T(8,128)}, f32[200,7936]{1,0:T(8,128)}, f32[200,7936]{1,0:T(8,128)}) custom-call(s32[16]{0:T(128)} %copy-done.22, s32[32768]{0:T(1024)} %bitcast.48, bf16[16,208,384]{2,1,0:T(8,128)(2,1)S(1)} %get-tuple-element.119.came_ref, f32[15888,128]{1,0:T(8,128)} %copy-done.7, f32[200,7936]{1,0:T(8,128)} %weights_ref.1, ...), custom_call_target="tpu_custom_call" | custom-call | bytes 60000000 | tf_op jit(solution)/shard_map/finish_entities/pallas_call | solution.py:760
  (173 shorter events, 79.4 us)
Async XLA Ops:
  7.2 180.2 %all-gather.8.cloned.1.call-start = ((), (), s32[]{:S(2)}) async-start(), calls=%async_computation.8 | async-start | bytes 36765696 | tf_op jit(solution)/shard_map/all_gather | solution.py:824
  13.2 272.0 %all-gather.10.cloned.1.call-start = ((), (), s32[]{:S(2)}) async-start(), calls=%async_computation.9 | async-start | bytes 19427328 | tf_op jit(solution)/shard_map/all_gather | solution.py:824
  30.5 12.0 %copy-start.32 = (f32[3200]{0:T(1024)S(1)}, f32[3200]{0:T(1024)}, u32[]{:S(2)}) copy-start(f32[3200]{0:T(1024)} %param.20) | copy-start | bytes 38404
  231.9 5.9 copy-start.2
  231.9 7.3 copy-start.33
  231.9 7.4 copy-start.21
  237.8 37.5 %collective-permute-start = (bf16[96,8192]{1,0:T(8,128)(2,1)}, bf16[96,8192]{1,0:T(8,128)(2,1)}, u32[]{:S(2)}, u32[]{:S(2)}) collective-permute-start(bf16[96,8192]{1,0:T(8,128)(2,1)} %get-tuple-element.58.refs_0_), channel_id=1, source_target_pairs={{0,1},{1,0},{2,3},{3,2},{4,5},{5,4},{6,7},{7,6},{8,9},{9,8},{10,11... | collective-permute-start | bytes 4718600 | tf_op jit(solution)/shard_map/ppermute | solution.py:836
  239.4 18.6 %slice-start = ((s8[12587008]{0:T(1024)(128)(4,1)}), s8[4194304]{0:T(1024)(128)(4,1)S(1)}, s32[]{:S(2)}) async-start(s8[12587008]{0:T(1024)(128)(4,1)} %bitcast.43), calls=%async_computation.10 | async-start | bytes 8388608
  239.4 18.6 %slice-start.1 = ((s8[12587008]{0:T(1024)(128)(4,1)}), s8[4194304]{0:T(1024)(128)(4,1)S(1)}, s32[]{:S(2)}) async-start(s8[12587008]{0:T(1024)(128)(4,1)} %bitcast.43), calls=%async_computation.11 | async-start | bytes 8388608
  239.4 18.6 %slice-start.2 = ((s8[12587008]{0:T(1024)(128)(4,1)}), s8[4194304]{0:T(1024)(128)(4,1)S(1)}, s32[]{:S(2)}) async-start(s8[12587008]{0:T(1024)(128)(4,1)} %bitcast.43), calls=%async_computation.12 | async-start | bytes 8388608
  239.4 18.6 %slice-start.3 = ((s8[12587008]{0:T(1024)(128)(4,1)}), s8[4096]{0:T(1024)(128)(4,1)S(1)}, s32[]{:S(2)}) async-start(s8[12587008]{0:T(1024)(128)(4,1)} %bitcast.43), calls=%async_computation.13 | async-start | bytes 8192
  264.7 65.7 %copy-start.15 = (bf16[160,8192]{1,0:T(8,128)(2,1)}, bf16[160,8192]{1,0:T(8,128)(2,1)S(1)}, u32[]{:S(2)}) copy-start(bf16[160,8192]{1,0:T(8,128)(2,1)S(1)} %get-tuple-element.62.refs_1_) | copy-start | bytes 7864324
  264.7 95.7 %collective-permute-start.1 = (bf16[160,8192]{1,0:T(8,128)(2,1)S(1)}, bf16[160,8192]{1,0:T(8,128)(2,1)}, u32[]{:S(2)}, u32[]{:S(2)}) collective-permute-start(bf16[160,8192]{1,0:T(8,128)(2,1)S(1)} %get-tuple-element.62.refs_1_), channel_id=1, source_target_pairs={{0,1},{1,0},{2,3},{3,2},{4,5},{5,4},{6,7},{7,6},{8,9},{9,8},{10,11... | collective-permute-start | bytes 7864328 | tf_op jit(solution)/shard_map/ppermute | solution.py:836
  285.2 45.2 %copy-start.9 = (f32[8192,128]{1,0:T(8,128)S(1)}, f32[8192,128]{1,0:T(8,128)}, u32[]{:S(2)}) copy-start(f32[8192,128]{1,0:T(8,128)} %copy-done.8) | copy-start | bytes 12582916
  330.4 5.0 copy-start
  330.4 8.7 %copy-start.27 = (s32[256,128]{1,0:T(8,128)S(1)}, s32[256,128]{1,0:T(8,128)}, u32[]{:S(2)}) copy-start(s32[256,128]{1,0:T(8,128)} %get-tuple-element.102) | copy-start | bytes 393220
  337.6 31.9 %collective-permute-start.3 = (bf16[2,80,4096]{2,1,0:T(8,128)(2,1)}, bf16[2,80,4096]{2,1,0:T(8,128)(2,1)}, u32[]{:S(2)}, u32[]{:S(2)}) collective-permute-start(bf16[2,80,4096]{2,1,0:T(8,128)(2,1)} %get-tuple-element.71.refs_2_), channel_id=1, source_target_pairs={{0,1},{1,0},{2,3},{3,2},{4,5},{5,4},{6,7},{7,6},{8,9},{9,8},{10,11... | collective-permute-start | bytes 3932168 | tf_op jit(solution)/shard_map/ppermute | solution.py:836
  341.2 18.6 %all-to-all-start.1 = ((s32[16,1,2176]{2,1,0:T(1,128)}), s32[16,1,2176]{2,1,0:T(1,128)S(1)}, u32[]{:S(2)}, u32[]{:S(2)}) async-start(s32[16,1,2176]{2,1,0:T(1,128)} %all_to_all.20), calls=%async_computation.1 | async-start | bytes 278528 | tf_op jit(solution)/shard_map/all_to_all | solution.py:881
  359.2 37.8 %collective-permute-start.2 = (bf16[2,80,4096]{2,1,0:T(8,128)(2,1)}, bf16[2,80,4096]{2,1,0:T(8,128)(2,1)}, u32[]{:S(2)}, u32[]{:S(2)}) collective-permute-start(bf16[2,80,4096]{2,1,0:T(8,128)(2,1)} %get-tuple-element.66.refs_2_), channel_id=1, source_target_pairs={{0,1},{1,0},{2,3},{3,2},{4,5},{5,4},{6,7},{7,6},{8,9},{9,8},{10,11... | collective-permute-start | bytes 3932168 | tf_op jit(solution)/shard_map/ppermute | solution.py:836
  446.7 8.4 %copy-start.26 = (s32[256,128]{1,0:T(8,128)S(1)}, s32[256,128]{1,0:T(8,128)}, u32[]{:S(2)}) copy-start(s32[256,128]{1,0:T(8,128)} %get-tuple-element.111) | copy-start | bytes 393220
  446.7 8.4 %copy-start.36 = (s32[8]{0:T(128)S(1)}, s32[8]{0:T(128)}, u32[]{:S(2)}) copy-start(s32[8]{0:T(128)} %live_ref.3) | copy-start | bytes 100
  446.7 8.5 %copy-start.34 = (f32[8,128]{1,0:T(8,128)S(1)}, f32[8,128]{1,0:T(8,128)}, u32[]{:S(2)}) copy-start(f32[8,128]{1,0:T(8,128)} %get-tuple-element.77) | copy-start | bytes 12292
  446.7 8.5 %copy-start.35 = (f32[8,128]{1,0:T(8,128)S(1)}, f32[8,128]{1,0:T(8,128)}, u32[]{:S(2)}) copy-start(f32[8,128]{1,0:T(8,128)} %get-tuple-element.78) | copy-start | bytes 12292
  446.7 60.6 %all-to-all-start.2 = ((bf16[16,200,384]{2,1,0:T(8,128)(2,1)}), bf16[16,200,384]{2,1,0:T(8,128)(2,1)S(1)}, u32[]{:S(2)}, u32[]{:S(2)}) async-start(bf16[16,200,384]{2,1,0:T(8,128)(2,1)} %copy-done.17), calls=%async_computation.2 | async-start | bytes 4915200 | tf_op jit(solution)/shard_map/all_to_all | solution.py:916
  507.3 150.9 %all-to-all-start.4 = ((bf16[16,200,896]{2,1,0:T(8,128)(2,1)}), bf16[16,200,896]{2,1,0:T(8,128)(2,1)}, u32[]{:S(2)}, u32[]{:S(2)}) async-start(bf16[16,200,896]{2,1,0:T(8,128)(2,1)} %copy-done.11), calls=%async_computation.5 | async-start | bytes 11468800 | tf_op jit(solution)/shard_map/all_to_all | solution.py:916
  512.6 134.4 %reduce-scatter.2.cloned.1.call-start = ((), (), s32[]{:S(2)}) async-start(), calls=%async_computation.6 | async-start | bytes 3481600 | tf_op jit(solution)/shard_map/reduce_scatter | solution.py:936
  550.3 209.6 %all-gather.6.cloned.1.call-start = ((), (), s32[]{:S(2)}) async-start(), calls=%async_computation.7 | async-start | bytes 2715648 | tf_op jit(solution)/shard_map/all_gather | solution.py:940
  550.5 181.0 %copy-start.22 = (s32[16]{0:T(128)}, s32[16]{0:T(128)S(1)}, u32[]{:S(2)}) copy-start(s32[16]{0:T(128)S(1)} %get-tuple-element.114.counts_ref) | copy-start | bytes 196
  550.5 180.9 %copy-start.13 = (s32[2,16,8,128]{3,1,2,0:T(8,128)}, s32[2,16,8,128]{3,1,2,0:T(8,128)S(1)}, u32[]{:S(2)}) copy-start(s32[2,16,8,128]{3,1,2,0:T(8,128)S(1)} %copy.40) | copy-start | bytes 393220
  599.6 64.6 %copy-start.25 = (f32[200,200]{1,0:T(8,128)S(1)}, f32[200,200]{1,0:T(8,128)}, u32[]{:S(2)}) copy-start(f32[200,200]{1,0:T(8,128)} %param.25) | copy-start | bytes 480004
  650.1 14.0 %copy-start.28 = (f32[200,200]{1,0:T(8,128)S(1)}, f32[200,200]{1,0:T(8,128)}, u32[]{:S(2)}) copy-start(f32[200,200]{1,0:T(8,128)} %reduce-scatter.2.cloned.1.call-done) | copy-start | bytes 480004
  658.2 73.3 %all-to-all-start.3 = ((bf16[16,200,384]{2,1,0:T(8,128)(2,1)}), bf16[16,200,384]{2,1,0:T(8,128)(2,1)S(1)}, u32[]{:S(2)}, u32[]{:S(2)}) async-start(bf16[16,200,384]{2,1,0:T(8,128)(2,1)} %copy-done.16), calls=%async_computation.4 | async-start | bytes 4915200 | tf_op jit(solution)/shard_map/all_to_all | solution.py:916
  (21 other events, 43.9 us)
Sparse Core Ops, SparseCore 0:
  13.3 174.0 all-gather.7
  189.0 96.1 all-gather.9
  550.4 96.4 reduce-scatter.1
  650.3 71.3 all-gather.5

commit v13 on v12

--- a/solution.py
+++ b/solution.py
@@ -353,7 +353,8 @@
 
 def last_kernel(depth, n_given, head_ref, tail_ref, neg_ref, rel_ref, *refs):
     biases, norms = refs[:n_given], refs[n_given : 2 * n_given]
-    off_ref, tail_out, pair_ref = refs[-3:]
+    off_ref, tail_out, pair_ref, token = refs[-4:]
+    token[...] = jnp.zeros_like(token)
     shifted_t, bias = edge_parts(depth, head_ref, tail_ref, rel_ref, off_ref, tail_out)
     neg_t = neg_ref[...].T
     norm = column_sum(neg_t)
@@ -379,6 +380,7 @@
             jax.ShapeDtypeStruct((count, LANES), F32),
             jax.ShapeDtypeStruct((count, LANES), BF16),
             jax.ShapeDtypeStruct((2, tall, count), BF16),
+            token_shape(),
         ],
         grid=(part,),
         in_specs=[rows(0), rows(1), rows(2), rows(0)]
@@ -389,6 +391,7 @@
             pl.BlockSpec((block_len, LANES), lambda b: (b, 0)),
             pl.BlockSpec((block_len, LANES), lambda b: (b, 0)),
             pl.BlockSpec((2, tall, block_len), lambda b: (0, 0, b)),
+            pl.BlockSpec((8, LANES), lambda b: (0, 0)),
         ],
         compiler_params=params(16),
         cost_estimate=cost(0, 20e6),
@@ -715,9 +718,11 @@
     slices,
     capacity,
     begin,
+    last_begin,
     counts_ref,
     row_ref,
     came_ref,
+    last_ref,
     total_ref,
     weights_ref,
     first_ref,
@@ -725,7 +730,8 @@
     *refs,
 ):
     n = len(slices)
-    outs, (total, tile, gradient) = refs[:3], refs[3:]
+    width = sum(depth for _, depth in slices)
+    outs, loss_ref, (total, tile, gradient) = refs[:3], refs[3], refs[4:]
     cols = weights_ref.shape[1]
     step = pl.program_id(0)
 
@@ -733,6 +739,15 @@
     def _():
         total[: total_ref.shape[0], :] = total_ref[...]
         add_rows(slices, capacity, begin, counts_ref, row_ref, came_ref, total, tile)
+        add_rows(slices, capacity, last_begin, counts_ref, row_ref, last_ref, total, tile)
+        terms = jnp.zeros((SPARE, LANES), F32)
+        for group in range(last_ref.shape[0]):
+            terms = terms + last_ref[group, last_rows(width) :, :LANES].astype(F32)
+        place = lax.broadcasted_iota(jnp.int32, terms.shape, 0)
+        for k in range(2):
+            own = (place >= k * TERMS) & (place < (k + 1) * TERMS)
+            loss_ref[k : k + 1, :] = jnp.sum(jnp.where(own, terms, 0.0), axis=0, keepdims=True)
+        loss_ref[2:, :] = jnp.zeros((6, LANES), F32)
 
     for m, (start, depth) in enumerate(slices):
         part = total[pl.ds(step * (n * cols) + m, cols, stride=n), :]
@@ -749,7 +764,9 @@
     outs[2][...] = new_second
 
 
-def finish_entities(counts, row_list, came, total, begin, weights, first, second, slices):
+def finish_entities(
+    counts, row_list, came, last, total, begin, last_begin, weights, first, second, slices
+):
     width, ent_rows = weights.shape
     capacity = row_list.shape[1]
     cols = 1024
@@ -758,20 +775,20 @@
     table = pl.BlockSpec((width, cols), lambda i: (0, i))
     tall = max(n * cols * steps, total.shape[0])
     return pl.pallas_call(
-        functools.partial(finish_kernel, slices, capacity, begin),
-        out_shape=[jax.ShapeDtypeStruct((width, ent_rows), F32)] * 3,
+        functools.partial(finish_kernel, slices, capacity, begin, last_begin),
+        out_shape=[jax.ShapeDtypeStruct((width, ent_rows), F32)] * 3 + [token_shape()],
         grid=(steps,),
-        in_specs=[whole(SMEM)] * 2 + [whole(VMEM)] * 2 + [table] * 3,
-        out_specs=[table] * 3,
+        in_specs=[whole(SMEM)] * 2 + [whole(VMEM)] * 3 + [table] * 3,
+        out_specs=[table] * 3 + [pl.BlockSpec((8, LANES), lambda i: (0, 0))],
         scratch_shapes=[
             pltpu.VMEM((tall, LANES), F32),
-            pltpu.VMEM((n * came.shape[2], LANES), F32),
+            pltpu.VMEM((n * max(came.shape[2], last.shape[2]), LANES), F32),
             pltpu.VMEM((width, cols), F32),
         ],
         compiler_params=params(56),
         cost_estimate=cost(0, 60e6),
         name="finish_entities",
-    )(counts, row_list.reshape(-1), came, total, weights, first, second)
+    )(counts, row_list.reshape(-1), came, last, total, weights, first, second)
 
 
 def chunk_bounds(capacity):
@@ -863,21 +880,23 @@
             rel_rows = relation_rows(rel_places, dense[0], rel_scale, slices, [])
 
     def finish(half, after):
-        off, tail, pair = last_slice(
+        off, tail, pair, token = last_slice(
             fetched, rel_rows[-1], biases, norms, slices[-1][1], blocks, block_len, half, after
         )
         offs[half].append(off)
         tails[half].append(tail)
         for col, piece in enumerate([pair] + from_others(pair)):
             given[half][col].append(piece)
+        return token
 
     grad, loss_tiles = None, []
+    half_token = []
     for half in range(HALVES):
-        finish(half, [corner(offs[half - 1][-1])] if half > 0 else [])
-    row_list, _ = lax.optimization_barrier((row_list, corner(offs[-1][-1])))
+        half_token = [finish(half, half_token)]
     bounds = chunk_bounds(capacity)
     few = jnp.sum((counts > bounds[-2]).astype(jnp.int32)) <= 1
-    flag = jnp.broadcast_to(few.astype(jnp.int32), (groups, LANES))
+    flag = few.astype(jnp.int32) + half_token[0][0, 0].astype(jnp.int32)
+    flag = jnp.broadcast_to(flag, (groups, LANES))
     asked = lax.all_to_all(
         jnp.concatenate([row_list, flag], axis=1), "edge", split_axis=0, concat_axis=0, tiled=True
     )
@@ -929,7 +948,7 @@
             )
             after = [excess_token]
         if k == 1:
-            before = [corner(arrived[0]), excess_token]
+            before = [corner(arrived[0]), excess_token, sent_token]
             rel_terms, token = relation_sums(relation_ids, grad, n, rel_total, before)
             after = [token]
             rel_terms = rel_terms.reshape(rel_total, n * LANES)[:, :width]
@@ -943,43 +962,31 @@
             total, token = collect(
                 asked_counts, asked, arrived[k - 1], total, slices, bounds[k - 1], ent_rows, after
             )
-            after = [token, corner(rel_terms)]
+            after = [token, corner(relation_grad)]
 
     def by_all_to_all():
         spare = last_rows(width) + SPARE - width
         sent, _ = outgoing(counts, safe_places, flat, slices, begin, size, [], spare)
-        return lax.all_to_all(sent, "edge", split_axis=0, concat_axis=0, tiled=True)
+        rows = lax.all_to_all(sent, "edge", split_axis=0, concat_axis=0, tiled=True)
+        return rows.at[:, last_rows(width) :].set(gathered[:, last_rows(width) :])
 
     k = chunks - 2
-    total, token = collect(
+    here = jnp.where(arrived[k][0, 0, 0] > 0, 1, 2) > 0
+    came = lax.cond(all_few & here & (token[0, 0] == 0.0), lambda: gathered, by_all_to_all)
+    new_entity, new_entity_first, new_entity_second, sums = finish_entities(
         asked_counts,
         asked,
         arrived[k],
-        total,
-        slices,
-        bounds[k],
-        ent_rows,
-        [],
-    )
-    came = lax.cond(all_few & (token[0, 0] == 0.0), lambda: gathered, by_all_to_all)
-    own_sums = gathered[:, last_rows(width) :, 0].astype(F32)
-    loss_pair = jnp.stack(
-        [
-            jnp.sum(jnp.sum(own_sums[:, :TERMS], axis=1)),
-            jnp.sum(jnp.sum(own_sums[:, TERMS : 2 * TERMS], axis=1)),
-        ]
-    )
-    new_entity, new_entity_first, new_entity_second = finish_entities(
-        asked_counts,
-        asked,
         came,
         total,
+        bounds[k],
         begin,
         entity_table,
         entity_first,
         entity_second,
         slices,
     )
+    loss_pair = sums[:2, 0]
     new_relation, new_relation_first, new_relation_second = adamw_update(
         relation_table, relation_grad, relation_first, relation_second
     )

time: 798 us -> 811 us (1.016); the launches traced: 798 us -> 802 us
  waiting for transfers between devices: 228 us -> 238 us
    reduce_scatter x1, waiting for transfers between devices: 46.2 us -> 67.1 us  [shards(): lax.psum_scatter(rel_terms, 'edge', scatter_dimension=0, tiled=True)]
    pallas_call x3 -> x2, Pallas kernels: 104 us -> 89 us  [collect(): pl.pallas_call(functools.partial(collect_kernel, slices, capacity, begin,...]
    pallas_call x1, Pallas kernels: 26.7 us -> 37.6 us  [finish_entities(): pl.pallas_call(functools.partial(finish_kernel, slices, capacity, begin,...]
    all_to_all x3, waiting for transfers between devices: 10.8 us -> 0.91 us  [shards(): lax.all_to_all(sent, 'edge', split_axis=0, concat_axis=0, tiled=True)]
    unnamed x90 -> x85, local copies, waits for them, and re-layouts: 40.7 us -> 33.8 us
  transfers between devices with their start and end apart: 12 -> 12, of which waited for: 9 -> 8; matrix products, arithmetic and copies ran while one was open for 6% -> 6% of each run, Pallas kernels for 44% -> 42%
where the time goes in v13:
time: 811 us; the launch traced here: 802 us
  Pallas kernels  421 us (52%)
  waiting for transfers between devices  238 us (29%)
  local copies, waits for them, and re-layouts  52 us (6%)
  other arithmetic  29.8 us (4%)
  starting transfers between devices  25.7 us (3%)
  between operations  22.4 us (3%)
  matrix products  12.3 us (2%)
    all_gather x2, waiting for transfers between devices, shards(): dense.append(lax.all_gather(sent, 'edge', axis=0, tiled=False))  150 us
    pallas_call x2, Pallas kernels, fetch(): pl.pallas_call(functools.partial(fetch_kernel, capacity, moves, ent_rows)...  89.6 us
    pallas_call x2, Pallas kernels, collect(): pl.pallas_call(functools.partial(collect_kernel, slices, capacity, begin,...  89 us
    pallas_call x3, Pallas kernels, outgoing(): pl.pallas_call(functools.partial(outgoing_kernel, slices, capacity, begin...  80 us
    reduce_scatter x1, waiting for transfers between devices, shards(): lax.psum_scatter(rel_terms, 'edge', scatter_dimension=0, tiled=True)  67.1 us
    pallas_call x2, Pallas kernels, block_math(): pl.pallas_call(functools.partial(block_kernel, slices, n_col, half), out_...  52.2 us
    pallas_call x1, Pallas kernels, finish_entities(): pl.pallas_call(functools.partial(finish_kernel, slices, capacity, begin,...  37.6 us
    unnamed x85, local copies, waits for them, and re-layouts  33.8 us
  transfers between devices with their start and end apart: 12, of which 8 were waited for; matrix products, arithmetic and copies ran while one was open for 6% of the time, Pallas kernels for 42%

profile of v13, /device:TPU:16, one launch (start us, length us, event | category | flops | bytes accessed | tf_op | source)
XLA Modules:
  0.0 802.0 jit_solution(6929256836982002874)
XLA Ops:
  24.6 8.8 %broadcast_multiply_fusion = bf16[4,128,24576]{2,1,0:T(8,128)(2,1)} fusion(bf16[128,24576]{1,0:T(8,128)(2,1)S(1)} %fusion.2, bf16[4,24576]{1,0:T(4,128)(2,1)S(1)} %pad_maximum_fusion), kind=kLoop, calls=%fused_computation.3 | loop fusion | flops 12582912 | bytes 31653888 | tf_op jit(solution)/shard_map/mul | solution.py:93
  33.4 11.8 %fusion.8 = s32[256,512]{1,0:T(8,128)S(1)} fusion(bf16[512,24576]{1,0:T(8,128)(2,1)} %bitcast.60, s32[24576]{0:T(1024)S(1)} %get-tuple-element.134), kind=kOutput, calls=%fused_computation.17 | convolution fusion | flops 6448873472 | bytes 25788416 | tf_op jit(solution)/shard_map/dot_general | solution.py:94
  49.2 141.1 %all-gather.10.cloned.1.call-done = bf16[2048,8448]{1,0:T(8,128)(2,1)} async-done(((bf16[128,8448]{1,0:T(8,128)(2,1)}), bf16[2048,8448]{1,0:T(8,128)(2,1)}) %all-gather.10.cloned.1.call-update) | async-done | bytes 34603024 | tf_op jit(solution)/shard_map/all_gather | solution.py:841
  190.3 44.5 %fetch_rows.2.neg_ref.head_ref.tail_ref = f32[24584,128]{1,0:T(8,128)S(1)} custom-call(s32[16]{0:T(128)S(1)} %convert_element_type.79.counts_ref, s32[32768]{0:T(1024)S(1)} %bitcast.45, s32[32768]{0:T(1024)S(1)} %bitcast.48, bf16[16,128,8448]{2,1,0:T(8,128)(2,1)} %bitcast.57), custom_call_target="tpu_custom_call" | custom-call | bytes 170000000 | tf_op jit(solution)/shard_map/fetch_rows/pallas_call | solution.py:231
  234.8 5.8 negatives.1
  242.3 16.6 %relation_rows.1 = (f32[8192,128]{1,0:T(8,128)S(1)}, f32[8192,128]{1,0:T(8,128)S(1)}) custom-call(s32[8192]{0:T(1024)S(1)} %fusion.28.ids_ref, f32[16,256]{1,0:T(8,128)S(1)} %pad.17.scale_ref, bf16[16,128,8448]{2,1,0:T(8,128)(2,1)} %bitcast.58, bf16[16,128,8448]{2,1,0:T(8,128)(2,1)} %bitcast.59, f32[1,8192]{1,0:T(1,128)S(1)} %get-tuple-element.77.refs_2_.refs_1_), custom_call_target="tpu_custom_call" | custom-call | bytes 80000000 | tf_op jit(solution)/shard_map/relation_rows/pallas_call | solution.py:139
  268.1 10.0 %collective-permute-done.refs_3_ = bf16[96,8192]{1,0:T(8,128)(2,1)} collective-permute-done((bf16[96,8192]{1,0:T(8,128)(2,1)}, bf16[96,8192]{1,0:T(8,128)(2,1)}, u32[]{:S(2)}, u32[]{:S(2)}) %collective-permute-start) | collective-permute-done | bytes 1572896 | tf_op jit(solution)/shard_map/ppermute | solution.py:853
  278.8 9.3 %all-gather.8.cloned.1.call-done = bf16[1152,7936]{1,0:T(8,128)(2,1)} async-done(((bf16[72,7936]{1,0:T(8,128)(2,1)}), bf16[1152,7936]{1,0:T(8,128)(2,1)}) %all-gather.8.cloned.1.call-update) | async-done | bytes 18284560 | tf_op jit(solution)/shard_map/all_gather | solution.py:841
  288.1 45.2 %fetch_rows.3.head_ref.tail_ref.neg_ref = f32[24584,128]{1,0:T(8,128)S(1)} custom-call(s32[16]{0:T(128)S(1)} %convert_element_type.79.counts_ref, s32[32768]{0:T(1024)S(1)} %bitcast.46, s32[32768]{0:T(1024)S(1)} %bitcast.49, bf16[16,72,7936]{2,1,0:T(8,128)(2,1)} %bitcast.61, bf16[8,128]{1,0:T(8,128)(2,1)S(1)} %slice.120.refs_0_), custom_call_target="tpu_custom_call" | custom-call | bytes 170000000 | tf_op jit(solution)/shard_map/fetch_rows/pallas_call | solution.py:231
  333.3 4.6 last_slice.2
  343.3 4.6 copy-done.1
  357.5 5.1 all-to-all-start.1
  363.3 5.1 all-to-all-done.1
  369.0 3.4 collective-permute-done.3.refs_5_
  372.4 26.0 %block_math.2 = (f32[3,16384,128]{2,1,0:T(8,128)}, f32[8,128]{1,0:T(8,128)}) custom-call(s32[1]{0:T(128)} %bitcast.10.me_ref, s32[8]{0:T(128)} %live_ref.3, bf16[96,8192]{1,0:T(8,128)(2,1)} %get-tuple-element.76.refs_0_, bf16[160,8192]{1,0:T(8,128)(2,1)} %copy-done.12, bf16[2,80,4096]{2,1,0:T(8,128)(2,1)} %get-tuple-element.90.refs_2_, ...), custom_call_target="tpu_custom_call" | custom-call | flops 6710886400 | bytes 120000000 | tf_op jit(solution)/shard_map/block_math/pallas_call | solution.py:525
  399.8 26.2 %block_math.3 = (f32[3,16384,128]{2,1,0:T(8,128)}, f32[8,128]{1,0:T(8,128)}) custom-call(s32[1]{0:T(128)} %bitcast.10.me_ref, s32[8]{0:T(128)} %live_ref.3, bf16[96,8192]{1,0:T(8,128)(2,1)} %get-tuple-element.76.refs_0_, bf16[160,8192]{1,0:T(8,128)(2,1)} %copy-done.12, bf16[2,80,4096]{2,1,0:T(8,128)(2,1)} %copy-done.17, ...), custom_call_target="tpu_custom_call", output_to_operand_aliasing={{0}: (12, {})} | custom-call | flops 6710886400 | bytes 120000000 | tf_op jit(solution)/shard_map/block_math/pallas_call | solution.py:525
  426.0 22.0 %outgoing.5 = (bf16[16,200,384]{2,1,0:T(8,128)(2,1)S(1)}, f32[8,128]{1,0:T(8,128)S(1)}) custom-call(s32[16]{0:T(128)S(1)} %convert_element_type.79.counts_ref, s32[32768]{0:T(1024)S(1)} %broadcast_minimum_fusion.place_ref, f32[49152,128]{1,0:T(8,128)} %bitcast.52), custom_call_target="tpu_custom_call" | custom-call | bytes 80000000 | tf_op jit(solution)/shard_map/outgoing/pallas_call | solution.py:621
  449.5 5.3 all-to-all-start.2
  458.0 9.6 %excess_rows.1 = (bf16[1,208,384]{2,1,0:T(8,128)(2,1)S(1)}, f32[8,128]{1,0:T(8,128)S(1)}) custom-call(s32[1]{0:T(128)} %dynamic_slice.6.counts_ref, s32[2048]{0:T(1024)S(1)} %bitcast.51, s32[8]{0:T(128)S(1)} %broadcast_minimum_fusion.1.live_ref, f32[49152,128]{1,0:T(8,128)} %bitcast.53, f32[8,128]{1,0:T(8,128)S(1)} %add.195.loss_ref, ...), custom_call_target="tpu_custom_call" | custom-call | bytes 80000000 | tf_op jit(solution)/shard_map/excess_rows/pallas_call | solution.py:602
  467.7 39.0 %outgoing.6 = (bf16[16,200,896]{2,1,0:T(8,128)(2,1)S(1)}, f32[8,128]{1,0:T(8,128)S(1)}) custom-call(s32[16]{0:T(128)S(1)} %convert_element_type.79.counts_ref, s32[32768]{0:T(1024)S(1)} %broadcast_minimum_fusion.place_ref, f32[49152,128]{1,0:T(8,128)} %bitcast.54, f32[8,128]{1,0:T(8,128)S(1)} %get-tuple-element.100.refs_0_.refs_1_), custom_call_target="tpu_custom_call" | custom-call | bytes 80000000 | tf_op jit(solution)/shard_map/outgoing/pallas_call | solution.py:621
  510.1 5.1 all-to-all-start.4
  515.3 31.1 %relation_sums.1 = (f32[6400,128]{1,0:T(8,128)S(1)}, f32[8,128]{1,0:T(8,128)S(1)}) custom-call(s32[8192]{0:T(1024)S(1)} %copy-done.19, f32[3,16384,128]{2,1,0:T(8,128)} %get-tuple-element.94.grad, bf16[8,128]{1,0:T(8,128)(2,1)S(1)} %slice_bitcast_fusion.1.refs_0_, f32[8,128]{1,0:T(8,128)S(1)} %get-tuple-element.100.refs_0_.refs_1_, ...), custom_call_target="tpu_custom_call" | custom-call | bytes 120000000 | tf_op jit(solution)/shard_map/relation_sums/pallas_call | solution.py:704
  548.1 4.9 reshape.779
  553.2 26.2 %collect.2 = (f32[15888,128]{1,0:T(8,128)S(1)}, f32[8,128]{1,0:T(8,128)S(1)}) custom-call(s32[16]{0:T(128)S(1)} %get-tuple-element.133.counts_ref, s32[32768]{0:T(1024)S(1)} %bitcast.42, bf16[16,200,384]{2,1,0:T(8,128)(2,1)S(1)} %all-to-all-done.2.came_ref, f32[8,128]{1,0:T(8,128)S(1)} %get-tuple-element.102.refs_0_), custom_call_target="tpu_custom_call" | custom-call | bytes 120000000 | tf_op jit(solution)/shard_map/collect/pallas_call | solution.py:672
  579.4 3.2 copy-done.3
  582.6 67.1 %reduce-scatter.2.cloned.1.call-done = f32[200,200]{1,0:T(8,128)} async-done(((f32[3200,200]{1,0:T(8,128)}), f32[200,200]{1,0:T(8,128)}) %reduce-scatter.2.cloned.1.call-update) | async-done | bytes 160016 | tf_op jit(solution)/shard_map/reduce_scatter | solution.py:955
  650.3 19.0 %outgoing.7 = (bf16[16,200,384]{2,1,0:T(8,128)(2,1)}, f32[8,128]{1,0:T(8,128)S(1)}) custom-call(s32[16]{0:T(128)S(1)} %convert_element_type.79.counts_ref, s32[32768]{0:T(1024)S(1)} %broadcast_minimum_fusion.place_ref, f32[49152,128]{1,0:T(8,128)} %bitcast.55, f32[8,128]{1,0:T(8,128)S(1)} %get-tuple-element.103.refs_0_, f32[8,128]{1,0:T(8,128)S(1)} %slice.125.refs_1_), custom_call_target="tpu_custom_call" | custom-call | bytes 80000000 | tf_op jit(solution)/shard_map/outgoing/pallas_call | solution.py:621
  673.7 5.9 all-to-all-start.3
  682.9 3.3 copy-done.4
  686.2 62.8 %collect.3 = (f32[15888,128]{1,0:T(8,128)S(1)}, f32[8,128]{1,0:T(8,128)S(1)}) custom-call(s32[16]{0:T(128)S(1)} %get-tuple-element.133.counts_ref, s32[32768]{0:T(1024)S(1)} %bitcast.43, bf16[16,200,896]{2,1,0:T(8,128)(2,1)} %all-to-all-done.4.came_ref, f32[15888,128]{1,0:T(8,128)S(1)} %copy-done.4, ...), custom_call_target="tpu_custom_call", output_to_operand_aliasing={{0}: (3, {})} | custom-call | bytes 120000000 | tf_op jit(solution)/shard_map/collect/pallas_call | solution.py:672
  749.1 3.2 copy-done.5
  756.6 37.6 %finish_entities.1 = (f32[200,7936]{1,0:T(8,128)}, f32[200,7936]{1,0:T(8,128)}, f32[200,7936]{1,0:T(8,128)}, f32[8,128]{1,0:T(8,128)}) custom-call(s32[16]{0:T(128)} %copy-done.20, s32[32768]{0:T(1024)} %bitcast.44, bf16[16,200,384]{2,1,0:T(8,128)(2,1)} %copy-done.23, bf16[16,208,384]{2,1,0:T(8,128)(2,1)S(1)} %get-tuple-element.138.last_ref, ...), custom_call_target="tpu_custom_call" | custom-call | bytes 60000000 | tf_op jit(solution)/shard_map/finish_entities/pallas_call | solution.py:777
  (164 shorter events, 68.2 us)
Async XLA Ops:
  7.2 183.1 %all-gather.10.cloned.1.call-start = ((), (), s32[]{:S(2)}) async-start(), calls=%async_computation.9 | async-start | bytes 36765696 | tf_op jit(solution)/shard_map/all_gather | solution.py:841
  16.0 272.0 %all-gather.8.cloned.1.call-start = ((), (), s32[]{:S(2)}) async-start(), calls=%async_computation.8 | async-start | bytes 19427328 | tf_op jit(solution)/shard_map/all_gather | solution.py:841
  33.4 12.0 %copy-start.30 = (f32[3200]{0:T(1024)S(1)}, f32[3200]{0:T(1024)}, u32[]{:S(2)}) copy-start(f32[3200]{0:T(1024)} %param.22) | copy-start | bytes 38404
  234.7 5.8 copy-start.2
  234.8 7.3 copy-start.31
  234.8 7.4 copy-start.19
  240.6 37.5 %collective-permute-start = (bf16[96,8192]{1,0:T(8,128)(2,1)}, bf16[96,8192]{1,0:T(8,128)(2,1)}, u32[]{:S(2)}, u32[]{:S(2)}) collective-permute-start(bf16[96,8192]{1,0:T(8,128)(2,1)} %get-tuple-element.76.refs_0_), channel_id=1, source_target_pairs={{0,1},{1,0},{2,3},{3,2},{4,5},{5,4},{6,7},{7,6},{8,9},{9,8},{10,11... | collective-permute-start | bytes 4718600 | tf_op jit(solution)/shard_map/ppermute | solution.py:853
  242.2 18.6 %slice-start = ((s8[12587008]{0:T(1024)(128)(4,1)}), s8[4194304]{0:T(1024)(128)(4,1)S(1)}, s32[]{:S(2)}) async-start(s8[12587008]{0:T(1024)(128)(4,1)} %bitcast.40), calls=%async_computation.10 | async-start | bytes 8388608
  242.2 18.6 %slice-start.1 = ((s8[12587008]{0:T(1024)(128)(4,1)}), s8[4194304]{0:T(1024)(128)(4,1)S(1)}, s32[]{:S(2)}) async-start(s8[12587008]{0:T(1024)(128)(4,1)} %bitcast.40), calls=%async_computation.11 | async-start | bytes 8388608
  242.2 18.6 %slice-start.2 = ((s8[12587008]{0:T(1024)(128)(4,1)}), s8[4194304]{0:T(1024)(128)(4,1)S(1)}, s32[]{:S(2)}) async-start(s8[12587008]{0:T(1024)(128)(4,1)} %bitcast.40), calls=%async_computation.12 | async-start | bytes 8388608
  242.2 18.6 %slice-start.3 = ((s8[12587008]{0:T(1024)(128)(4,1)}), s8[4096]{0:T(1024)(128)(4,1)S(1)}, s32[]{:S(2)}) async-start(s8[12587008]{0:T(1024)(128)(4,1)} %bitcast.40), calls=%async_computation.13 | async-start | bytes 8192
  267.5 65.8 %copy-start.12 = (bf16[160,8192]{1,0:T(8,128)(2,1)}, bf16[160,8192]{1,0:T(8,128)(2,1)S(1)}, u32[]{:S(2)}) copy-start(bf16[160,8192]{1,0:T(8,128)(2,1)S(1)} %get-tuple-element.84.refs_1_) | copy-start | bytes 7864324
  267.5 101.5 %collective-permute-start.1 = (bf16[160,8192]{1,0:T(8,128)(2,1)S(1)}, bf16[160,8192]{1,0:T(8,128)(2,1)}, u32[]{:S(2)}, u32[]{:S(2)}) collective-permute-start(bf16[160,8192]{1,0:T(8,128)(2,1)S(1)} %get-tuple-element.84.refs_1_), channel_id=1, source_target_pairs={{0,1},{1,0},{2,3},{3,2},{4,5},{5,4},{6,7},{7,6},{8,9},{9,8},{10,11... | collective-permute-start | bytes 7864328 | tf_op jit(solution)/shard_map/ppermute | solution.py:853
  288.1 45.2 %copy-start.7 = (f32[8192,128]{1,0:T(8,128)S(1)}, f32[8192,128]{1,0:T(8,128)}, u32[]{:S(2)}) copy-start(f32[8192,128]{1,0:T(8,128)} %copy-done.6) | copy-start | bytes 12582916
  333.3 4.9 copy-start
  333.3 9.9 %copy-start.26 = (s32[256,128]{1,0:T(8,128)S(1)}, s32[256,128]{1,0:T(8,128)}, u32[]{:S(2)}) copy-start(s32[256,128]{1,0:T(8,128)} %get-tuple-element.130) | copy-start | bytes 393220
  340.5 31.9 %collective-permute-start.3 = (bf16[2,80,4096]{2,1,0:T(8,128)(2,1)}, bf16[2,80,4096]{2,1,0:T(8,128)(2,1)}, u32[]{:S(2)}, u32[]{:S(2)}) collective-permute-start(bf16[2,80,4096]{2,1,0:T(8,128)(2,1)} %get-tuple-element.90.refs_2_), channel_id=1, source_target_pairs={{0,1},{1,0},{2,3},{3,2},{4,5},{5,4},{6,7},{7,6},{8,9},{9,8},{10,11... | collective-permute-start | bytes 3932168 | tf_op jit(solution)/shard_map/ppermute | solution.py:853
  343.3 4.6 copy-start.1
  357.5 10.9 %all-to-all-start.1 = ((s32[16,1,2176]{2,1,0:T(1,128)}), s32[16,1,2176]{2,1,0:T(1,128)S(1)}, u32[]{:S(2)}, u32[]{:S(2)}) async-start(s32[16,1,2176]{2,1,0:T(1,128)} %all_to_all.20), calls=%async_computation.1 | async-start | bytes 278528 | tf_op jit(solution)/shard_map/all_to_all | solution.py:900
  362.6 37.2 %collective-permute-start.2 = (bf16[2,80,4096]{2,1,0:T(8,128)(2,1)}, bf16[2,80,4096]{2,1,0:T(8,128)(2,1)}, u32[]{:S(2)}, u32[]{:S(2)}) collective-permute-start(bf16[2,80,4096]{2,1,0:T(8,128)(2,1)} %copy-done.17), channel_id=1, source_target_pairs={{0,1},{1,0},{2,3},{3,2},{4,5},{5,4},{6,7},{7,6},{8,9},{9,8},{10,11... | collective-permute-start | bytes 3932168 | tf_op jit(solution)/shard_map/ppermute | solution.py:853
  449.5 5.3 copy-start.25
  449.5 8.5 %copy-start.34 = (s32[8]{0:T(128)S(1)}, s32[8]{0:T(128)}, u32[]{:S(2)}) copy-start(s32[8]{0:T(128)} %live_ref.3) | copy-start | bytes 100
  449.5 8.5 %copy-start.32 = (f32[8,128]{1,0:T(8,128)S(1)}, f32[8,128]{1,0:T(8,128)}, u32[]{:S(2)}) copy-start(f32[8,128]{1,0:T(8,128)} %get-tuple-element.97) | copy-start | bytes 12292
  449.5 8.5 %copy-start.33 = (f32[8,128]{1,0:T(8,128)S(1)}, f32[8,128]{1,0:T(8,128)}, u32[]{:S(2)}) copy-start(f32[8,128]{1,0:T(8,128)} %get-tuple-element.98) | copy-start | bytes 12292
  449.5 60.6 %all-to-all-start.2 = ((bf16[16,200,384]{2,1,0:T(8,128)(2,1)}), bf16[16,200,384]{2,1,0:T(8,128)(2,1)S(1)}, u32[]{:S(2)}, u32[]{:S(2)}) async-start(bf16[16,200,384]{2,1,0:T(8,128)(2,1)} %copy-done.13), calls=%async_computation.2 | async-start | bytes 4915200 | tf_op jit(solution)/shard_map/all_to_all | solution.py:935
  510.1 163.5 %all-to-all-start.4 = ((bf16[16,200,896]{2,1,0:T(8,128)(2,1)}), bf16[16,200,896]{2,1,0:T(8,128)(2,1)}, u32[]{:S(2)}, u32[]{:S(2)}) async-start(bf16[16,200,896]{2,1,0:T(8,128)(2,1)} %copy-done.9), calls=%async_computation.5 | async-start | bytes 11468800 | tf_op jit(solution)/shard_map/all_to_all | solution.py:935
  515.2 134.4 %reduce-scatter.2.cloned.1.call-start = ((), (), s32[]{:S(2)}) async-start(), calls=%async_computation.6 | async-start | bytes 3481600 | tf_op jit(solution)/shard_map/reduce_scatter | solution.py:955
  553.0 201.7 %all-gather.6.cloned.1.call-start = ((), (), s32[]{:S(2)}) async-start(), calls=%async_computation.7 | async-start | bytes 2715648 | tf_op jit(solution)/shard_map/all_gather | solution.py:959
  553.2 129.7 %copy-start.20 = (s32[16]{0:T(128)}, s32[16]{0:T(128)S(1)}, u32[]{:S(2)}) copy-start(s32[16]{0:T(128)S(1)} %get-tuple-element.133.counts_ref) | copy-start | bytes 196
  553.2 129.7 %copy-start.14 = (s32[2,16,8,128]{3,1,2,0:T(8,128)}, s32[2,16,8,128]{3,1,2,0:T(8,128)S(1)}, u32[]{:S(2)}) copy-start(s32[2,16,8,128]{3,1,2,0:T(8,128)S(1)} %copy.42) | copy-start | bytes 393220
  673.6 7.2 copy-start.24
  673.7 79.7 %all-to-all-start.3 = ((bf16[16,200,384]{2,1,0:T(8,128)(2,1)}), bf16[16,200,384]{2,1,0:T(8,128)(2,1)S(1)}, u32[]{:S(2)}, u32[]{:S(2)}) async-start(bf16[16,200,384]{2,1,0:T(8,128)(2,1)} %get-tuple-element.105), calls=%async_computation.4 | async-start | bytes 4915200 | tf_op jit(solution)/shard_map/all_to_all | solution.py:935
  (19 other events, 34.0 us)
Sparse Core Ops, SparseCore 0:
  16.2 174.0 all-gather.9
  191.9 96.1 all-gather.7
  553.1 96.4 reduce-scatter.1
  673.8 69.4 all-gather.5

commit v14 on v13

--- a/solution.py
+++ b/solution.py
@@ -241,7 +241,7 @@
         + [whole(pl.ANY)] * len(after),
         out_specs=whole(VMEM),
         scratch_shapes=[pltpu.VMEM((ent_rows + 8, LANES), F32)] * 2,
-        compiler_params=params(32),
+        compiler_params=params(26),
         cost_estimate=cost(0, 170e6),
         name="fetch_rows",
     )(counts, place_list, row_list, dense, *after)
@@ -274,7 +274,7 @@
             pl.BlockSpec((LANES - EARLY, block_len), lambda b: (0, b)),
             pl.BlockSpec((1, block_len), lambda b: (0, b)),
         ],
-        compiler_params=params(12),
+        compiler_params=params(5),
         cost_estimate=cost(0, 10e6),
         name="negatives",
     )(fetched)
@@ -325,7 +325,7 @@
             pl.BlockSpec((tall, block_len), lambda b: (0, b)),
             pl.BlockSpec((1, block_len), lambda b: (0, b)),
         ],
-        compiler_params=params(16),
+        compiler_params=params(9),
         cost_estimate=cost(0, 30e6),
         name="edges",
     )(fetched, fetched, rel_rows, late)
@@ -393,7 +393,7 @@
             pl.BlockSpec((2, tall, block_len), lambda b: (0, 0, b)),
             pl.BlockSpec((8, LANES), lambda b: (0, 0)),
         ],
-        compiler_params=params(16),
+        compiler_params=params(9),
         cost_estimate=cost(0, 20e6),
         name="last_slice",
     )(fetched, fetched, fetched, rel_rows, *biases, *norms, *after)
@@ -557,6 +557,23 @@
     return pl.ds(pl.multiple_of(row * n, n), n)
 
 
+def pass_on_kernel(array_ref, *refs):
+    refs[-1][...] = jnp.zeros((8, LANES), F32)
+
+
+def pass_on(array, after):
+    return pl.pallas_call(
+        pass_on_kernel,
+        out_shape=[jax.ShapeDtypeStruct(array.shape, array.dtype), token_shape()],
+        in_specs=[whole(pl.ANY)] * (1 + len(after)),
+        out_specs=[whole(pl.ANY), whole(VMEM)],
+        input_output_aliases={0: 0},
+        compiler_params=params(2),
+        cost_estimate=cost(0, 1e3),
+        name="pass_on",
+    )(array, *after)[0]
+
+
 def outgoing_kernel(slices, capacity, begin, counts_ref, place_ref, grad, *refs):
     n = len(slices)
     out_ref, token, tile = refs[-3:]
@@ -852,13 +869,16 @@
         turns = [[(c, (c + away) % n_col) for c in range(n_col)] for away in range(1, n_col)]
         return [lax.ppermute(array, "col", turn) for turn in turns]
 
+    bounds = chunk_bounds(capacity)
+    few = jnp.sum((counts > bounds[-2]).astype(jnp.int32)) <= 1
+    flag = jnp.broadcast_to(few.astype(jnp.int32), (groups, LANES))
     me = lax.axis_index("col").astype(jnp.int32).reshape(1)
     given = [[[] for _ in range(n_col)] for _ in range(HALVES)]
     offs = [[] for _ in range(HALVES)]
     tails = [[] for _ in range(HALVES)]
     biases, norms, first_sent, rel_rows = [], [], [], None
     for k, (start, depth) in enumerate(slices):
-        sent = first_sent if k > 0 else []
+        sent = first_sent if k > 0 else [flag]
         fetched = fetch(counts, place_flat, row_flat, dense[k], id_count, ent_rows, sent)
         if k < n - 1:
             early, late, norm = negatives(fetched, blocks, block_len)
@@ -893,10 +913,7 @@
     half_token = []
     for half in range(HALVES):
         half_token = [finish(half, half_token)]
-    bounds = chunk_bounds(capacity)
-    few = jnp.sum((counts > bounds[-2]).astype(jnp.int32)) <= 1
-    flag = few.astype(jnp.int32) + half_token[0][0, 0].astype(jnp.int32)
-    flag = jnp.broadcast_to(flag, (groups, LANES))
+    flag = flag + half_token[0][0, 0].astype(jnp.int32)
     asked = lax.all_to_all(
         jnp.concatenate([row_list, flag], axis=1), "edge", split_axis=0, concat_axis=0, tiled=True
     )
@@ -932,6 +949,8 @@
         sent, sent_token = outgoing(
             counts, safe_places, flat, slices, bounds[k], bounds[k + 1] - bounds[k], after
         )
+        if k == chunks - 2:
+            sent = pass_on(sent, [corner(relation_grad)])
         arrived.append(lax.all_to_all(sent, "edge", split_axis=0, concat_axis=0, tiled=True))
         after = []
         if k == 0:
@@ -962,7 +981,7 @@
             total, token = collect(
                 asked_counts, asked, arrived[k - 1], total, slices, bounds[k - 1], ent_rows, after
             )
-            after = [token, corner(relation_grad)]
+            after = [token]
 
     def by_all_to_all():
         spare = last_rows(width) + SPARE - width

time: 811 us -> 797 us (0.983)
  waiting for transfers between devices: 238 us -> 225 us
    reduce_scatter x1, waiting for transfers between devices: 67.1 us -> 46.8 us  [shards(): lax.psum_scatter(rel_terms, 'edge', scatter_dimension=0, tiled=True)]
  transfers between devices with their start and end apart: 12 -> 12, of which waited for: 8 -> 9; matrix products, arithmetic and copies ran while one was open for 6% -> 6% of each run, Pallas kernels for 42% -> 43%
where the time goes in v14:
time: 797 us; the launch traced here: 788 us
  Pallas kernels  422 us (53%)
  waiting for transfers between devices  225 us (28%)
  local copies, waits for them, and re-layouts  52 us (7%)
  other arithmetic  29.7 us (4%)
  starting transfers between devices  24.5 us (3%)
  between operations  22.3 us (3%)
  matrix products  12.3 us (2%)
    all_gather x2, waiting for transfers between devices, shards(): dense.append(lax.all_gather(sent, 'edge', axis=0, tiled=False))  149 us
    pallas_call x2, Pallas kernels, fetch(): pl.pallas_call(functools.partial(fetch_kernel, capacity, moves, ent_rows)...  89.7 us
    pallas_call x2, Pallas kernels, collect(): pl.pallas_call(functools.partial(collect_kernel, slices, capacity, begin,...  89 us
    pallas_call x3, Pallas kernels, outgoing(): pl.pallas_call(functools.partial(outgoing_kernel, slices, capacity, begin...  80.1 us
    pallas_call x2, Pallas kernels, block_math(): pl.pallas_call(functools.partial(block_kernel, slices, n_col, half), out_...  52.2 us
    reduce_scatter x1, waiting for transfers between devices, shards(): lax.psum_scatter(rel_terms, 'edge', scatter_dimension=0, tiled=True)  46.8 us
    pallas_call x1, Pallas kernels, finish_entities(): pl.pallas_call(functools.partial(finish_kernel, slices, capacity, begin,...  37.3 us
    unnamed x85, local copies, waits for them, and re-layouts  33.9 us
  transfers between devices with their start and end apart: 12, of which 9 were waited for; matrix products, arithmetic and copies ran while one was open for 6% of the time, Pallas kernels for 43%

profile of v14, /device:TPU:16, one launch (start us, length us, event | category | flops | bytes accessed | tf_op | source)
XLA Modules:
  0.0 787.8 jit_solution(4158284829532652389)
XLA Ops:
  24.6 8.7 %broadcast_multiply_fusion = bf16[4,128,24576]{2,1,0:T(8,128)(2,1)} fusion(bf16[128,24576]{1,0:T(8,128)(2,1)S(1)} %fusion.2, bf16[4,24576]{1,0:T(4,128)(2,1)S(1)} %pad_maximum_fusion), kind=kLoop, calls=%fused_computation.3 | loop fusion | flops 12582912 | bytes 31653888 | tf_op jit(solution)/shard_map/mul | solution.py:93
  33.3 11.8 %fusion.8 = s32[256,512]{1,0:T(8,128)S(1)} fusion(bf16[512,24576]{1,0:T(8,128)(2,1)} %bitcast.60, s32[24576]{0:T(1024)S(1)} %get-tuple-element.136), kind=kOutput, calls=%fused_computation.17 | convolution fusion | flops 6448873472 | bytes 25788416 | tf_op jit(solution)/shard_map/dot_general | solution.py:94
  50.4 139.9 %all-gather.10.cloned.1.call-done = bf16[2048,8448]{1,0:T(8,128)(2,1)} async-done(((bf16[128,8448]{1,0:T(8,128)(2,1)}), bf16[2048,8448]{1,0:T(8,128)(2,1)}) %all-gather.10.cloned.1.call-update) | async-done | bytes 34603024 | tf_op jit(solution)/shard_map/all_gather | solution.py:858
  190.3 44.5 %fetch_rows.2.neg_ref.head_ref.tail_ref = f32[24584,128]{1,0:T(8,128)S(1)} custom-call(s32[16]{0:T(128)S(1)} %convert_element_type.79.counts_ref, s32[32768]{0:T(1024)S(1)} %bitcast.45, s32[32768]{0:T(1024)S(1)} %bitcast.48, bf16[16,128,8448]{2,1,0:T(8,128)(2,1)} %bitcast.57, s32[16,128]{1,0:T(8,128)S(1)} %broadcast_in_dim.35.refs_0_), custom_call_target="tpu_custom_call" | custom-call | bytes 170000000 | tf_op jit(solution)/shard_map/fetch_rows/pallas_call | solution.py:231
  234.8 5.8 negatives.1
  242.3 16.6 %relation_rows.1 = (f32[8192,128]{1,0:T(8,128)S(1)}, f32[8192,128]{1,0:T(8,128)S(1)}) custom-call(s32[8192]{0:T(1024)S(1)} %fusion.28.ids_ref, f32[16,256]{1,0:T(8,128)S(1)} %pad.17.scale_ref, bf16[16,128,8448]{2,1,0:T(8,128)(2,1)} %bitcast.58, bf16[16,128,8448]{2,1,0:T(8,128)(2,1)} %bitcast.59, f32[1,8192]{1,0:T(1,128)S(1)} %get-tuple-element.78.refs_2_.refs_1_), custom_call_target="tpu_custom_call" | custom-call | bytes 80000000 | tf_op jit(solution)/shard_map/relation_rows/pallas_call | solution.py:139
  261.0 3.2 edges.1
  268.2 10.0 %collective-permute-done.refs_3_ = bf16[96,8192]{1,0:T(8,128)(2,1)} collective-permute-done((bf16[96,8192]{1,0:T(8,128)(2,1)}, bf16[96,8192]{1,0:T(8,128)(2,1)}, u32[]{:S(2)}, u32[]{:S(2)}) %collective-permute-start) | collective-permute-done | bytes 1572896 | tf_op jit(solution)/shard_map/ppermute | solution.py:870
  278.9 9.2 %all-gather.8.cloned.1.call-done = bf16[1152,7936]{1,0:T(8,128)(2,1)} async-done(((bf16[72,7936]{1,0:T(8,128)(2,1)}), bf16[1152,7936]{1,0:T(8,128)(2,1)}) %all-gather.8.cloned.1.call-update) | async-done | bytes 18284560 | tf_op jit(solution)/shard_map/all_gather | solution.py:858
  288.1 45.2 %fetch_rows.3.head_ref.tail_ref.neg_ref = f32[24584,128]{1,0:T(8,128)S(1)} custom-call(s32[16]{0:T(128)S(1)} %convert_element_type.79.counts_ref, s32[32768]{0:T(1024)S(1)} %bitcast.46, s32[32768]{0:T(1024)S(1)} %bitcast.49, bf16[16,72,7936]{2,1,0:T(8,128)(2,1)} %bitcast.61, bf16[8,128]{1,0:T(8,128)(2,1)S(1)} %slice.120.refs_0_), custom_call_target="tpu_custom_call" | custom-call | bytes 170000000 | tf_op jit(solution)/shard_map/fetch_rows/pallas_call | solution.py:231
  333.4 4.6 last_slice.2
  342.0 4.6 copy-done.1
  356.3 5.1 all-to-all-start.1
  362.0 5.1 all-to-all-done.1
  367.7 4.8 collective-permute-done.3.refs_5_
  372.4 26.0 %block_math.2 = (f32[3,16384,128]{2,1,0:T(8,128)}, f32[8,128]{1,0:T(8,128)}) custom-call(s32[1]{0:T(128)} %bitcast.10.me_ref, s32[8]{0:T(128)} %live_ref.3, bf16[96,8192]{1,0:T(8,128)(2,1)} %get-tuple-element.77.refs_0_, bf16[160,8192]{1,0:T(8,128)(2,1)} %copy-done.12, bf16[2,80,4096]{2,1,0:T(8,128)(2,1)} %get-tuple-element.91.refs_2_, ...), custom_call_target="tpu_custom_call" | custom-call | flops 6710886400 | bytes 120000000 | tf_op jit(solution)/shard_map/block_math/pallas_call | solution.py:525
  399.8 26.2 %block_math.3 = (f32[3,16384,128]{2,1,0:T(8,128)}, f32[8,128]{1,0:T(8,128)}) custom-call(s32[1]{0:T(128)} %bitcast.10.me_ref, s32[8]{0:T(128)} %live_ref.3, bf16[96,8192]{1,0:T(8,128)(2,1)} %get-tuple-element.77.refs_0_, bf16[160,8192]{1,0:T(8,128)(2,1)} %copy-done.12, bf16[2,80,4096]{2,1,0:T(8,128)(2,1)} %copy-done.17, ...), custom_call_target="tpu_custom_call", output_to_operand_aliasing={{0}: (12, {})} | custom-call | flops 6710886400 | bytes 120000000 | tf_op jit(solution)/shard_map/block_math/pallas_call | solution.py:525
  426.0 22.0 %outgoing.5 = (bf16[16,200,384]{2,1,0:T(8,128)(2,1)S(1)}, f32[8,128]{1,0:T(8,128)S(1)}) custom-call(s32[16]{0:T(128)S(1)} %convert_element_type.79.counts_ref, s32[32768]{0:T(1024)S(1)} %broadcast_minimum_fusion.place_ref, f32[49152,128]{1,0:T(8,128)} %bitcast.52), custom_call_target="tpu_custom_call" | custom-call | bytes 80000000 | tf_op jit(solution)/shard_map/outgoing/pallas_call | solution.py:638
  449.5 5.3 all-to-all-start.2
  458.1 9.6 %excess_rows.1 = (bf16[1,208,384]{2,1,0:T(8,128)(2,1)S(1)}, f32[8,128]{1,0:T(8,128)S(1)}) custom-call(s32[1]{0:T(128)} %dynamic_slice.6.counts_ref, s32[2048]{0:T(1024)S(1)} %bitcast.51, s32[8]{0:T(128)S(1)} %broadcast_minimum_fusion.1.live_ref, f32[49152,128]{1,0:T(8,128)} %bitcast.53, f32[8,128]{1,0:T(8,128)S(1)} %add.197.loss_ref, ...), custom_call_target="tpu_custom_call" | custom-call | bytes 80000000 | tf_op jit(solution)/shard_map/excess_rows/pallas_call | solution.py:619
  467.7 39.0 %outgoing.6 = (bf16[16,200,896]{2,1,0:T(8,128)(2,1)S(1)}, f32[8,128]{1,0:T(8,128)S(1)}) custom-call(s32[16]{0:T(128)S(1)} %convert_element_type.79.counts_ref, s32[32768]{0:T(1024)S(1)} %broadcast_minimum_fusion.place_ref, f32[49152,128]{1,0:T(8,128)} %bitcast.54, f32[8,128]{1,0:T(8,128)S(1)} %get-tuple-element.101.refs_0_.refs_1_), custom_call_target="tpu_custom_call" | custom-call | bytes 80000000 | tf_op jit(solution)/shard_map/outgoing/pallas_call | solution.py:638
  510.2 5.1 all-to-all-start.4
  515.3 31.1 %relation_sums.1 = (f32[6400,128]{1,0:T(8,128)S(1)}, f32[8,128]{1,0:T(8,128)S(1)}) custom-call(s32[8192]{0:T(1024)S(1)} %copy-done.19, f32[3,16384,128]{2,1,0:T(8,128)} %get-tuple-element.95.grad, bf16[8,128]{1,0:T(8,128)(2,1)S(1)} %slice_bitcast_fusion.1.refs_0_, f32[8,128]{1,0:T(8,128)S(1)} %get-tuple-element.101.refs_0_.refs_1_, ...), custom_call_target="tpu_custom_call" | custom-call | bytes 120000000 | tf_op jit(solution)/shard_map/relation_sums/pallas_call | solution.py:721
  548.1 4.9 reshape.779
  553.3 26.2 %collect.2 = (f32[15888,128]{1,0:T(8,128)S(1)}, f32[8,128]{1,0:T(8,128)S(1)}) custom-call(s32[16]{0:T(128)S(1)} %get-tuple-element.135.counts_ref, s32[32768]{0:T(1024)S(1)} %bitcast.42, bf16[16,200,384]{2,1,0:T(8,128)(2,1)S(1)} %all-to-all-done.2.came_ref, f32[8,128]{1,0:T(8,128)S(1)} %get-tuple-element.103.refs_0_), custom_call_target="tpu_custom_call" | custom-call | bytes 120000000 | tf_op jit(solution)/shard_map/collect/pallas_call | solution.py:689
  582.6 19.1 %outgoing.7 = (bf16[16,200,384]{2,1,0:T(8,128)(2,1)}, f32[8,128]{1,0:T(8,128)S(1)}) custom-call(s32[16]{0:T(128)S(1)} %convert_element_type.79.counts_ref, s32[32768]{0:T(1024)S(1)} %broadcast_minimum_fusion.place_ref, f32[49152,128]{1,0:T(8,128)} %bitcast.55, f32[8,128]{1,0:T(8,128)S(1)} %get-tuple-element.104.refs_0_), custom_call_target="tpu_custom_call" | custom-call | bytes 80000000 | tf_op jit(solution)/shard_map/outgoing/pallas_call | solution.py:638
  602.9 46.8 %reduce-scatter.2.cloned.1.call-done = f32[200,200]{1,0:T(8,128)} async-done(((f32[3200,200]{1,0:T(8,128)}), f32[200,200]{1,0:T(8,128)}) %reduce-scatter.2.cloned.1.call-update) | async-done | bytes 160016 | tf_op jit(solution)/shard_map/reduce_scatter | solution.py:974
  654.1 6.8 all-to-all-done.4.came_ref
  660.9 4.7 all-to-all-start.3
  668.9 3.3 copy-done.4
  672.3 62.8 %collect.3 = (f32[15888,128]{1,0:T(8,128)S(1)}, f32[8,128]{1,0:T(8,128)S(1)}) custom-call(s32[16]{0:T(128)S(1)} %get-tuple-element.135.counts_ref, s32[32768]{0:T(1024)S(1)} %bitcast.43, bf16[16,200,896]{2,1,0:T(8,128)(2,1)} %all-to-all-done.4.came_ref, f32[15888,128]{1,0:T(8,128)S(1)} %copy-done.4, ...), custom_call_target="tpu_custom_call", output_to_operand_aliasing={{0}: (3, {})} | custom-call | bytes 120000000 | tf_op jit(solution)/shard_map/collect/pallas_call | solution.py:689
  742.6 37.3 %finish_entities.1 = (f32[200,7936]{1,0:T(8,128)}, f32[200,7936]{1,0:T(8,128)}, f32[200,7936]{1,0:T(8,128)}, f32[8,128]{1,0:T(8,128)}) custom-call(s32[16]{0:T(128)} %copy-done.20, s32[32768]{0:T(1024)} %bitcast.44, bf16[16,200,384]{2,1,0:T(8,128)(2,1)} %copy-done.23, bf16[16,208,384]{2,1,0:T(8,128)(2,1)S(1)} %get-tuple-element.140.last_ref, ...), custom_call_target="tpu_custom_call" | custom-call | bytes 60000000 | tf_op jit(solution)/shard_map/finish_entities/pallas_call | solution.py:794
  (166 shorter events, 71.8 us)
Async XLA Ops:
  7.2 183.1 %all-gather.10.cloned.1.call-start = ((), (), s32[]{:S(2)}) async-start(), calls=%async_computation.9 | async-start | bytes 36765696 | tf_op jit(solution)/shard_map/all_gather | solution.py:858
  16.0 272.0 %all-gather.8.cloned.1.call-start = ((), (), s32[]{:S(2)}) async-start(), calls=%async_computation.8 | async-start | bytes 19427328 | tf_op jit(solution)/shard_map/all_gather | solution.py:858
  33.3 13.3 %copy-start.30 = (f32[3200]{0:T(1024)S(1)}, f32[3200]{0:T(1024)}, u32[]{:S(2)}) copy-start(f32[3200]{0:T(1024)} %param.22) | copy-start | bytes 38404
  234.8 5.9 copy-start.2
  234.8 7.3 copy-start.31
  234.8 7.4 copy-start.19
  240.7 37.6 %collective-permute-start = (bf16[96,8192]{1,0:T(8,128)(2,1)}, bf16[96,8192]{1,0:T(8,128)(2,1)}, u32[]{:S(2)}, u32[]{:S(2)}) collective-permute-start(bf16[96,8192]{1,0:T(8,128)(2,1)} %get-tuple-element.77.refs_0_), channel_id=1, source_target_pairs={{0,1},{1,0},{2,3},{3,2},{4,5},{5,4},{6,7},{7,6},{8,9},{9,8},{10,11... | collective-permute-start | bytes 4718600 | tf_op jit(solution)/shard_map/ppermute | solution.py:870
  242.3 18.6 %slice-start = ((s8[12587008]{0:T(1024)(128)(4,1)}), s8[4194304]{0:T(1024)(128)(4,1)S(1)}, s32[]{:S(2)}) async-start(s8[12587008]{0:T(1024)(128)(4,1)} %bitcast.40), calls=%async_computation.10 | async-start | bytes 8388608
  242.3 18.6 %slice-start.1 = ((s8[12587008]{0:T(1024)(128)(4,1)}), s8[4194304]{0:T(1024)(128)(4,1)S(1)}, s32[]{:S(2)}) async-start(s8[12587008]{0:T(1024)(128)(4,1)} %bitcast.40), calls=%async_computation.11 | async-start | bytes 8388608
  242.3 18.6 %slice-start.2 = ((s8[12587008]{0:T(1024)(128)(4,1)}), s8[4194304]{0:T(1024)(128)(4,1)S(1)}, s32[]{:S(2)}) async-start(s8[12587008]{0:T(1024)(128)(4,1)} %bitcast.40), calls=%async_computation.12 | async-start | bytes 8388608
  242.3 18.6 %slice-start.3 = ((s8[12587008]{0:T(1024)(128)(4,1)}), s8[4096]{0:T(1024)(128)(4,1)S(1)}, s32[]{:S(2)}) async-start(s8[12587008]{0:T(1024)(128)(4,1)} %bitcast.40), calls=%async_computation.13 | async-start | bytes 8192
  267.6 65.7 %copy-start.12 = (bf16[160,8192]{1,0:T(8,128)(2,1)}, bf16[160,8192]{1,0:T(8,128)(2,1)S(1)}, u32[]{:S(2)}) copy-start(bf16[160,8192]{1,0:T(8,128)(2,1)S(1)} %get-tuple-element.85.refs_1_) | copy-start | bytes 7864324
  267.6 100.0 %collective-permute-start.1 = (bf16[160,8192]{1,0:T(8,128)(2,1)S(1)}, bf16[160,8192]{1,0:T(8,128)(2,1)}, u32[]{:S(2)}, u32[]{:S(2)}) collective-permute-start(bf16[160,8192]{1,0:T(8,128)(2,1)S(1)} %get-tuple-element.85.refs_1_), channel_id=1, source_target_pairs={{0,1},{1,0},{2,3},{3,2},{4,5},{5,4},{6,7},{7,6},{8,9},{9,8},{10,11... | collective-permute-start | bytes 7864328 | tf_op jit(solution)/shard_map/ppermute | solution.py:870
  288.1 45.3 %copy-start.7 = (f32[8192,128]{1,0:T(8,128)S(1)}, f32[8192,128]{1,0:T(8,128)}, u32[]{:S(2)}) copy-start(f32[8192,128]{1,0:T(8,128)} %copy-done.6) | copy-start | bytes 12582916
  333.3 5.0 copy-start
  333.3 8.7 %copy-start.26 = (s32[256,128]{1,0:T(8,128)S(1)}, s32[256,128]{1,0:T(8,128)}, u32[]{:S(2)}) copy-start(s32[256,128]{1,0:T(8,128)} %get-tuple-element.132) | copy-start | bytes 393220
  340.5 31.9 %collective-permute-start.3 = (bf16[2,80,4096]{2,1,0:T(8,128)(2,1)}, bf16[2,80,4096]{2,1,0:T(8,128)(2,1)}, u32[]{:S(2)}, u32[]{:S(2)}) collective-permute-start(bf16[2,80,4096]{2,1,0:T(8,128)(2,1)} %get-tuple-element.91.refs_2_), channel_id=1, source_target_pairs={{0,1},{1,0},{2,3},{3,2},{4,5},{5,4},{6,7},{7,6},{8,9},{9,8},{10,11... | collective-permute-start | bytes 3932168 | tf_op jit(solution)/shard_map/ppermute | solution.py:870
  342.0 4.6 copy-start.1
  356.3 10.8 %all-to-all-start.1 = ((s32[16,1,2176]{2,1,0:T(1,128)}), s32[16,1,2176]{2,1,0:T(1,128)S(1)}, u32[]{:S(2)}, u32[]{:S(2)}) async-start(s32[16,1,2176]{2,1,0:T(1,128)} %all_to_all.20), calls=%async_computation.1 | async-start | bytes 278528 | tf_op jit(solution)/shard_map/all_to_all | solution.py:917
  361.4 38.5 %collective-permute-start.2 = (bf16[2,80,4096]{2,1,0:T(8,128)(2,1)}, bf16[2,80,4096]{2,1,0:T(8,128)(2,1)}, u32[]{:S(2)}, u32[]{:S(2)}) collective-permute-start(bf16[2,80,4096]{2,1,0:T(8,128)(2,1)} %copy-done.17), channel_id=1, source_target_pairs={{0,1},{1,0},{2,3},{3,2},{4,5},{5,4},{6,7},{7,6},{8,9},{9,8},{10,11... | collective-permute-start | bytes 3932168 | tf_op jit(solution)/shard_map/ppermute | solution.py:870
  449.5 5.3 copy-start.25
  449.5 8.5 %copy-start.34 = (s32[8]{0:T(128)S(1)}, s32[8]{0:T(128)}, u32[]{:S(2)}) copy-start(s32[8]{0:T(128)} %live_ref.3) | copy-start | bytes 100
  449.5 8.5 %copy-start.32 = (f32[8,128]{1,0:T(8,128)S(1)}, f32[8,128]{1,0:T(8,128)}, u32[]{:S(2)}) copy-start(f32[8,128]{1,0:T(8,128)} %get-tuple-element.98) | copy-start | bytes 12292
  449.5 8.6 %copy-start.33 = (f32[8,128]{1,0:T(8,128)S(1)}, f32[8,128]{1,0:T(8,128)}, u32[]{:S(2)}) copy-start(f32[8,128]{1,0:T(8,128)} %get-tuple-element.99) | copy-start | bytes 12292
  449.5 60.7 %all-to-all-start.2 = ((bf16[16,200,384]{2,1,0:T(8,128)(2,1)}), bf16[16,200,384]{2,1,0:T(8,128)(2,1)S(1)}, u32[]{:S(2)}, u32[]{:S(2)}) async-start(bf16[16,200,384]{2,1,0:T(8,128)(2,1)} %copy-done.13), calls=%async_computation.2 | async-start | bytes 4915200 | tf_op jit(solution)/shard_map/all_to_all | solution.py:954
  510.2 150.7 %all-to-all-start.4 = ((bf16[16,200,896]{2,1,0:T(8,128)(2,1)}), bf16[16,200,896]{2,1,0:T(8,128)(2,1)}, u32[]{:S(2)}, u32[]{:S(2)}) async-start(bf16[16,200,896]{2,1,0:T(8,128)(2,1)} %copy-done.9), calls=%async_computation.5 | async-start | bytes 11468800 | tf_op jit(solution)/shard_map/all_to_all | solution.py:954
  515.3 134.4 %reduce-scatter.2.cloned.1.call-start = ((), (), s32[]{:S(2)}) async-start(), calls=%async_computation.6 | async-start | bytes 3481600 | tf_op jit(solution)/shard_map/reduce_scatter | solution.py:974
  553.0 187.6 %all-gather.6.cloned.1.call-start = ((), (), s32[]{:S(2)}) async-start(), calls=%async_computation.7 | async-start | bytes 2715648 | tf_op jit(solution)/shard_map/all_gather | solution.py:978
  553.2 115.7 %copy-start.20 = (s32[16]{0:T(128)}, s32[16]{0:T(128)S(1)}, u32[]{:S(2)}) copy-start(s32[16]{0:T(128)S(1)} %get-tuple-element.135.counts_ref) | copy-start | bytes 196
  553.3 115.7 %copy-start.14 = (s32[2,16,8,128]{3,1,2,0:T(8,128)}, s32[2,16,8,128]{3,1,2,0:T(8,128)S(1)}, u32[]{:S(2)}) copy-start(s32[2,16,8,128]{3,1,2,0:T(8,128)S(1)} %copy.43) | copy-start | bytes 393220
  654.1 12.7 %copy-start.24 = (f32[200,200]{1,0:T(8,128)S(1)}, f32[200,200]{1,0:T(8,128)}, u32[]{:S(2)}) copy-start(f32[200,200]{1,0:T(8,128)} %param.27) | copy-start | bytes 480004
  660.9 78.5 %all-to-all-start.3 = ((bf16[16,200,384]{2,1,0:T(8,128)(2,1)}), bf16[16,200,384]{2,1,0:T(8,128)(2,1)S(1)}, u32[]{:S(2)}, u32[]{:S(2)}) async-start(bf16[16,200,384]{2,1,0:T(8,128)(2,1)} %get-tuple-element.107), calls=%async_computation.4 | async-start | bytes 4915200 | tf_op jit(solution)/shard_map/all_to_all | solution.py:954
  (19 other events, 34.0 us)
Sparse Core Ops, SparseCore 0:
  16.2 174.0 all-gather.9
  191.9 96.1 all-gather.7
  553.2 96.4 reduce-scatter.1
  653.0 71.3 all-gather.5

commit v15 on v14

--- a/solution.py
+++ b/solution.py
@@ -695,7 +695,7 @@
         + [whole(pl.ANY)] * len(after),
         out_specs=[whole(VMEM)] * 2,
         scratch_shapes=[pltpu.VMEM((n * chunk, LANES), F32)],
-        compiler_params=params(26),
+        compiler_params=params(60),
         cost_estimate=cost(0, 120e6),
         name="collect",
     )(counts, row_list.reshape(-1), came, *given, *after)

time: 797 us -> 791 us (level)
  local copies, waits for them, and re-layouts: 52 us -> 40.7 us
    unnamed x85 -> x97, local copies, waits for them, and re-layouts: 33.9 us -> 24.7 us
  transfers between devices with their start and end apart: 12 -> 12, of which waited for: 9 -> 10; matrix products, arithmetic and copies ran while one was open for 6% -> 6% of each run, Pallas kernels for 43% -> 43%
where the time goes in v15:
time: 791 us; the launch traced here: 786 us
  Pallas kernels  425 us (54%)
  waiting for transfers between devices  231 us (29%)
  local copies, waits for them, and re-layouts  40.7 us (5%)
  other arithmetic  29.1 us (4%)
  starting transfers between devices  25.2 us (3%)
  between operations  22.3 us (3%)
  matrix products  12.3 us (2%)
    all_gather x2, waiting for transfers between devices, shards(): dense.append(lax.all_gather(sent, 'edge', axis=0, tiled=False))  149 us
    pallas_call x2, Pallas kernels, fetch(): pl.pallas_call(functools.partial(fetch_kernel, capacity, moves, ent_rows)...  89.7 us
    pallas_call x2, Pallas kernels, collect(): pl.pallas_call(functools.partial(collect_kernel, slices, capacity, begin,...  88.5 us
    pallas_call x3, Pallas kernels, outgoing(): pl.pallas_call(functools.partial(outgoing_kernel, slices, capacity, begin...  81.6 us
    pallas_call x2, Pallas kernels, block_math(): pl.pallas_call(functools.partial(block_kernel, slices, n_col, half), out_...  52.1 us
    reduce_scatter x1, waiting for transfers between devices, shards(): lax.psum_scatter(rel_terms, 'edge', scatter_dimension=0, tiled=True)  47.3 us
    pallas_call x1, Pallas kernels, finish_entities(): pl.pallas_call(functools.partial(finish_kernel, slices, capacity, begin,...  39.7 us
    pallas_call x1, Pallas kernels, relation_sums(): pl.pallas_call(functools.partial(relation_sums_kernel, n), out_shape=[jax...  31.1 us
  transfers between devices with their start and end apart: 12, of which 10 were waited for; matrix products, arithmetic and copies ran while one was open for 6% of the time, Pallas kernels for 43%

profile of v15, /device:TPU:16, one launch (start us, length us, event | category | flops | bytes accessed | tf_op | source)
XLA Modules:
  0.0 785.6 jit_solution(9780095064577353743)
XLA Ops:
  8.2 3.1 convert.20
  24.6 8.8 %broadcast_multiply_fusion = bf16[4,128,24576]{2,1,0:T(8,128)(2,1)} fusion(bf16[128,24576]{1,0:T(8,128)(2,1)S(1)} %fusion.2, bf16[4,24576]{1,0:T(4,128)(2,1)S(1)} %pad_maximum_fusion), kind=kLoop, calls=%fused_computation.3 | loop fusion | flops 12582912 | bytes 31653888 | tf_op jit(solution)/shard_map/mul | solution.py:93
  33.4 11.8 %fusion.8 = s32[256,512]{1,0:T(8,128)S(1)} fusion(bf16[512,24576]{1,0:T(8,128)(2,1)} %bitcast.57, s32[24576]{0:T(1024)S(1)} %get-tuple-element.136), kind=kOutput, calls=%fused_computation.17 | convolution fusion | flops 6448873472 | bytes 25788416 | tf_op jit(solution)/shard_map/dot_general | solution.py:94
  50.4 139.9 %all-gather.10.cloned.1.call-done = bf16[2048,8448]{1,0:T(8,128)(2,1)} async-done(((bf16[128,8448]{1,0:T(8,128)(2,1)}), bf16[2048,8448]{1,0:T(8,128)(2,1)}) %all-gather.10.cloned.1.call-update) | async-done | bytes 34603024 | tf_op jit(solution)/shard_map/all_gather | solution.py:858
  190.3 44.5 %fetch_rows.2.neg_ref.head_ref.tail_ref = f32[24584,128]{1,0:T(8,128)S(1)} custom-call(s32[16]{0:T(128)S(1)} %convert_element_type.79.counts_ref, s32[32768]{0:T(1024)S(1)} %bitcast.42, s32[32768]{0:T(1024)S(1)} %bitcast.45, bf16[16,128,8448]{2,1,0:T(8,128)(2,1)} %bitcast.54, s32[16,128]{1,0:T(8,128)S(1)} %broadcast_in_dim.35.refs_0_), custom_call_target="tpu_custom_call" | custom-call | bytes 170000000 | tf_op jit(solution)/shard_map/fetch_rows/pallas_call | solution.py:231
  234.8 5.9 negatives.1
  242.3 16.6 %relation_rows.1 = (f32[8192,128]{1,0:T(8,128)S(1)}, f32[8192,128]{1,0:T(8,128)S(1)}) custom-call(s32[8192]{0:T(1024)S(1)} %fusion.28.ids_ref, f32[16,256]{1,0:T(8,128)S(1)} %pad.17.scale_ref, bf16[16,128,8448]{2,1,0:T(8,128)(2,1)} %bitcast.55, bf16[16,128,8448]{2,1,0:T(8,128)(2,1)} %bitcast.56, f32[1,8192]{1,0:T(1,128)S(1)} %get-tuple-element.78.refs_2_.refs_1_), custom_call_target="tpu_custom_call" | custom-call | bytes 80000000 | tf_op jit(solution)/shard_map/relation_rows/pallas_call | solution.py:139
  261.0 3.2 edges.1
  268.3 9.9 %collective-permute-done.refs_3_ = bf16[96,8192]{1,0:T(8,128)(2,1)} collective-permute-done((bf16[96,8192]{1,0:T(8,128)(2,1)}, bf16[96,8192]{1,0:T(8,128)(2,1)}, u32[]{:S(2)}, u32[]{:S(2)}) %collective-permute-start) | collective-permute-done | bytes 1572896 | tf_op jit(solution)/shard_map/ppermute | solution.py:870
  278.8 9.2 %all-gather.8.cloned.1.call-done = bf16[1152,7936]{1,0:T(8,128)(2,1)} async-done(((bf16[72,7936]{1,0:T(8,128)(2,1)}), bf16[1152,7936]{1,0:T(8,128)(2,1)}) %all-gather.8.cloned.1.call-update) | async-done | bytes 18284560 | tf_op jit(solution)/shard_map/all_gather | solution.py:858
  288.1 45.2 %fetch_rows.3.head_ref.tail_ref.neg_ref = f32[24584,128]{1,0:T(8,128)S(1)} custom-call(s32[16]{0:T(128)S(1)} %convert_element_type.79.counts_ref, s32[32768]{0:T(1024)S(1)} %bitcast.43, s32[32768]{0:T(1024)S(1)} %bitcast.46, bf16[16,72,7936]{2,1,0:T(8,128)(2,1)} %bitcast.58, bf16[8,128]{1,0:T(8,128)(2,1)S(1)} %slice.120.refs_0_), custom_call_target="tpu_custom_call" | custom-call | bytes 170000000 | tf_op jit(solution)/shard_map/fetch_rows/pallas_call | solution.py:231
  333.3 4.6 last_slice.2
  342.0 4.6 copy-done.1
  356.3 5.2 all-to-all-start.1
  362.1 5.1 all-to-all-done.1
  367.8 4.6 collective-permute-done.3.refs_5_
  372.4 26.0 %block_math.2 = (f32[3,16384,128]{2,1,0:T(8,128)}, f32[8,128]{1,0:T(8,128)}) custom-call(s32[1]{0:T(128)} %bitcast.10.me_ref, s32[8]{0:T(128)} %live_ref.3, bf16[96,8192]{1,0:T(8,128)(2,1)} %get-tuple-element.77.refs_0_, bf16[160,8192]{1,0:T(8,128)(2,1)} %copy-done.8, bf16[2,80,4096]{2,1,0:T(8,128)(2,1)} %get-tuple-element.91.refs_2_, ...), custom_call_target="tpu_custom_call" | custom-call | flops 6710886400 | bytes 120000000 | tf_op jit(solution)/shard_map/block_math/pallas_call | solution.py:525
  399.9 26.1 %block_math.3 = (f32[3,16384,128]{2,1,0:T(8,128)}, f32[8,128]{1,0:T(8,128)}) custom-call(s32[1]{0:T(128)} %bitcast.10.me_ref, s32[8]{0:T(128)} %live_ref.3, bf16[96,8192]{1,0:T(8,128)(2,1)} %get-tuple-element.77.refs_0_, bf16[160,8192]{1,0:T(8,128)(2,1)} %copy-done.8, bf16[2,80,4096]{2,1,0:T(8,128)(2,1)} %copy-done.11, ...), custom_call_target="tpu_custom_call", output_to_operand_aliasing={{0}: (12, {})} | custom-call | flops 6710886400 | bytes 120000000 | tf_op jit(solution)/shard_map/block_math/pallas_call | solution.py:525
  426.0 23.5 %outgoing.5 = (bf16[16,200,384]{2,1,0:T(8,128)(2,1)}, f32[8,128]{1,0:T(8,128)S(1)}) custom-call(s32[16]{0:T(128)S(1)} %convert_element_type.79.counts_ref, s32[32768]{0:T(1024)S(1)} %broadcast_minimum_fusion.place_ref, f32[49152,128]{1,0:T(8,128)} %bitcast.49), custom_call_target="tpu_custom_call" | custom-call | bytes 80000000 | tf_op jit(solution)/shard_map/outgoing/pallas_call | solution.py:638
  449.5 5.3 all-to-all-start.2
  458.0 9.6 %excess_rows.1 = (bf16[1,208,384]{2,1,0:T(8,128)(2,1)S(1)}, f32[8,128]{1,0:T(8,128)S(1)}) custom-call(s32[1]{0:T(128)} %dynamic_slice.6.counts_ref, s32[2048]{0:T(1024)S(1)} %bitcast.48, s32[8]{0:T(128)S(1)} %broadcast_minimum_fusion.1.live_ref, f32[49152,128]{1,0:T(8,128)} %bitcast.50, f32[8,128]{1,0:T(8,128)S(1)} %add.197.loss_ref, ...), custom_call_target="tpu_custom_call" | custom-call | bytes 80000000 | tf_op jit(solution)/shard_map/excess_rows/pallas_call | solution.py:619
  468.3 39.0 %outgoing.6 = (bf16[16,200,896]{2,1,0:T(8,128)(2,1)S(1)}, f32[8,128]{1,0:T(8,128)S(1)}) custom-call(s32[16]{0:T(128)S(1)} %convert_element_type.79.counts_ref, s32[32768]{0:T(1024)S(1)} %broadcast_minimum_fusion.place_ref, f32[49152,128]{1,0:T(8,128)} %bitcast.51, f32[8,128]{1,0:T(8,128)S(1)} %get-tuple-element.101.refs_0_.refs_1_), custom_call_target="tpu_custom_call" | custom-call | bytes 80000000 | tf_op jit(solution)/shard_map/outgoing/pallas_call | solution.py:638
  510.1 5.8 all-to-all-start.4
  516.0 31.1 %relation_sums.1 = (f32[6400,128]{1,0:T(8,128)S(1)}, f32[8,128]{1,0:T(8,128)S(1)}) custom-call(s32[8192]{0:T(1024)S(1)} %copy-done.15, f32[3,16384,128]{2,1,0:T(8,128)} %get-tuple-element.95.grad, bf16[8,128]{1,0:T(8,128)(2,1)S(1)} %slice_bitcast_fusion.1.refs_0_, f32[8,128]{1,0:T(8,128)S(1)} %get-tuple-element.101.refs_0_.refs_1_, ...), custom_call_target="tpu_custom_call" | custom-call | bytes 120000000 | tf_op jit(solution)/shard_map/relation_sums/pallas_call | solution.py:721
  552.1 30.0 %collect.2 = (f32[15888,128]{1,0:T(8,128)}, f32[8,128]{1,0:T(8,128)}) custom-call(s32[16]{0:T(128)} %get-tuple-element.135.counts_ref, s32[32768]{0:T(1024)} %bitcast.60, bf16[16,200,384]{2,1,0:T(8,128)(2,1)} %copy-done.21, f32[8,128]{1,0:T(8,128)} %copy-done.17), custom_call_target="tpu_custom_call" | custom-call | bytes 120000000 | tf_op jit(solution)/shard_map/collect/pallas_call | solution.py:689
  582.7 19.1 %outgoing.7 = (bf16[16,200,384]{2,1,0:T(8,128)(2,1)}, f32[8,128]{1,0:T(8,128)S(1)}) custom-call(s32[16]{0:T(128)S(1)} %convert_element_type.79.counts_ref, s32[32768]{0:T(1024)S(1)} %broadcast_minimum_fusion.place_ref, f32[49152,128]{1,0:T(8,128)} %bitcast.52, f32[8,128]{1,0:T(8,128)S(1)} %copy-done.18), custom_call_target="tpu_custom_call" | custom-call | bytes 80000000 | tf_op jit(solution)/shard_map/outgoing/pallas_call | solution.py:638
  603.0 47.3 %reduce-scatter.2.cloned.1.call-done = f32[200,200]{1,0:T(8,128)} async-done(((f32[3200,200]{1,0:T(8,128)}), f32[200,200]{1,0:T(8,128)}) %reduce-scatter.2.cloned.1.call-update) | async-done | bytes 160016 | tf_op jit(solution)/shard_map/reduce_scatter | solution.py:974
  654.8 6.7 all-to-all-done.4.came_ref
  661.5 4.7 all-to-all-start.3
  668.5 58.5 %collect.3 = (f32[15888,128]{1,0:T(8,128)}, f32[8,128]{1,0:T(8,128)}) custom-call(s32[16]{0:T(128)} %get-tuple-element.135.counts_ref, s32[32768]{0:T(1024)} %bitcast.61, bf16[16,200,896]{2,1,0:T(8,128)(2,1)} %all-to-all-done.4.came_ref, f32[15888,128]{1,0:T(8,128)} %get-tuple-element.109.refs_0_, f32[8,128]{1,0:T(8,128)} %copy-done.16), custom_call_target="tpu_custom_call", output_to_operand_aliasing={{0}: (3, {})} | custom-call | bytes 120000000 | tf_op jit(solution)/shard_map/collect/pallas_call | solution.py:689
  728.7 6.1 all-to-all-done.3.came_ref
  738.0 39.7 %finish_entities.1 = (f32[200,7936]{1,0:T(8,128)}, f32[200,7936]{1,0:T(8,128)}, f32[200,7936]{1,0:T(8,128)}, f32[8,128]{1,0:T(8,128)}) custom-call(s32[16]{0:T(128)} %get-tuple-element.135.counts_ref, s32[32768]{0:T(1024)} %bitcast.62, bf16[16,200,384]{2,1,0:T(8,128)(2,1)} %copy-done.22, bf16[16,208,384]{2,1,0:T(8,128)(2,1)S(1)} %get-tuple-element.140.last_ref, ...), custom_call_target="tpu_custom_call" | custom-call | bytes 60000000 | tf_op jit(solution)/shard_map/finish_entities/pallas_call | solution.py:794
  (178 shorter events, 64.4 us)
Async XLA Ops:
  7.2 183.1 %all-gather.10.cloned.1.call-start = ((), (), s32[]{:S(2)}) async-start(), calls=%async_computation.9 | async-start | bytes 36765696 | tf_op jit(solution)/shard_map/all_gather | solution.py:858
  16.0 272.0 %all-gather.8.cloned.1.call-start = ((), (), s32[]{:S(2)}) async-start(), calls=%async_computation.8 | async-start | bytes 19427328 | tf_op jit(solution)/shard_map/all_gather | solution.py:858
  33.4 13.3 %copy-start.36 = (f32[3200]{0:T(1024)S(1)}, f32[3200]{0:T(1024)}, u32[]{:S(2)}) copy-start(f32[3200]{0:T(1024)} %param.22) | copy-start | bytes 38404
  234.8 7.4 copy-start.37
  234.8 7.5 copy-start.15
  240.7 37.5 %collective-permute-start = (bf16[96,8192]{1,0:T(8,128)(2,1)}, bf16[96,8192]{1,0:T(8,128)(2,1)}, u32[]{:S(2)}, u32[]{:S(2)}) collective-permute-start(bf16[96,8192]{1,0:T(8,128)(2,1)} %get-tuple-element.77.refs_0_), channel_id=1, source_target_pairs={{0,1},{1,0},{2,3},{3,2},{4,5},{5,4},{6,7},{7,6},{8,9},{9,8},{10,11... | collective-permute-start | bytes 4718600 | tf_op jit(solution)/shard_map/ppermute | solution.py:870
  242.3 18.6 %slice-start = ((s8[12587008]{0:T(1024)(128)(4,1)}), s8[4194304]{0:T(1024)(128)(4,1)S(1)}, s32[]{:S(2)}) async-start(s8[12587008]{0:T(1024)(128)(4,1)} %bitcast.40), calls=%async_computation.10 | async-start | bytes 8388608
  242.3 18.6 %slice-start.1 = ((s8[12587008]{0:T(1024)(128)(4,1)}), s8[4194304]{0:T(1024)(128)(4,1)S(1)}, s32[]{:S(2)}) async-start(s8[12587008]{0:T(1024)(128)(4,1)} %bitcast.40), calls=%async_computation.11 | async-start | bytes 8388608
  242.3 18.6 %slice-start.2 = ((s8[12587008]{0:T(1024)(128)(4,1)}), s8[4194304]{0:T(1024)(128)(4,1)S(1)}, s32[]{:S(2)}) async-start(s8[12587008]{0:T(1024)(128)(4,1)} %bitcast.40), calls=%async_computation.12 | async-start | bytes 8388608
  242.3 18.6 %slice-start.3 = ((s8[12587008]{0:T(1024)(128)(4,1)}), s8[4096]{0:T(1024)(128)(4,1)S(1)}, s32[]{:S(2)}) async-start(s8[12587008]{0:T(1024)(128)(4,1)} %bitcast.40), calls=%async_computation.13 | async-start | bytes 8192
  267.7 65.6 %copy-start.8 = (bf16[160,8192]{1,0:T(8,128)(2,1)}, bf16[160,8192]{1,0:T(8,128)(2,1)S(1)}, u32[]{:S(2)}) copy-start(bf16[160,8192]{1,0:T(8,128)(2,1)S(1)} %get-tuple-element.85.refs_1_) | copy-start | bytes 7864324
  267.7 100.1 %collective-permute-start.1 = (bf16[160,8192]{1,0:T(8,128)(2,1)S(1)}, bf16[160,8192]{1,0:T(8,128)(2,1)}, u32[]{:S(2)}, u32[]{:S(2)}) collective-permute-start(bf16[160,8192]{1,0:T(8,128)(2,1)S(1)} %get-tuple-element.85.refs_1_), channel_id=1, source_target_pairs={{0,1},{1,0},{2,3},{3,2},{4,5},{5,4},{6,7},{7,6},{8,9},{9,8},{10,11... | collective-permute-start | bytes 7864328 | tf_op jit(solution)/shard_map/ppermute | solution.py:870
  288.1 45.2 %copy-start.4 = (f32[8192,128]{1,0:T(8,128)S(1)}, f32[8192,128]{1,0:T(8,128)}, u32[]{:S(2)}) copy-start(f32[8192,128]{1,0:T(8,128)} %copy-done.3) | copy-start | bytes 12582916
  333.3 8.6 %copy-start.29 = (s32[256,128]{1,0:T(8,128)S(1)}, s32[256,128]{1,0:T(8,128)}, u32[]{:S(2)}) copy-start(s32[256,128]{1,0:T(8,128)} %get-tuple-element.132) | copy-start | bytes 393220
  340.5 31.9 %collective-permute-start.3 = (bf16[2,80,4096]{2,1,0:T(8,128)(2,1)}, bf16[2,80,4096]{2,1,0:T(8,128)(2,1)}, u32[]{:S(2)}, u32[]{:S(2)}) collective-permute-start(bf16[2,80,4096]{2,1,0:T(8,128)(2,1)} %get-tuple-element.91.refs_2_), channel_id=1, source_target_pairs={{0,1},{1,0},{2,3},{3,2},{4,5},{5,4},{6,7},{7,6},{8,9},{9,8},{10,11... | collective-permute-start | bytes 3932168 | tf_op jit(solution)/shard_map/ppermute | solution.py:870
  356.3 10.9 %all-to-all-start.1 = ((s32[16,1,2176]{2,1,0:T(1,128)}), s32[16,1,2176]{2,1,0:T(1,128)S(1)}, u32[]{:S(2)}, u32[]{:S(2)}) async-start(s32[16,1,2176]{2,1,0:T(1,128)} %all_to_all.20), calls=%async_computation.1 | async-start | bytes 278528 | tf_op jit(solution)/shard_map/all_to_all | solution.py:917
  361.4 38.4 %collective-permute-start.2 = (bf16[2,80,4096]{2,1,0:T(8,128)(2,1)}, bf16[2,80,4096]{2,1,0:T(8,128)(2,1)}, u32[]{:S(2)}, u32[]{:S(2)}) collective-permute-start(bf16[2,80,4096]{2,1,0:T(8,128)(2,1)} %copy-done.11), channel_id=1, source_target_pairs={{0,1},{1,0},{2,3},{3,2},{4,5},{5,4},{6,7},{7,6},{8,9},{9,8},{10,11... | collective-permute-start | bytes 3932168 | tf_op jit(solution)/shard_map/ppermute | solution.py:870
  449.5 8.5 %copy-start.40 = (s32[8]{0:T(128)S(1)}, s32[8]{0:T(128)}, u32[]{:S(2)}) copy-start(s32[8]{0:T(128)} %live_ref.3) | copy-start | bytes 100
  449.5 8.5 %copy-start.38 = (f32[8,128]{1,0:T(8,128)S(1)}, f32[8,128]{1,0:T(8,128)}, u32[]{:S(2)}) copy-start(f32[8,128]{1,0:T(8,128)} %get-tuple-element.98) | copy-start | bytes 12292
  449.5 8.5 %copy-start.39 = (f32[8,128]{1,0:T(8,128)S(1)}, f32[8,128]{1,0:T(8,128)}, u32[]{:S(2)}) copy-start(f32[8,128]{1,0:T(8,128)} %get-tuple-element.99) | copy-start | bytes 12292
  449.5 60.6 %all-to-all-start.2 = ((bf16[16,200,384]{2,1,0:T(8,128)(2,1)}), bf16[16,200,384]{2,1,0:T(8,128)(2,1)S(1)}, u32[]{:S(2)}, u32[]{:S(2)}) async-start(bf16[16,200,384]{2,1,0:T(8,128)(2,1)} %get-tuple-element.96), calls=%async_computation.2 | async-start | bytes 4915200 | tf_op jit(solution)/shard_map/all_to_all | solution.py:954
  454.8 12.9 %copy-start.26 = (s32[16,2048]{1,0:T(8,128)}, s32[16,2048]{1,0:T(8,128)S(1)}, u32[]{:S(2)}) copy-start(s32[16,2048]{1,0:T(8,128)S(1)} %reshape.781) | copy-start | bytes 393220
  510.1 151.4 %all-to-all-start.4 = ((bf16[16,200,896]{2,1,0:T(8,128)(2,1)}), bf16[16,200,896]{2,1,0:T(8,128)(2,1)}, u32[]{:S(2)}, u32[]{:S(2)}) async-start(bf16[16,200,896]{2,1,0:T(8,128)(2,1)} %copy-done.6), calls=%async_computation.5 | async-start | bytes 11468800 | tf_op jit(solution)/shard_map/all_to_all | solution.py:954
  515.9 134.4 %reduce-scatter.2.cloned.1.call-start = ((), (), s32[]{:S(2)}) async-start(), calls=%async_computation.6 | async-start | bytes 3481600 | tf_op jit(solution)/shard_map/reduce_scatter | solution.py:974
  549.9 186.2 %all-gather.6.cloned.1.call-start = ((), (), s32[]{:S(2)}) async-start(), calls=%async_computation.7 | async-start | bytes 2715648 | tf_op jit(solution)/shard_map/all_gather | solution.py:978
  582.7 70.1 %copy-start.14 = (bf16[1,208,384]{2,1,0:T(8,128)(2,1)S(1)}, bf16[1,208,384]{2,1,0:T(8,128)(2,1)}, u32[]{:S(2)}) copy-start(bf16[1,208,384]{2,1,0:T(8,128)(2,1)} %copy-done.13) | copy-start | bytes 479236
  654.8 12.7 %copy-start.23 = (f32[200,200]{1,0:T(8,128)S(1)}, f32[200,200]{1,0:T(8,128)}, u32[]{:S(2)}) copy-start(f32[200,200]{1,0:T(8,128)} %param.27) | copy-start | bytes 480004
  654.8 12.7 %copy-start.30 = (f32[200,200]{1,0:T(8,128)S(1)}, f32[200,200]{1,0:T(8,128)}, u32[]{:S(2)}) copy-start(f32[200,200]{1,0:T(8,128)} %reduce-scatter.2.cloned.1.call-done) | copy-start | bytes 480004
  654.8 12.7 %copy-start.31 = (f32[200,200]{1,0:T(8,128)S(1)}, f32[200,200]{1,0:T(8,128)}, u32[]{:S(2)}) copy-start(f32[200,200]{1,0:T(8,128)} %param.28) | copy-start | bytes 480004
  654.8 12.7 %copy-start.32 = (f32[200,200]{1,0:T(8,128)S(1)}, f32[200,200]{1,0:T(8,128)}, u32[]{:S(2)}) copy-start(f32[200,200]{1,0:T(8,128)} %param.29) | copy-start | bytes 480004
  661.5 73.3 %all-to-all-start.3 = ((bf16[16,200,384]{2,1,0:T(8,128)(2,1)}), bf16[16,200,384]{2,1,0:T(8,128)(2,1)S(1)}, u32[]{:S(2)}, u32[]{:S(2)}) async-start(bf16[16,200,384]{2,1,0:T(8,128)(2,1)} %get-tuple-element.107), calls=%async_computation.4 | async-start | bytes 4915200 | tf_op jit(solution)/shard_map/all_to_all | solution.py:954
  668.5 67.6 %copy-start.27 = (s32[16,2048]{1,0:T(8,128)S(1)}, s32[16,2048]{1,0:T(8,128)}, u32[]{:S(2)}) copy-start(s32[16,2048]{1,0:T(8,128)} %copy-done.26) | copy-start | bytes 393220
  (25 other events, 58.5 us)
Sparse Core Ops, SparseCore 0:
  16.2 174.0 all-gather.9
  191.9 96.1 all-gather.7
  550.0 100.2 reduce-scatter.1
  653.6 71.8 all-gather.5

commit v16 on v15

--- a/solution.py
+++ b/solution.py
@@ -950,7 +950,7 @@
             counts, safe_places, flat, slices, bounds[k], bounds[k + 1] - bounds[k], after
         )
         if k == chunks - 2:
-            sent = pass_on(sent, [corner(relation_grad)])
+            sent = pass_on(sent, [corner(relation_pairs)])
         arrived.append(lax.all_to_all(sent, "edge", split_axis=0, concat_axis=0, tiled=True))
         after = []
         if k == 0:
@@ -970,13 +970,12 @@
             before = [corner(arrived[0]), excess_token, sent_token]
             rel_terms, token = relation_sums(relation_ids, grad, n, rel_total, before)
             after = [token]
-            rel_terms = rel_terms.reshape(rel_total, n * LANES)[:, :width]
-            relation_grad = lax.psum_scatter(rel_terms, "edge", scatter_dimension=0, tiled=True)
+            relation_pairs = lax.psum_scatter(rel_terms, "edge", scatter_dimension=0, tiled=True)
         if k == 2:
-            ready = (relation_grad[0, 0] == relation_grad[0, 0]) & (sent_token[0, 0] == 0.0)
+            ready = (relation_pairs[0, 0] == relation_pairs[0, 0]) & (sent_token[0, 0] == 0.0)
             excess = jnp.where(ready, excess, jnp.zeros_like(excess))
             gathered = lax.all_gather(excess, "edge", axis=0, tiled=True)
-            after = [corner(relation_grad)]
+            after = [corner(relation_pairs)]
         if k > 0:
             total, token = collect(
                 asked_counts, asked, arrived[k - 1], total, slices, bounds[k - 1], ent_rows, after
@@ -1006,6 +1005,7 @@
         slices,
     )
     loss_pair = sums[:2, 0]
+    relation_grad = relation_pairs.reshape(rel_own, n * LANES)[:, :width]
     new_relation, new_relation_first, new_relation_second = adamw_update(
         relation_table, relation_grad, relation_first, relation_second
     )

time: 791 us -> 788 us (level)
    unnamed x97 -> x81, local copies, waits for them, and re-layouts: 24.7 us -> 23.1 us
where the time goes in v16:
time: 788 us; the launch traced here: 782 us
  Pallas kernels  422 us (54%)
  waiting for transfers between devices  233 us (30%)
  local copies, waits for them, and re-layouts  37.1 us (5%)
  other arithmetic  30.2 us (4%)
  starting transfers between devices  24.6 us (3%)
  between operations  22.3 us (3%)
  matrix products  12.3 us (2%)
    all_gather x2, waiting for transfers between devices, shards(): dense.append(lax.all_gather(sent, 'edge', axis=0, tiled=False))  149 us
    pallas_call x2, Pallas kernels, fetch(): pl.pallas_call(functools.partial(fetch_kernel, capacity, moves, ent_rows)...  89.8 us
    pallas_call x2, Pallas kernels, collect(): pl.pallas_call(functools.partial(collect_kernel, slices, capacity, begin,...  88.4 us
    pallas_call x3, Pallas kernels, outgoing(): pl.pallas_call(functools.partial(outgoing_kernel, slices, capacity, begin...  81.6 us
    pallas_call x2, Pallas kernels, block_math(): pl.pallas_call(functools.partial(block_kernel, slices, n_col, half), out_...  52.2 us
    reduce_scatter x1, waiting for transfers between devices, shards(): lax.psum_scatter(rel_terms, 'edge', scatter_dimension=0, tiled=True)  49.3 us
    pallas_call x1, Pallas kernels, finish_entities(): pl.pallas_call(functools.partial(finish_kernel, slices, capacity, begin,...  37.6 us
    pallas_call x1, Pallas kernels, relation_sums(): pl.pallas_call(functools.partial(relation_sums_kernel, n), out_shape=[jax...  30.1 us
  transfers between devices with their start and end apart: 12, of which 10 were waited for; matrix products, arithmetic and copies ran while one was open for 6% of the time, Pallas kernels for 43%

profile of v16, /device:TPU:16, one launch (start us, length us, event | category | flops | bytes accessed | tf_op | source)
XLA Modules:
  0.0 781.7 jit_solution(18119434366415921617)
XLA Ops:
  8.2 3.1 convert.20
  24.6 8.8 %broadcast_multiply_fusion = bf16[4,128,24576]{2,1,0:T(8,128)(2,1)} fusion(bf16[128,24576]{1,0:T(8,128)(2,1)S(1)} %fusion.2, bf16[4,24576]{1,0:T(4,128)(2,1)S(1)} %pad_maximum_fusion), kind=kLoop, calls=%fused_computation.3 | loop fusion | flops 12582912 | bytes 31653888 | tf_op jit(solution)/shard_map/mul | solution.py:93
  33.4 11.8 %fusion.8 = s32[256,512]{1,0:T(8,128)S(1)} fusion(bf16[512,24576]{1,0:T(8,128)(2,1)} %bitcast.56, s32[24576]{0:T(1024)S(1)} %get-tuple-element.136), kind=kOutput, calls=%fused_computation.17 | convolution fusion | flops 6448873472 | bytes 25788416 | tf_op jit(solution)/shard_map/dot_general | solution.py:94
  50.4 139.8 %all-gather.10.cloned.1.call-done = bf16[2048,8448]{1,0:T(8,128)(2,1)} async-done(((bf16[128,8448]{1,0:T(8,128)(2,1)}), bf16[2048,8448]{1,0:T(8,128)(2,1)}) %all-gather.10.cloned.1.call-update) | async-done | bytes 34603024 | tf_op jit(solution)/shard_map/all_gather | solution.py:858
  190.3 44.5 %fetch_rows.2.neg_ref.head_ref.tail_ref = f32[24584,128]{1,0:T(8,128)S(1)} custom-call(s32[16]{0:T(128)S(1)} %convert_element_type.79.counts_ref, s32[32768]{0:T(1024)S(1)} %bitcast.41, s32[32768]{0:T(1024)S(1)} %bitcast.44, bf16[16,128,8448]{2,1,0:T(8,128)(2,1)} %bitcast.53, s32[16,128]{1,0:T(8,128)S(1)} %broadcast_in_dim.35.refs_0_), custom_call_target="tpu_custom_call" | custom-call | bytes 170000000 | tf_op jit(solution)/shard_map/fetch_rows/pallas_call | solution.py:231
  234.8 5.8 negatives.1
  242.3 16.6 %relation_rows.1 = (f32[8192,128]{1,0:T(8,128)S(1)}, f32[8192,128]{1,0:T(8,128)S(1)}) custom-call(s32[8192]{0:T(1024)S(1)} %fusion.28.ids_ref, f32[16,256]{1,0:T(8,128)S(1)} %pad.17.scale_ref, bf16[16,128,8448]{2,1,0:T(8,128)(2,1)} %bitcast.54, bf16[16,128,8448]{2,1,0:T(8,128)(2,1)} %bitcast.55, f32[1,8192]{1,0:T(1,128)S(1)} %get-tuple-element.78.refs_2_.refs_1_), custom_call_target="tpu_custom_call" | custom-call | bytes 80000000 | tf_op jit(solution)/shard_map/relation_rows/pallas_call | solution.py:139
  261.0 3.2 edges.1
  268.2 10.0 %collective-permute-done.refs_3_ = bf16[96,8192]{1,0:T(8,128)(2,1)} collective-permute-done((bf16[96,8192]{1,0:T(8,128)(2,1)}, bf16[96,8192]{1,0:T(8,128)(2,1)}, u32[]{:S(2)}, u32[]{:S(2)}) %collective-permute-start) | collective-permute-done | bytes 1572896 | tf_op jit(solution)/shard_map/ppermute | solution.py:870
  278.9 9.2 %all-gather.8.cloned.1.call-done = bf16[1152,7936]{1,0:T(8,128)(2,1)} async-done(((bf16[72,7936]{1,0:T(8,128)(2,1)}), bf16[1152,7936]{1,0:T(8,128)(2,1)}) %all-gather.8.cloned.1.call-update) | async-done | bytes 18284560 | tf_op jit(solution)/shard_map/all_gather | solution.py:858
  288.1 45.2 %fetch_rows.3.head_ref.tail_ref.neg_ref = f32[24584,128]{1,0:T(8,128)S(1)} custom-call(s32[16]{0:T(128)S(1)} %convert_element_type.79.counts_ref, s32[32768]{0:T(1024)S(1)} %bitcast.42, s32[32768]{0:T(1024)S(1)} %bitcast.45, bf16[16,72,7936]{2,1,0:T(8,128)(2,1)} %bitcast.57, bf16[8,128]{1,0:T(8,128)(2,1)S(1)} %slice.120.refs_0_), custom_call_target="tpu_custom_call" | custom-call | bytes 170000000 | tf_op jit(solution)/shard_map/fetch_rows/pallas_call | solution.py:231
  333.4 4.6 last_slice.2
  342.0 4.6 copy-done.1
  356.2 5.1 all-to-all-start.1
  361.9 5.1 all-to-all-done.1
  367.6 4.8 collective-permute-done.3.refs_5_
  372.4 26.0 %block_math.2 = (f32[3,16384,128]{2,1,0:T(8,128)}, f32[8,128]{1,0:T(8,128)}) custom-call(s32[1]{0:T(128)} %bitcast.10.me_ref, s32[8]{0:T(128)} %live_ref.3, bf16[96,8192]{1,0:T(8,128)(2,1)} %get-tuple-element.77.refs_0_, bf16[160,8192]{1,0:T(8,128)(2,1)} %copy-done.8, bf16[2,80,4096]{2,1,0:T(8,128)(2,1)} %get-tuple-element.91.refs_2_, ...), custom_call_target="tpu_custom_call" | custom-call | flops 6710886400 | bytes 120000000 | tf_op jit(solution)/shard_map/block_math/pallas_call | solution.py:525
  399.8 26.2 %block_math.3 = (f32[3,16384,128]{2,1,0:T(8,128)}, f32[8,128]{1,0:T(8,128)}) custom-call(s32[1]{0:T(128)} %bitcast.10.me_ref, s32[8]{0:T(128)} %live_ref.3, bf16[96,8192]{1,0:T(8,128)(2,1)} %get-tuple-element.77.refs_0_, bf16[160,8192]{1,0:T(8,128)(2,1)} %copy-done.8, bf16[2,80,4096]{2,1,0:T(8,128)(2,1)} %copy-done.11, ...), custom_call_target="tpu_custom_call", output_to_operand_aliasing={{0}: (12, {})} | custom-call | flops 6710886400 | bytes 120000000 | tf_op jit(solution)/shard_map/block_math/pallas_call | solution.py:525
  426.0 23.5 %outgoing.5 = (bf16[16,200,384]{2,1,0:T(8,128)(2,1)}, f32[8,128]{1,0:T(8,128)S(1)}) custom-call(s32[16]{0:T(128)S(1)} %convert_element_type.79.counts_ref, s32[32768]{0:T(1024)S(1)} %broadcast_minimum_fusion.place_ref, f32[49152,128]{1,0:T(8,128)} %bitcast.48), custom_call_target="tpu_custom_call" | custom-call | bytes 80000000 | tf_op jit(solution)/shard_map/outgoing/pallas_call | solution.py:638
  449.5 5.3 all-to-all-start.2
  458.0 9.6 %excess_rows.1 = (bf16[1,208,384]{2,1,0:T(8,128)(2,1)S(1)}, f32[8,128]{1,0:T(8,128)S(1)}) custom-call(s32[1]{0:T(128)} %dynamic_slice.6.counts_ref, s32[2048]{0:T(1024)S(1)} %bitcast.47, s32[8]{0:T(128)S(1)} %broadcast_minimum_fusion.1.live_ref, f32[49152,128]{1,0:T(8,128)} %bitcast.49, f32[8,128]{1,0:T(8,128)S(1)} %add.197.loss_ref, ...), custom_call_target="tpu_custom_call" | custom-call | bytes 80000000 | tf_op jit(solution)/shard_map/excess_rows/pallas_call | solution.py:619
  467.7 39.0 %outgoing.6 = (bf16[16,200,896]{2,1,0:T(8,128)(2,1)S(1)}, f32[8,128]{1,0:T(8,128)S(1)}) custom-call(s32[16]{0:T(128)S(1)} %convert_element_type.79.counts_ref, s32[32768]{0:T(1024)S(1)} %broadcast_minimum_fusion.place_ref, f32[49152,128]{1,0:T(8,128)} %bitcast.50, f32[8,128]{1,0:T(8,128)S(1)} %get-tuple-element.101.refs_0_.refs_1_), custom_call_target="tpu_custom_call" | custom-call | bytes 80000000 | tf_op jit(solution)/shard_map/outgoing/pallas_call | solution.py:638
  510.1 5.1 all-to-all-start.4
  515.3 30.1 %relation_sums.1 = (f32[6400,128]{1,0:T(8,128)}, f32[8,128]{1,0:T(8,128)S(1)}) custom-call(s32[8192]{0:T(1024)S(1)} %copy-done.13, f32[3,16384,128]{2,1,0:T(8,128)} %get-tuple-element.95.grad, bf16[8,128]{1,0:T(8,128)(2,1)S(1)} %slice_bitcast_fusion.1.refs_0_, f32[8,128]{1,0:T(8,128)S(1)} %get-tuple-element.101.refs_0_.refs_1_, ...), custom_call_target="tpu_custom_call" | custom-call | bytes 120000000 | tf_op jit(solution)/shard_map/relation_sums/pallas_call | solution.py:721
  547.4 30.0 %collect.2 = (f32[15888,128]{1,0:T(8,128)}, f32[8,128]{1,0:T(8,128)}) custom-call(s32[16]{0:T(128)} %get-tuple-element.135.counts_ref, s32[32768]{0:T(1024)} %bitcast.58, bf16[16,200,384]{2,1,0:T(8,128)(2,1)} %copy-done.19, f32[8,128]{1,0:T(8,128)} %copy-done.15), custom_call_target="tpu_custom_call" | custom-call | bytes 120000000 | tf_op jit(solution)/shard_map/collect/pallas_call | solution.py:689
  578.1 19.0 %outgoing.7 = (bf16[16,200,384]{2,1,0:T(8,128)(2,1)}, f32[8,128]{1,0:T(8,128)S(1)}) custom-call(s32[16]{0:T(128)S(1)} %convert_element_type.79.counts_ref, s32[32768]{0:T(1024)S(1)} %broadcast_minimum_fusion.place_ref, f32[49152,128]{1,0:T(8,128)} %bitcast.51, f32[8,128]{1,0:T(8,128)S(1)} %copy-done.16), custom_call_target="tpu_custom_call" | custom-call | bytes 80000000 | tf_op jit(solution)/shard_map/outgoing/pallas_call | solution.py:638
  598.3 49.3 %reduce-scatter.2.cloned.1.call-done = f32[400,128]{1,0:T(8,128)} async-done(((f32[6400,128]{1,0:T(8,128)}), f32[400,128]{1,0:T(8,128)}) %reduce-scatter.2.cloned.1.call-update) | async-done | bytes 204816 | tf_op jit(solution)/shard_map/reduce_scatter | solution.py:973
  652.1 8.8 %all-to-all-done.4.came_ref = bf16[16,200,896]{2,1,0:T(8,128)(2,1)} async-done(((bf16[16,200,896]{2,1,0:T(8,128)(2,1)}), bf16[16,200,896]{2,1,0:T(8,128)(2,1)}, u32[]{:S(2)}, u32[]{:S(2)}) %all-to-all-start.4) | async-done | bytes 5734432 | tf_op jit(solution)/shard_map/all_to_all | solution.py:954
  660.9 4.8 all-to-all-start.3
  669.0 58.4 %collect.3 = (f32[15888,128]{1,0:T(8,128)}, f32[8,128]{1,0:T(8,128)}) custom-call(s32[16]{0:T(128)} %get-tuple-element.135.counts_ref, s32[32768]{0:T(1024)} %bitcast.59, bf16[16,200,896]{2,1,0:T(8,128)(2,1)} %all-to-all-done.4.came_ref, f32[15888,128]{1,0:T(8,128)} %get-tuple-element.109.refs_0_, f32[8,128]{1,0:T(8,128)} %copy-done.14), custom_call_target="tpu_custom_call", output_to_operand_aliasing={{0}: (3, {})} | custom-call | bytes 120000000 | tf_op jit(solution)/shard_map/collect/pallas_call | solution.py:689
  729.4 3.6 all-to-all-done.3.came_ref
  736.2 37.6 %finish_entities.1 = (f32[200,7936]{1,0:T(8,128)}, f32[200,7936]{1,0:T(8,128)}, f32[200,7936]{1,0:T(8,128)}, f32[8,128]{1,0:T(8,128)}) custom-call(s32[16]{0:T(128)} %get-tuple-element.135.counts_ref, s32[32768]{0:T(1024)} %bitcast.60, bf16[16,200,384]{2,1,0:T(8,128)(2,1)} %copy-done.20, bf16[16,208,384]{2,1,0:T(8,128)(2,1)S(1)} %get-tuple-element.140.last_ref, ...), custom_call_target="tpu_custom_call" | custom-call | bytes 60000000 | tf_op jit(solution)/shard_map/finish_entities/pallas_call | solution.py:794
  (162 shorter events, 62.4 us)
Async XLA Ops:
  7.2 183.1 %all-gather.10.cloned.1.call-start = ((), (), s32[]{:S(2)}) async-start(), calls=%async_computation.9 | async-start | bytes 36765696 | tf_op jit(solution)/shard_map/all_gather | solution.py:858
  16.0 272.0 %all-gather.8.cloned.1.call-start = ((), (), s32[]{:S(2)}) async-start(), calls=%async_computation.8 | async-start | bytes 19427328 | tf_op jit(solution)/shard_map/all_gather | solution.py:858
  33.4 13.3 %copy-start.28 = (f32[3200]{0:T(1024)S(1)}, f32[3200]{0:T(1024)}, u32[]{:S(2)}) copy-start(f32[3200]{0:T(1024)} %param.22) | copy-start | bytes 38404
  234.8 5.9 copy-start.2
  234.8 7.3 copy-start.29
  234.8 7.4 copy-start.13
  240.7 37.5 %collective-permute-start = (bf16[96,8192]{1,0:T(8,128)(2,1)}, bf16[96,8192]{1,0:T(8,128)(2,1)}, u32[]{:S(2)}, u32[]{:S(2)}) collective-permute-start(bf16[96,8192]{1,0:T(8,128)(2,1)} %get-tuple-element.77.refs_0_), channel_id=1, source_target_pairs={{0,1},{1,0},{2,3},{3,2},{4,5},{5,4},{6,7},{7,6},{8,9},{9,8},{10,11... | collective-permute-start | bytes 4718600 | tf_op jit(solution)/shard_map/ppermute | solution.py:870
  242.3 18.6 %slice-start = ((s8[12587008]{0:T(1024)(128)(4,1)}), s8[4194304]{0:T(1024)(128)(4,1)S(1)}, s32[]{:S(2)}) async-start(s8[12587008]{0:T(1024)(128)(4,1)} %bitcast.39), calls=%async_computation.10 | async-start | bytes 8388608
  242.3 18.6 %slice-start.1 = ((s8[12587008]{0:T(1024)(128)(4,1)}), s8[4194304]{0:T(1024)(128)(4,1)S(1)}, s32[]{:S(2)}) async-start(s8[12587008]{0:T(1024)(128)(4,1)} %bitcast.39), calls=%async_computation.11 | async-start | bytes 8388608
  242.3 18.6 %slice-start.2 = ((s8[12587008]{0:T(1024)(128)(4,1)}), s8[4194304]{0:T(1024)(128)(4,1)S(1)}, s32[]{:S(2)}) async-start(s8[12587008]{0:T(1024)(128)(4,1)} %bitcast.39), calls=%async_computation.12 | async-start | bytes 8388608
  242.3 18.6 %slice-start.3 = ((s8[12587008]{0:T(1024)(128)(4,1)}), s8[4096]{0:T(1024)(128)(4,1)S(1)}, s32[]{:S(2)}) async-start(s8[12587008]{0:T(1024)(128)(4,1)} %bitcast.39), calls=%async_computation.13 | async-start | bytes 8192
  267.6 65.7 %copy-start.8 = (bf16[160,8192]{1,0:T(8,128)(2,1)}, bf16[160,8192]{1,0:T(8,128)(2,1)S(1)}, u32[]{:S(2)}) copy-start(bf16[160,8192]{1,0:T(8,128)(2,1)S(1)} %get-tuple-element.85.refs_1_) | copy-start | bytes 7864324
  267.6 100.0 %collective-permute-start.1 = (bf16[160,8192]{1,0:T(8,128)(2,1)S(1)}, bf16[160,8192]{1,0:T(8,128)(2,1)}, u32[]{:S(2)}, u32[]{:S(2)}) collective-permute-start(bf16[160,8192]{1,0:T(8,128)(2,1)S(1)} %get-tuple-element.85.refs_1_), channel_id=1, source_target_pairs={{0,1},{1,0},{2,3},{3,2},{4,5},{5,4},{6,7},{7,6},{8,9},{9,8},{10,11... | collective-permute-start | bytes 7864328 | tf_op jit(solution)/shard_map/ppermute | solution.py:870
  288.1 45.3 %copy-start.4 = (f32[8192,128]{1,0:T(8,128)S(1)}, f32[8192,128]{1,0:T(8,128)}, u32[]{:S(2)}) copy-start(f32[8192,128]{1,0:T(8,128)} %copy-done.3) | copy-start | bytes 12582916
  333.3 4.9 copy-start
  333.4 8.6 %copy-start.23 = (s32[256,128]{1,0:T(8,128)S(1)}, s32[256,128]{1,0:T(8,128)}, u32[]{:S(2)}) copy-start(s32[256,128]{1,0:T(8,128)} %get-tuple-element.132) | copy-start | bytes 393220
  340.5 31.9 %collective-permute-start.3 = (bf16[2,80,4096]{2,1,0:T(8,128)(2,1)}, bf16[2,80,4096]{2,1,0:T(8,128)(2,1)}, u32[]{:S(2)}, u32[]{:S(2)}) collective-permute-start(bf16[2,80,4096]{2,1,0:T(8,128)(2,1)} %get-tuple-element.91.refs_2_), channel_id=1, source_target_pairs={{0,1},{1,0},{2,3},{3,2},{4,5},{5,4},{6,7},{7,6},{8,9},{9,8},{10,11... | collective-permute-start | bytes 3932168 | tf_op jit(solution)/shard_map/ppermute | solution.py:870
  356.2 10.8 %all-to-all-start.1 = ((s32[16,1,2176]{2,1,0:T(1,128)}), s32[16,1,2176]{2,1,0:T(1,128)S(1)}, u32[]{:S(2)}, u32[]{:S(2)}) async-start(s32[16,1,2176]{2,1,0:T(1,128)} %all_to_all.20), calls=%async_computation.1 | async-start | bytes 278528 | tf_op jit(solution)/shard_map/all_to_all | solution.py:917
  361.3 38.5 %collective-permute-start.2 = (bf16[2,80,4096]{2,1,0:T(8,128)(2,1)}, bf16[2,80,4096]{2,1,0:T(8,128)(2,1)}, u32[]{:S(2)}, u32[]{:S(2)}) collective-permute-start(bf16[2,80,4096]{2,1,0:T(8,128)(2,1)} %copy-done.11), channel_id=1, source_target_pairs={{0,1},{1,0},{2,3},{3,2},{4,5},{5,4},{6,7},{7,6},{8,9},{9,8},{10,11... | collective-permute-start | bytes 3932168 | tf_op jit(solution)/shard_map/ppermute | solution.py:870
  449.5 5.3 copy-start.22
  449.5 8.5 %copy-start.32 = (s32[8]{0:T(128)S(1)}, s32[8]{0:T(128)}, u32[]{:S(2)}) copy-start(s32[8]{0:T(128)} %live_ref.3) | copy-start | bytes 100
  449.5 8.5 %copy-start.30 = (f32[8,128]{1,0:T(8,128)S(1)}, f32[8,128]{1,0:T(8,128)}, u32[]{:S(2)}) copy-start(f32[8,128]{1,0:T(8,128)} %get-tuple-element.98) | copy-start | bytes 12292
  449.5 8.5 %copy-start.31 = (f32[8,128]{1,0:T(8,128)S(1)}, f32[8,128]{1,0:T(8,128)}, u32[]{:S(2)}) copy-start(f32[8,128]{1,0:T(8,128)} %get-tuple-element.99) | copy-start | bytes 12292
  449.5 60.6 %all-to-all-start.2 = ((bf16[16,200,384]{2,1,0:T(8,128)(2,1)}), bf16[16,200,384]{2,1,0:T(8,128)(2,1)S(1)}, u32[]{:S(2)}, u32[]{:S(2)}) async-start(bf16[16,200,384]{2,1,0:T(8,128)(2,1)} %get-tuple-element.96), calls=%async_computation.2 | async-start | bytes 4915200 | tf_op jit(solution)/shard_map/all_to_all | solution.py:954
  510.1 5.2 copy-start.19
  510.1 150.7 %all-to-all-start.4 = ((bf16[16,200,896]{2,1,0:T(8,128)(2,1)}), bf16[16,200,896]{2,1,0:T(8,128)(2,1)}, u32[]{:S(2)}, u32[]{:S(2)}) async-start(bf16[16,200,896]{2,1,0:T(8,128)(2,1)} %copy-done.6), calls=%async_computation.5 | async-start | bytes 11468800 | tf_op jit(solution)/shard_map/all_to_all | solution.py:954
  515.2 132.3 %reduce-scatter.2.cloned.1.call-start = ((), (), s32[]{:S(2)}) async-start(), calls=%async_computation.6 | async-start | bytes 3481600 | tf_op jit(solution)/shard_map/reduce_scatter | solution.py:973
  546.0 188.3 %all-gather.6.cloned.1.call-start = ((), (), s32[]{:S(2)}) async-start(), calls=%async_computation.7 | async-start | bytes 2715648 | tf_op jit(solution)/shard_map/all_gather | solution.py:977
  651.5 9.4 %copy-start.14 = (f32[8,128]{1,0:T(8,128)}, f32[8,128]{1,0:T(8,128)S(1)}, u32[]{:S(2)}) copy-start(f32[8,128]{1,0:T(8,128)S(1)} %slice.124.refs_0_.refs_1_) | copy-start | bytes 12292
  652.1 14.9 %copy-start.24 = (f32[400,128]{1,0:T(8,128)S(1)}, f32[400,128]{1,0:T(8,128)}, u32[]{:S(2)}) copy-start(f32[400,128]{1,0:T(8,128)} %reduce-scatter.2.cloned.1.call-done) | copy-start | bytes 614404
  660.9 6.2 copy-start.21
  660.9 72.2 %all-to-all-start.3 = ((bf16[16,200,384]{2,1,0:T(8,128)(2,1)}), bf16[16,200,384]{2,1,0:T(8,128)(2,1)S(1)}, u32[]{:S(2)}, u32[]{:S(2)}) async-start(bf16[16,200,384]{2,1,0:T(8,128)(2,1)} %get-tuple-element.107), calls=%async_computation.4 | async-start | bytes 4915200 | tf_op jit(solution)/shard_map/all_to_all | solution.py:954
  (17 other events, 27.0 us)
Sparse Core Ops, SparseCore 0:
  16.2 174.0 all-gather.9
  191.9 96.1 all-gather.7
  546.2 101.3 reduce-scatter.1
  650.9 69.5 all-gather.5

commit v17 on v15

--- a/solution.py
+++ b/solution.py
@@ -786,7 +786,7 @@
 ):
     width, ent_rows = weights.shape
     capacity = row_list.shape[1]
-    cols = 1024
+    cols = 2048
     steps = pl.cdiv(ent_rows, cols)
     n = len(slices)
     table = pl.BlockSpec((width, cols), lambda i: (0, i))

time: 791 us -> 787 us (level)
  no operation moved by 1% of the time
where the time goes in v17:
time: 787 us; the launch traced here: 784 us
  Pallas kernels  423 us (54%)
  waiting for transfers between devices  231 us (29%)
  local copies, waits for them, and re-layouts  40.7 us (5%)
  other arithmetic  29.1 us (4%)
  starting transfers between devices  25.2 us (3%)
  between operations  22.3 us (3%)
  matrix products  12.3 us (2%)
    all_gather x2, waiting for transfers between devices, shards(): dense.append(lax.all_gather(sent, 'edge', axis=0, tiled=False))  149 us
    pallas_call x2, Pallas kernels, fetch(): pl.pallas_call(functools.partial(fetch_kernel, capacity, moves, ent_rows)...  89.7 us
    pallas_call x2, Pallas kernels, collect(): pl.pallas_call(functools.partial(collect_kernel, slices, capacity, begin,...  88.5 us
    pallas_call x3, Pallas kernels, outgoing(): pl.pallas_call(functools.partial(outgoing_kernel, slices, capacity, begin...  81.6 us
    pallas_call x2, Pallas kernels, block_math(): pl.pallas_call(functools.partial(block_kernel, slices, n_col, half), out_...  52.1 us
    reduce_scatter x1, waiting for transfers between devices, shards(): lax.psum_scatter(rel_terms, 'edge', scatter_dimension=0, tiled=True)  47.3 us
    pallas_call x1, Pallas kernels, finish_entities(): pl.pallas_call(functools.partial(finish_kernel, slices, capacity, begin,...  37.7 us
    pallas_call x1, Pallas kernels, relation_sums(): pl.pallas_call(functools.partial(relation_sums_kernel, n), out_shape=[jax...  31.1 us
  transfers between devices with their start and end apart: 12, of which 10 were waited for; matrix products, arithmetic and copies ran while one was open for 6% of the time, Pallas kernels for 43%

profile of v17, /device:TPU:16, one launch (start us, length us, event | category | flops | bytes accessed | tf_op | source)
XLA Modules:
  0.0 783.5 jit_solution(14865903605902952649)
XLA Ops:
  8.2 3.1 convert.20
  24.6 8.8 %broadcast_multiply_fusion = bf16[4,128,24576]{2,1,0:T(8,128)(2,1)} fusion(bf16[128,24576]{1,0:T(8,128)(2,1)S(1)} %fusion.2, bf16[4,24576]{1,0:T(4,128)(2,1)S(1)} %pad_maximum_fusion), kind=kLoop, calls=%fused_computation.3 | loop fusion | flops 12582912 | bytes 31653888 | tf_op jit(solution)/shard_map/mul | solution.py:93
  33.4 11.8 %fusion.8 = s32[256,512]{1,0:T(8,128)S(1)} fusion(bf16[512,24576]{1,0:T(8,128)(2,1)} %bitcast.57, s32[24576]{0:T(1024)S(1)} %get-tuple-element.136), kind=kOutput, calls=%fused_computation.17 | convolution fusion | flops 6448873472 | bytes 25788416 | tf_op jit(solution)/shard_map/dot_general | solution.py:94
  50.4 139.9 %all-gather.10.cloned.1.call-done = bf16[2048,8448]{1,0:T(8,128)(2,1)} async-done(((bf16[128,8448]{1,0:T(8,128)(2,1)}), bf16[2048,8448]{1,0:T(8,128)(2,1)}) %all-gather.10.cloned.1.call-update) | async-done | bytes 34603024 | tf_op jit(solution)/shard_map/all_gather | solution.py:858
  190.3 44.5 %fetch_rows.2.neg_ref.head_ref.tail_ref = f32[24584,128]{1,0:T(8,128)S(1)} custom-call(s32[16]{0:T(128)S(1)} %convert_element_type.79.counts_ref, s32[32768]{0:T(1024)S(1)} %bitcast.42, s32[32768]{0:T(1024)S(1)} %bitcast.45, bf16[16,128,8448]{2,1,0:T(8,128)(2,1)} %bitcast.54, s32[16,128]{1,0:T(8,128)S(1)} %broadcast_in_dim.35.refs_0_), custom_call_target="tpu_custom_call" | custom-call | bytes 170000000 | tf_op jit(solution)/shard_map/fetch_rows/pallas_call | solution.py:231
  234.8 5.9 negatives.1
  242.3 16.6 %relation_rows.1 = (f32[8192,128]{1,0:T(8,128)S(1)}, f32[8192,128]{1,0:T(8,128)S(1)}) custom-call(s32[8192]{0:T(1024)S(1)} %fusion.28.ids_ref, f32[16,256]{1,0:T(8,128)S(1)} %pad.17.scale_ref, bf16[16,128,8448]{2,1,0:T(8,128)(2,1)} %bitcast.55, bf16[16,128,8448]{2,1,0:T(8,128)(2,1)} %bitcast.56, f32[1,8192]{1,0:T(1,128)S(1)} %get-tuple-element.78.refs_2_.refs_1_), custom_call_target="tpu_custom_call" | custom-call | bytes 80000000 | tf_op jit(solution)/shard_map/relation_rows/pallas_call | solution.py:139
  261.0 3.2 edges.1
  268.3 9.9 %collective-permute-done.refs_3_ = bf16[96,8192]{1,0:T(8,128)(2,1)} collective-permute-done((bf16[96,8192]{1,0:T(8,128)(2,1)}, bf16[96,8192]{1,0:T(8,128)(2,1)}, u32[]{:S(2)}, u32[]{:S(2)}) %collective-permute-start) | collective-permute-done | bytes 1572896 | tf_op jit(solution)/shard_map/ppermute | solution.py:870
  278.8 9.3 %all-gather.8.cloned.1.call-done = bf16[1152,7936]{1,0:T(8,128)(2,1)} async-done(((bf16[72,7936]{1,0:T(8,128)(2,1)}), bf16[1152,7936]{1,0:T(8,128)(2,1)}) %all-gather.8.cloned.1.call-update) | async-done | bytes 18284560 | tf_op jit(solution)/shard_map/all_gather | solution.py:858
  288.1 45.2 %fetch_rows.3.head_ref.tail_ref.neg_ref = f32[24584,128]{1,0:T(8,128)S(1)} custom-call(s32[16]{0:T(128)S(1)} %convert_element_type.79.counts_ref, s32[32768]{0:T(1024)S(1)} %bitcast.43, s32[32768]{0:T(1024)S(1)} %bitcast.46, bf16[16,72,7936]{2,1,0:T(8,128)(2,1)} %bitcast.58, bf16[8,128]{1,0:T(8,128)(2,1)S(1)} %slice.120.refs_0_), custom_call_target="tpu_custom_call" | custom-call | bytes 170000000 | tf_op jit(solution)/shard_map/fetch_rows/pallas_call | solution.py:231
  333.3 4.6 last_slice.2
  342.0 4.6 copy-done.1
  356.2 5.1 all-to-all-start.1
  362.0 5.1 all-to-all-done.1
  367.8 4.6 collective-permute-done.3.refs_5_
  372.4 26.0 %block_math.2 = (f32[3,16384,128]{2,1,0:T(8,128)}, f32[8,128]{1,0:T(8,128)}) custom-call(s32[1]{0:T(128)} %bitcast.10.me_ref, s32[8]{0:T(128)} %live_ref.3, bf16[96,8192]{1,0:T(8,128)(2,1)} %get-tuple-element.77.refs_0_, bf16[160,8192]{1,0:T(8,128)(2,1)} %copy-done.8, bf16[2,80,4096]{2,1,0:T(8,128)(2,1)} %get-tuple-element.91.refs_2_, ...), custom_call_target="tpu_custom_call" | custom-call | flops 6710886400 | bytes 120000000 | tf_op jit(solution)/shard_map/block_math/pallas_call | solution.py:525
  399.9 26.1 %block_math.3 = (f32[3,16384,128]{2,1,0:T(8,128)}, f32[8,128]{1,0:T(8,128)}) custom-call(s32[1]{0:T(128)} %bitcast.10.me_ref, s32[8]{0:T(128)} %live_ref.3, bf16[96,8192]{1,0:T(8,128)(2,1)} %get-tuple-element.77.refs_0_, bf16[160,8192]{1,0:T(8,128)(2,1)} %copy-done.8, bf16[2,80,4096]{2,1,0:T(8,128)(2,1)} %copy-done.11, ...), custom_call_target="tpu_custom_call", output_to_operand_aliasing={{0}: (12, {})} | custom-call | flops 6710886400 | bytes 120000000 | tf_op jit(solution)/shard_map/block_math/pallas_call | solution.py:525
  426.0 23.5 %outgoing.5 = (bf16[16,200,384]{2,1,0:T(8,128)(2,1)}, f32[8,128]{1,0:T(8,128)S(1)}) custom-call(s32[16]{0:T(128)S(1)} %convert_element_type.79.counts_ref, s32[32768]{0:T(1024)S(1)} %broadcast_minimum_fusion.place_ref, f32[49152,128]{1,0:T(8,128)} %bitcast.49), custom_call_target="tpu_custom_call" | custom-call | bytes 80000000 | tf_op jit(solution)/shard_map/outgoing/pallas_call | solution.py:638
  449.5 5.3 all-to-all-start.2
  458.0 9.6 %excess_rows.1 = (bf16[1,208,384]{2,1,0:T(8,128)(2,1)S(1)}, f32[8,128]{1,0:T(8,128)S(1)}) custom-call(s32[1]{0:T(128)} %dynamic_slice.6.counts_ref, s32[2048]{0:T(1024)S(1)} %bitcast.48, s32[8]{0:T(128)S(1)} %broadcast_minimum_fusion.1.live_ref, f32[49152,128]{1,0:T(8,128)} %bitcast.50, f32[8,128]{1,0:T(8,128)S(1)} %add.197.loss_ref, ...), custom_call_target="tpu_custom_call" | custom-call | bytes 80000000 | tf_op jit(solution)/shard_map/excess_rows/pallas_call | solution.py:619
  468.3 39.0 %outgoing.6 = (bf16[16,200,896]{2,1,0:T(8,128)(2,1)S(1)}, f32[8,128]{1,0:T(8,128)S(1)}) custom-call(s32[16]{0:T(128)S(1)} %convert_element_type.79.counts_ref, s32[32768]{0:T(1024)S(1)} %broadcast_minimum_fusion.place_ref, f32[49152,128]{1,0:T(8,128)} %bitcast.51, f32[8,128]{1,0:T(8,128)S(1)} %get-tuple-element.101.refs_0_.refs_1_), custom_call_target="tpu_custom_call" | custom-call | bytes 80000000 | tf_op jit(solution)/shard_map/outgoing/pallas_call | solution.py:638
  510.1 5.8 all-to-all-start.4
  516.0 31.1 %relation_sums.1 = (f32[6400,128]{1,0:T(8,128)S(1)}, f32[8,128]{1,0:T(8,128)S(1)}) custom-call(s32[8192]{0:T(1024)S(1)} %copy-done.15, f32[3,16384,128]{2,1,0:T(8,128)} %get-tuple-element.95.grad, bf16[8,128]{1,0:T(8,128)(2,1)S(1)} %slice_bitcast_fusion.1.refs_0_, f32[8,128]{1,0:T(8,128)S(1)} %get-tuple-element.101.refs_0_.refs_1_, ...), custom_call_target="tpu_custom_call" | custom-call | bytes 120000000 | tf_op jit(solution)/shard_map/relation_sums/pallas_call | solution.py:721
  552.1 30.0 %collect.2 = (f32[15888,128]{1,0:T(8,128)}, f32[8,128]{1,0:T(8,128)}) custom-call(s32[16]{0:T(128)} %get-tuple-element.135.counts_ref, s32[32768]{0:T(1024)} %bitcast.60, bf16[16,200,384]{2,1,0:T(8,128)(2,1)} %copy-done.21, f32[8,128]{1,0:T(8,128)} %copy-done.17), custom_call_target="tpu_custom_call" | custom-call | bytes 120000000 | tf_op jit(solution)/shard_map/collect/pallas_call | solution.py:689
  582.7 19.1 %outgoing.7 = (bf16[16,200,384]{2,1,0:T(8,128)(2,1)}, f32[8,128]{1,0:T(8,128)S(1)}) custom-call(s32[16]{0:T(128)S(1)} %convert_element_type.79.counts_ref, s32[32768]{0:T(1024)S(1)} %broadcast_minimum_fusion.place_ref, f32[49152,128]{1,0:T(8,128)} %bitcast.52, f32[8,128]{1,0:T(8,128)S(1)} %copy-done.18), custom_call_target="tpu_custom_call" | custom-call | bytes 80000000 | tf_op jit(solution)/shard_map/outgoing/pallas_call | solution.py:638
  603.0 47.3 %reduce-scatter.2.cloned.1.call-done = f32[200,200]{1,0:T(8,128)} async-done(((f32[3200,200]{1,0:T(8,128)}), f32[200,200]{1,0:T(8,128)}) %reduce-scatter.2.cloned.1.call-update) | async-done | bytes 160016 | tf_op jit(solution)/shard_map/reduce_scatter | solution.py:974
  654.8 6.7 all-to-all-done.4.came_ref
  661.5 4.7 all-to-all-start.3
  668.5 58.5 %collect.3 = (f32[15888,128]{1,0:T(8,128)}, f32[8,128]{1,0:T(8,128)}) custom-call(s32[16]{0:T(128)} %get-tuple-element.135.counts_ref, s32[32768]{0:T(1024)} %bitcast.61, bf16[16,200,896]{2,1,0:T(8,128)(2,1)} %all-to-all-done.4.came_ref, f32[15888,128]{1,0:T(8,128)} %get-tuple-element.109.refs_0_, f32[8,128]{1,0:T(8,128)} %copy-done.16), custom_call_target="tpu_custom_call", output_to_operand_aliasing={{0}: (3, {})} | custom-call | bytes 120000000 | tf_op jit(solution)/shard_map/collect/pallas_call | solution.py:689
  728.7 6.1 all-to-all-done.3.came_ref
  738.0 37.7 %finish_entities.1 = (f32[200,7936]{1,0:T(8,128)}, f32[200,7936]{1,0:T(8,128)}, f32[200,7936]{1,0:T(8,128)}, f32[8,128]{1,0:T(8,128)}) custom-call(s32[16]{0:T(128)} %get-tuple-element.135.counts_ref, s32[32768]{0:T(1024)} %bitcast.62, bf16[16,200,384]{2,1,0:T(8,128)(2,1)} %copy-done.22, bf16[16,208,384]{2,1,0:T(8,128)(2,1)S(1)} %get-tuple-element.140.last_ref, ...), custom_call_target="tpu_custom_call" | custom-call | bytes 60000000 | tf_op jit(solution)/shard_map/finish_entities/pallas_call | solution.py:794
  (178 shorter events, 64.4 us)
Async XLA Ops:
  7.2 183.1 %all-gather.10.cloned.1.call-start = ((), (), s32[]{:S(2)}) async-start(), calls=%async_computation.9 | async-start | bytes 36765696 | tf_op jit(solution)/shard_map/all_gather | solution.py:858
  16.0 272.0 %all-gather.8.cloned.1.call-start = ((), (), s32[]{:S(2)}) async-start(), calls=%async_computation.8 | async-start | bytes 19427328 | tf_op jit(solution)/shard_map/all_gather | solution.py:858
  33.4 13.3 %copy-start.36 = (f32[3200]{0:T(1024)S(1)}, f32[3200]{0:T(1024)}, u32[]{:S(2)}) copy-start(f32[3200]{0:T(1024)} %param.22) | copy-start | bytes 38404
  234.8 7.5 copy-start.15
  240.6 37.5 %collective-permute-start = (bf16[96,8192]{1,0:T(8,128)(2,1)}, bf16[96,8192]{1,0:T(8,128)(2,1)}, u32[]{:S(2)}, u32[]{:S(2)}) collective-permute-start(bf16[96,8192]{1,0:T(8,128)(2,1)} %get-tuple-element.77.refs_0_), channel_id=1, source_target_pairs={{0,1},{1,0},{2,3},{3,2},{4,5},{5,4},{6,7},{7,6},{8,9},{9,8},{10,11... | collective-permute-start | bytes 4718600 | tf_op jit(solution)/shard_map/ppermute | solution.py:870
  242.3 18.6 %slice-start = ((s8[12587008]{0:T(1024)(128)(4,1)}), s8[4194304]{0:T(1024)(128)(4,1)S(1)}, s32[]{:S(2)}) async-start(s8[12587008]{0:T(1024)(128)(4,1)} %bitcast.40), calls=%async_computation.10 | async-start | bytes 8388608
  242.3 18.6 %slice-start.1 = ((s8[12587008]{0:T(1024)(128)(4,1)}), s8[4194304]{0:T(1024)(128)(4,1)S(1)}, s32[]{:S(2)}) async-start(s8[12587008]{0:T(1024)(128)(4,1)} %bitcast.40), calls=%async_computation.11 | async-start | bytes 8388608
  242.3 18.6 %slice-start.2 = ((s8[12587008]{0:T(1024)(128)(4,1)}), s8[4194304]{0:T(1024)(128)(4,1)S(1)}, s32[]{:S(2)}) async-start(s8[12587008]{0:T(1024)(128)(4,1)} %bitcast.40), calls=%async_computation.12 | async-start | bytes 8388608
  242.3 18.6 %slice-start.3 = ((s8[12587008]{0:T(1024)(128)(4,1)}), s8[4096]{0:T(1024)(128)(4,1)S(1)}, s32[]{:S(2)}) async-start(s8[12587008]{0:T(1024)(128)(4,1)} %bitcast.40), calls=%async_computation.13 | async-start | bytes 8192
  267.7 65.6 %copy-start.8 = (bf16[160,8192]{1,0:T(8,128)(2,1)}, bf16[160,8192]{1,0:T(8,128)(2,1)S(1)}, u32[]{:S(2)}) copy-start(bf16[160,8192]{1,0:T(8,128)(2,1)S(1)} %get-tuple-element.85.refs_1_) | copy-start | bytes 7864324
  267.7 100.1 %collective-permute-start.1 = (bf16[160,8192]{1,0:T(8,128)(2,1)S(1)}, bf16[160,8192]{1,0:T(8,128)(2,1)}, u32[]{:S(2)}, u32[]{:S(2)}) collective-permute-start(bf16[160,8192]{1,0:T(8,128)(2,1)S(1)} %get-tuple-element.85.refs_1_), channel_id=1, source_target_pairs={{0,1},{1,0},{2,3},{3,2},{4,5},{5,4},{6,7},{7,6},{8,9},{9,8},{10,11... | collective-permute-start | bytes 7864328 | tf_op jit(solution)/shard_map/ppermute | solution.py:870
  288.1 45.2 %copy-start.4 = (f32[8192,128]{1,0:T(8,128)S(1)}, f32[8192,128]{1,0:T(8,128)}, u32[]{:S(2)}) copy-start(f32[8192,128]{1,0:T(8,128)} %copy-done.3) | copy-start | bytes 12582916
  333.3 8.6 %copy-start.29 = (s32[256,128]{1,0:T(8,128)S(1)}, s32[256,128]{1,0:T(8,128)}, u32[]{:S(2)}) copy-start(s32[256,128]{1,0:T(8,128)} %get-tuple-element.132) | copy-start | bytes 393220
  340.5 31.9 %collective-permute-start.3 = (bf16[2,80,4096]{2,1,0:T(8,128)(2,1)}, bf16[2,80,4096]{2,1,0:T(8,128)(2,1)}, u32[]{:S(2)}, u32[]{:S(2)}) collective-permute-start(bf16[2,80,4096]{2,1,0:T(8,128)(2,1)} %get-tuple-element.91.refs_2_), channel_id=1, source_target_pairs={{0,1},{1,0},{2,3},{3,2},{4,5},{5,4},{6,7},{7,6},{8,9},{9,8},{10,11... | collective-permute-start | bytes 3932168 | tf_op jit(solution)/shard_map/ppermute | solution.py:870
  356.2 10.9 %all-to-all-start.1 = ((s32[16,1,2176]{2,1,0:T(1,128)}), s32[16,1,2176]{2,1,0:T(1,128)S(1)}, u32[]{:S(2)}, u32[]{:S(2)}) async-start(s32[16,1,2176]{2,1,0:T(1,128)} %all_to_all.20), calls=%async_computation.1 | async-start | bytes 278528 | tf_op jit(solution)/shard_map/all_to_all | solution.py:917
  361.4 38.5 %collective-permute-start.2 = (bf16[2,80,4096]{2,1,0:T(8,128)(2,1)}, bf16[2,80,4096]{2,1,0:T(8,128)(2,1)}, u32[]{:S(2)}, u32[]{:S(2)}) collective-permute-start(bf16[2,80,4096]{2,1,0:T(8,128)(2,1)} %copy-done.11), channel_id=1, source_target_pairs={{0,1},{1,0},{2,3},{3,2},{4,5},{5,4},{6,7},{7,6},{8,9},{9,8},{10,11... | collective-permute-start | bytes 3932168 | tf_op jit(solution)/shard_map/ppermute | solution.py:870
  449.5 8.5 %copy-start.40 = (s32[8]{0:T(128)S(1)}, s32[8]{0:T(128)}, u32[]{:S(2)}) copy-start(s32[8]{0:T(128)} %live_ref.3) | copy-start | bytes 100
  449.5 8.5 %copy-start.38 = (f32[8,128]{1,0:T(8,128)S(1)}, f32[8,128]{1,0:T(8,128)}, u32[]{:S(2)}) copy-start(f32[8,128]{1,0:T(8,128)} %get-tuple-element.98) | copy-start | bytes 12292
  449.5 8.5 %copy-start.39 = (f32[8,128]{1,0:T(8,128)S(1)}, f32[8,128]{1,0:T(8,128)}, u32[]{:S(2)}) copy-start(f32[8,128]{1,0:T(8,128)} %get-tuple-element.99) | copy-start | bytes 12292
  449.5 60.6 %all-to-all-start.2 = ((bf16[16,200,384]{2,1,0:T(8,128)(2,1)}), bf16[16,200,384]{2,1,0:T(8,128)(2,1)S(1)}, u32[]{:S(2)}, u32[]{:S(2)}) async-start(bf16[16,200,384]{2,1,0:T(8,128)(2,1)} %get-tuple-element.96), calls=%async_computation.2 | async-start | bytes 4915200 | tf_op jit(solution)/shard_map/all_to_all | solution.py:954
  454.8 12.9 %copy-start.26 = (s32[16,2048]{1,0:T(8,128)}, s32[16,2048]{1,0:T(8,128)S(1)}, u32[]{:S(2)}) copy-start(s32[16,2048]{1,0:T(8,128)S(1)} %reshape.781) | copy-start | bytes 393220
  510.1 151.4 %all-to-all-start.4 = ((bf16[16,200,896]{2,1,0:T(8,128)(2,1)}), bf16[16,200,896]{2,1,0:T(8,128)(2,1)}, u32[]{:S(2)}, u32[]{:S(2)}) async-start(bf16[16,200,896]{2,1,0:T(8,128)(2,1)} %copy-done.6), calls=%async_computation.5 | async-start | bytes 11468800 | tf_op jit(solution)/shard_map/all_to_all | solution.py:954
  515.9 134.4 %reduce-scatter.2.cloned.1.call-start = ((), (), s32[]{:S(2)}) async-start(), calls=%async_computation.6 | async-start | bytes 3481600 | tf_op jit(solution)/shard_map/reduce_scatter | solution.py:974
  549.9 186.2 %all-gather.6.cloned.1.call-start = ((), (), s32[]{:S(2)}) async-start(), calls=%async_computation.7 | async-start | bytes 2715648 | tf_op jit(solution)/shard_map/all_gather | solution.py:978
  582.7 70.1 %copy-start.14 = (bf16[1,208,384]{2,1,0:T(8,128)(2,1)S(1)}, bf16[1,208,384]{2,1,0:T(8,128)(2,1)}, u32[]{:S(2)}) copy-start(bf16[1,208,384]{2,1,0:T(8,128)(2,1)} %copy-done.13) | copy-start | bytes 479236
  654.2 7.4 copy-start.16
  654.8 12.7 %copy-start.23 = (f32[200,200]{1,0:T(8,128)S(1)}, f32[200,200]{1,0:T(8,128)}, u32[]{:S(2)}) copy-start(f32[200,200]{1,0:T(8,128)} %param.27) | copy-start | bytes 480004
  654.8 12.7 %copy-start.30 = (f32[200,200]{1,0:T(8,128)S(1)}, f32[200,200]{1,0:T(8,128)}, u32[]{:S(2)}) copy-start(f32[200,200]{1,0:T(8,128)} %reduce-scatter.2.cloned.1.call-done) | copy-start | bytes 480004
  654.8 12.7 %copy-start.31 = (f32[200,200]{1,0:T(8,128)S(1)}, f32[200,200]{1,0:T(8,128)}, u32[]{:S(2)}) copy-start(f32[200,200]{1,0:T(8,128)} %param.28) | copy-start | bytes 480004
  654.8 12.8 %copy-start.32 = (f32[200,200]{1,0:T(8,128)S(1)}, f32[200,200]{1,0:T(8,128)}, u32[]{:S(2)}) copy-start(f32[200,200]{1,0:T(8,128)} %param.29) | copy-start | bytes 480004
  661.5 73.3 %all-to-all-start.3 = ((bf16[16,200,384]{2,1,0:T(8,128)(2,1)}), bf16[16,200,384]{2,1,0:T(8,128)(2,1)S(1)}, u32[]{:S(2)}, u32[]{:S(2)}) async-start(bf16[16,200,384]{2,1,0:T(8,128)(2,1)} %get-tuple-element.107), calls=%async_computation.4 | async-start | bytes 4915200 | tf_op jit(solution)/shard_map/all_to_all | solution.py:954
  668.5 67.6 %copy-start.27 = (s32[16,2048]{1,0:T(8,128)S(1)}, s32[16,2048]{1,0:T(8,128)}, u32[]{:S(2)}) copy-start(s32[16,2048]{1,0:T(8,128)} %copy-done.26) | copy-start | bytes 393220
  (25 other events, 58.5 us)
Sparse Core Ops, SparseCore 0:
  16.2 174.0 all-gather.9
  191.9 96.1 all-gather.7
  550.0 100.2 reduce-scatter.1
  653.6 71.7 all-gather.5
